TPU v7x, 32 devices: a whole 2x2x4 slice. The times are simulated.
32 devices in a mesh: groups: 2 (over y), wide: 4 (over z), narrow: 4 (over x, core).
Axes of the slice: x: 2, y: 2, z: 4, core: 2. Of those that a mesh axis runs over, the one named last changes fastest.
Arguments:
- grid_state: bfloat16 [128, 128, 256], P(('groups', 'wide'), 'narrow'), parts along dimension 0, may hold values from -6 to 6
- boundary_rows: bfloat16 [1024, 256], P(('groups', 'wide', 'narrow')), parts along dimension 0, may hold values from -6 to 6
- row_count: int32 [32], P(('groups', 'wide', 'narrow')), parts along dimension 0, may hold values from 24 to 32, as said below
- target_x: int32 [1024], P(('groups', 'wide', 'narrow')), parts along dimension 0, may hold values from 0 to 63, as said below
- target_y: int32 [1024], P(('groups', 'wide', 'narrow')), parts along dimension 0, may hold values from 0 to 127, as said below
- g2m_mask: int32 [36, 32, 32], P(None, ('groups', 'wide'), 'narrow'), parts along dimension 1, may hold values 0 or 1
- mesh_cotangent: bfloat16 [32, 32, 256], P(('groups', 'wide'), 'narrow'), parts along dimension 0, may hold values from -6 to 6
- w_force: bfloat16 [256, 256], replicated, may hold values from -0.375 to 0.375
- w_embed: bfloat16 [256, 256], replicated, may hold values from -0.375 to 0.375
- w_message: bfloat16 [256, 256], replicated, may hold values from -0.375 to 0.375
- w_level_one: bfloat16 [256, 256], replicated, may hold values from -0.375 to 0.375
- w_level_two: bfloat16 [256, 256], replicated, may hold values from -0.375 to 0.375
Outputs:
- grad_state: bfloat16 [128, 128, 256], P(('groups', 'wide'), 'narrow'), parts along dimension 0
- grad_rows: bfloat16 [1024, 256], P(('groups', 'wide', 'narrow')), parts along dimension 0
- weight_grads: float32 [10, 256, 256], P('groups'), parts along dimension 0
There are 2 independent parts, one for each index of `groups`. A program takes and returns all parts, laid end to end along the dimension named above; an argument that names none is the same for every part. Nothing has to cross between parts.
Inputs may be any that keep to these rules, and one draw needn't show every extreme that they name: `row_count`: every tile has at least max(16, 24) live rows and tile 0 has 32. The rows of tile t = 4 * w + n target only cells whose second coordinate lies in [n * 32, (n + 1) * 32). Of one tile's live rows at most 16 target cells with the same value of target_x // 16, and tile 0 has exactly 16 such rows for some value. `target_y`: see target_x.
All inputs are finite; a program needn't handle non-finite values. No bound on the sum of `g2m_mask` on one device may be relied on, other than what follows from the above.
Results may differ from a plain program's by a relative error of at most 0.017.
Values may be sent and summed in bfloat16 or wider, within the bound.
No kernel may reach another device: no remote copies, remote signals or barrier semaphores. Data moves between devices by JAX's collectives and lax.ppermute only.
A program may use at most 64 MiB of HBM per device.

v0:
```python
import math

import jax
import jax.numpy as jnp
from jax import lax
from jax.sharding import PartitionSpec as P

CAP = 16


def padded_2(cells, sides, width):
    for axis, dim in sides:
        count = lax.axis_size(axis)
        ends = count - 1
        head = lax.slice_in_dim(cells, 0, width, axis=dim)
        tail = lax.slice_in_dim(cells, cells.shape[dim] - width, cells.shape[dim], axis=dim)
        cells = jnp.concatenate(
            [
                lax.ppermute(tail, axis, [(i, (i + 1) % count) for i in range(ends)]),
                cells,
                lax.ppermute(head, axis, [((i + 1) % count, i) for i in range(ends)]),
            ],
            axis=dim,
        )
    return cells


def silu_slope(argument):
    logistic = jax.nn.sigmoid(argument)
    return logistic * (1.0 + argument * (1.0 - logistic))


def gather_window(padded, window_mask):
    node_x = window_mask.shape[1]
    node_y = window_mask.shape[2]
    accumulated = jnp.zeros((node_x, node_y, padded.shape[2]), jnp.float32)
    for shift_x in range(6):
        for shift_y in range(6):
            window_piece = padded[
                shift_x : shift_x + 4 * node_x - 3 : 4, shift_y : shift_y + 4 * node_y - 3 : 4
            ]
            scale = window_mask[shift_x * 6 + shift_y].astype(jnp.float32)
            accumulated = accumulated + scale[:, :, None] * window_piece.astype(jnp.float32)
    return accumulated / 6.0


def spread_window(node_bar, window_mask):
    node_x, node_y, channels = node_bar.shape
    table = window_mask.astype(jnp.float32).reshape(6, 6, node_x, node_y)
    table = jnp.pad(table, ((0, 2), (0, 2), (0, 0), (0, 0)))
    summed = jnp.zeros((4 * node_x + 4, 4 * node_y + 4, channels), jnp.float32)
    for offset_x in range(2):
        for offset_y in range(2):
            scales = table[
                4 * offset_x : 4 * offset_x + 4, 4 * offset_y : 4 * offset_y + 4
            ].transpose(2, 0, 3, 1)
            placed = (scales[..., None] * node_bar[:, None, :, None, :]).reshape(
                4 * node_x, 4 * node_y, channels
            )
            summed = summed + jnp.pad(
                placed, ((4 * offset_x, 4 - 4 * offset_x), (4 * offset_y, 4 - 4 * offset_y), (0, 0))
            )
    return summed[: 4 * node_x + 2, : 4 * node_y + 2] / 6.0


def grid_forward(blended, w_embed, w_message):
    pre_embed = jnp.dot(blended, w_embed, preferred_element_type=jnp.float32)
    latent = (blended.astype(jnp.float32) + jax.nn.silu(pre_embed)).astype(jnp.bfloat16)
    pre_message = jnp.dot(latent, w_message, preferred_element_type=jnp.float32)
    message = jax.nn.silu(pre_message).astype(jnp.bfloat16)
    return (pre_embed, latent, pre_message, message)


def grid_backward(message_bar, blended, pre_embed, latent, pre_message, w_embed, w_message):
    pre_message_bar = (message_bar * silu_slope(pre_message)).astype(jnp.bfloat16)
    grad_message = jnp.dot(latent.T, pre_message_bar, preferred_element_type=jnp.float32)
    latent_bar = jnp.dot(pre_message_bar, w_message.T, preferred_element_type=jnp.float32)
    pre_embed_bar = (latent_bar * silu_slope(pre_embed)).astype(jnp.bfloat16)
    grad_embed = jnp.dot(blended.T, pre_embed_bar, preferred_element_type=jnp.float32)
    grad_state = (
        latent_bar + jnp.dot(pre_embed_bar, w_embed.T, preferred_element_type=jnp.float32)
    ).astype(jnp.bfloat16)
    return (grad_state, grad_embed, grad_message)


def mesh_backward(level_one, cotangent, w_level_one, w_level_two):
    node_x, node_y, channels = level_one.shape
    flat_one = level_one.reshape(-1, channels)
    pre_one = jnp.dot(flat_one, w_level_one, preferred_element_type=jnp.float32)
    state_one = flat_one.astype(jnp.float32) + jax.nn.silu(pre_one)
    pooled = (
        state_one.reshape(node_x // 2, 2, node_y // 2, 2, channels)
        .mean(axis=(1, 3))
        .astype(jnp.bfloat16)
    )
    flat_two = pooled.reshape(-1, channels)
    pre_two = jnp.dot(flat_two, w_level_two, preferred_element_type=jnp.float32)
    upstream = cotangent.astype(jnp.float32).reshape(node_x // 2, 2, node_y // 2, 2, channels)
    two_bar = upstream.sum(axis=(1, 3)).reshape(-1, channels)
    pre_two_bar = (two_bar * silu_slope(pre_two)).astype(jnp.bfloat16)
    grad_two = jnp.dot(flat_two.T, pre_two_bar, preferred_element_type=jnp.float32)
    pooled_bar = two_bar + jnp.dot(pre_two_bar, w_level_two.T, preferred_element_type=jnp.float32)
    one_bar = upstream + 0.25 * pooled_bar.reshape(node_x // 2, 1, node_y // 2, 1, channels)
    one_bar = one_bar.reshape(-1, channels)
    pre_one_bar = (one_bar * silu_slope(pre_one)).astype(jnp.bfloat16)
    grad_one = jnp.dot(flat_one.T, pre_one_bar, preferred_element_type=jnp.float32)
    level_bar = one_bar + jnp.dot(pre_one_bar, w_level_one.T, preferred_element_type=jnp.float32)
    return (level_bar.reshape(node_x, node_y, channels), grad_one, grad_two)


def local(
    grid_state,
    boundary_rows,
    row_count,
    target_x,
    target_y,
    g2m_mask,
    mesh_cotangent,
    w_force,
    w_embed,
    w_message,
    w_level_one,
    w_level_two,
):
    tile_x, tile_y, channels = grid_state.shape
    wide_count = lax.axis_size("wide")
    narrow_count = lax.axis_size("narrow")
    tile_cells = tile_x * tile_y
    slot_count = wide_count * CAP
    held_rows = boundary_rows.shape[0]
    live_rows = jnp.arange(held_rows) < row_count[0]
    destination = target_x // tile_x
    target_cell = target_x % tile_x * tile_y + target_y - lax.axis_index("narrow") * tile_y
    matches = (destination[:, None] == jnp.arange(wide_count)[None, :]) & live_rows[:, None]
    running = jnp.cumsum(matches.astype(jnp.int32), axis=0) - 1
    slot_index = jnp.sum(jnp.where(matches, running, 0), axis=1)
    send_slot = jnp.where(live_rows, destination * CAP + slot_index, slot_count)
    slot_cells = (
        jnp.full((slot_count,), tile_cells, jnp.int32).at[send_slot].set(target_cell, mode="drop")
    )
    outgoing = (
        jnp.zeros((slot_count, channels), jnp.bfloat16)
        .at[send_slot]
        .set(boundary_rows, mode="drop")
    )
    arrived, arrived_cells = (
        lax.all_to_all(
            outgoing.reshape(wide_count, CAP, channels),
            "wide",
            split_axis=0,
            concat_axis=0,
            tiled=True,
        ),
        lax.all_to_all(
            slot_cells.reshape(wide_count, CAP), "wide", split_axis=0, concat_axis=0, tiled=True
        ),
    )
    arrived = arrived.reshape(slot_count, channels)
    arrived_cells = arrived_cells.reshape(slot_count)
    projected = jnp.dot(arrived, w_force, preferred_element_type=jnp.float32).astype(jnp.bfloat16)
    force = (
        jnp.zeros((tile_cells, channels), jnp.float32)
        .at[arrived_cells]
        .add(projected.astype(jnp.float32), mode="drop")
    )
    blended = (grid_state.reshape(tile_cells, channels).astype(jnp.float32) + force).astype(
        jnp.bfloat16
    )
    pre_embed, latent, pre_message, message = grid_forward(blended, w_embed, w_message)
    padded = padded_2(message.reshape(tile_x, tile_y, channels), (("wide", 0), ("narrow", 1)), 1)
    level_one = gather_window(padded, g2m_mask).astype(jnp.bfloat16)
    level_bar, grad_one, grad_two = mesh_backward(
        level_one, mesh_cotangent, w_level_one, w_level_two
    )
    spread = spread_window(level_bar, g2m_mask)
    received = padded_2(spread, (("wide", 0), ("narrow", 1)), 1)
    interior = spread[1:-1, 1:-1]
    interior = interior.at[0].add(received[0, 2:-2])
    interior = interior.at[-1].add(received[-1, 2:-2])
    interior = interior.at[:, 0].add(received[2:-2, 0])
    interior = interior.at[:, -1].add(received[2:-2, -1])
    interior = interior.at[0, 0].add(received[0, 0])
    interior = interior.at[0, -1].add(received[0, -1])
    interior = interior.at[-1, 0].add(received[-1, 0])
    interior = interior.at[-1, -1].add(received[-1, -1])
    grad_state, grad_embed, grad_message = grid_backward(
        interior.reshape(tile_cells, channels),
        blended,
        pre_embed,
        latent,
        pre_message,
        w_embed,
        w_message,
    )
    slot_bar = jnp.take(grad_state, arrived_cells, axis=0, mode="fill", fill_value=0)
    back_payload = jnp.dot(slot_bar, w_force.T, preferred_element_type=jnp.float32).astype(
        jnp.bfloat16
    )
    grad_force = jnp.dot(arrived.T, slot_bar, preferred_element_type=jnp.float32)
    returned = lax.all_to_all(
        back_payload.reshape(wide_count, CAP, channels),
        "wide",
        split_axis=0,
        concat_axis=0,
        tiled=True,
    )
    row_back = jnp.take(
        returned.reshape(slot_count, channels), send_slot, axis=0, mode="fill", fill_value=0
    )
    totals = lax.psum(
        (grad_force, grad_embed, grad_message, grad_one, grad_two), ("wide", "narrow")
    )
    cell_total = tile_cells * wide_count * narrow_count
    row_total = held_rows * wide_count * narrow_count
    weight_grads = jnp.stack(
        [
            totals[0] / math.sqrt(row_total),
            totals[1] / math.sqrt(cell_total),
            totals[2] / math.sqrt(cell_total),
            totals[3] / math.sqrt(cell_total // 16),
            totals[4] / math.sqrt(cell_total // 64),
        ]
    )
    return (grad_state.reshape(tile_x, tile_y, channels), row_back, weight_grads)


def solution(mesh):
    in_specs = (
        P(("groups", "wide"), "narrow", None),
        P(("groups", "wide", "narrow"), None),
        P(("groups", "wide", "narrow")),
        P(("groups", "wide", "narrow")),
        P(("groups", "wide", "narrow")),
        P(None, ("groups", "wide"), "narrow"),
        P(("groups", "wide"), "narrow", None),
        P(),
        P(),
        P(),
        P(),
        P(),
    )
    out_specs = (
        P(("groups", "wide"), "narrow", None),
        P(("groups", "wide", "narrow"), None),
        P("groups", None, None),
    )
    return jax.shard_map(local, mesh=mesh, in_specs=in_specs, out_specs=out_specs, check_vma=False)
```

profile of v0, /device:TPU:0, one launch (start us, length us, event | category | flops | bytes accessed | tf_op | source)
XLA Modules:
  0.0 191.1 jit_solution(1363430985343592712)
XLA Ops:
  10.3 6.3 %all-to-all-start = ((s32[4,1,16]{2,1,0:T(1,128)}), s32[4,1,16]{2,1,0:T(1,128)S(1)}, u32[]{:S(2)}, u32[]{:S(2)}) async-start(s32[4,1,16]{2,1,0:T(1,128)} %bitcast.4), calls=%async_computation | async-start | bytes 4096 | tf_op jit(solution)/shard_map/all_to_all | solution.py:154
  16.6 1.7 convert_reduce_fusion.35
  18.3 1.6 convert_reduce_fusion.34
  20.7 1.0 bitcast_convert_fusion
  23.8 1.5 scatter_custom_fusion.1
  25.3 5.1 %all-to-all-start.1 = ((bf16[4,16,256]{2,1,0:T(8,128)(2,1)}), bf16[4,16,256]{2,1,0:T(8,128)(2,1)S(1)}, u32[]{:S(2)}, u32[]{:S(2)}) async-start(bf16[4,16,256]{2,1,0:T(8,128)(2,1)} %bitcast.6), calls=%async_computation.1 | async-start | bytes 65536 | tf_op jit(solution)/shard_map/all_to_all | solution.py:147
  31.7 4.3 %all-to-all-done.1 = bf16[4,16,256]{2,1,0:T(8,128)(2,1)S(1)} async-done(((bf16[4,16,256]{2,1,0:T(8,128)(2,1)}), bf16[4,16,256]{2,1,0:T(8,128)(2,1)S(1)}, u32[]{:S(2)}, u32[]{:S(2)}) %all-to-all-start.1) | async-done | bytes 32800 | tf_op jit(solution)/shard_map/all_to_all | solution.py:147
  36.2 1.2 scatter_fusion
  37.3 1.0 add_convert_fusion
  38.7 2.6 %collective-permute-start = (bf16[1,32,256]{2,1,0:T(8,128)(2,1)S(1)}, bf16[1,32,256]{2,1,0:T(8,128)(2,1)S(1)}, u32[]{:S(2)}, u32[]{:S(2)}) collective-permute-start(bf16[1,32,256]{2,1,0:T(8,128)(2,1)S(1)} %get-tuple-element.152), channel_id=1, source_target_pairs={{0,4},{4,8},{8,12},{1,5},{5,9},{9,13},{2,6},{6,10},{10,14},{3,7},{... | collective-permute-start | bytes 49160 | tf_op jit(solution)/shard_map/ppermute | solution.py:19
  41.4 1.3 collective-permute-start.1
  42.8 4.2 %collective-permute-done.1 = bf16[1,32,256]{2,1,0:T(8,128)(2,1)S(1)} collective-permute-done((bf16[1,32,256]{2,1,0:T(8,128)(2,1)S(1)}, bf16[1,32,256]{2,1,0:T(8,128)(2,1)S(1)}, u32[]{:S(2)}, u32[]{:S(2)}) %collective-permute-start.1) | collective-permute-done | bytes 16416 | tf_op jit(solution)/shard_map/ppermute | solution.py:21
  47.1 1.3 collective-permute-start.2
  48.4 1.3 collective-permute-start.3
  60.1 2.4 %collective-permute-start.4 = (f32[1,34,256]{2,1,0:T(8,128)S(1)}, f32[1,34,256]{2,1,0:T(8,128)S(1)}, u32[]{:S(2)}, u32[]{:S(2)}) collective-permute-start(f32[1,34,256]{2,1,0:T(8,128)S(1)} %get-tuple-element.145), channel_id=1, source_target_pairs={{0,4},{4,8},{8,12},{1,5},{5,9},{9,13},{2,6},{6,10},{10,14},{3,7},{... | collective-permute-start | bytes 104456 | tf_op jit(solution)/shard_map/ppermute | solution.py:19
  62.5 1.3 collective-permute-start.5
  64.8 3.6 %collective-permute-done.5 = f32[1,34,256]{2,1,0:T(8,128)S(1)} collective-permute-done((f32[1,34,256]{2,1,0:T(8,128)S(1)}, f32[1,34,256]{2,1,0:T(8,128)S(1)}, u32[]{:S(2)}, u32[]{:S(2)}) %collective-permute-start.5) | collective-permute-done | bytes 34848 | tf_op jit(solution)/shard_map/ppermute | solution.py:21
  68.4 3.3 %collective-permute-start.6 = (f32[20,1,256]{2,1,0:T(1,128)S(1)}, f32[20,1,256]{2,1,0:T(1,128)S(1)}, u32[]{:S(2)}, u32[]{:S(2)}) collective-permute-start(f32[20,1,256]{2,1,0:T(1,128)S(1)} %get-tuple-element.143), channel_id=1, source_target_pairs={{0,1},{1,2},{2,3},{4,5},{5,6},{6,7},{8,9},{9,10},{10,11},{12,13},{... | collective-permute-start | bytes 61448 | tf_op jit(solution)/shard_map/ppermute | solution.py:19
  71.7 1.3 collective-permute-start.7
  73.2 4.3 %collective-permute-done.7 = f32[20,1,256]{2,1,0:T(1,128)S(1)} collective-permute-done((f32[20,1,256]{2,1,0:T(1,128)S(1)}, f32[20,1,256]{2,1,0:T(1,128)S(1)}, u32[]{:S(2)}, u32[]{:S(2)}) %collective-permute-start.7) | collective-permute-done | bytes 20512 | tf_op jit(solution)/shard_map/ppermute | solution.py:21
  77.7 1.9 broadcast_select_fusion.4
  79.6 1.3 scatter-add.44
  81.2 1.0 fusion.42
  82.5 1.1 fusion.29
  84.6 0.9 fusion.19
  86.4 3.3 %all-to-all-start.2 = ((bf16[4,16,256]{2,1,0:T(8,128)(2,1)}), bf16[4,16,256]{2,1,0:T(8,128)(2,1)S(1)}, u32[]{:S(2)}, u32[]{:S(2)}) async-start(bf16[4,16,256]{2,1,0:T(8,128)(2,1)} %bitcast.20), calls=%async_computation.2 | async-start | bytes 65536 | tf_op jit(solution)/shard_map/all_to_all | solution.py:200
  89.7 5.6 %all-to-all-done.2 = bf16[4,16,256]{2,1,0:T(8,128)(2,1)S(1)} async-done(((bf16[4,16,256]{2,1,0:T(8,128)(2,1)}), bf16[4,16,256]{2,1,0:T(8,128)(2,1)S(1)}, u32[]{:S(2)}, u32[]{:S(2)}) %all-to-all-start.2) | async-done | bytes 32800 | tf_op jit(solution)/shard_map/all_to_all | solution.py:200
  96.6 83.5 %all-reduce.8.cloned.1.call-done = (f32[256,256]{1,0:T(8,128)}, f32[256,256]{1,0:T(8,128)}, f32[256,256]{1,0:T(8,128)}, f32[256,256]{1,0:T(8,128)}, f32[256,256]{1,0:T(8,128)}) async-done(((f32[256,256]{1,0:T(8,128)}, f32[256,256]{1,0:T(8,128)}, f32[256,256]{1,0:T(8,128)}, f32[256,256]{1,0:T(8,128)}, f32[256,256]{1,0:T(8,128)}), (f32[256,256]{1,0:T(8,128)}, f32[256,256]{1,0:T(8,128)}, f32[256,256]{1,0:T(8,128)}, ...) | async-done | bytes 1310736 | tf_op jit(solution)/shard_map/psum | solution.py:210
  180.1 1.0 bitcast_dynamic-update-slice_fusion.4
  181.1 1.0 bitcast_dynamic-update-slice_fusion.3
  182.1 1.0 bitcast_dynamic-update-slice_fusion.2
  183.2 1.0 copy-done.7
  (148 shorter events, 22.3 us)
Async XLA Ops:
  7.2 31.2 %copy-start = (bf16[256,256]{1,0:T(8,128)(2,1)S(1)}, bf16[256,256]{1,0:T(8,128)(2,1)}, u32[]{:S(2)}) copy-start(bf16[256,256]{1,0:T(8,128)(2,1)} %param.37) | copy-start | bytes 393220
  7.2 14.5 %copy-start.6 = (bf16[4,8,256]{2,1,0:T(8,128)(2,1)S(1)}, bf16[4,8,256]{2,1,0:T(8,128)(2,1)}, u32[]{:S(2)}) copy-start(bf16[4,8,256]{2,1,0:T(8,128)(2,1)} %param.34) | copy-start | bytes 49156
  10.3 15.0 %all-to-all-start = ((s32[4,1,16]{2,1,0:T(1,128)}), s32[4,1,16]{2,1,0:T(1,128)S(1)}, u32[]{:S(2)}, u32[]{:S(2)}) async-start(s32[4,1,16]{2,1,0:T(1,128)} %bitcast.4), calls=%async_computation | async-start | bytes 4096 | tf_op jit(solution)/shard_map/all_to_all | solution.py:154
  16.6 6.3 %copy-start.8 = (s32[3]{0:T(128)S(1)}, s32[3]{0:T(128)}, u32[]{:S(2)}) copy-start(s32[3]{0:T(128)} %constant.326.clone.1) | copy-start | bytes 40
  19.9 16.1 %copy-start.1 = (bf16[256,256]{1,0:T(8,128)(2,1)S(1)}, bf16[256,256]{1,0:T(8,128)(2,1)}, u32[]{:S(2)}) copy-start(bf16[256,256]{1,0:T(8,128)(2,1)} %param.35) | copy-start | bytes 393220
  21.8 15.5 %copy-start.10 = (bf16[256,256]{1,0:T(8,128)(2,1)S(1)}, bf16[256,256]{1,0:T(8,128)(2,1)}, u32[]{:S(2)}) copy-start(bf16[256,256]{1,0:T(8,128)(2,1)} %param.36) | copy-start | bytes 393220
  25.3 10.7 %all-to-all-start.1 = ((bf16[4,16,256]{2,1,0:T(8,128)(2,1)}), bf16[4,16,256]{2,1,0:T(8,128)(2,1)S(1)}, u32[]{:S(2)}, u32[]{:S(2)}) async-start(bf16[4,16,256]{2,1,0:T(8,128)(2,1)} %bitcast.6), calls=%async_computation.1 | async-start | bytes 65536 | tf_op jit(solution)/shard_map/all_to_all | solution.py:147
  30.4 149.7 %all-reduce.8.cloned.1.call-start = ((), (), s32[]{:S(2)}) async-start(), calls=%async_computation.3 | async-start | bytes 2621440 | tf_op jit(solution)/shard_map/psum | solution.py:210
  38.7 4.1 %collective-permute-start = (bf16[1,32,256]{2,1,0:T(8,128)(2,1)S(1)}, bf16[1,32,256]{2,1,0:T(8,128)(2,1)S(1)}, u32[]{:S(2)}, u32[]{:S(2)}) collective-permute-start(bf16[1,32,256]{2,1,0:T(8,128)(2,1)S(1)} %get-tuple-element.152), channel_id=1, source_target_pairs={{0,4},{4,8},{8,12},{1,5},{5,9},{9,13},{2,6},{6,10},{10,14},{3,7},{... | collective-permute-start | bytes 49160 | tf_op jit(solution)/shard_map/ppermute | solution.py:19
  41.4 5.6 %collective-permute-start.1 = (bf16[1,32,256]{2,1,0:T(8,128)(2,1)S(1)}, bf16[1,32,256]{2,1,0:T(8,128)(2,1)S(1)}, u32[]{:S(2)}, u32[]{:S(2)}) collective-permute-start(bf16[1,32,256]{2,1,0:T(8,128)(2,1)S(1)} %get-tuple-element.153), channel_id=1, source_target_pairs={{4,0},{8,4},{12,8},{5,1},{9,5},{13,9},{6,2},{10,6},{14,10},{7,3},{... | collective-permute-start | bytes 49160 | tf_op jit(solution)/shard_map/ppermute | solution.py:21
  47.1 7.4 %collective-permute-start.2 = (bf16[18,1,256]{2,1,0:T(2,128)(2,1)S(1)}, bf16[18,1,256]{2,1,0:T(2,128)(2,1)S(1)}, u32[]{:S(2)}, u32[]{:S(2)}) collective-permute-start(bf16[18,1,256]{2,1,0:T(2,128)(2,1)S(1)} %get-tuple-element.150), channel_id=1, source_target_pairs={{0,1},{1,2},{2,3},{4,5},{5,6},{6,7},{8,9},{9,10},{10,11},{12,13},{... | collective-permute-start | bytes 27656 | tf_op jit(solution)/shard_map/ppermute | solution.py:19
  48.4 6.2 %collective-permute-start.3 = (bf16[18,1,256]{2,1,0:T(2,128)(2,1)S(1)}, bf16[18,1,256]{2,1,0:T(2,128)(2,1)S(1)}, u32[]{:S(2)}, u32[]{:S(2)}) collective-permute-start(bf16[18,1,256]{2,1,0:T(2,128)(2,1)S(1)} %get-tuple-element.151), channel_id=1, source_target_pairs={{1,0},{2,1},{3,2},{5,4},{6,5},{7,6},{9,8},{10,9},{11,10},{13,12},{... | collective-permute-start | bytes 27656 | tf_op jit(solution)/shard_map/ppermute | solution.py:21
  49.7 7.7 %copy-start.9 = (bf16[256,256]{1,0:T(8,128)(2,1)S(1)}, bf16[256,256]{1,0:T(8,128)(2,1)}, u32[]{:S(2)}) copy-start(bf16[256,256]{1,0:T(8,128)(2,1)} %param.38) | copy-start | bytes 393220
  52.0 5.7 %copy-start.2 = (bf16[256,256]{1,0:T(8,128)(2,1)S(1)}, bf16[256,256]{1,0:T(8,128)(2,1)}, u32[]{:S(2)}) copy-start(bf16[256,256]{1,0:T(8,128)(2,1)} %param.39) | copy-start | bytes 393220
  60.1 4.7 %collective-permute-start.4 = (f32[1,34,256]{2,1,0:T(8,128)S(1)}, f32[1,34,256]{2,1,0:T(8,128)S(1)}, u32[]{:S(2)}, u32[]{:S(2)}) collective-permute-start(f32[1,34,256]{2,1,0:T(8,128)S(1)} %get-tuple-element.145), channel_id=1, source_target_pairs={{0,4},{4,8},{8,12},{1,5},{5,9},{9,13},{2,6},{6,10},{10,14},{3,7},{... | collective-permute-start | bytes 104456 | tf_op jit(solution)/shard_map/ppermute | solution.py:19
  62.5 5.9 %collective-permute-start.5 = (f32[1,34,256]{2,1,0:T(8,128)S(1)}, f32[1,34,256]{2,1,0:T(8,128)S(1)}, u32[]{:S(2)}, u32[]{:S(2)}) collective-permute-start(f32[1,34,256]{2,1,0:T(8,128)S(1)} %get-tuple-element.144), channel_id=1, source_target_pairs={{4,0},{8,4},{12,8},{5,1},{9,5},{13,9},{6,2},{10,6},{14,10},{7,3},{... | collective-permute-start | bytes 104456 | tf_op jit(solution)/shard_map/ppermute | solution.py:21
  68.4 4.7 %collective-permute-start.6 = (f32[20,1,256]{2,1,0:T(1,128)S(1)}, f32[20,1,256]{2,1,0:T(1,128)S(1)}, u32[]{:S(2)}, u32[]{:S(2)}) collective-permute-start(f32[20,1,256]{2,1,0:T(1,128)S(1)} %get-tuple-element.143), channel_id=1, source_target_pairs={{0,1},{1,2},{2,3},{4,5},{5,6},{6,7},{8,9},{9,10},{10,11},{12,13},{... | collective-permute-start | bytes 61448 | tf_op jit(solution)/shard_map/ppermute | solution.py:19
  71.7 5.7 %collective-permute-start.7 = (f32[20,1,256]{2,1,0:T(1,128)S(1)}, f32[20,1,256]{2,1,0:T(1,128)S(1)}, u32[]{:S(2)}, u32[]{:S(2)}) collective-permute-start(f32[20,1,256]{2,1,0:T(1,128)S(1)} %get-tuple-element.142), channel_id=1, source_target_pairs={{1,0},{2,1},{3,2},{5,4},{6,5},{7,6},{9,8},{10,9},{11,10},{13,12},{... | collective-permute-start | bytes 61448 | tf_op jit(solution)/shard_map/ppermute | solution.py:21
  81.0 1.5 copy-start.11
  83.9 97.2 %copy-start.3 = (bf16[512,256]{1,0:T(8,128)(2,1)}, bf16[512,256]{1,0:T(8,128)(2,1)S(1)}, u32[]{:S(2)}) copy-start(bf16[512,256]{1,0:T(8,128)(2,1)S(1)} %fusion) | copy-start | bytes 786436
  86.4 8.9 %all-to-all-start.2 = ((bf16[4,16,256]{2,1,0:T(8,128)(2,1)}), bf16[4,16,256]{2,1,0:T(8,128)(2,1)S(1)}, u32[]{:S(2)}, u32[]{:S(2)}) async-start(bf16[4,16,256]{2,1,0:T(8,128)(2,1)} %bitcast.20), calls=%async_computation.2 | async-start | bytes 65536 | tf_op jit(solution)/shard_map/all_to_all | solution.py:200
  180.1 3.0 %copy-start.5 = (f32[256,256]{1,0:T(8,128)S(1)}, f32[256,256]{1,0:T(8,128)}, u32[]{:S(2)}) copy-start(f32[256,256]{1,0:T(8,128)} %get-tuple-element.138) | copy-start | bytes 786436
  180.1 3.1 %copy-start.4 = (f32[256,256]{1,0:T(8,128)S(1)}, f32[256,256]{1,0:T(8,128)}, u32[]{:S(2)}) copy-start(f32[256,256]{1,0:T(8,128)} %get-tuple-element.139) | copy-start | bytes 786436
  183.2 1.1 copy-start.7
Sparse Core Ops, SparseCore 0:
  85.7 94.3 all-reduce.7
where the time goes:
time: 192 us; the launch traced here: 191 us
  waiting for transfers between devices  106 us (55%)
  starting transfers between devices  29.5 us (15%)
  local copies, waits for them, and re-layouts  16.2 us (8%)
  other arithmetic  15.8 us (8%)
  between operations  15.6 us (8%)
  matrix products  8.39 us (4%)
    psum x1, waiting for transfers between devices, local(): lax.psum((grad_force, grad_embed, grad_message, grad_one, grad_two), ('wi...  83.5 us
    ppermute x4, waiting for transfers between devices, padded_2(): lax.ppermute(head, axis, [((i + 1) % count, i) for i in range(ends)])  12.1 us
    ppermute x4, starting transfers between devices, padded_2(): lax.ppermute(tail, axis, [(i, (i + 1) % count) for i in range(ends)])  9.65 us
    slice x36, local copies, waits for them, and re-layouts, gather_window(): padded[shift_x:shift_x + 4 * node_x - 3:4, shift_y:shift_y + 4 * node_y -...  6.91 us
    all_to_all x1, starting transfers between devices, local(): lax.all_to_all(slot_cells.reshape(wide_count, CAP), 'wide', split_axis=0,...  6.32 us
    all_to_all x1, waiting for transfers between devices, local(): lax.all_to_all(back_payload.reshape(wide_count, CAP, channels), 'wide', s...  5.62 us
    ppermute x4, starting transfers between devices, padded_2(): lax.ppermute(head, axis, [((i + 1) % count, i) for i in range(ends)])  5.17 us
    all_to_all x1, starting transfers between devices, local(): lax.all_to_all(outgoing.reshape(wide_count, CAP, channels), 'wide', split...  5.09 us
  transfers between devices with their start and end apart: 12, of which 7 were waited for; matrix products, arithmetic and copies ran while one was open for 9% of the time, Pallas kernels for 0%

commit v1 on v0

--- a/solution.py
+++ b/solution.py
@@ -23,6 +23,57 @@
             axis=dim,
         )
     return cells
+
+
+def swapped(block, axis, bit):
+    count = lax.axis_size(axis)
+    return lax.ppermute(block, axis, [(i, i ^ bit) for i in range(count)])
+
+
+def shifted(block, axis, step):
+    count = lax.axis_size(axis)
+    return lax.ppermute(block, axis, [(i, (i + step) % count) for i in range(count)])
+
+
+def summed_over_part(terms):
+    wide_count = lax.axis_size("wide")
+    narrow_count = lax.axis_size("narrow")
+    wide_at = lax.axis_index("wide")
+    narrow_at = lax.axis_index("narrow")
+    bits = []
+    while 1 << len(bits) < narrow_count:
+        bits.append(1 << len(bits))
+    piece = terms
+    for bit in bits:
+        half = piece.shape[0] // 2
+        upper = (narrow_at // bit) % 2
+        sent = lax.dynamic_slice_in_dim(piece, (1 - upper) * half, half).astype(jnp.bfloat16)
+        kept = lax.dynamic_slice_in_dim(piece, upper * half, half)
+        piece = kept + swapped(sent, "narrow", bit).astype(jnp.float32)
+    part = piece.shape[0] // wide_count
+    rounded = piece.astype(jnp.bfloat16)
+    total = lax.dynamic_slice_in_dim(piece, wide_at * part, part)
+    for step in range(1, wide_count):
+        target = (wide_at + step) % wide_count
+        sent = lax.dynamic_slice_in_dim(rounded, target * part, part)
+        total = total + shifted(sent, "wide", step).astype(jnp.float32)
+    own = total.astype(jnp.bfloat16)
+    gathered = jnp.zeros((wide_count * part, own.shape[1]), jnp.bfloat16)
+    gathered = lax.dynamic_update_slice_in_dim(gathered, own, wide_at * part, 0)
+    for step in range(1, wide_count):
+        source = (wide_at - step) % wide_count
+        gathered = lax.dynamic_update_slice_in_dim(
+            gathered, shifted(own, "wide", step), source * part, 0
+        )
+    for bit in reversed(bits):
+        upper = (narrow_at // bit) % 2
+        other = swapped(gathered, "narrow", bit)
+        gathered = jnp.where(
+            upper == 0,
+            jnp.concatenate([gathered, other]),
+            jnp.concatenate([other, gathered]),
+        )
+    return gathered
 
 
 def silu_slope(argument):
@@ -207,20 +258,22 @@
     row_back = jnp.take(
         returned.reshape(slot_count, channels), send_slot, axis=0, mode="fill", fill_value=0
     )
-    totals = lax.psum(
-        (grad_force, grad_embed, grad_message, grad_one, grad_two), ("wide", "narrow")
+    totals = summed_over_part(
+        jnp.concatenate([grad_force, grad_embed, grad_message, grad_one, grad_two], axis=0)
     )
     cell_total = tile_cells * wide_count * narrow_count
     row_total = held_rows * wide_count * narrow_count
-    weight_grads = jnp.stack(
+    scales = jnp.array(
         [
-            totals[0] / math.sqrt(row_total),
-            totals[1] / math.sqrt(cell_total),
-            totals[2] / math.sqrt(cell_total),
-            totals[3] / math.sqrt(cell_total // 16),
-            totals[4] / math.sqrt(cell_total // 64),
-        ]
-    )
+            1.0 / math.sqrt(row_total),
+            1.0 / math.sqrt(cell_total),
+            1.0 / math.sqrt(cell_total),
+            1.0 / math.sqrt(cell_total // 16),
+            1.0 / math.sqrt(cell_total // 64),
+        ],
+        jnp.float32,
+    )
+    weight_grads = totals.reshape(5, channels, channels).astype(jnp.float32) * scales[:, None, None]
     return (grad_state.reshape(tile_x, tile_y, channels), row_back, weight_grads)
 
 

time: 192 us -> 119 us (0.62)
  waiting for transfers between devices: 106 us -> 32.7 us
  starting transfers between devices: 29.5 us -> 43.2 us
  between operations: 15.6 us -> 2.46 us
    psum x1 -> x0, waiting for transfers between devices: 83.5 us -> none  [local(): lax.psum((grad_force, grad_embed, grad_message, grad_one, grad_two), ('wi...]
    ppermute x0 -> x10, waiting for transfers between devices: none -> 13.7 us  [the longest x4 7.91 us: swapped(): return lax.ppermute(block, axis, [(i, i ^ bit) for i in range(count)])]
    ppermute x0 -> x10, starting transfers between devices: none -> 11.7 us  [the longest x6 8.47 us: shifted(): lax.ppermute(block, axis, [(i, (i + step) % count) for i in range(count)])]
    unnamed x4 -> x0, other arithmetic: 3.01 us -> none
    ppermute x4, waiting for transfers between devices: 12.1 us -> 9.36 us  [padded_2(): lax.ppermute(head, axis, [((i + 1) % count, i) for i in range(ends)])]
    mul x6, local copies, waits for them, and re-layouts: 0.6 us -> 3.02 us  [spread_window(): scales[..., None] * node_bar[:, None, :, None, :]]
  transfers between devices with their start and end apart: 12 -> 21, of which waited for: 7 -> 14; matrix products, arithmetic and copies ran while one was open for 9% -> 17% of each run, Pallas kernels for 0% -> 0%
where the time goes in v1:
time: 119 us; the launch traced here: 118 us
  starting transfers between devices  43.2 us (36%)
  waiting for transfers between devices  32.7 us (27%)
  local copies, waits for them, and re-layouts  17.6 us (15%)
  other arithmetic  15.6 us (13%)
  matrix products  6.54 us (5%)
  between operations  2.46 us (2%)
    ppermute x4, starting transfers between devices, padded_2(): lax.ppermute(tail, axis, [(i, (i + 1) % count) for i in range(ends)])  11 us
    ppermute x4, waiting for transfers between devices, padded_2(): lax.ppermute(head, axis, [((i + 1) % count, i) for i in range(ends)])  9.36 us
    ppermute x6, starting transfers between devices, shifted(): lax.ppermute(block, axis, [(i, (i + step) % count) for i in range(count)])  8.47 us
    ppermute x4, waiting for transfers between devices, swapped(): return lax.ppermute(block, axis, [(i, i ^ bit) for i in range(count)])  7.91 us
    slice x36, local copies, waits for them, and re-layouts, gather_window(): padded[shift_x:shift_x + 4 * node_x - 3:4, shift_y:shift_y + 4 * node_y -...  6.89 us
    all_to_all x1, starting transfers between devices, local(): lax.all_to_all(slot_cells.reshape(wide_count, CAP), 'wide', split_axis=0,...  6.32 us
    ppermute x6, waiting for transfers between devices, shifted(): lax.ppermute(block, axis, [(i, (i + step) % count) for i in range(count)])  5.81 us
    ppermute x4, starting transfers between devices, padded_2(): lax.ppermute(head, axis, [((i + 1) % count, i) for i in range(ends)])  5.3 us
  transfers between devices with their start and end apart: 21, of which 14 were waited for; matrix products, arithmetic and copies ran while one was open for 17% of the time, Pallas kernels for 0%

profile of v1, /device:TPU:0, one launch (start us, length us, event | category | flops | bytes accessed | tf_op | source)
XLA Modules:
  0.0 118.1 jit_solution(7020800325042619102)
XLA Ops:
  4.3 6.3 %all-to-all-start = ((s32[4,1,16]{2,1,0:T(1,128)}), s32[4,1,16]{2,1,0:T(1,128)S(1)}, u32[]{:S(2)}, u32[]{:S(2)}) async-start(s32[4,1,16]{2,1,0:T(1,128)} %bitcast.4), calls=%async_computation | async-start | bytes 4096 | tf_op jit(solution)/shard_map/all_to_all | solution.py:205
  10.6 1.7 %convert_reduce_fusion.35 = (f32[4,8]{1,0:T(4,128)S(1)}, f32[4,8]{1,0:T(4,128)S(1)}, f32[4,8]{1,0:T(4,128)S(1)}, f32[4,8]{1,0:T(4,128)S(1)}, f32[4,8]{1,0:T(4,12...) fusion(s32[36,4,8]{0,2,1:T(8,128)} %param.34), kind=kLoop, calls=%fused_computation.111 | loop fusion | flops 608 | bytes 4864 | tf_op jit(solution)/shard_map/convert_element_type | solution.py:93
  12.3 1.6 %convert_reduce_fusion.34 = (f32[4,8]{1,0:T(4,128)S(1)}, f32[4,8]{1,0:T(4,128)S(1)}, f32[4,8]{1,0:T(4,128)S(1)}, f32[4,8]{1,0:T(4,128)S(1)}, f32[4,8]{1,0:T(4,12...) fusion(s32[36,4,8]{0,2,1:T(8,128)} %param.34), kind=kLoop, calls=%fused_computation.106 | loop fusion | flops 544 | bytes 4352 | tf_op jit(solution)/shard_map/convert_element_type | solution.py:93
  16.7 1.5 %scatter_custom_fusion.1 = bf16[64,256]{1,0:T(8,128)(2,1)} fusion(s32[32]{0:T(128)S(1)} %get-tuple-element.140, bf16[32,256]{1,0:T(8,128)(2,1)} %param.30, bf16[]{:T(256)} %constant.395.clone.1), kind=kCustom, calls=%fused_computation.107 | custom fusion | bytes 33280 | tf_op jit(solution)/shard_map/scatter | solution.py:195
  18.1 5.1 %all-to-all-start.1 = ((bf16[4,16,256]{2,1,0:T(8,128)(2,1)}), bf16[4,16,256]{2,1,0:T(8,128)(2,1)S(1)}, u32[]{:S(2)}, u32[]{:S(2)}) async-start(bf16[4,16,256]{2,1,0:T(8,128)(2,1)} %bitcast.6), calls=%async_computation.1 | async-start | bytes 65536 | tf_op jit(solution)/shard_map/all_to_all | solution.py:198
  24.5 4.4 %all-to-all-done.1 = bf16[4,16,256]{2,1,0:T(8,128)(2,1)S(1)} async-done(((bf16[4,16,256]{2,1,0:T(8,128)(2,1)}), bf16[4,16,256]{2,1,0:T(8,128)(2,1)S(1)}, u32[]{:S(2)}, u32[]{:S(2)}) %all-to-all-start.1) | async-done | bytes 32800 | tf_op jit(solution)/shard_map/all_to_all | solution.py:198
  29.0 1.2 scatter_fusion
  30.2 1.0 add_convert_fusion
  31.6 2.6 %collective-permute-start = (bf16[1,32,256]{2,1,0:T(8,128)(2,1)S(1)}, bf16[1,32,256]{2,1,0:T(8,128)(2,1)S(1)}, u32[]{:S(2)}, u32[]{:S(2)}) collective-permute-start(bf16[1,32,256]{2,1,0:T(8,128)(2,1)S(1)} %get-tuple-element.151), channel_id=1, source_target_pairs={{0,4},{4,8},{8,12},{1,5},{5,9},{9,13},{2,6},{6,10},{10,14},{3,7},{... | collective-permute-start | bytes 49160 | tf_op jit(solution)/shard_map/ppermute | solution.py:19
  34.2 1.3 %collective-permute-start.1 = (bf16[1,32,256]{2,1,0:T(8,128)(2,1)S(1)}, bf16[1,32,256]{2,1,0:T(8,128)(2,1)S(1)}, u32[]{:S(2)}, u32[]{:S(2)}) collective-permute-start(bf16[1,32,256]{2,1,0:T(8,128)(2,1)S(1)} %get-tuple-element.152), channel_id=1, source_target_pairs={{4,0},{8,4},{12,8},{5,1},{9,5},{13,9},{6,2},{10,6},{14,10},{7,3},{... | collective-permute-start | bytes 49160 | tf_op jit(solution)/shard_map/ppermute | solution.py:21
  40.0 1.3 %collective-permute-start.2 = (bf16[18,1,256]{2,1,0:T(2,128)(2,1)S(1)}, bf16[18,1,256]{2,1,0:T(2,128)(2,1)S(1)}, u32[]{:S(2)}, u32[]{:S(2)}) collective-permute-start(bf16[18,1,256]{2,1,0:T(2,128)(2,1)S(1)} %get-tuple-element.149), channel_id=1, source_target_pairs={{0,1},{1,2},{2,3},{4,5},{5,6},{6,7},{8,9},{9,10},{10,11},{12,13},{... | collective-permute-start | bytes 27656 | tf_op jit(solution)/shard_map/ppermute | solution.py:19
  41.3 1.3 %collective-permute-start.3 = (bf16[18,1,256]{2,1,0:T(2,128)(2,1)S(1)}, bf16[18,1,256]{2,1,0:T(2,128)(2,1)S(1)}, u32[]{:S(2)}, u32[]{:S(2)}) collective-permute-start(bf16[18,1,256]{2,1,0:T(2,128)(2,1)S(1)} %get-tuple-element.150), channel_id=1, source_target_pairs={{1,0},{2,1},{3,2},{5,4},{6,5},{7,6},{9,8},{10,9},{11,10},{13,12},{... | collective-permute-start | bytes 27656 | tf_op jit(solution)/shard_map/ppermute | solution.py:21
  52.7 3.7 %collective-permute-start.4 = (f32[1,34,256]{2,1,0:T(8,128)S(1)}, f32[1,34,256]{2,1,0:T(8,128)S(1)}, u32[]{:S(2)}, u32[]{:S(2)}) collective-permute-start(f32[1,34,256]{2,1,0:T(8,128)S(1)} %get-tuple-element.144), channel_id=1, source_target_pairs={{0,4},{4,8},{8,12},{1,5},{5,9},{9,13},{2,6},{6,10},{10,14},{3,7},{... | collective-permute-start | bytes 104456 | tf_op jit(solution)/shard_map/ppermute | solution.py:19
  56.4 1.3 %collective-permute-start.5 = (f32[1,34,256]{2,1,0:T(8,128)S(1)}, f32[1,34,256]{2,1,0:T(8,128)S(1)}, u32[]{:S(2)}, u32[]{:S(2)}) collective-permute-start(f32[1,34,256]{2,1,0:T(8,128)S(1)} %get-tuple-element.143), channel_id=1, source_target_pairs={{4,0},{8,4},{12,8},{5,1},{9,5},{13,9},{6,2},{10,6},{14,10},{7,3},{... | collective-permute-start | bytes 104456 | tf_op jit(solution)/shard_map/ppermute | solution.py:21
  58.1 4.2 %collective-permute-done.5 = f32[1,34,256]{2,1,0:T(8,128)S(1)} collective-permute-done((f32[1,34,256]{2,1,0:T(8,128)S(1)}, f32[1,34,256]{2,1,0:T(8,128)S(1)}, u32[]{:S(2)}, u32[]{:S(2)}) %collective-permute-start.5) | collective-permute-done | bytes 34848 | tf_op jit(solution)/shard_map/ppermute | solution.py:21
  62.4 3.3 %collective-permute-start.6 = (f32[20,1,256]{2,1,0:T(1,128)S(1)}, f32[20,1,256]{2,1,0:T(1,128)S(1)}, u32[]{:S(2)}, u32[]{:S(2)}) collective-permute-start(f32[20,1,256]{2,1,0:T(1,128)S(1)} %get-tuple-element.142), channel_id=1, source_target_pairs={{0,1},{1,2},{2,3},{4,5},{5,6},{6,7},{8,9},{9,10},{10,11},{12,13},{... | collective-permute-start | bytes 61448 | tf_op jit(solution)/shard_map/ppermute | solution.py:19
  65.7 1.4 %collective-permute-start.7 = (f32[20,1,256]{2,1,0:T(1,128)S(1)}, f32[20,1,256]{2,1,0:T(1,128)S(1)}, u32[]{:S(2)}, u32[]{:S(2)}) collective-permute-start(f32[20,1,256]{2,1,0:T(1,128)S(1)} %get-tuple-element.141), channel_id=1, source_target_pairs={{1,0},{2,1},{3,2},{5,4},{6,5},{7,6},{9,8},{10,9},{11,10},{13,12},{... | collective-permute-start | bytes 61448 | tf_op jit(solution)/shard_map/ppermute | solution.py:21
  67.3 4.3 %collective-permute-done.7 = f32[20,1,256]{2,1,0:T(1,128)S(1)} collective-permute-done((f32[20,1,256]{2,1,0:T(1,128)S(1)}, f32[20,1,256]{2,1,0:T(1,128)S(1)}, u32[]{:S(2)}, u32[]{:S(2)}) %collective-permute-start.7) | collective-permute-done | bytes 20512 | tf_op jit(solution)/shard_map/ppermute | solution.py:21
  71.8 1.9 %broadcast_select_fusion.4 = f32[1,1,256]{2,1,0:T(1,128)S(1)} fusion(pred[]{:T(512)} %and_reduce_fusion, f32[16,32,256]{2,1,0:T(8,128)S(1)} %scatter-add.41, s32[]{:T(128)} %bitcast.16, s32[]{:T(128)} %bitcast.17, f32[20,1,256]{2,1,0:T(1,128)S(1)} %collective-permute-done.7), kind=kLoop, calls=%fused_computation.134 | loop fusion | flops 512 | bytes 3081 | tf_op jit(solution)/shard_map/select.13
  73.7 1.3 %scatter-add.44 = f32[16,32,256]{2,1,0:T(8,128)S(1)} dynamic-update-slice(f32[16,32,256]{2,1,0:T(8,128)S(1)} %scatter-add.41, f32[1,1,256]{2,1,0:T(1,128)S(1)} %broadcast_select_fusion.4, s32[]{:T(128)} %bitcast.16, s32[]{:T(128)} %bitcast.17, s32[]{:T(128)} %constant.387.clone.1) | dynamic-update-slice | bytes 2052 | tf_op jit(solution)/shard_map/scatter-add | solution.py:234
  77.6 1.4 %convolution_dynamic-update-slice_fusion.3 = f32[1280,256]{1,0:T(8,128)S(1)} fusion(f32[1280,256]{1,0:T(8,128)S(1)} %convolution_dynamic-update-slice_fusion.4, f32[512,256]{1,0:T(8,128)S(1)} %scatter_fusion, f32[512,256]{1,0:T(8,128)S(1)} %fusion.38, f32[512,256]{1,0:T(8,128)} %get-tuple-element.165), kind=kOutput, calls=%fused_computation.10 | convolution fusion | flops 68419584 | bytes 1835008 | tf_op jit(solution)/shard_map/dot_general | solution.py:130
  79.8 2.6 %collective-permute-start.8 = (bf16[640,256]{1,0:T(8,128)(2,1)S(1)}, bf16[640,256]{1,0:T(8,128)(2,1)S(1)}, u32[]{:S(2)}, u32[]{:S(2)}) collective-permute-start(bf16[640,256]{1,0:T(8,128)(2,1)S(1)} %dynamic-slice_convert_fusion), channel_id=1, source_target_pairs={{0,1},{1,0},{2,3},{3,2},{4,5},{5,4},{6,7},{7,6},{8,9},{9,8},{10,11... | collective-permute-start | bytes 983048 | tf_op jit(solution)/shard_map/ppermute | solution.py:30
  82.4 1.3 %collective-permute-done.8 = bf16[640,256]{1,0:T(8,128)(2,1)S(1)} collective-permute-done((bf16[640,256]{1,0:T(8,128)(2,1)S(1)}, bf16[640,256]{1,0:T(8,128)(2,1)S(1)}, u32[]{:S(2)}, u32[]{:S(2)}) %collective-permute-start.8) | collective-permute-done | bytes 327712 | tf_op jit(solution)/shard_map/ppermute | solution.py:30
  84.1 6.2 %collective-permute-done.9 = bf16[320,256]{1,0:T(8,128)(2,1)S(1)} collective-permute-done((bf16[320,256]{1,0:T(8,128)(2,1)S(1)}, bf16[320,256]{1,0:T(8,128)(2,1)S(1)}, u32[]{:S(2)}, u32[]{:S(2)}) %collective-permute-start.9) | collective-permute-done | bytes 163872 | tf_op jit(solution)/shard_map/ppermute | solution.py:30
  91.0 3.3 %collective-permute-start.12 = (bf16[80,256]{1,0:T(8,128)(2,1)S(1)}, bf16[80,256]{1,0:T(8,128)(2,1)S(1)}, u32[]{:S(2)}, u32[]{:S(2)}) collective-permute-start(bf16[80,256]{1,0:T(8,128)(2,1)S(1)} %get-tuple-element.154), channel_id=1, source_target_pairs={{0,12},{4,0},{8,4},{12,8},{1,13},{5,1},{9,5},{13,9},{2,14},{6,2},{... | collective-permute-start | bytes 122888 | tf_op jit(solution)/shard_map/ppermute | solution.py:35
  94.3 2.0 %collective-permute-done.10 = bf16[80,256]{1,0:T(8,128)(2,1)S(1)} collective-permute-done((bf16[80,256]{1,0:T(8,128)(2,1)S(1)}, bf16[80,256]{1,0:T(8,128)(2,1)S(1)}, u32[]{:S(2)}, u32[]{:S(2)}) %collective-permute-start.10) | collective-permute-done | bytes 40992 | tf_op jit(solution)/shard_map/ppermute | solution.py:35
  96.9 2.1 %collective-permute-start.13 = (bf16[80,256]{1,0:T(8,128)(2,1)S(1)}, bf16[80,256]{1,0:T(8,128)(2,1)S(1)}, u32[]{:S(2)}, u32[]{:S(2)}) collective-permute-start(bf16[80,256]{1,0:T(8,128)(2,1)S(1)} %get-tuple-element.136), channel_id=1, source_target_pairs={{0,4},{4,8},{8,12},{12,0},{1,5},{5,9},{9,13},{13,1},{2,6},{6,10},{... | collective-permute-start | bytes 122888 | tf_op jit(solution)/shard_map/ppermute | solution.py:35
  99.0 1.8 %collective-permute-start.14 = (bf16[80,256]{1,0:T(8,128)(2,1)S(1)}, bf16[80,256]{1,0:T(8,128)(2,1)S(1)}, u32[]{:S(2)}, u32[]{:S(2)}) collective-permute-start(bf16[80,256]{1,0:T(8,128)(2,1)S(1)} %get-tuple-element.136), channel_id=1, source_target_pairs={{0,8},{4,12},{8,0},{12,4},{1,9},{5,13},{9,1},{13,5},{2,10},{6,14},... | collective-permute-start | bytes 122888 | tf_op jit(solution)/shard_map/ppermute | solution.py:35
  101.5 1.5 %collective-permute-done.13 = bf16[80,256]{1,0:T(8,128)(2,1)S(1)} collective-permute-done((bf16[80,256]{1,0:T(8,128)(2,1)S(1)}, bf16[80,256]{1,0:T(8,128)(2,1)S(1)}, u32[]{:S(2)}, u32[]{:S(2)}) %collective-permute-start.13) | collective-permute-done | bytes 40992 | tf_op jit(solution)/shard_map/ppermute | solution.py:35
  105.9 3.8 %all-to-all-start.2 = ((bf16[4,16,256]{2,1,0:T(8,128)(2,1)}), bf16[4,16,256]{2,1,0:T(8,128)(2,1)S(1)}, u32[]{:S(2)}, u32[]{:S(2)}) async-start(bf16[4,16,256]{2,1,0:T(8,128)(2,1)} %bitcast.20), calls=%async_computation.2 | async-start | bytes 65536 | tf_op jit(solution)/shard_map/all_to_all | solution.py:251
  110.3 5.0 %all-to-all-done.2 = bf16[4,16,256]{2,1,0:T(8,128)(2,1)S(1)} async-done(((bf16[4,16,256]{2,1,0:T(8,128)(2,1)}), bf16[4,16,256]{2,1,0:T(8,128)(2,1)S(1)}, u32[]{:S(2)}, u32[]{:S(2)}) %all-to-all-start.2) | async-done | bytes 32800 | tf_op jit(solution)/shard_map/all_to_all | solution.py:251
  116.9 1.2 %convert_multiply_fusion = f32[5,256,256]{2,1,0:T(8,128)} fusion(bf16[5,256,256]{2,1,0:T(8,128)(2,1)S(1)} %bitcast.82, f32[5]{0:T(128)S(1)} %copy-done.19), kind=kLoop, calls=%fused_computation.5 | loop fusion | flops 655360 | bytes 1966100 | tf_op jit(solution)/shard_map/mul | solution.py:276
  (199 shorter events, 32.8 us)
Async XLA Ops:
  0.6 30.6 %copy-start = (bf16[256,256]{1,0:T(8,128)(2,1)S(1)}, bf16[256,256]{1,0:T(8,128)(2,1)}, u32[]{:S(2)}) copy-start(bf16[256,256]{1,0:T(8,128)(2,1)} %param.38) | copy-start | bytes 393220
  0.6 15.2 %copy-start.20 = (s32[3]{0:T(128)S(1)}, s32[3]{0:T(128)}, u32[]{:S(2)}) copy-start(s32[3]{0:T(128)} %constant.400.clone.1) | copy-start | bytes 40
  0.7 28.2 %copy-start.1 = (bf16[256,256]{1,0:T(8,128)(2,1)S(1)}, bf16[256,256]{1,0:T(8,128)(2,1)}, u32[]{:S(2)}) copy-start(bf16[256,256]{1,0:T(8,128)(2,1)} %param.36) | copy-start | bytes 393220
  2.9 21.5 %copy-start.17 = (s32[32]{0:T(128)}, s32[32]{0:T(128)S(1)}, u32[]{:S(2)}) copy-start(s32[32]{0:T(128)S(1)} %get-tuple-element.140) | copy-start | bytes 388
  4.3 13.9 %all-to-all-start = ((s32[4,1,16]{2,1,0:T(1,128)}), s32[4,1,16]{2,1,0:T(1,128)S(1)}, u32[]{:S(2)}, u32[]{:S(2)}) async-start(s32[4,1,16]{2,1,0:T(1,128)} %bitcast.4), calls=%async_computation | async-start | bytes 4096 | tf_op jit(solution)/shard_map/all_to_all | solution.py:205
  14.6 15.6 %copy-start.22 = (bf16[256,256]{1,0:T(8,128)(2,1)S(1)}, bf16[256,256]{1,0:T(8,128)(2,1)}, u32[]{:S(2)}) copy-start(bf16[256,256]{1,0:T(8,128)(2,1)} %param.37) | copy-start | bytes 393220
  18.1 10.7 %all-to-all-start.1 = ((bf16[4,16,256]{2,1,0:T(8,128)(2,1)}), bf16[4,16,256]{2,1,0:T(8,128)(2,1)S(1)}, u32[]{:S(2)}, u32[]{:S(2)}) async-start(bf16[4,16,256]{2,1,0:T(8,128)(2,1)} %bitcast.6), calls=%async_computation.1 | async-start | bytes 65536 | tf_op jit(solution)/shard_map/all_to_all | solution.py:198
  31.6 7.4 %collective-permute-start = (bf16[1,32,256]{2,1,0:T(8,128)(2,1)S(1)}, bf16[1,32,256]{2,1,0:T(8,128)(2,1)S(1)}, u32[]{:S(2)}, u32[]{:S(2)}) collective-permute-start(bf16[1,32,256]{2,1,0:T(8,128)(2,1)S(1)} %get-tuple-element.151), channel_id=1, source_target_pairs={{0,4},{4,8},{8,12},{1,5},{5,9},{9,13},{2,6},{6,10},{10,14},{3,7},{... | collective-permute-start | bytes 49160 | tf_op jit(solution)/shard_map/ppermute | solution.py:19
  34.2 5.6 %collective-permute-start.1 = (bf16[1,32,256]{2,1,0:T(8,128)(2,1)S(1)}, bf16[1,32,256]{2,1,0:T(8,128)(2,1)S(1)}, u32[]{:S(2)}, u32[]{:S(2)}) collective-permute-start(bf16[1,32,256]{2,1,0:T(8,128)(2,1)S(1)} %get-tuple-element.152), channel_id=1, source_target_pairs={{4,0},{8,4},{12,8},{5,1},{9,5},{13,9},{6,2},{10,6},{14,10},{7,3},{... | collective-permute-start | bytes 49160 | tf_op jit(solution)/shard_map/ppermute | solution.py:21
  40.0 8.0 %collective-permute-start.2 = (bf16[18,1,256]{2,1,0:T(2,128)(2,1)S(1)}, bf16[18,1,256]{2,1,0:T(2,128)(2,1)S(1)}, u32[]{:S(2)}, u32[]{:S(2)}) collective-permute-start(bf16[18,1,256]{2,1,0:T(2,128)(2,1)S(1)} %get-tuple-element.149), channel_id=1, source_target_pairs={{0,1},{1,2},{2,3},{4,5},{5,6},{6,7},{8,9},{9,10},{10,11},{12,13},{... | collective-permute-start | bytes 27656 | tf_op jit(solution)/shard_map/ppermute | solution.py:19
  41.3 6.7 %collective-permute-start.3 = (bf16[18,1,256]{2,1,0:T(2,128)(2,1)S(1)}, bf16[18,1,256]{2,1,0:T(2,128)(2,1)S(1)}, u32[]{:S(2)}, u32[]{:S(2)}) collective-permute-start(bf16[18,1,256]{2,1,0:T(2,128)(2,1)S(1)} %get-tuple-element.150), channel_id=1, source_target_pairs={{1,0},{2,1},{3,2},{5,4},{6,5},{7,6},{9,8},{10,9},{11,10},{13,12},{... | collective-permute-start | bytes 27656 | tf_op jit(solution)/shard_map/ppermute | solution.py:21
  52.7 5.4 %collective-permute-start.4 = (f32[1,34,256]{2,1,0:T(8,128)S(1)}, f32[1,34,256]{2,1,0:T(8,128)S(1)}, u32[]{:S(2)}, u32[]{:S(2)}) collective-permute-start(f32[1,34,256]{2,1,0:T(8,128)S(1)} %get-tuple-element.144), channel_id=1, source_target_pairs={{0,4},{4,8},{8,12},{1,5},{5,9},{9,13},{2,6},{6,10},{10,14},{3,7},{... | collective-permute-start | bytes 104456 | tf_op jit(solution)/shard_map/ppermute | solution.py:19
  56.4 5.9 %collective-permute-start.5 = (f32[1,34,256]{2,1,0:T(8,128)S(1)}, f32[1,34,256]{2,1,0:T(8,128)S(1)}, u32[]{:S(2)}, u32[]{:S(2)}) collective-permute-start(f32[1,34,256]{2,1,0:T(8,128)S(1)} %get-tuple-element.143), channel_id=1, source_target_pairs={{4,0},{8,4},{12,8},{5,1},{9,5},{13,9},{6,2},{10,6},{14,10},{7,3},{... | collective-permute-start | bytes 104456 | tf_op jit(solution)/shard_map/ppermute | solution.py:21
  62.4 4.8 %collective-permute-start.6 = (f32[20,1,256]{2,1,0:T(1,128)S(1)}, f32[20,1,256]{2,1,0:T(1,128)S(1)}, u32[]{:S(2)}, u32[]{:S(2)}) collective-permute-start(f32[20,1,256]{2,1,0:T(1,128)S(1)} %get-tuple-element.142), channel_id=1, source_target_pairs={{0,1},{1,2},{2,3},{4,5},{5,6},{6,7},{8,9},{9,10},{10,11},{12,13},{... | collective-permute-start | bytes 61448 | tf_op jit(solution)/shard_map/ppermute | solution.py:19
  65.7 9.9 %copy-start.23 = (bf16[256,256]{1,0:T(8,128)(2,1)S(1)}, bf16[256,256]{1,0:T(8,128)(2,1)}, u32[]{:S(2)}) copy-start(bf16[256,256]{1,0:T(8,128)(2,1)} %param.37) | copy-start | bytes 393220
  65.7 9.9 %copy-start.24 = (f32[512,256]{1,0:T(8,128)S(1)}, f32[512,256]{1,0:T(8,128)}, u32[]{:S(2)}) copy-start(f32[512,256]{1,0:T(8,128)} %get-tuple-element.165) | copy-start | bytes 1572868
  65.7 5.9 %collective-permute-start.7 = (f32[20,1,256]{2,1,0:T(1,128)S(1)}, f32[20,1,256]{2,1,0:T(1,128)S(1)}, u32[]{:S(2)}, u32[]{:S(2)}) collective-permute-start(f32[20,1,256]{2,1,0:T(1,128)S(1)} %get-tuple-element.141), channel_id=1, source_target_pairs={{1,0},{2,1},{3,2},{5,4},{6,5},{7,6},{9,8},{10,9},{11,10},{13,12},{... | collective-permute-start | bytes 61448 | tf_op jit(solution)/shard_map/ppermute | solution.py:21
  79.8 3.8 %collective-permute-start.8 = (bf16[640,256]{1,0:T(8,128)(2,1)S(1)}, bf16[640,256]{1,0:T(8,128)(2,1)S(1)}, u32[]{:S(2)}, u32[]{:S(2)}) collective-permute-start(bf16[640,256]{1,0:T(8,128)(2,1)S(1)} %dynamic-slice_convert_fusion), channel_id=1, source_target_pairs={{0,1},{1,0},{2,3},{3,2},{4,5},{5,4},{6,7},{7,6},{8,9},{9,8},{10,11... | collective-permute-start | bytes 983048 | tf_op jit(solution)/shard_map/ppermute | solution.py:30
  83.7 21.3 %copy-start.13 = (pred[64]{0:T(512)(128)(4,1)S(1)}, pred[64]{0:T(512)(128)(4,1)}, u32[]{:S(2)}) copy-start(pred[64]{0:T(512)(128)(4,1)} %compare_and_fusion) | copy-start | bytes 196
  83.8 6.5 %collective-permute-start.9 = (bf16[320,256]{1,0:T(8,128)(2,1)S(1)}, bf16[320,256]{1,0:T(8,128)(2,1)S(1)}, u32[]{:S(2)}, u32[]{:S(2)}) collective-permute-start(bf16[320,256]{1,0:T(8,128)(2,1)S(1)} %dynamic-slice_convert_fusion.1), channel_id=1, source_target_pairs={{0,2},{1,3},{2,0},{3,1},{4,6},{5,7},{6,4},{7,5},{8,10},{9,11},{10,... | collective-permute-start | bytes 491528 | tf_op jit(solution)/shard_map/ppermute | solution.py:30
  84.1 26.2 %copy-start.18 = (s32[32]{0:T(128)S(1)}, s32[32]{0:T(128)}, u32[]{:S(2)}) copy-start(s32[32]{0:T(128)} %copy-done.17) | copy-start | bytes 388
  90.4 25.6 %copy-start.14 = (pred[32]{0:T(512)(128)(4,1)S(1)}, pred[32]{0:T(512)(128)(4,1)}, u32[]{:S(2)}) copy-start(pred[32]{0:T(512)(128)(4,1)} %get-tuple-element.139) | copy-start | bytes 100
  90.4 5.9 %collective-permute-start.10 = (bf16[80,256]{1,0:T(8,128)(2,1)S(1)}, bf16[80,256]{1,0:T(8,128)(2,1)S(1)}, u32[]{:S(2)}, u32[]{:S(2)}) collective-permute-start(bf16[80,256]{1,0:T(8,128)(2,1)S(1)} %get-tuple-element.153), channel_id=1, source_target_pairs={{0,4},{4,8},{8,12},{12,0},{1,5},{5,9},{9,13},{13,1},{2,6},{6,10},{... | collective-permute-start | bytes 122888 | tf_op jit(solution)/shard_map/ppermute | solution.py:35
  91.0 5.4 %collective-permute-start.11 = (bf16[80,256]{1,0:T(8,128)(2,1)S(1)}, bf16[80,256]{1,0:T(8,128)(2,1)S(1)}, u32[]{:S(2)}, u32[]{:S(2)}) collective-permute-start(bf16[80,256]{1,0:T(8,128)(2,1)S(1)} %get-tuple-element.155), channel_id=1, source_target_pairs={{0,8},{4,12},{8,0},{12,4},{1,9},{5,13},{9,1},{13,5},{2,10},{6,14},... | collective-permute-start | bytes 122888 | tf_op jit(solution)/shard_map/ppermute | solution.py:35
  91.0 5.8 %collective-permute-start.12 = (bf16[80,256]{1,0:T(8,128)(2,1)S(1)}, bf16[80,256]{1,0:T(8,128)(2,1)S(1)}, u32[]{:S(2)}, u32[]{:S(2)}) collective-permute-start(bf16[80,256]{1,0:T(8,128)(2,1)S(1)} %get-tuple-element.154), channel_id=1, source_target_pairs={{0,12},{4,0},{8,4},{12,8},{1,13},{5,1},{9,5},{13,9},{2,14},{6,2},{... | collective-permute-start | bytes 122888 | tf_op jit(solution)/shard_map/ppermute | solution.py:35
  96.9 6.0 %collective-permute-start.13 = (bf16[80,256]{1,0:T(8,128)(2,1)S(1)}, bf16[80,256]{1,0:T(8,128)(2,1)S(1)}, u32[]{:S(2)}, u32[]{:S(2)}) collective-permute-start(bf16[80,256]{1,0:T(8,128)(2,1)S(1)} %get-tuple-element.136), channel_id=1, source_target_pairs={{0,4},{4,8},{8,12},{12,0},{1,5},{5,9},{9,13},{13,1},{2,6},{6,10},{... | collective-permute-start | bytes 122888 | tf_op jit(solution)/shard_map/ppermute | solution.py:35
  99.0 4.9 %collective-permute-start.14 = (bf16[80,256]{1,0:T(8,128)(2,1)S(1)}, bf16[80,256]{1,0:T(8,128)(2,1)S(1)}, u32[]{:S(2)}, u32[]{:S(2)}) collective-permute-start(bf16[80,256]{1,0:T(8,128)(2,1)S(1)} %get-tuple-element.136), channel_id=1, source_target_pairs={{0,8},{4,12},{8,0},{12,4},{1,9},{5,13},{9,1},{13,5},{2,10},{6,14},... | collective-permute-start | bytes 122888 | tf_op jit(solution)/shard_map/ppermute | solution.py:35
  100.8 4.0 %collective-permute-start.15 = (bf16[80,256]{1,0:T(8,128)(2,1)S(1)}, bf16[80,256]{1,0:T(8,128)(2,1)S(1)}, u32[]{:S(2)}, u32[]{:S(2)}) collective-permute-start(bf16[80,256]{1,0:T(8,128)(2,1)S(1)} %get-tuple-element.136), channel_id=1, source_target_pairs={{0,12},{4,0},{8,4},{12,8},{1,13},{5,1},{9,5},{13,9},{2,14},{6,2},{... | collective-permute-start | bytes 122888 | tf_op jit(solution)/shard_map/ppermute | solution.py:35
  102.9 13.9 %copy-start.19 = (f32[5]{0:T(128)S(1)}, f32[5]{0:T(128)}, u32[]{:S(2)}) copy-start(f32[5]{0:T(128)} %constant.413.clone) | copy-start | bytes 64
  104.8 5.3 %collective-permute-start.16 = (bf16[320,256]{1,0:T(8,128)(2,1)S(1)}, bf16[320,256]{1,0:T(8,128)(2,1)S(1)}, u32[]{:S(2)}, u32[]{:S(2)}) collective-permute-start(bf16[320,256]{1,0:T(8,128)(2,1)S(1)} %constant_dynamic-update-slice_fusion), channel_id=1, source_target_pairs={{0,2},{1,3},{2,0},{3,1},{4,6},{5,7},{6,4},{7,5},{8,10},{9,11},{10,... | collective-permute-start | bytes 491528 | tf_op jit(solution)/shard_map/ppermute | solution.py:30
  105.9 9.4 %all-to-all-start.2 = ((bf16[4,16,256]{2,1,0:T(8,128)(2,1)}), bf16[4,16,256]{2,1,0:T(8,128)(2,1)S(1)}, u32[]{:S(2)}, u32[]{:S(2)}) async-start(bf16[4,16,256]{2,1,0:T(8,128)(2,1)} %bitcast.20), calls=%async_computation.2 | async-start | bytes 65536 | tf_op jit(solution)/shard_map/all_to_all | solution.py:251
  110.2 6.4 %collective-permute-start.17 = (bf16[640,256]{1,0:T(8,128)(2,1)S(1)}, bf16[640,256]{1,0:T(8,128)(2,1)S(1)}, u32[]{:S(2)}, u32[]{:S(2)}) collective-permute-start(bf16[640,256]{1,0:T(8,128)(2,1)S(1)} %maximum_select_fusion.1), channel_id=1, source_target_pairs={{0,1},{1,0},{2,3},{3,2},{4,5},{5,4},{6,7},{7,6},{8,9},{9,8},{10,11... | collective-permute-start | bytes 983048 | tf_op jit(solution)/shard_map/ppermute | solution.py:30
  (14 other events, 44.7 us)

commit v2 on v0

v2 whole, which is shorter than its diff:
```python
import functools
import math

import jax
import jax.numpy as jnp
import numpy as np
from jax import lax
from jax.experimental import pallas as pl
from jax.experimental.pallas import tpu as pltpu
from jax.sharding import PartitionSpec as P

CAP = 16
REACH = 9
NODES_OUT = 2
SIDE = 16
SLOTS = 16
LANES = 256
VMEM_LIMIT = 48 * 1024 * 1024
F32 = jnp.float32
BF16 = jnp.bfloat16


def swapped(block, axis, bit):
    count = lax.axis_size(axis)
    return lax.ppermute(block, axis, [(i, i ^ bit) for i in range(count)])


def shifted(block, axis, step):
    count = lax.axis_size(axis)
    return lax.ppermute(block, axis, [(i, (i + step) % count) for i in range(count)])


def dot(left, right):
    return jnp.dot(left, right, preferred_element_type=F32)


def dot_right_t(left, right):
    return lax.dot_general(left, right, (((1,), (1,)), ((), ())), preferred_element_type=F32)


def dot_left_t(left, right):
    return lax.dot_general(left, right, (((0,), (0,)), ((), ())), preferred_element_type=F32)


def sigmoid(value):
    return 0.5 * jnp.tanh(0.5 * value) + 0.5


def silu_and_slope(value):
    logistic = sigmoid(value)
    return value * logistic, logistic * (1.0 + value * (1.0 - logistic))


def silu(value):
    return value * sigmoid(value)


def pieces(start, stop, size):
    return [(at, min(size, stop - at)) for at in range(start, stop, size)]


def two_halves(value):
    high = value.astype(BF16)
    low = (value - high.astype(F32)).astype(BF16)
    return jnp.concatenate([high, low], axis=0)


class Shape:
    def __init__(self, tile_x, tile_y):
        self.tile_x = tile_x
        self.tile_y = tile_y
        self.cells = tile_x * tile_y
        self.rows_x = tile_x + 2 * REACH
        self.halo = REACH * tile_y
        self.center = self.rows_x * tile_y
        self.side = self.rows_x * SIDE
        self.pitch = tile_y + 2 * SIDE
        self.node_x = tile_x // 4
        self.node_y = tile_y // 4
        self.out_x = self.node_x + 2 * NODES_OUT
        self.nodes = self.out_x * SLOTS
        self.edge = NODES_OUT * self.node_y
        self.own_nodes = self.node_x * self.node_y
        self.window = 6 * self.pitch
        self.side_nodes = NODES_OUT * self.out_x

    def center_row(self, at_x, at_y, kind):
        edge, own = self.edge, self.own_nodes
        if at_x < NODES_OUT:
            return kind * edge + at_x * self.node_y + at_y
        at_x -= NODES_OUT
        if at_x < self.node_x:
            return 2 * edge + kind * own + at_x * self.node_y + at_y
        at_x -= self.node_x
        return 2 * edge + 2 * own + kind * edge + at_x * self.node_y + at_y

    def tables(self):
        stack = 4 * self.edge + 2 * self.own_nodes
        side = self.side_nodes
        to_left = np.zeros((2 * side, stack), np.float32)
        to_right = np.zeros((2 * side, stack), np.float32)
        for kind in range(2):
            for at_x in range(self.out_x):
                for k in range(NODES_OUT):
                    row = kind * side + at_x * NODES_OUT + k
                    to_left[row, self.center_row(at_x, k, kind)] = 1
                    last = self.node_y - NODES_OUT + k
                    to_right[row, self.center_row(at_x, last, kind)] = 1
        place = np.zeros((2, self.nodes, stack + 4 * side), np.float32)
        for kind in range(2):
            for at_x in range(self.out_x):
                for slot in range(self.node_y + 2 * NODES_OUT):
                    at_y = slot - NODES_OUT
                    if at_y < 0:
                        column = stack + kind * side + at_x * NODES_OUT + slot
                    elif at_y < self.node_y:
                        column = self.center_row(at_x, at_y, kind)
                    else:
                        k = at_y - self.node_y
                        column = stack + 2 * side + kind * side + at_x * NODES_OUT + k
                    place[kind, at_x * SLOTS + slot, column] = 1
        spread = np.zeros((2, 128, self.window), np.float32)
        match = np.zeros((2, SLOTS, self.window), np.float32)
        for dx in range(6):
            for at in range(self.pitch):
                if at < self.tile_y:
                    y = at
                elif at < self.tile_y + SIDE:
                    y = at - self.tile_y - SIDE
                else:
                    y = at - SIDE
                quotient, rest = (y + REACH) // 4, (y + REACH) % 4
                lane = dx * self.pitch + at
                spread[0, dx * 6 + rest, lane] = 1
                if 0 <= quotient < SLOTS:
                    match[0, quotient, lane] = 1
                if rest < 2:
                    spread[1, dx * 6 + rest + 4, lane] = 1
                    if 0 <= quotient - 1 < SLOTS:
                        match[1, quotient - 1, lane] = 1
        node = np.arange(self.nodes)
        quad = node // SLOTS // 2 * SLOTS + node % SLOTS // 2
        same = (quad[:, None] == quad[None, :]).astype(np.float32)
        return {
            "to_left": to_left,
            "to_right": to_right,
            "place": place,
            "spread": spread,
            "match": match,
            "quad": np.concatenate([same, same], axis=1),
        }


def blend_kernel(shape, wide_count, units, unit_rows, *refs):
    (wide_ref, own_ref, mesh_ref, w_force_ref, left_ref, right_ref, own_rows_ref) = refs[:7]
    count = len(units) - 1
    arrived = refs[7 : 7 + count]
    (blended_ref, to_left_ref, to_right_ref, stack_ref, rows_ref, key_ref) = refs[7 + count : 13 + count]
    (projected_ref,) = refs[13 + count :]
    from_prev, from_next = arrived[0], arrived[-1]
    wide_at = wide_ref[0]
    held = [own_rows_ref] + list(arrived)
    total = unit_rows * len(units)
    for k, start in enumerate(units):
        rows_ref[k * unit_rows : (k + 1) * unit_rows] = held[k][start : start + unit_rows]
    blocks = []
    if total <= LANES:
        metas = [
            held[k][start + unit_rows : start + unit_rows + 16].astype(F32)
            for k, start in enumerate(units)
        ]
        blocks.append(functools.reduce(lambda a, b: a + b, metas)[:, :total])
    else:
        for k, start in enumerate(units):
            for part in range(unit_rows // LANES):
                at = start + unit_rows + 16 * part
                blocks.append(held[k][at : at + 16].astype(F32))
    keys = []
    for block in blocks:
        whole = block.astype(jnp.int32)
        at_x = whole[0:1] * shape.tile_x + whole[1:2] - wide_at * shape.tile_x + REACH
        at_y = whole[2:3]
        inside = (at_x >= 0) & (at_x < shape.rows_x) & (at_y < shape.tile_y)
        keys.append(jnp.where(inside, at_x * shape.tile_y + at_y, -1))
    width = keys[0].shape[1]
    for k, key in enumerate(keys):
        key_ref[:, k * width : (k + 1) * width] = jnp.broadcast_to(key, (8, width))
    projected_ref[...] = dot(rows_ref[...], w_force_ref[...]).astype(BF16)

    mesh = 2 * shape.edge
    keep_prev = (wide_at > 0).astype(F32)
    keep_next = (wide_at < wide_count - 1).astype(F32)
    prev_mesh = from_prev[shape.halo : shape.halo + mesh].astype(F32) * keep_prev
    next_mesh = from_next[shape.halo : shape.halo + mesh].astype(F32) * keep_next
    stack = jnp.concatenate(
        [prev_mesh.astype(BF16), mesh_ref[...], next_mesh.astype(BF16)], axis=0
    )
    stack_ref[...] = stack
    to_left_ref[shape.side :] = dot(left_ref[...], stack).astype(BF16)
    to_right_ref[shape.side :] = dot(right_ref[...], stack).astype(BF16)

    tile_y = shape.tile_y
    inner = shape.halo + shape.cells
    jobs = [(from_prev, at, n, 0, keep_prev) for at, n in pieces(0, shape.halo, 3 * tile_y)]
    jobs += [(own_ref, at, n, shape.halo, None) for at, n in pieces(0, shape.cells, 4 * tile_y)]
    jobs += [(from_next, at, n, inner, keep_next) for at, n in pieces(0, shape.halo, 3 * tile_y)]
    for ref, at, n, base, keep in jobs:
        first = base + at
        value = ref[at : at + n].astype(F32)
        if keep is not None:
            value = value * keep
        cell = lax.broadcasted_iota(jnp.int32, (n, width), 0) + first
        for k, key in enumerate(keys):
            hit = jnp.where(cell == key, 1.0, 0.0).astype(BF16)
            value = value + dot(hit, projected_ref[k * width : (k + 1) * width])
        value = value.astype(BF16)
        blended_ref[first : first + n] = value
        for t in range(n // tile_y):
            row = first // tile_y + t
            to_left_ref[row * SIDE : (row + 1) * SIDE] = value[t * tile_y : t * tile_y + SIDE]
            to_right_ref[row * SIDE : (row + 1) * SIDE] = value[
                (t + 1) * tile_y - SIDE : (t + 1) * tile_y
            ]


def forward_kernel(
    shape, blended_ref, w_embed_ref, w_message_ref, message_ref, latent_ref, embed_ref, slope_ref
):
    inner = shape.halo + shape.cells
    jobs = pieces(0, shape.halo, 96) + pieces(shape.halo, inner, 128)
    jobs += pieces(inner, shape.center, 96)
    for at, n in jobs:
        blended = blended_ref[at : at + n]
        pre_embed = dot(blended, w_embed_ref[...])
        value, slope = silu_and_slope(pre_embed)
        latent = (blended.astype(F32) + value).astype(BF16)
        pre_message = dot(latent, w_message_ref[...])
        message, message_slope = silu_and_slope(pre_message)
        message_ref[at : at + n] = message.astype(BF16)
        if shape.halo <= at < inner:
            own = at - shape.halo
            latent_ref[own : own + n] = latent
            embed_ref[own : own + n] = slope
            slope_ref[own : own + n] = message_slope


def backward_kernel(shape, total_rows, *refs):
    (
        narrow_ref,
        from_left_ref,
        from_right_ref,
        stack_ref,
        blended_ref,
        message_ref,
        latent_ref,
        embed_ref,
        slope_ref,
        rows_ref,
        key_ref,
        place_ref,
        spread_ref,
        match_ref,
        quad_ref,
        w_force_ref,
        w_embed_ref,
        w_message_ref,
        w_one_ref,
        w_two_ref,
        state_ref,
        back_ref,
        sent_ref,
        kept_ref,
        padded_ref,
        level_ref,
        cover_ref,
        pmb_ref,
        peb_ref,
        grads_ref,
    ) = refs
    tile_y, pitch = shape.tile_y, shape.pitch
    channels = blended_ref.shape[1]

    for ref, offset in ((from_left_ref, tile_y), (from_right_ref, tile_y + SIDE)):
        for at, n in pieces(0, shape.side, 8 * SIDE):
            blended = ref[at : at + n]
            latent = (blended.astype(F32) + silu(dot(blended, w_embed_ref[...]))).astype(BF16)
            message = silu(dot(latent, w_message_ref[...])).astype(BF16)
            for t in range(n // SIDE):
                row = (at // SIDE + t) * pitch + offset
                padded_ref[row : row + SIDE] = message[t * SIDE : (t + 1) * SIDE]
    for row in range(shape.rows_x):
        padded_ref[row * pitch : row * pitch + tile_y] = message_ref[
            row * tile_y : (row + 1) * tile_y
        ]

    stack = jnp.concatenate(
        [stack_ref[...], from_left_ref[shape.side :], from_right_ref[shape.side :]], axis=0
    )
    cotangent = dot(place_ref[0], stack)
    mask = dot(place_ref[1], stack[:, :128]).astype(BF16)
    near = dot(mask, spread_ref[0])
    far = dot(mask, spread_ref[1])
    windows = []
    for at_x in range(shape.out_x):
        rows = slice(at_x * SLOTS, (at_x + 1) * SLOTS)
        windows.append(near[rows] * match_ref[0] + far[rows] * match_ref[1])
        level_ref[rows] = (
            dot(
                windows[-1].astype(BF16),
                padded_ref[4 * at_x * pitch : 4 * at_x * pitch + shape.window],
            )
            / 6.0
        ).astype(BF16)
    turned = jnp.concatenate(windows, axis=0).T
    node_x = lax.broadcasted_iota(jnp.int32, (tile_y, shape.nodes), 1) // SLOTS
    for at_x in range(shape.tile_x):
        quotient, rest = (at_x + REACH) // 4, (at_x + REACH) % 4
        cover = jnp.where(node_x == quotient, turned[rest * pitch : rest * pitch + tile_y], 0.0)
        if rest < 2:
            again = (rest + 4) * pitch
            cover = cover + jnp.where(
                node_x == quotient - 1, turned[again : again + tile_y], 0.0
            )
        cover = cover.astype(BF16)
        cover_ref[at_x * tile_y : (at_x + 1) * tile_y] = jnp.concatenate([cover, cover], axis=1)

    level_one = level_ref[...]
    pre_one = dot(level_one, w_one_ref[...])
    value, slope_one = silu_and_slope(pre_one)
    state_one = level_one.astype(F32) + value
    level_two = (0.25 * dot(quad_ref[...], two_halves(state_one))).astype(BF16)
    pre_two = dot(level_two, w_two_ref[...])
    two_bar = dot(quad_ref[:, : shape.nodes], cotangent.astype(BF16))
    pre_two_bar = (two_bar * silu_and_slope(pre_two)[1]).astype(BF16)
    pooled_bar = two_bar + dot_right_t(pre_two_bar, w_two_ref[...])
    one_bar = cotangent + 0.25 * pooled_bar
    pre_one_bar = (one_bar * slope_one).astype(BF16)
    level_bar = one_bar + dot_right_t(pre_one_bar, w_one_ref[...])

    node = lax.broadcasted_iota(jnp.int32, (shape.nodes, channels), 0)
    at_x, at_y = node // SLOTS, node % SLOTS
    owned = (at_x >= NODES_OUT) & (at_x < NODES_OUT + shape.node_x)
    owned = owned & (at_y >= NODES_OUT) & (at_y < NODES_OUT + shape.node_y)
    first = owned & (at_x % 2 == 0) & (at_y % 2 == 0)
    grads_ref[3 * channels : 4 * channels] = dot_left_t(
        level_one, jnp.where(owned, pre_one_bar.astype(F32), 0.0).astype(BF16)
    )
    grads_ref[4 * channels :] = dot_left_t(
        level_two, jnp.where(first, pre_two_bar.astype(F32), 0.0).astype(BF16)
    )

    both = two_halves(level_bar)
    for at, n in pieces(0, shape.cells, 128):
        rows = slice(at, at + n)
        message_bar = dot(cover_ref[rows], both) / 6.0
        pre_message_bar = (message_bar * slope_ref[rows]).astype(BF16)
        pmb_ref[rows] = pre_message_bar
        latent_bar = dot_right_t(pre_message_bar, w_message_ref[...])
        pre_embed_bar = (latent_bar * embed_ref[rows]).astype(BF16)
        peb_ref[rows] = pre_embed_bar
        state_ref[rows] = (latent_bar + dot_right_t(pre_embed_bar, w_embed_ref[...])).astype(BF16)
    own = slice(shape.halo, shape.halo + shape.cells)
    grads_ref[channels : 2 * channels] = dot_left_t(blended_ref[own], peb_ref[...])
    grads_ref[2 * channels : 3 * channels] = dot_left_t(latent_ref[...], pmb_ref[...])

    width = min(total_rows, LANES)
    cell = lax.broadcasted_iota(jnp.int32, (shape.cells, width), 0) + shape.halo
    grad_force = None
    for at in range(0, total_rows, width):
        rows = slice(at, at + width)
        hit = jnp.where(cell == key_ref[0:1, rows], 1.0, 0.0).astype(BF16)
        slot_bar = dot_left_t(hit, state_ref[...]).astype(BF16)
        back_ref[rows] = dot_right_t(slot_bar, w_force_ref[...]).astype(BF16)
        term = dot_left_t(rows_ref[rows], slot_bar)
        grad_force = term if grad_force is None else grad_force + term
    grads_ref[:channels] = grad_force

    half = sent_ref.shape[0]
    upper = narrow_ref[0] % 2
    kept_at = pl.multiple_of(upper * half, half)
    sent_at = pl.multiple_of((1 - upper) * half, half)
    sent_ref[...] = grads_ref[pl.ds(sent_at, half)].astype(BF16)
    kept_ref[...] = grads_ref[pl.ds(kept_at, half)]


def call(kernel, out_shapes, operands, scratch=(), scalars=1, flops=0):
    specs = [pl.BlockSpec(memory_space=pltpu.SMEM)] * scalars
    specs += [pl.BlockSpec(memory_space=pltpu.VMEM)] * (len(operands) - scalars)
    moved = sum(math.prod(o.shape) * o.dtype.itemsize for o in list(operands) + list(out_shapes))
    return pl.pallas_call(
        kernel,
        out_shape=tuple(out_shapes),
        in_specs=specs,
        out_specs=tuple(pl.BlockSpec(memory_space=pltpu.VMEM) for _ in out_shapes),
        scratch_shapes=list(scratch),
        compiler_params=pltpu.CompilerParams(vmem_limit_bytes=VMEM_LIMIT),
        cost_estimate=pl.CostEstimate(flops=flops, bytes_accessed=moved, transcendentals=0),
    )(*operands)


def meta_rows(live, target_x, target_y, tile_x, unit_rows, slot, units):
    high = target_x // tile_x
    low = target_x % tile_x
    column = jnp.where(live, target_y, LANES - 1)
    fields = jnp.stack([high, low, column]).astype(F32)
    if unit_rows * units <= LANES:
        before = slot * unit_rows
        after = LANES - before - unit_rows
        return jnp.pad(fields, ((0, 13), (before, after))).astype(BF16)
    blocks = unit_rows // LANES
    fields = fields.reshape(3, blocks, LANES).transpose(1, 0, 2)
    return jnp.pad(fields, ((0, 0), (0, 13), (0, 0))).reshape(16 * blocks, LANES).astype(BF16)


def local(
    grid_state,
    boundary_rows,
    row_count,
    target_x,
    target_y,
    g2m_mask,
    mesh_cotangent,
    w_force,
    w_embed,
    w_message,
    w_level_one,
    w_level_two,
):
    tile_x, tile_y, channels = grid_state.shape
    wide_count = lax.axis_size("wide")
    narrow_count = lax.axis_size("narrow")
    wide_at = lax.axis_index("wide")
    narrow_at = lax.axis_index("narrow")
    held_rows = boundary_rows.shape[0]
    shape = Shape(tile_x, tile_y)
    table = {name: jnp.asarray(value, BF16) for name, value in shape.tables().items()}
    table["match"] = table["match"].astype(F32)

    live = jnp.arange(held_rows) < row_count[0]
    column = target_y - narrow_at * tile_y
    whole_column = held_rows * wide_count <= LANES
    if whole_column:
        units = wide_count
        unit_rows = held_rows
        rows, row_live, row_x, row_y = boundary_rows, live, target_x, column
    else:
        slot_count = wide_count * CAP
        destination = target_x // tile_x
        matches = (destination[:, None] == jnp.arange(wide_count)[None, :]) & live[:, None]
        running = jnp.cumsum(matches.astype(jnp.int32), axis=0) - 1
        slot_index = jnp.sum(jnp.where(matches, running, 0), axis=1)
        send_slot = jnp.where(live, destination * CAP + slot_index, slot_count)
        cells = jnp.full((slot_count,), -1, jnp.int32)
        cells = cells.at[send_slot].set(target_x % tile_x * tile_y + column, mode="drop")
        outgoing = jnp.zeros((slot_count, channels), BF16)
        outgoing = outgoing.at[send_slot].set(boundary_rows, mode="drop")
        outgoing = outgoing.reshape(wide_count, CAP, channels)
        rows = lax.all_to_all(outgoing, "wide", split_axis=0, concat_axis=0, tiled=True)
        cells = lax.all_to_all(
            cells.reshape(wide_count, CAP), "wide", split_axis=0, concat_axis=0, tiled=True
        )
        rows = rows.reshape(slot_count, channels)
        cells = cells.reshape(slot_count)
        units = 3
        unit_rows = slot_count
        row_live = cells >= 0
        row_x = jnp.where(row_live, wide_at * tile_x + cells // tile_y, 0)
        row_y = cells % tile_y

    def with_meta(slot):
        return [rows, meta_rows(row_live, row_x, row_y, tile_x, unit_rows, slot, units)]

    cells = grid_state.reshape(-1, channels)
    mask = g2m_mask.astype(BF16).transpose(1, 2, 0)
    mask = jnp.pad(mask, ((0, 0), (0, 0), (0, channels - 36)))
    edge = slice(0, NODES_OUT), slice(shape.node_x - NODES_OUT, shape.node_x)
    flat = [
        [mesh_cotangent[part].reshape(-1, channels), mask[part].reshape(-1, channels)]
        for part in edge
    ]
    mesh = jnp.concatenate([mesh_cotangent.reshape(-1, channels), mask.reshape(-1, channels)])
    to_prev = jnp.concatenate([cells[: shape.halo]] + flat[0] + with_meta(units - 1))
    to_next = jnp.concatenate([cells[-shape.halo :]] + flat[1] + with_meta(1))
    own_rows = jnp.concatenate(with_meta(0))
    arrived = [shifted(to_next, "wide", 1)]
    starts = [0, shape.halo + 2 * shape.edge]
    for step in range(2, units - 1):
        arrived.append(shifted(jnp.concatenate(with_meta(step)), "wide", step))
        starts.append(0)
    arrived.append(shifted(to_prev, "wide", -1))
    starts.append(shape.halo + 2 * shape.edge)

    total_rows = unit_rows * units
    stack_rows = 4 * shape.edge + 2 * shape.own_nodes
    struct = jax.ShapeDtypeStruct
    payload = struct((shape.side + 2 * shape.side_nodes, channels), BF16)
    blended, to_left, to_right, stack, all_rows, keys = call(
        functools.partial(blend_kernel, shape, wide_count, starts, unit_rows),
        [
            struct((shape.center, channels), BF16),
            payload,
            payload,
            struct((stack_rows, channels), BF16),
            struct((total_rows, channels), BF16),
            struct((8, total_rows), jnp.int32),
        ],
        [wide_at.reshape(1), cells, mesh, w_force, table["to_left"], table["to_right"], own_rows]
        + arrived,
        scratch=[pltpu.VMEM((total_rows, channels), BF16)],
        flops=2 * shape.center * total_rows * channels,
    )
    ends = narrow_count - 1
    from_left = lax.ppermute(to_right, "narrow", [(i, i + 1) for i in range(ends)])
    from_right = lax.ppermute(to_left, "narrow", [(i + 1, i) for i in range(ends)])
    message, latent, embed_slope, message_slope = call(
        functools.partial(forward_kernel, shape),
        [
            struct((shape.center, channels), BF16),
            struct((shape.cells, channels), BF16),
            struct((shape.cells, channels), F32),
            struct((shape.cells, channels), F32),
        ],
        [blended, w_embed, w_message],
        scalars=0,
        flops=4 * shape.center * channels * channels,
    )
    grad_rows_total = 5 * channels
    grad_state, back, sent, kept = call(
        functools.partial(backward_kernel, shape, total_rows),
        [
            struct((shape.cells, channels), BF16),
            struct((total_rows, channels), BF16),
            struct((grad_rows_total // 2, channels), BF16),
            struct((grad_rows_total // 2, channels), F32),
        ],
        [
            narrow_at.reshape(1),
            from_left,
            from_right,
            stack,
            blended,
            message,
            latent,
            embed_slope,
            message_slope,
            all_rows,
            keys,
            table["place"],
            table["spread"],
            table["match"],
            table["quad"],
            w_force,
            w_embed,
            w_message,
            w_level_one,
            w_level_two,
        ],
        scratch=[
            pltpu.VMEM((shape.rows_x * shape.pitch, channels), BF16),
            pltpu.VMEM((shape.nodes, channels), BF16),
            pltpu.VMEM((shape.cells, 2 * shape.nodes), BF16),
            pltpu.VMEM((shape.cells, channels), BF16),
            pltpu.VMEM((shape.cells, channels), BF16),
            pltpu.VMEM((grad_rows_total, channels), F32),
        ],
        flops=12 * shape.cells * channels * channels,
    )

    bits = [1 << k for k in range(narrow_count.bit_length() - 1)]
    piece = kept + swapped(sent, "narrow", bits[0]).astype(F32)
    for bit in bits[1:]:
        half = piece.shape[0] // 2
        upper = (narrow_at // bit) % 2
        sent = lax.dynamic_slice_in_dim(piece, (1 - upper) * half, half).astype(BF16)
        kept = lax.dynamic_slice_in_dim(piece, upper * half, half)
        piece = kept + swapped(sent, "narrow", bit).astype(F32)
    part = piece.shape[0] // wide_count
    rounded = piece.astype(BF16)
    total = lax.dynamic_slice_in_dim(piece, wide_at * part, part)
    row_back = back[:unit_rows].astype(F32)
    for step in range(1, wide_count):
        target = (wide_at + step) % wide_count
        sent = lax.dynamic_slice_in_dim(rounded, target * part, part)
        if whole_column:
            source = wide_count - step
            rows_back = back[source * unit_rows : (source + 1) * unit_rows]
            got = shifted(jnp.concatenate([sent, rows_back]), "wide", step).astype(F32)
            row_back = row_back + got[part:]
            total = total + got[:part]
        else:
            total = total + shifted(sent, "wide", step).astype(F32)
    if whole_column:
        row_back = row_back.astype(BF16)
    else:
        returned = lax.all_to_all(
            back[:unit_rows].reshape(wide_count, CAP, channels),
            "wide",
            split_axis=0,
            concat_axis=0,
            tiled=True,
        )
        row_back = jnp.take(
            returned.reshape(-1, channels), send_slot, axis=0, mode="fill", fill_value=0
        )
    own = total.astype(BF16)
    gathered = jnp.zeros((wide_count * part, channels), BF16)
    gathered = lax.dynamic_update_slice_in_dim(gathered, own, wide_at * part, 0)
    for step in range(1, wide_count):
        source = (wide_at - step) % wide_count
        gathered = lax.dynamic_update_slice_in_dim(
            gathered, shifted(own, "wide", step), source * part, 0
        )
    for bit in reversed(bits):
        upper = (narrow_at // bit) % 2
        other = swapped(gathered, "narrow", bit)
        gathered = jnp.where(
            upper == 0,
            jnp.concatenate([gathered, other]),
            jnp.concatenate([other, gathered]),
        )
    cell_total = shape.cells * wide_count * narrow_count
    row_total = held_rows * wide_count * narrow_count
    scales = np.array(
        [
            1.0 / math.sqrt(row_total),
            1.0 / math.sqrt(cell_total),
            1.0 / math.sqrt(cell_total),
            1.0 / math.sqrt(cell_total // 16),
            1.0 / math.sqrt(cell_total // 64),
        ],
        np.float32,
    )
    weight_grads = gathered.reshape(5, channels, channels).astype(F32) * scales[:, None, None]
    return (grad_state.reshape(tile_x, tile_y, channels), row_back, weight_grads)


def solution(mesh):
    in_specs = (
        P(("groups", "wide"), "narrow", None),
        P(("groups", "wide", "narrow"), None),
        P(("groups", "wide", "narrow")),
        P(("groups", "wide", "narrow")),
        P(("groups", "wide", "narrow")),
        P(None, ("groups", "wide"), "narrow"),
        P(("groups", "wide"), "narrow", None),
        P(),
        P(),
        P(),
        P(),
        P(),
    )
    out_specs = (
        P(("groups", "wide"), "narrow", None),
        P(("groups", "wide", "narrow"), None),
        P("groups", None, None),
    )
    return jax.shard_map(local, mesh=mesh, in_specs=in_specs, out_specs=out_specs, check_vma=False)
```

time: 192 us -> 67.6 us (0.35)
  waiting for transfers between devices: 106 us -> 31.4 us
  between operations: 15.6 us -> 1.69 us
  local copies, waits for them, and re-layouts: 16.2 us -> 3 us
  other arithmetic: 15.8 us -> 3.23 us
  matrix products: 8.39 us -> 0 us
  starting transfers between devices: 29.5 us -> 22.9 us
  Pallas kernels: 0 us -> 4.97 us
    psum x1 -> x0, waiting for transfers between devices: 83.5 us -> none  [local(): lax.psum((grad_force, grad_embed, grad_message, grad_one, grad_two), ('wi...]
    ppermute x8 -> x15, waiting for transfers between devices: 12.2 us -> 31.4 us  [the longest x9 15.6 us: shifted(): lax.ppermute(block, axis, [(i, (i + step) % count) for i in range(count)])]
    all_to_all x3 -> x0, starting transfers between devices: 14.7 us -> none  [the longest x1 6.32 us: local(): lax.all_to_all(slot_cells.reshape(wide_count, CAP), 'wide', split_axis=0,...]
    all_to_all x3 -> x0, waiting for transfers between devices: 9.93 us -> none  [the longest x1 5.62 us: local(): lax.all_to_all(back_payload.reshape(wide_count, CAP, channels), 'wide', s...]
    dot_general x15 -> x0, matrix products: 8.39 us -> none  [the longest x1 1.1 us: grid_backward(): jnp.dot(blended.T, pre_embed_bar, preferred_element_type=jnp.float32)]
    ppermute x8 -> x15, starting transfers between devices: 14.8 us -> 22.9 us  [the longest x9 14 us: shifted(): lax.ppermute(block, axis, [(i, (i + step) % count) for i in range(count)])]
    slice x40 -> x2, local copies, waits for them, and re-layouts: 7.01 us -> 1.14 us  [the longest x1 1.13 us: local(): cells[:shape.halo]]
    pallas_call x0 -> x3, Pallas kernels: none -> 4.97 us  [call(): pl.pallas_call(kernel, out_shape=tuple(out_shapes), in_specs=specs, out_s...]
  transfers between devices with their start and end apart: 12 -> 15, of which waited for: 7 -> 11; matrix products, arithmetic and copies ran while one was open for 9% -> 1% of each run, Pallas kernels for 0% -> 1%
where the time goes in v2:
time: 67.6 us; the launch traced here: 67.2 us
  waiting for transfers between devices  31.4 us (46%)
  starting transfers between devices  22.9 us (34%)
  Pallas kernels  4.97 us (7%)
  other arithmetic  3.23 us (5%)
  local copies, waits for them, and re-layouts  3 us (4%)
  between operations  1.69 us (2%)
    ppermute x9, waiting for transfers between devices, shifted(): lax.ppermute(block, axis, [(i, (i + step) % count) for i in range(count)])  15.6 us
    ppermute x9, starting transfers between devices, shifted(): lax.ppermute(block, axis, [(i, (i + step) % count) for i in range(count)])  14 us
    ppermute x4, waiting for transfers between devices, swapped(): return lax.ppermute(block, axis, [(i, i ^ bit) for i in range(count)])  13.5 us
    ppermute x4, starting transfers between devices, swapped(): return lax.ppermute(block, axis, [(i, i ^ bit) for i in range(count)])  5.7 us
    pallas_call x3, Pallas kernels, call(): pl.pallas_call(kernel, out_shape=tuple(out_shapes), in_specs=specs, out_s...  4.97 us
    ppermute x1, waiting for transfers between devices, local(): lax.ppermute(to_left, 'narrow', [(i + 1, i) for i in range(ends)])  2.3 us
    ppermute x1, starting transfers between devices, local(): lax.ppermute(to_right, 'narrow', [(i, i + 1) for i in range(ends)])  1.94 us
    unnamed x38, local copies, waits for them, and re-layouts  1.71 us
  transfers between devices with their start and end apart: 15, of which 11 were waited for; matrix products, arithmetic and copies ran while one was open for 1% of the time, Pallas kernels for 1%

profile of v2, /device:TPU:0, one launch (start us, length us, event | category | flops | bytes accessed | tf_op | source)
XLA Modules:
  0.0 67.2 jit_solution(4647941452958077156)
XLA Ops:
  0.7 1.1 %fusion.12 = (bf16[9,32,256]{2,1,0:T(8,128)(2,1)S(1)}, bf16[9,32,256]{2,1,0:T(8,128)(2,1)S(1)}) fusion(bf16[16,32,256]{2,1,0:T(8,128)(2,1)} %param.19), kind=kLoop, calls=%fused_computation.58 | loop fusion | bytes 589824 | tf_op jit(solution)/shard_map/slice | solution.py:482
  1.9 0.7 %convert_bitcast_fusion = bf16[4,8,36]{2,1,0:T(8,128)(2,1)S(1)} fusion(s32[36,4,8]{0,2,1:T(8,128)} %param.24), kind=kLoop, calls=%fused_computation.38 | loop fusion | flops 1152 | bytes 6912 | tf_op jit(solution)/shard_map/transpose | solution.py:474
  3.4 0.9 %constant_dynamic-update-slice_fusion.8 = (bf16[368,256]{1,0:T(8,128)(2,1)S(1)}, bf16[368,256]{1,0:T(8,128)(2,1)S(1)}) fusion(bf16[368,256]{1,0:T(8,128)(2,1)S(1)} %get-tuple-element.57, bf16[4,8,256]{2,1,0:T(8,128)(2,1)} %param.25, bf16[368,256]{1,0:T(8,128)(2,1)S(1)} %get-tuple-element.56), kind=kLoop, calls=%fused_computation.31 | loop fusion | bytes 32768
  4.2 0.7 %constant_dynamic-update-slice_fusion.6 = (bf16[368,256]{1,0:T(8,128)(2,1)S(1)}, bf16[368,256]{1,0:T(8,128)(2,1)S(1)}) fusion(bf16[368,256]{1,0:T(8,128)(2,1)S(1)} %get-tuple-element.49, bf16[32,256]{1,0:T(8,128)(2,1)} %param.20, bf16[368,256]{1,0:T(8,128)(2,1)S(1)} %get-tuple-element.50), kind=kLoop, calls=%fused_computation.29 | loop fusion | bytes 49152
  5.1 3.0 %collective-permute-start = (bf16[368,256]{1,0:T(8,128)(2,1)S(1)}, bf16[368,256]{1,0:T(8,128)(2,1)S(1)}, u32[]{:S(2)}, u32[]{:S(2)}) collective-permute-start(bf16[368,256]{1,0:T(8,128)(2,1)S(1)} %get-tuple-element.52), channel_id=1, source_target_pairs={{0,4},{4,8},{8,12},{12,0},{1,5},{5,9},{9,13},{13,1},{2,6},{6,10},{... | collective-permute-start | bytes 565256 | tf_op jit(solution)/shard_map/ppermute | solution.py:30
  8.1 2.1 %collective-permute-start.2 = (bf16[368,256]{1,0:T(8,128)(2,1)S(1)}, bf16[368,256]{1,0:T(8,128)(2,1)S(1)}, u32[]{:S(2)}, u32[]{:S(2)}) collective-permute-start(bf16[368,256]{1,0:T(8,128)(2,1)S(1)} %get-tuple-element.51), channel_id=1, source_target_pairs={{0,12},{4,0},{8,4},{12,8},{1,13},{5,1},{9,5},{13,9},{2,14},{6,2},{... | collective-permute-start | bytes 565256 | tf_op jit(solution)/shard_map/ppermute | solution.py:30
  10.3 1.0 %collective-permute-start.1 = (bf16[48,256]{1,0:T(8,128)(2,1)S(1)}, bf16[48,256]{1,0:T(8,128)(2,1)S(1)}, u32[]{:S(2)}, u32[]{:S(2)}) collective-permute-start(bf16[48,256]{1,0:T(8,128)(2,1)S(1)} %get-tuple-element.43), channel_id=1, source_target_pairs={{0,8},{4,12},{8,0},{12,4},{1,9},{5,13},{9,1},{13,5},{2,10},{6,14},... | collective-permute-start | bytes 73736 | tf_op jit(solution)/shard_map/ppermute | solution.py:30
  11.2 8.7 %collective-permute-done.1.refs_8_ = bf16[48,256]{1,0:T(8,128)(2,1)S(1)} collective-permute-done((bf16[48,256]{1,0:T(8,128)(2,1)S(1)}, bf16[48,256]{1,0:T(8,128)(2,1)S(1)}, u32[]{:S(2)}, u32[]{:S(2)}) %collective-permute-start.1) | collective-permute-done | bytes 24608 | tf_op jit(solution)/shard_map/ppermute | solution.py:30
  20.0 0.5 shard_map.202
  20.5 1.9 %collective-permute-start.3 = (bf16[576,256]{1,0:T(8,128)(2,1)S(1)}, bf16[576,256]{1,0:T(8,128)(2,1)S(1)}, u32[]{:S(2)}, u32[]{:S(2)}) collective-permute-start(bf16[576,256]{1,0:T(8,128)(2,1)S(1)} %get-tuple-element.17), channel_id=1, source_target_pairs={{0,1},{1,2},{2,3},{4,5},{5,6},{6,7},{8,9},{9,10},{10,11},{12,13},{... | collective-permute-start | bytes 884744 | tf_op jit(solution)/shard_map/ppermute | solution.py:513
  22.4 1.3 %collective-permute-start.4 = (bf16[576,256]{1,0:T(8,128)(2,1)S(1)}, bf16[576,256]{1,0:T(8,128)(2,1)S(1)}, u32[]{:S(2)}, u32[]{:S(2)}) collective-permute-start(bf16[576,256]{1,0:T(8,128)(2,1)S(1)} %get-tuple-element.18), channel_id=1, source_target_pairs={{1,0},{2,1},{3,2},{5,4},{6,5},{7,6},{9,8},{10,9},{11,10},{13,12},{... | collective-permute-start | bytes 884744 | tf_op jit(solution)/shard_map/ppermute | solution.py:514
  23.7 0.9 %shard_map.203 = (bf16[1088,256]{1,0:T(8,128)(2,1)S(1)}, bf16[512,256]{1,0:T(8,128)(2,1)S(1)}, f32[512,256]{1,0:T(8,128)S(1)}, f32[512,256]{1,0:T(8,128)S(1)}) custom-call(bf16[1088,256]{1,0:T(8,128)(2,1)S(1)} %get-tuple-element.20.blended_ref.refs_4_, bf16[256,256]{1,0:T(8,128)(2,1)S(1)} %copy-done.3, bf16[256,256]{1,0:T(8,128)(2,1)S(1)} %copy-done.4), custom_call_target="tpu_custom_call" | custom-call | flops 285212672 | bytes 2686976 | tf_op jit(solution)/shard_map/pallas_call | solution.py:390
  24.7 2.3 %collective-permute-done.4.refs_2_ = bf16[576,256]{1,0:T(8,128)(2,1)S(1)} collective-permute-done((bf16[576,256]{1,0:T(8,128)(2,1)S(1)}, bf16[576,256]{1,0:T(8,128)(2,1)S(1)}, u32[]{:S(2)}, u32[]{:S(2)}) %collective-permute-start.4) | collective-permute-done | bytes 294944 | tf_op jit(solution)/shard_map/ppermute | solution.py:514
  27.0 3.6 %shard_map.204 = (bf16[512,256]{1,0:T(8,128)(2,1)}, bf16[128,256]{1,0:T(8,128)(2,1)S(1)}, bf16[640,256]{1,0:T(8,128)(2,1)S(1)}, f32[640,256]{1,0:T(8,128)S(1)}) custom-call(s32[1]{0:T(128)} %bitcast.refs_0_, bf16[576,256]{1,0:T(8,128)(2,1)S(1)} %collective-permute-done.3.refs_1_, bf16[576,256]{1,0:T(8,128)(2,1)S(1)} %collective-permute-done.4.refs_2_, ...), custom_call_target="tpu_custom_call" | custom-call | flops 402653184 | bytes 5525508 | tf_op jit(solution)/shard_map/pallas_call | solution.py:390
  30.6 5.1 %collective-permute-start.5 = (bf16[640,256]{1,0:T(8,128)(2,1)S(1)}, bf16[640,256]{1,0:T(8,128)(2,1)S(1)}, u32[]{:S(2)}, u32[]{:S(2)}) collective-permute-start(bf16[640,256]{1,0:T(8,128)(2,1)S(1)} %get-tuple-element.30), channel_id=1, source_target_pairs={{0,1},{1,0},{2,3},{3,2},{4,5},{5,4},{6,7},{7,6},{8,9},{9,8},{10,11... | collective-permute-start | bytes 983048 | tf_op jit(solution)/shard_map/ppermute | solution.py:25
  35.6 1.3 %collective-permute-done.5 = bf16[640,256]{1,0:T(8,128)(2,1)S(1)} collective-permute-done((bf16[640,256]{1,0:T(8,128)(2,1)S(1)}, bf16[640,256]{1,0:T(8,128)(2,1)S(1)}, u32[]{:S(2)}, u32[]{:S(2)}) %collective-permute-start.5) | collective-permute-done | bytes 327712 | tf_op jit(solution)/shard_map/ppermute | solution.py:25
  37.2 6.4 %collective-permute-done.6 = bf16[320,256]{1,0:T(8,128)(2,1)S(1)} collective-permute-done((bf16[320,256]{1,0:T(8,128)(2,1)S(1)}, bf16[320,256]{1,0:T(8,128)(2,1)S(1)}, u32[]{:S(2)}, u32[]{:S(2)}) %collective-permute-start.6) | collective-permute-done | bytes 163872 | tf_op jit(solution)/shard_map/ppermute | solution.py:25
  43.9 2.0 %collective-permute-start.8 = (bf16[112,256]{1,0:T(8,128)(2,1)S(1)}, bf16[112,256]{1,0:T(8,128)(2,1)S(1)}, u32[]{:S(2)}, u32[]{:S(2)}) collective-permute-start(bf16[112,256]{1,0:T(8,128)(2,1)S(1)} %pad_maximum_fusion.1), channel_id=1, source_target_pairs={{0,8},{4,12},{8,0},{12,4},{1,9},{5,13},{9,1},{13,5},{2,10},{6,14},... | collective-permute-start | bytes 172040 | tf_op jit(solution)/shard_map/ppermute | solution.py:30
  45.9 1.7 %collective-permute-start.9 = (bf16[112,256]{1,0:T(8,128)(2,1)S(1)}, bf16[112,256]{1,0:T(8,128)(2,1)S(1)}, u32[]{:S(2)}, u32[]{:S(2)}) collective-permute-start(bf16[112,256]{1,0:T(8,128)(2,1)S(1)} %pad_maximum_fusion.2), channel_id=1, source_target_pairs={{0,12},{4,0},{8,4},{12,8},{1,13},{5,1},{9,5},{13,9},{2,14},{6,2},{... | collective-permute-start | bytes 172040 | tf_op jit(solution)/shard_map/ppermute | solution.py:30
  47.6 2.5 %collective-permute-done.7 = bf16[112,256]{1,0:T(8,128)(2,1)S(1)} collective-permute-done((bf16[112,256]{1,0:T(8,128)(2,1)S(1)}, bf16[112,256]{1,0:T(8,128)(2,1)S(1)}, u32[]{:S(2)}, u32[]{:S(2)}) %collective-permute-start.7) | collective-permute-done | bytes 57376 | tf_op jit(solution)/shard_map/ppermute | solution.py:30
  50.1 0.9 %collective-permute-done.8 = bf16[112,256]{1,0:T(8,128)(2,1)S(1)} collective-permute-done((bf16[112,256]{1,0:T(8,128)(2,1)S(1)}, bf16[112,256]{1,0:T(8,128)(2,1)S(1)}, u32[]{:S(2)}, u32[]{:S(2)}) %collective-permute-start.8) | collective-permute-done | bytes 57376 | tf_op jit(solution)/shard_map/ppermute | solution.py:30
  51.2 1.4 %collective-permute-start.10 = (bf16[80,256]{1,0:T(8,128)(2,1)S(1)}, bf16[80,256]{1,0:T(8,128)(2,1)S(1)}, u32[]{:S(2)}, u32[]{:S(2)}) collective-permute-start(bf16[80,256]{1,0:T(8,128)(2,1)S(1)} %get-tuple-element.32), channel_id=1, source_target_pairs={{0,4},{4,8},{8,12},{12,0},{1,5},{5,9},{9,13},{13,1},{2,6},{6,10},{... | collective-permute-start | bytes 122888 | tf_op jit(solution)/shard_map/ppermute | solution.py:30
  52.6 1.8 %collective-permute-start.11 = (bf16[80,256]{1,0:T(8,128)(2,1)S(1)}, bf16[80,256]{1,0:T(8,128)(2,1)S(1)}, u32[]{:S(2)}, u32[]{:S(2)}) collective-permute-start(bf16[80,256]{1,0:T(8,128)(2,1)S(1)} %get-tuple-element.32), channel_id=1, source_target_pairs={{0,8},{4,12},{8,0},{12,4},{1,9},{5,13},{9,1},{13,5},{2,10},{6,14},... | collective-permute-start | bytes 122888 | tf_op jit(solution)/shard_map/ppermute | solution.py:30
  54.4 0.7 %collective-permute-start.12 = (bf16[80,256]{1,0:T(8,128)(2,1)S(1)}, bf16[80,256]{1,0:T(8,128)(2,1)S(1)}, u32[]{:S(2)}, u32[]{:S(2)}) collective-permute-start(bf16[80,256]{1,0:T(8,128)(2,1)S(1)} %get-tuple-element.32), channel_id=1, source_target_pairs={{0,12},{4,0},{8,4},{12,8},{1,13},{5,1},{9,5},{13,9},{2,14},{6,2},{... | collective-permute-start | bytes 122888 | tf_op jit(solution)/shard_map/ppermute | solution.py:30
  55.1 2.2 %collective-permute-done.10 = bf16[80,256]{1,0:T(8,128)(2,1)S(1)} collective-permute-done((bf16[80,256]{1,0:T(8,128)(2,1)S(1)}, bf16[80,256]{1,0:T(8,128)(2,1)S(1)}, u32[]{:S(2)}, u32[]{:S(2)}) %collective-permute-start.10) | collective-permute-done | bytes 40992 | tf_op jit(solution)/shard_map/ppermute | solution.py:30
  57.4 0.7 %collective-permute-done.11 = bf16[80,256]{1,0:T(8,128)(2,1)S(1)} collective-permute-done((bf16[80,256]{1,0:T(8,128)(2,1)S(1)}, bf16[80,256]{1,0:T(8,128)(2,1)S(1)}, u32[]{:S(2)}, u32[]{:S(2)}) %collective-permute-start.11) | collective-permute-done | bytes 40992 | tf_op jit(solution)/shard_map/ppermute | solution.py:30
  58.1 0.4 collective-permute-done.12
  58.6 0.4 collective-permute-start.13
  59.0 4.9 %collective-permute-done.13 = bf16[320,256]{1,0:T(8,128)(2,1)S(1)} collective-permute-done((bf16[320,256]{1,0:T(8,128)(2,1)S(1)}, bf16[320,256]{1,0:T(8,128)(2,1)S(1)}, u32[]{:S(2)}, u32[]{:S(2)}) %collective-permute-start.13) | collective-permute-done | bytes 163872 | tf_op jit(solution)/shard_map/ppermute | solution.py:25
  64.1 0.6 fusion.3
  64.7 1.0 %collective-permute-done.14 = bf16[640,256]{1,0:T(8,128)(2,1)S(1)} collective-permute-done((bf16[640,256]{1,0:T(8,128)(2,1)S(1)}, bf16[640,256]{1,0:T(8,128)(2,1)S(1)}, u32[]{:S(2)}, u32[]{:S(2)}) %collective-permute-start.14) | collective-permute-done | bytes 327712 | tf_op jit(solution)/shard_map/ppermute | solution.py:25
  66.0 1.2 %convert_multiply_fusion = f32[5,256,256]{2,1,0:T(8,128)} fusion(bf16[5,256,256]{2,1,0:T(8,128)(2,1)S(1)} %bitcast.34, f32[5]{0:T(128)S(1)} %copy-done.14), kind=kLoop, calls=%fused_computation | loop fusion | flops 655360 | bytes 1966100 | tf_op jit(solution)/shard_map/mul | solution.py:633
  (67 shorter events, 1.4 us)
Async XLA Ops:
  0.6 19.3 %copy-start.10 = (bf16[32,128]{1,0:T(8,128)(2,1)S(1)}, bf16[32,128]{1,0:T(8,128)(2,1)}, u32[]{:S(2)}) copy-start(bf16[32,128]{1,0:T(8,128)(2,1)} %constant.153.clone.refs_4_) | copy-start | bytes 24580
  0.6 19.3 %copy-start.11 = (bf16[32,128]{1,0:T(8,128)(2,1)S(1)}, bf16[32,128]{1,0:T(8,128)(2,1)}, u32[]{:S(2)}) copy-start(bf16[32,128]{1,0:T(8,128)(2,1)} %constant.154.clone.refs_5_) | copy-start | bytes 24580
  0.7 19.3 %copy-start = (bf16[16,32,256]{2,1,0:T(8,128)(2,1)S(1)}, bf16[16,32,256]{2,1,0:T(8,128)(2,1)}, u32[]{:S(2)}) copy-start(bf16[16,32,256]{2,1,0:T(8,128)(2,1)} %param.19) | copy-start | bytes 786436
  0.7 10.6 %copy-start.13 = (bf16[4,8,256]{2,1,0:T(8,128)(2,1)S(1)}, bf16[4,8,256]{2,1,0:T(8,128)(2,1)}, u32[]{:S(2)}) copy-start(bf16[4,8,256]{2,1,0:T(8,128)(2,1)} %param.25) | copy-start | bytes 49156
  0.7 9.5 %copy-start.12 = (bf16[32,256]{1,0:T(8,128)(2,1)S(1)}, bf16[32,256]{1,0:T(8,128)(2,1)}, u32[]{:S(2)}) copy-start(bf16[32,256]{1,0:T(8,128)(2,1)} %param.20) | copy-start | bytes 49156
  0.7 4.3 %copy-start.15 = (s32[32]{0:T(128)S(1)}, s32[32]{0:T(128)}, u32[]{:S(2)}) copy-start(s32[32]{0:T(128)} %param.22) | copy-start | bytes 388
  0.7 4.3 %copy-start.16 = (s32[32]{0:T(128)S(1)}, s32[32]{0:T(128)}, u32[]{:S(2)}) copy-start(s32[32]{0:T(128)} %param.23) | copy-start | bytes 388
  0.7 19.3 %copy-start.1 = (bf16[256,256]{1,0:T(8,128)(2,1)S(1)}, bf16[256,256]{1,0:T(8,128)(2,1)}, u32[]{:S(2)}) copy-start(bf16[256,256]{1,0:T(8,128)(2,1)} %refs_15_.1) | copy-start | bytes 393220
  0.7 23.0 %copy-start.3 = (bf16[256,256]{1,0:T(8,128)(2,1)S(1)}, bf16[256,256]{1,0:T(8,128)(2,1)}, u32[]{:S(2)}) copy-start(bf16[256,256]{1,0:T(8,128)(2,1)} %refs_16_.1) | copy-start | bytes 393220
  0.7 23.0 %copy-start.4 = (bf16[256,256]{1,0:T(8,128)(2,1)S(1)}, bf16[256,256]{1,0:T(8,128)(2,1)}, u32[]{:S(2)}) copy-start(bf16[256,256]{1,0:T(8,128)(2,1)} %refs_17_.1) | copy-start | bytes 393220
  3.3 23.7 %copy-start.2 = (bf16[2,128,384]{2,1,0:T(8,128)(2,1)S(1)}, bf16[2,128,384]{2,1,0:T(8,128)(2,1)}, u32[]{:S(2)}) copy-start(bf16[2,128,384]{2,1,0:T(8,128)(2,1)} %constant.156.clone.refs_12_) | copy-start | bytes 589828
  3.3 23.7 %copy-start.5 = (bf16[256,256]{1,0:T(8,128)(2,1)S(1)}, bf16[256,256]{1,0:T(8,128)(2,1)}, u32[]{:S(2)}) copy-start(bf16[256,256]{1,0:T(8,128)(2,1)} %refs_18_.1) | copy-start | bytes 393220
  3.3 23.7 %copy-start.6 = (bf16[256,256]{1,0:T(8,128)(2,1)S(1)}, bf16[256,256]{1,0:T(8,128)(2,1)}, u32[]{:S(2)}) copy-start(bf16[256,256]{1,0:T(8,128)(2,1)} %refs_19_.1) | copy-start | bytes 393220
  3.3 23.7 %copy-start.7 = (bf16[2,128,192]{2,1,0:T(8,128)(2,1)S(1)}, bf16[2,128,192]{2,1,0:T(8,128)(2,1)}, u32[]{:S(2)}) copy-start(bf16[2,128,192]{2,1,0:T(8,128)(2,1)} %constant.155.clone.refs_11_) | copy-start | bytes 294916
  3.3 23.7 %copy-start.8 = (bf16[128,256]{1,0:T(8,128)(2,1)S(1)}, bf16[128,256]{1,0:T(8,128)(2,1)}, u32[]{:S(2)}) copy-start(bf16[128,256]{1,0:T(8,128)(2,1)} %constant.158.clone.refs_14_) | copy-start | bytes 196612
  3.3 23.7 %copy-start.9 = (f32[2,16,384]{2,1,0:T(8,128)S(1)}, f32[2,16,384]{2,1,0:T(8,128)}, u32[]{:S(2)}) copy-start(f32[2,16,384]{2,1,0:T(8,128)} %constant.173.refs_13_) | copy-start | bytes 147460
  5.1 14.9 %collective-permute-start = (bf16[368,256]{1,0:T(8,128)(2,1)S(1)}, bf16[368,256]{1,0:T(8,128)(2,1)S(1)}, u32[]{:S(2)}, u32[]{:S(2)}) collective-permute-start(bf16[368,256]{1,0:T(8,128)(2,1)S(1)} %get-tuple-element.52), channel_id=1, source_target_pairs={{0,4},{4,8},{8,12},{12,0},{1,5},{5,9},{9,13},{13,1},{2,6},{6,10},{... | collective-permute-start | bytes 565256 | tf_op jit(solution)/shard_map/ppermute | solution.py:30
  8.1 11.8 %collective-permute-start.2 = (bf16[368,256]{1,0:T(8,128)(2,1)S(1)}, bf16[368,256]{1,0:T(8,128)(2,1)S(1)}, u32[]{:S(2)}, u32[]{:S(2)}) collective-permute-start(bf16[368,256]{1,0:T(8,128)(2,1)S(1)} %get-tuple-element.51), channel_id=1, source_target_pairs={{0,12},{4,0},{8,4},{12,8},{1,13},{5,1},{9,5},{13,9},{2,14},{6,2},{... | collective-permute-start | bytes 565256 | tf_op jit(solution)/shard_map/ppermute | solution.py:30
  10.3 9.7 %collective-permute-start.1 = (bf16[48,256]{1,0:T(8,128)(2,1)S(1)}, bf16[48,256]{1,0:T(8,128)(2,1)S(1)}, u32[]{:S(2)}, u32[]{:S(2)}) collective-permute-start(bf16[48,256]{1,0:T(8,128)(2,1)S(1)} %get-tuple-element.43), channel_id=1, source_target_pairs={{0,8},{4,12},{8,0},{12,4},{1,9},{5,13},{9,1},{13,5},{2,10},{6,14},... | collective-permute-start | bytes 73736 | tf_op jit(solution)/shard_map/ppermute | solution.py:30
  20.5 4.2 %collective-permute-start.3 = (bf16[576,256]{1,0:T(8,128)(2,1)S(1)}, bf16[576,256]{1,0:T(8,128)(2,1)S(1)}, u32[]{:S(2)}, u32[]{:S(2)}) collective-permute-start(bf16[576,256]{1,0:T(8,128)(2,1)S(1)} %get-tuple-element.17), channel_id=1, source_target_pairs={{0,1},{1,2},{2,3},{4,5},{5,6},{6,7},{8,9},{9,10},{10,11},{12,13},{... | collective-permute-start | bytes 884744 | tf_op jit(solution)/shard_map/ppermute | solution.py:513
  22.4 4.6 %collective-permute-start.4 = (bf16[576,256]{1,0:T(8,128)(2,1)S(1)}, bf16[576,256]{1,0:T(8,128)(2,1)S(1)}, u32[]{:S(2)}, u32[]{:S(2)}) collective-permute-start(bf16[576,256]{1,0:T(8,128)(2,1)S(1)} %get-tuple-element.18), channel_id=1, source_target_pairs={{1,0},{2,1},{3,2},{5,4},{6,5},{7,6},{9,8},{10,9},{11,10},{13,12},{... | collective-permute-start | bytes 884744 | tf_op jit(solution)/shard_map/ppermute | solution.py:514
  30.6 6.3 %collective-permute-start.5 = (bf16[640,256]{1,0:T(8,128)(2,1)S(1)}, bf16[640,256]{1,0:T(8,128)(2,1)S(1)}, u32[]{:S(2)}, u32[]{:S(2)}) collective-permute-start(bf16[640,256]{1,0:T(8,128)(2,1)S(1)} %get-tuple-element.30), channel_id=1, source_target_pairs={{0,1},{1,0},{2,3},{3,2},{4,5},{5,4},{6,7},{7,6},{8,9},{9,8},{10,11... | collective-permute-start | bytes 983048 | tf_op jit(solution)/shard_map/ppermute | solution.py:25
  37.0 6.5 %collective-permute-start.6 = (bf16[320,256]{1,0:T(8,128)(2,1)S(1)}, bf16[320,256]{1,0:T(8,128)(2,1)S(1)}, u32[]{:S(2)}, u32[]{:S(2)}) collective-permute-start(bf16[320,256]{1,0:T(8,128)(2,1)S(1)} %dynamic-slice_convert_fusion), channel_id=1, source_target_pairs={{0,2},{1,3},{2,0},{3,1},{4,6},{5,7},{6,4},{7,5},{8,10},{9,11},{10,... | collective-permute-start | bytes 491528 | tf_op jit(solution)/shard_map/ppermute | solution.py:25
  43.6 6.5 %collective-permute-start.7 = (bf16[112,256]{1,0:T(8,128)(2,1)S(1)}, bf16[112,256]{1,0:T(8,128)(2,1)S(1)}, u32[]{:S(2)}, u32[]{:S(2)}) collective-permute-start(bf16[112,256]{1,0:T(8,128)(2,1)S(1)} %pad_maximum_fusion), channel_id=1, source_target_pairs={{0,4},{4,8},{8,12},{12,0},{1,5},{5,9},{9,13},{13,1},{2,6},{6,10},{... | collective-permute-start | bytes 172040 | tf_op jit(solution)/shard_map/ppermute | solution.py:30
  43.9 7.2 %collective-permute-start.8 = (bf16[112,256]{1,0:T(8,128)(2,1)S(1)}, bf16[112,256]{1,0:T(8,128)(2,1)S(1)}, u32[]{:S(2)}, u32[]{:S(2)}) collective-permute-start(bf16[112,256]{1,0:T(8,128)(2,1)S(1)} %pad_maximum_fusion.1), channel_id=1, source_target_pairs={{0,8},{4,12},{8,0},{12,4},{1,9},{5,13},{9,1},{13,5},{2,10},{6,14},... | collective-permute-start | bytes 172040 | tf_op jit(solution)/shard_map/ppermute | solution.py:30
  45.9 5.2 %collective-permute-start.9 = (bf16[112,256]{1,0:T(8,128)(2,1)S(1)}, bf16[112,256]{1,0:T(8,128)(2,1)S(1)}, u32[]{:S(2)}, u32[]{:S(2)}) collective-permute-start(bf16[112,256]{1,0:T(8,128)(2,1)S(1)} %pad_maximum_fusion.2), channel_id=1, source_target_pairs={{0,12},{4,0},{8,4},{12,8},{1,13},{5,1},{9,5},{13,9},{2,14},{6,2},{... | collective-permute-start | bytes 172040 | tf_op jit(solution)/shard_map/ppermute | solution.py:30
  51.2 14.8 %copy-start.14 = (f32[5]{0:T(128)S(1)}, f32[5]{0:T(128)}, u32[]{:S(2)}) copy-start(f32[5]{0:T(128)} %constant.174) | copy-start | bytes 64
  51.2 6.2 %collective-permute-start.10 = (bf16[80,256]{1,0:T(8,128)(2,1)S(1)}, bf16[80,256]{1,0:T(8,128)(2,1)S(1)}, u32[]{:S(2)}, u32[]{:S(2)}) collective-permute-start(bf16[80,256]{1,0:T(8,128)(2,1)S(1)} %get-tuple-element.32), channel_id=1, source_target_pairs={{0,4},{4,8},{8,12},{12,0},{1,5},{5,9},{9,13},{13,1},{2,6},{6,10},{... | collective-permute-start | bytes 122888 | tf_op jit(solution)/shard_map/ppermute | solution.py:30
  52.6 5.5 %collective-permute-start.11 = (bf16[80,256]{1,0:T(8,128)(2,1)S(1)}, bf16[80,256]{1,0:T(8,128)(2,1)S(1)}, u32[]{:S(2)}, u32[]{:S(2)}) collective-permute-start(bf16[80,256]{1,0:T(8,128)(2,1)S(1)} %get-tuple-element.32), channel_id=1, source_target_pairs={{0,8},{4,12},{8,0},{12,4},{1,9},{5,13},{9,1},{13,5},{2,10},{6,14},... | collective-permute-start | bytes 122888 | tf_op jit(solution)/shard_map/ppermute | solution.py:30
  54.4 4.1 %collective-permute-start.12 = (bf16[80,256]{1,0:T(8,128)(2,1)S(1)}, bf16[80,256]{1,0:T(8,128)(2,1)S(1)}, u32[]{:S(2)}, u32[]{:S(2)}) collective-permute-start(bf16[80,256]{1,0:T(8,128)(2,1)S(1)} %get-tuple-element.32), channel_id=1, source_target_pairs={{0,12},{4,0},{8,4},{12,8},{1,13},{5,1},{9,5},{13,9},{2,14},{6,2},{... | collective-permute-start | bytes 122888 | tf_op jit(solution)/shard_map/ppermute | solution.py:30
  58.6 5.3 %collective-permute-start.13 = (bf16[320,256]{1,0:T(8,128)(2,1)S(1)}, bf16[320,256]{1,0:T(8,128)(2,1)S(1)}, u32[]{:S(2)}, u32[]{:S(2)}) collective-permute-start(bf16[320,256]{1,0:T(8,128)(2,1)S(1)} %constant_dynamic-update-slice_fusion.10), channel_id=1, source_target_pairs={{0,2},{1,3},{2,0},{3,1},{4,6},{5,7},{6,4},{7,5},{8,10},{9,11},{10,... | collective-permute-start | bytes 491528 | tf_op jit(solution)/shard_map/ppermute | solution.py:25
  64.0 1.7 %collective-permute-start.14 = (bf16[640,256]{1,0:T(8,128)(2,1)S(1)}, bf16[640,256]{1,0:T(8,128)(2,1)S(1)}, u32[]{:S(2)}, u32[]{:S(2)}) collective-permute-start(bf16[640,256]{1,0:T(8,128)(2,1)S(1)} %maximum_select_fusion.1), channel_id=1, source_target_pairs={{0,1},{1,0},{2,3},{3,2},{4,5},{5,4},{6,7},{7,6},{8,9},{9,8},{10,11... | collective-permute-start | bytes 983048 | tf_op jit(solution)/shard_map/ppermute | solution.py:25

commit v3 on v2

--- a/solution.py
+++ b/solution.py
@@ -20,14 +20,26 @@
 BF16 = jnp.bfloat16
 
 
-def swapped(block, axis, bit):
+def swapped(block, axis, bits):
     count = lax.axis_size(axis)
-    return lax.ppermute(block, axis, [(i, i ^ bit) for i in range(count)])
-
-
-def shifted(block, axis, step):
+    return lax.ppermute(block, axis, [(i, i ^ bits) for i in range(count)])
+
+
+def swapped_between(block, axis):
     count = lax.axis_size(axis)
-    return lax.ppermute(block, axis, [(i, (i + step) % count) for i in range(count)])
+    pairs = [(i, i + 1) for i in range(1, count - 1, 2)]
+    return lax.ppermute(block, axis, pairs + [(j, i) for i, j in pairs])
+
+
+def swapped_both(block, wide_bits, narrow_bits):
+    wide_count = lax.axis_size("wide")
+    narrow_count = lax.axis_size("narrow")
+    pairs = [
+        (w * narrow_count + n, (w ^ wide_bits) * narrow_count + (n ^ narrow_bits))
+        for w in range(wide_count)
+        for n in range(narrow_count)
+    ]
+    return lax.ppermute(block, ("wide", "narrow"), pairs)
 
 
 def dot(left, right):
@@ -142,8 +154,7 @@
         quad = node // SLOTS // 2 * SLOTS + node % SLOTS // 2
         same = (quad[:, None] == quad[None, :]).astype(np.float32)
         return {
-            "to_left": to_left,
-            "to_right": to_right,
+            "to_side": np.stack([to_left, to_right]),
             "place": place,
             "spread": spread,
             "match": match,
@@ -151,30 +162,91 @@
         }
 
 
-def blend_kernel(shape, wide_count, units, unit_rows, *refs):
-    (wide_ref, own_ref, mesh_ref, w_force_ref, left_ref, right_ref, own_rows_ref) = refs[:7]
-    count = len(units) - 1
-    arrived = refs[7 : 7 + count]
-    (blended_ref, to_left_ref, to_right_ref, stack_ref, rows_ref, key_ref) = refs[7 + count : 13 + count]
-    (projected_ref,) = refs[13 + count :]
-    from_prev, from_next = arrived[0], arrived[-1]
-    wide_at = wide_ref[0]
-    held = [own_rows_ref] + list(arrived)
-    total = unit_rows * len(units)
-    for k, start in enumerate(units):
-        rows_ref[k * unit_rows : (k + 1) * unit_rows] = held[k][start : start + unit_rows]
+def pack_kernel(
+    shape,
+    units,
+    place_ref,
+    own_ref,
+    cotangent_ref,
+    mask_ref,
+    rows_ref,
+    target_x_ref,
+    target_y_ref,
+    first_ref,
+    second_ref,
+    third_ref,
+    fourth_ref,
+    mesh_ref,
+    own_rows_ref,
+):
+    edge, own_nodes, halo = shape.edge, shape.own_nodes, shape.halo
+    held = rows_ref.shape[0]
+    even = place_ref[0] % 2 == 0
+    row_count = place_ref[1]
+    target_x = target_x_ref[...]
+    column = target_y_ref[...] - place_ref[2] * shape.tile_y
+    slot = lax.broadcasted_iota(jnp.int32, (1, held), 1)
+    column = jnp.where(slot < row_count, column, LANES - 1)
+    line = lax.broadcasted_iota(jnp.int32, (16, held), 0)
+    fields = jnp.where(line == 0, target_x // shape.tile_x, 0)
+    fields = fields + jnp.where(line == 1, target_x % shape.tile_x, 0)
+    fields = fields + jnp.where(line == 2, column, 0)
+    lane = lax.broadcasted_iota(jnp.int32, (held, LANES), 1)
+    repeat = lane % held == lax.broadcasted_iota(jnp.int32, (held, LANES), 0)
+    spread = dot(fields.astype(F32).astype(BF16), jnp.where(repeat, 1.0, 0.0).astype(BF16))
+    lane = lax.broadcasted_iota(jnp.int32, (16, LANES), 1)
+
+    mesh_ref[:own_nodes] = cotangent_ref[...]
+    mesh_ref[own_nodes:] = mask_ref[...]
+    targets = (own_rows_ref, first_ref, third_ref, second_ref, fourth_ref)
+    for ref, number in zip(targets, (0, 1, 2, 3, 3)):
+        at = ref.shape[0] - held - 16
+        ref[at : at + held] = rows_ref[...]
+        ref[at + held :] = jnp.where(lane // held == number, spread, 0.0).astype(BF16)
+    for ref, upward in ((first_ref, even), (second_ref, jnp.logical_not(even))):
+        start = pl.multiple_of(jnp.where(upward, shape.cells - halo, 0), shape.tile_y)
+        ref[:halo] = own_ref[pl.ds(start, halo)]
+        start = pl.multiple_of(jnp.where(upward, own_nodes - edge, 0), 16)
+        ref[halo : halo + edge] = mesh_ref[pl.ds(start, edge)]
+        start = pl.multiple_of(jnp.where(upward, 2 * own_nodes - edge, own_nodes), 16)
+        ref[halo + edge : halo + 2 * edge] = mesh_ref[pl.ds(start, edge)]
+
+
+def blend_kernel(shape, units, unit_rows, *refs):
+    (place_ref, own_ref, mesh_ref, w_force_ref, side_ref, own_rows_ref) = refs[:6]
+    count = units if units > 3 else 2
+    arrived = refs[6 : 6 + count]
+    (blended_ref, first_ref, second_ref, stack_ref, rows_ref, key_ref) = refs[6 + count : 12 + count]
+    (projected_ref,) = refs[12 + count :]
+    wide_at = place_ref[0]
+    even = wide_at % 2 == 0
+    near, between = arrived[0], arrived[1]
+    mesh = 2 * shape.edge
+    first_row = shape.halo + mesh
+
+    def held(k, at, n):
+        if k == 0:
+            return own_rows_ref[at : at + n]
+        if k == 1:
+            return near[first_row + at : first_row + at + n]
+        if k < units - 1:
+            return arrived[k][at : at + n]
+        value = between[first_row + at : first_row + at + n]
+        if units > 3:
+            value = value + arrived[-1][at : at + n]
+        return value
+
+    total = unit_rows * units
+    for k in range(units):
+        rows_ref[k * unit_rows : (k + 1) * unit_rows] = held(k, 0, unit_rows)
     blocks = []
     if total <= LANES:
-        metas = [
-            held[k][start + unit_rows : start + unit_rows + 16].astype(F32)
-            for k, start in enumerate(units)
-        ]
+        metas = [held(k, unit_rows, 16).astype(F32) for k in range(units)]
         blocks.append(functools.reduce(lambda a, b: a + b, metas)[:, :total])
     else:
-        for k, start in enumerate(units):
+        for k in range(units):
             for part in range(unit_rows // LANES):
-                at = start + unit_rows + 16 * part
-                blocks.append(held[k][at : at + 16].astype(F32))
+                blocks.append(held(k, unit_rows + 16 * part, 16).astype(F32))
     keys = []
     for block in blocks:
         whole = block.astype(jnp.int32)
@@ -187,40 +259,42 @@
         key_ref[:, k * width : (k + 1) * width] = jnp.broadcast_to(key, (8, width))
     projected_ref[...] = dot(rows_ref[...], w_force_ref[...]).astype(BF16)
 
-    mesh = 2 * shape.edge
-    keep_prev = (wide_at > 0).astype(F32)
-    keep_next = (wide_at < wide_count - 1).astype(F32)
-    prev_mesh = from_prev[shape.halo : shape.halo + mesh].astype(F32) * keep_prev
-    next_mesh = from_next[shape.halo : shape.halo + mesh].astype(F32) * keep_next
+    def facing(at, n, forward):
+        one, other = near[at : at + n], between[at : at + n]
+        return jnp.where(even, one, other) if forward else jnp.where(even, other, one)
+
     stack = jnp.concatenate(
-        [prev_mesh.astype(BF16), mesh_ref[...], next_mesh.astype(BF16)], axis=0
+        [facing(shape.halo, mesh, False), mesh_ref[...], facing(shape.halo, mesh, True)], axis=0
     )
     stack_ref[...] = stack
-    to_left_ref[shape.side :] = dot(left_ref[...], stack).astype(BF16)
-    to_right_ref[shape.side :] = dot(right_ref[...], stack).astype(BF16)
+    narrow_even = place_ref[2] % 2 == 0
+    column = pl.multiple_of(jnp.where(narrow_even, shape.tile_y - SIDE, 0), SIDE)
+    other = pl.multiple_of(jnp.where(narrow_even, 0, shape.tile_y - SIDE), SIDE)
+    to_left = dot(side_ref[0], stack).astype(BF16)
+    to_right = dot(side_ref[1], stack).astype(BF16)
+    first_ref[shape.side :] = jnp.where(narrow_even, to_right, to_left)
+    second_ref[shape.side :] = jnp.where(narrow_even, to_left, to_right)
 
     tile_y = shape.tile_y
     inner = shape.halo + shape.cells
-    jobs = [(from_prev, at, n, 0, keep_prev) for at, n in pieces(0, shape.halo, 3 * tile_y)]
-    jobs += [(own_ref, at, n, shape.halo, None) for at, n in pieces(0, shape.cells, 4 * tile_y)]
-    jobs += [(from_next, at, n, inner, keep_next) for at, n in pieces(0, shape.halo, 3 * tile_y)]
-    for ref, at, n, base, keep in jobs:
+    jobs = [(0, at, n) for at, n in pieces(0, shape.halo, 3 * tile_y)]
+    jobs += [(shape.halo, at, n) for at, n in pieces(0, shape.cells, 4 * tile_y)]
+    jobs += [(inner, at, n) for at, n in pieces(0, shape.halo, 3 * tile_y)]
+    for base, at, n in jobs:
         first = base + at
-        value = ref[at : at + n].astype(F32)
-        if keep is not None:
-            value = value * keep
+        if base == shape.halo:
+            value = own_ref[at : at + n].astype(F32)
+        else:
+            value = facing(at, n, base == inner).astype(F32)
         cell = lax.broadcasted_iota(jnp.int32, (n, width), 0) + first
         for k, key in enumerate(keys):
             hit = jnp.where(cell == key, 1.0, 0.0).astype(BF16)
             value = value + dot(hit, projected_ref[k * width : (k + 1) * width])
-        value = value.astype(BF16)
-        blended_ref[first : first + n] = value
-        for t in range(n // tile_y):
-            row = first // tile_y + t
-            to_left_ref[row * SIDE : (row + 1) * SIDE] = value[t * tile_y : t * tile_y + SIDE]
-            to_right_ref[row * SIDE : (row + 1) * SIDE] = value[
-                (t + 1) * tile_y - SIDE : (t + 1) * tile_y
-            ]
+        blended_ref[first : first + n] = value.astype(BF16)
+    for row in range(shape.rows_x):
+        target = slice(row * SIDE, (row + 1) * SIDE)
+        first_ref[target] = blended_ref[pl.ds(row * tile_y + column, SIDE)]
+        second_ref[target] = blended_ref[pl.ds(row * tile_y + other, SIDE)]
 
 
 def forward_kernel(
@@ -247,8 +321,8 @@
 def backward_kernel(shape, total_rows, *refs):
     (
         narrow_ref,
-        from_left_ref,
-        from_right_ref,
+        first_ref,
+        second_ref,
         stack_ref,
         blended_ref,
         message_ref,
@@ -280,21 +354,25 @@
     tile_y, pitch = shape.tile_y, shape.pitch
     channels = blended_ref.shape[1]
 
-    for ref, offset in ((from_left_ref, tile_y), (from_right_ref, tile_y + SIDE)):
+    even = narrow_ref[0] % 2 == 0
+    first_at = pl.multiple_of(tile_y + jnp.where(even, SIDE, 0), SIDE)
+    second_at = pl.multiple_of(tile_y + jnp.where(even, 0, SIDE), SIDE)
+    for ref, offset in ((first_ref, first_at), (second_ref, second_at)):
         for at, n in pieces(0, shape.side, 8 * SIDE):
             blended = ref[at : at + n]
             latent = (blended.astype(F32) + silu(dot(blended, w_embed_ref[...]))).astype(BF16)
             message = silu(dot(latent, w_message_ref[...])).astype(BF16)
             for t in range(n // SIDE):
                 row = (at // SIDE + t) * pitch + offset
-                padded_ref[row : row + SIDE] = message[t * SIDE : (t + 1) * SIDE]
+                padded_ref[pl.ds(row, SIDE)] = message[t * SIDE : (t + 1) * SIDE]
     for row in range(shape.rows_x):
         padded_ref[row * pitch : row * pitch + tile_y] = message_ref[
             row * tile_y : (row + 1) * tile_y
         ]
 
+    first, second = first_ref[shape.side :], second_ref[shape.side :]
     stack = jnp.concatenate(
-        [stack_ref[...], from_left_ref[shape.side :], from_right_ref[shape.side :]], axis=0
+        [stack_ref[...], jnp.where(even, second, first), jnp.where(even, first, second)], axis=0
     )
     cotangent = dot(place_ref[0], stack)
     mask = dot(place_ref[1], stack[:, :128]).astype(BF16)
@@ -383,6 +461,21 @@
     kept_ref[...] = grads_ref[pl.ds(kept_at, half)]
 
 
+def finish_kernel(scales, place_ref, own_ref, other_ref, out_ref):
+    even = place_ref[2] % 2 == 0
+    half = own_ref.shape[0]
+    channels = own_ref.shape[1]
+    for k, scale in enumerate(scales):
+        for start, stop, lower in ((0, half, True), (half, 2 * half, False)):
+            at = max(k * channels, start)
+            end = min((k + 1) * channels, stop)
+            if at >= end:
+                continue
+            own, other = own_ref[at - start : end - start], other_ref[at - start : end - start]
+            value = jnp.where(even, own, other) if lower else jnp.where(even, other, own)
+            out_ref[k, at - k * channels : end - k * channels] = value.astype(F32) * scale
+
+
 def call(kernel, out_shapes, operands, scratch=(), scalars=1, flops=0):
     specs = [pl.BlockSpec(memory_space=pltpu.SMEM)] * scalars
     specs += [pl.BlockSpec(memory_space=pltpu.VMEM)] * (len(operands) - scalars)
@@ -438,7 +531,7 @@
 
     live = jnp.arange(held_rows) < row_count[0]
     column = target_y - narrow_at * tile_y
-    whole_column = held_rows * wide_count <= LANES
+    whole_column = wide_count == 4 and held_rows * wide_count <= LANES
     if whole_column:
         units = wide_count
         unit_rows = held_rows
@@ -467,35 +560,55 @@
         row_x = jnp.where(row_live, wide_at * tile_x + cells // tile_y, 0)
         row_y = cells % tile_y
 
-    def with_meta(slot):
-        return [rows, meta_rows(row_live, row_x, row_y, tile_x, unit_rows, slot, units)]
-
     cells = grid_state.reshape(-1, channels)
-    mask = g2m_mask.astype(BF16).transpose(1, 2, 0)
-    mask = jnp.pad(mask, ((0, 0), (0, 0), (0, channels - 36)))
-    edge = slice(0, NODES_OUT), slice(shape.node_x - NODES_OUT, shape.node_x)
-    flat = [
-        [mesh_cotangent[part].reshape(-1, channels), mask[part].reshape(-1, channels)]
-        for part in edge
-    ]
-    mesh = jnp.concatenate([mesh_cotangent.reshape(-1, channels), mask.reshape(-1, channels)])
-    to_prev = jnp.concatenate([cells[: shape.halo]] + flat[0] + with_meta(units - 1))
-    to_next = jnp.concatenate([cells[-shape.halo :]] + flat[1] + with_meta(1))
-    own_rows = jnp.concatenate(with_meta(0))
-    arrived = [shifted(to_next, "wide", 1)]
-    starts = [0, shape.halo + 2 * shape.edge]
-    for step in range(2, units - 1):
-        arrived.append(shifted(jnp.concatenate(with_meta(step)), "wide", step))
-        starts.append(0)
-    arrived.append(shifted(to_prev, "wide", -1))
-    starts.append(shape.halo + 2 * shape.edge)
+    cotangent = mesh_cotangent.reshape(-1, channels)
+    mask = g2m_mask.astype(BF16).transpose(1, 2, 0).reshape(-1, 36)
+    mask = jnp.pad(mask, ((0, 0), (0, channels - 36)))
+    place = jnp.stack([wide_at, row_count[0], narrow_at])
+    struct = jax.ShapeDtypeStruct
+    long = struct((shape.halo + 2 * shape.edge + unit_rows + 16, channels), BF16)
+    short = struct((unit_rows + 16, channels), BF16)
+    if whole_column:
+        first, second, third, fourth, mesh, own_rows = call(
+            functools.partial(pack_kernel, shape, units),
+            [long, long, short, short, struct((2 * shape.own_nodes, channels), BF16), short],
+            [
+                place,
+                cells,
+                cotangent,
+                mask,
+                rows,
+                target_x.reshape(1, -1),
+                target_y.reshape(1, -1),
+            ],
+        )
+        arrived = [
+            swapped(first, "wide", 1),
+            swapped_between(second, "wide"),
+            swapped(third, "wide", 2),
+            lax.ppermute(fourth, "wide", [(0, 3), (3, 0)]),
+        ]
+    else:
+
+        def with_meta(slot):
+            return [rows, meta_rows(row_live, row_x, row_y, tile_x, unit_rows, slot, units)]
+
+        mesh = jnp.concatenate([cotangent, mask])
+        own_rows = jnp.concatenate(with_meta(0))
+        edge = shape.edge
+        to_prev = [cells[: shape.halo], cotangent[:edge], mask[:edge]]
+        to_next = [cells[-shape.halo :], cotangent[-edge:], mask[-edge:]]
+        to_prev, to_next = jnp.concatenate(to_prev), jnp.concatenate(to_next)
+        upward = wide_at % 2 == 0
+        first = jnp.concatenate([jnp.where(upward, to_next, to_prev)] + with_meta(1))
+        second = jnp.concatenate([jnp.where(upward, to_prev, to_next)] + with_meta(2))
+        arrived = [swapped(first, "wide", 1), swapped_between(second, "wide")]
 
     total_rows = unit_rows * units
     stack_rows = 4 * shape.edge + 2 * shape.own_nodes
-    struct = jax.ShapeDtypeStruct
     payload = struct((shape.side + 2 * shape.side_nodes, channels), BF16)
-    blended, to_left, to_right, stack, all_rows, keys = call(
-        functools.partial(blend_kernel, shape, wide_count, starts, unit_rows),
+    blended, first, second, stack, all_rows, keys = call(
+        functools.partial(blend_kernel, shape, units, unit_rows),
         [
             struct((shape.center, channels), BF16),
             payload,
@@ -504,14 +617,12 @@
             struct((total_rows, channels), BF16),
             struct((8, total_rows), jnp.int32),
         ],
-        [wide_at.reshape(1), cells, mesh, w_force, table["to_left"], table["to_right"], own_rows]
-        + arrived,
+        [place, cells, mesh, w_force, table["to_side"], own_rows] + arrived,
         scratch=[pltpu.VMEM((total_rows, channels), BF16)],
         flops=2 * shape.center * total_rows * channels,
     )
-    ends = narrow_count - 1
-    from_left = lax.ppermute(to_right, "narrow", [(i, i + 1) for i in range(ends)])
-    from_right = lax.ppermute(to_left, "narrow", [(i + 1, i) for i in range(ends)])
+    second = swapped_between(second, "narrow")
+    first = swapped(first, "narrow", 1)
     message, latent, embed_slope, message_slope = call(
         functools.partial(forward_kernel, shape),
         [
@@ -535,8 +646,8 @@
         ],
         [
             narrow_at.reshape(1),
-            from_left,
-            from_right,
+            first,
+            second,
             stack,
             blended,
             message,
@@ -566,34 +677,66 @@
         flops=12 * shape.cells * channels * channels,
     )
 
-    bits = [1 << k for k in range(narrow_count.bit_length() - 1)]
-    piece = kept + swapped(sent, "narrow", bits[0]).astype(F32)
-    for bit in bits[1:]:
-        half = piece.shape[0] // 2
-        upper = (narrow_at // bit) % 2
-        sent = lax.dynamic_slice_in_dim(piece, (1 - upper) * half, half).astype(BF16)
-        kept = lax.dynamic_slice_in_dim(piece, upper * half, half)
-        piece = kept + swapped(sent, "narrow", bit).astype(F32)
-    part = piece.shape[0] // wide_count
-    rounded = piece.astype(BF16)
-    total = lax.dynamic_slice_in_dim(piece, wide_at * part, part)
-    row_back = back[:unit_rows].astype(F32)
-    for step in range(1, wide_count):
-        target = (wide_at + step) % wide_count
-        sent = lax.dynamic_slice_in_dim(rounded, target * part, part)
-        if whole_column:
-            source = wide_count - step
-            rows_back = back[source * unit_rows : (source + 1) * unit_rows]
-            got = shifted(jnp.concatenate([sent, rows_back]), "wide", step).astype(F32)
-            row_back = row_back + got[part:]
-            total = total + got[:part]
-        else:
-            total = total + shifted(sent, "wide", step).astype(F32)
+    piece = kept + swapped(sent, "narrow", 1).astype(F32)
+    back_blocks = back.reshape(units, unit_rows, channels)
+    row_back = back_blocks[0].astype(F32)
+    others = narrow_count // 2
+    if wide_count * others <= 8:
+        group = wide_count * others
+        part = piece.shape[0] // group
+        at = wide_at * others + narrow_at // 2
+        rounded = piece.astype(BF16)
+        own = lax.dynamic_slice_in_dim(piece, at * part, part)
+        order = sorted(range(1, group), key=lambda k: (k // others < 2, k % others == 0))
+        for k in order:
+            wide_bits, narrow_bits = k // others, k % others
+            sent = lax.dynamic_slice_in_dim(rounded, (at ^ k) * part, part)
+            if narrow_bits == 0 and whole_column:
+                sent = jnp.concatenate([sent, back_blocks[wide_bits]])
+            got = swapped_both(sent, wide_bits, 2 * narrow_bits).astype(F32)
+            own = own + got[:part]
+            if narrow_bits == 0 and whole_column:
+                row_back = row_back + got[part:]
+        own = own.astype(BF16)
+        gathered = jnp.zeros((group * part, channels), BF16)
+        gathered = lax.dynamic_update_slice_in_dim(gathered, own, at * part, 0)
+        for k in order:
+            got = swapped_both(own, k // others, 2 * (k % others))
+            gathered = lax.dynamic_update_slice_in_dim(gathered, got, (at ^ k) * part, 0)
+    else:
+        bits = [1 << k for k in range(1, narrow_count.bit_length() - 1)]
+        for bit in bits:
+            half = piece.shape[0] // 2
+            upper = (narrow_at // bit) % 2
+            sent = lax.dynamic_slice_in_dim(piece, (1 - upper) * half, half).astype(BF16)
+            kept = lax.dynamic_slice_in_dim(piece, upper * half, half)
+            piece = kept + swapped(sent, "narrow", bit).astype(F32)
+        part = piece.shape[0] // wide_count
+        rounded = piece.astype(BF16)
+        own = lax.dynamic_slice_in_dim(piece, wide_at * part, part)
+        for k in range(1, wide_count):
+            sent = lax.dynamic_slice_in_dim(rounded, (wide_at ^ k) * part, part)
+            own = own + swapped(sent, "wide", k).astype(F32)
+        own = own.astype(BF16)
+        gathered = jnp.zeros((wide_count * part, channels), BF16)
+        gathered = lax.dynamic_update_slice_in_dim(gathered, own, wide_at * part, 0)
+        for k in range(1, wide_count):
+            got = swapped(own, "wide", k)
+            gathered = lax.dynamic_update_slice_in_dim(gathered, got, (wide_at ^ k) * part, 0)
+        for bit in reversed(bits):
+            upper = (narrow_at // bit) % 2
+            other = swapped(gathered, "narrow", bit)
+            gathered = jnp.where(
+                upper == 0,
+                jnp.concatenate([gathered, other]),
+                jnp.concatenate([other, gathered]),
+            )
+    other = swapped(gathered, "narrow", 1)
     if whole_column:
         row_back = row_back.astype(BF16)
     else:
         returned = lax.all_to_all(
-            back[:unit_rows].reshape(wide_count, CAP, channels),
+            back_blocks[0].reshape(wide_count, CAP, channels),
             "wide",
             split_axis=0,
             concat_axis=0,
@@ -602,35 +745,14 @@
         row_back = jnp.take(
             returned.reshape(-1, channels), send_slot, axis=0, mode="fill", fill_value=0
         )
-    own = total.astype(BF16)
-    gathered = jnp.zeros((wide_count * part, channels), BF16)
-    gathered = lax.dynamic_update_slice_in_dim(gathered, own, wide_at * part, 0)
-    for step in range(1, wide_count):
-        source = (wide_at - step) % wide_count
-        gathered = lax.dynamic_update_slice_in_dim(
-            gathered, shifted(own, "wide", step), source * part, 0
-        )
-    for bit in reversed(bits):
-        upper = (narrow_at // bit) % 2
-        other = swapped(gathered, "narrow", bit)
-        gathered = jnp.where(
-            upper == 0,
-            jnp.concatenate([gathered, other]),
-            jnp.concatenate([other, gathered]),
-        )
     cell_total = shape.cells * wide_count * narrow_count
     row_total = held_rows * wide_count * narrow_count
-    scales = np.array(
-        [
-            1.0 / math.sqrt(row_total),
-            1.0 / math.sqrt(cell_total),
-            1.0 / math.sqrt(cell_total),
-            1.0 / math.sqrt(cell_total // 16),
-            1.0 / math.sqrt(cell_total // 64),
-        ],
-        np.float32,
-    )
-    weight_grads = gathered.reshape(5, channels, channels).astype(F32) * scales[:, None, None]
+    sizes = [row_total, cell_total, cell_total, cell_total // 16, cell_total // 64]
+    (weight_grads,) = call(
+        functools.partial(finish_kernel, [1.0 / math.sqrt(size) for size in sizes]),
+        [struct((5, channels, channels), F32)],
+        [place, gathered, other],
+    )
     return (grad_state.reshape(tile_x, tile_y, channels), row_back, weight_grads)
 
 

time: 67.6 us -> 69.8 us (1.033)
  waiting for transfers between devices: 31.4 us -> 10.7 us
  starting transfers between devices: 22.9 us -> 40 us
  local copies, waits for them, and re-layouts: 3 us -> 7.27 us
  Pallas kernels: 4.97 us -> 8.06 us
  other arithmetic: 3.23 us -> 1.62 us
    ppermute x15 -> x22, waiting for transfers between devices: 31.4 us -> 10.7 us  [the longest x14 5.73 us: swapped_both(): return lax.ppermute(block, ('wide', 'narrow'), pairs)]
    ppermute x15 -> x22, starting transfers between devices: 22.9 us -> 40 us  [the longest x14 21.8 us: swapped_both(): return lax.ppermute(block, ('wide', 'narrow'), pairs)]
    unnamed x38 -> x32, local copies, waits for them, and re-layouts: 1.71 us -> 7.15 us
    pallas_call x3 -> x5, Pallas kernels: 4.97 us -> 8.06 us  [call(): pl.pallas_call(kernel, out_shape=tuple(out_shapes), in_specs=specs, out_s...]
    mul x1 -> x0, other arithmetic: 1.24 us -> none  [local(): gathered.reshape(5, channels, channels).astype(F32) * scales[:, None, None]]
    slice x2 -> x1, local copies, waits for them, and re-layouts: 1.14 us -> 0.01 us  [local(): sent = jnp.concatenate([sent, back_blocks[wide_bits]])]
    transpose x1 -> x0, other arithmetic: 0.72 us -> none  [local(): mask = g2m_mask.astype(BF16).transpose(1, 2, 0)]
    reshape x0 -> x1, other arithmetic: none -> 0.72 us  [local(): mask = g2m_mask.astype(BF16).transpose(1, 2, 0).reshape(-1, 36)]
  transfers between devices with their start and end apart: 15 -> 22, of which waited for: 11 -> 13; matrix products, arithmetic and copies ran while one was open for 1% -> 1% of each run, Pallas kernels for 1% -> 1%
where the time goes in v3:
time: 69.8 us; the launch traced here: 69.2 us
  starting transfers between devices  40 us (57%)
  waiting for transfers between devices  10.7 us (15%)
  Pallas kernels  8.06 us (12%)
  local copies, waits for them, and re-layouts  7.27 us (10%)
  other arithmetic  1.62 us (2%)
  between operations  1.57 us (2%)
    ppermute x14, starting transfers between devices, swapped_both(): return lax.ppermute(block, ('wide', 'narrow'), pairs)  21.8 us
    ppermute x5, starting transfers between devices, swapped(): return lax.ppermute(block, axis, [(i, i ^ bits) for i in range(count)])  12.1 us
    pallas_call x5, Pallas kernels, call(): pl.pallas_call(kernel, out_shape=tuple(out_shapes), in_specs=specs, out_s...  8.06 us
    unnamed x32, local copies, waits for them, and re-layouts  7.15 us
    ppermute x14, waiting for transfers between devices, swapped_both(): return lax.ppermute(block, ('wide', 'narrow'), pairs)  5.73 us
    ppermute x1, starting transfers between devices, local(): lax.ppermute(fourth, 'wide', [(0, 3), (3, 0)])  4.81 us
    ppermute x5, waiting for transfers between devices, swapped(): return lax.ppermute(block, axis, [(i, i ^ bits) for i in range(count)])  2.85 us
    ppermute x1, waiting for transfers between devices, local(): lax.ppermute(fourth, 'wide', [(0, 3), (3, 0)])  2.1 us
  transfers between devices with their start and end apart: 22, of which 13 were waited for; matrix products, arithmetic and copies ran while one was open for 1% of the time, Pallas kernels for 1%

profile of v3, /device:TPU:0, one launch (start us, length us, event | category | flops | bytes accessed | tf_op | source)
XLA Modules:
  0.0 69.2 jit_solution(9238139484728198838)
XLA Ops:
  1.3 0.7 %convert_bitcast_fusion = bf16[32,36]{1,0:T(8,128)(2,1)S(1)} fusion(s32[36,4,8]{0,2,1:T(8,128)} %param.22), kind=kLoop, calls=%fused_computation.14 | loop fusion | flops 1152 | bytes 6912 | tf_op jit(solution)/shard_map/reshape | solution.py:565
  2.1 0.9 %copy-done = bf16[16,32,256]{2,1,0:T(8,128)(2,1)S(1)} copy-done((bf16[16,32,256]{2,1,0:T(8,128)(2,1)S(1)}, bf16[16,32,256]{2,1,0:T(8,128)(2,1)}, u32[]{:S(2)}) %copy-start) | copy-done | bytes 262168
  3.1 0.7 %copy-done.12 = bf16[4,8,256]{2,1,0:T(8,128)(2,1)S(1)} copy-done((bf16[4,8,256]{2,1,0:T(8,128)(2,1)S(1)}, bf16[4,8,256]{2,1,0:T(8,128)(2,1)}, u32[]{:S(2)}) %copy-start.12) | copy-done | bytes 16408
  6.5 3.0 %collective-permute-start = (bf16[368,256]{1,0:T(8,128)(2,1)S(1)}, bf16[368,256]{1,0:T(8,128)(2,1)S(1)}, u32[]{:S(2)}, u32[]{:S(2)}) collective-permute-start(bf16[368,256]{1,0:T(8,128)(2,1)S(1)} %get-tuple-element.25), channel_id=1, source_target_pairs={{0,4},{4,0},{8,12},{12,8},{1,5},{5,1},{9,13},{13,9},{2,6},{6,2},{1... | collective-permute-start | bytes 565256 | tf_op jit(solution)/shard_map/ppermute | solution.py:25
  10.2 3.9 %collective-permute-start.2 = (bf16[48,256]{1,0:T(8,128)(2,1)S(1)}, bf16[48,256]{1,0:T(8,128)(2,1)S(1)}, u32[]{:S(2)}, u32[]{:S(2)}) collective-permute-start(bf16[48,256]{1,0:T(8,128)(2,1)S(1)} %get-tuple-element.27), channel_id=1, source_target_pairs={{0,8},{4,12},{8,0},{12,4},{1,9},{5,13},{9,1},{13,5},{2,10},{6,14},... | collective-permute-start | bytes 73736 | tf_op jit(solution)/shard_map/ppermute | solution.py:25
  14.1 4.8 %collective-permute-start.3 = (bf16[48,256]{1,0:T(8,128)(2,1)S(1)}, bf16[48,256]{1,0:T(8,128)(2,1)S(1)}, u32[]{:S(2)}, u32[]{:S(2)}) collective-permute-start(bf16[48,256]{1,0:T(8,128)(2,1)S(1)} %get-tuple-element.28), channel_id=1, source_target_pairs={{0,12},{12,0},{1,13},{13,1},{2,14},{14,2},{3,15},{15,3},{16,28},{2... | collective-permute-start | bytes 73736 | tf_op jit(solution)/shard_map/ppermute | solution.py:589
  19.5 2.1 %collective-permute-done.3.refs_9_ = bf16[48,256]{1,0:T(8,128)(2,1)S(1)} collective-permute-done((bf16[48,256]{1,0:T(8,128)(2,1)S(1)}, bf16[48,256]{1,0:T(8,128)(2,1)S(1)}, u32[]{:S(2)}, u32[]{:S(2)}) %collective-permute-start.3) | collective-permute-done | bytes 24608 | tf_op jit(solution)/shard_map/ppermute | solution.py:589
  21.6 0.9 %copy-done.1 = bf16[256,256]{1,0:T(8,128)(2,1)S(1)} copy-done((bf16[256,256]{1,0:T(8,128)(2,1)S(1)}, bf16[256,256]{1,0:T(8,128)(2,1)}, u32[]{:S(2)}) %copy-start.1) | copy-done | bytes 131096
  22.5 0.7 %copy-done.11 = bf16[2,32,128]{2,1,0:T(8,128)(2,1)S(1)} copy-done((bf16[2,32,128]{2,1,0:T(8,128)(2,1)S(1)}, bf16[2,32,128]{2,1,0:T(8,128)(2,1)}, u32[]{:S(2)}) %copy-start.11) | copy-done | bytes 16408
  23.3 1.2 %shard_map.185 = (bf16[1088,256]{1,0:T(8,128)(2,1)S(1)}, bf16[576,256]{1,0:T(8,128)(2,1)S(1)}, bf16[576,256]{1,0:T(8,128)(2,1)S(1)}, bf16[128,256]{1,0:T(8,128)(...) custom-call(s32[3]{0:T(128)S(1)} %pad_add_fusion.place_ref.refs_0_, bf16[512,256]{1,0:T(8,128)(2,1)S(1)} %bitcast.12, ...), custom_call_target="tpu_custom_call" | custom-call | flops 71303168 | bytes 2174988 | tf_op jit(solution)/shard_map/pallas_call | solution.py:483
  25.2 0.9 %copy-done.3 = bf16[256,256]{1,0:T(8,128)(2,1)S(1)} copy-done((bf16[256,256]{1,0:T(8,128)(2,1)S(1)}, bf16[256,256]{1,0:T(8,128)(2,1)}, u32[]{:S(2)}) %copy-start.3) | copy-done | bytes 131096
  26.1 0.9 %copy-done.5 = bf16[256,256]{1,0:T(8,128)(2,1)S(1)} copy-done((bf16[256,256]{1,0:T(8,128)(2,1)S(1)}, bf16[256,256]{1,0:T(8,128)(2,1)}, u32[]{:S(2)}) %copy-start.5) | copy-done | bytes 131096
  27.0 0.9 %shard_map.186 = (bf16[1088,256]{1,0:T(8,128)(2,1)S(1)}, bf16[512,256]{1,0:T(8,128)(2,1)S(1)}, f32[512,256]{1,0:T(8,128)S(1)}, f32[512,256]{1,0:T(8,128)S(1)}) custom-call(bf16[1088,256]{1,0:T(8,128)(2,1)S(1)} %get-tuple-element.32.blended_ref.refs_4_, bf16[256,256]{1,0:T(8,128)(2,1)S(1)} %copy-done.3, bf16[256,256]{1,0:T(8,128)(2,1)S(1)} %copy-done.5), custom_call_target="tpu_custom_call" | custom-call | flops 285212672 | bytes 2686976 | tf_op jit(solution)/shard_map/pallas_call | solution.py:483
  28.0 3.6 %shard_map.187 = (bf16[512,256]{1,0:T(8,128)(2,1)}, bf16[128,256]{1,0:T(8,128)(2,1)S(1)}, bf16[640,256]{1,0:T(8,128)(2,1)S(1)}, f32[640,256]{1,0:T(8,128)S(1)}) custom-call(s32[1]{0:T(128)} %bitcast.refs_0_, bf16[576,256]{1,0:T(8,128)(2,1)S(1)} %collective-permute-done.4.refs_1_, bf16[576,256]{1,0:T(8,128)(2,1)S(1)} %collective-permute-done.5.refs_2_, ...), custom_call_target="tpu_custom_call" | custom-call | flops 402653184 | bytes 5525508 | tf_op jit(solution)/shard_map/pallas_call | solution.py:483
  31.6 5.1 %collective-permute-start.6 = (bf16[640,256]{1,0:T(8,128)(2,1)S(1)}, bf16[640,256]{1,0:T(8,128)(2,1)S(1)}, u32[]{:S(2)}, u32[]{:S(2)}) collective-permute-start(bf16[640,256]{1,0:T(8,128)(2,1)S(1)} %get-tuple-element.42), channel_id=1, source_target_pairs={{0,1},{1,0},{2,3},{3,2},{4,5},{5,4},{6,7},{7,6},{8,9},{9,8},{10,11... | collective-permute-start | bytes 983048 | tf_op jit(solution)/shard_map/ppermute | solution.py:25
  36.7 1.3 %collective-permute-done.6 = bf16[640,256]{1,0:T(8,128)(2,1)S(1)} collective-permute-done((bf16[640,256]{1,0:T(8,128)(2,1)S(1)}, bf16[640,256]{1,0:T(8,128)(2,1)S(1)}, u32[]{:S(2)}, u32[]{:S(2)}) %collective-permute-start.6) | collective-permute-done | bytes 327712 | tf_op jit(solution)/shard_map/ppermute | solution.py:25
  38.2 3.0 %collective-permute-start.8 = (bf16[112,256]{1,0:T(8,128)(2,1)S(1)}, bf16[112,256]{1,0:T(8,128)(2,1)S(1)}, u32[]{:S(2)}, u32[]{:S(2)}) collective-permute-start(bf16[112,256]{1,0:T(8,128)(2,1)S(1)} %pad_maximum_fusion.1), channel_id=1, source_target_pairs={{0,12},{1,13},{2,14},{3,15},{4,8},{5,9},{6,10},{7,11},{8,4},{9,5},... | collective-permute-start | bytes 172040 | tf_op jit(solution)/shard_map/ppermute | solution.py:42
  41.7 2.3 %collective-permute-start.10 = (bf16[80,256]{1,0:T(8,128)(2,1)S(1)}, bf16[80,256]{1,0:T(8,128)(2,1)S(1)}, u32[]{:S(2)}, u32[]{:S(2)}) collective-permute-start(bf16[80,256]{1,0:T(8,128)(2,1)S(1)} %get-tuple-element.47), channel_id=1, source_target_pairs={{0,10},{1,11},{2,8},{3,9},{4,14},{5,15},{6,12},{7,13},{8,2},{9,3},... | collective-permute-start | bytes 122888 | tf_op jit(solution)/shard_map/ppermute | solution.py:42
  44.0 2.5 %collective-permute-start.11 = (bf16[80,256]{1,0:T(8,128)(2,1)S(1)}, bf16[80,256]{1,0:T(8,128)(2,1)S(1)}, u32[]{:S(2)}, u32[]{:S(2)}) collective-permute-start(bf16[80,256]{1,0:T(8,128)(2,1)S(1)} %get-tuple-element.50), channel_id=1, source_target_pairs={{0,14},{1,15},{2,12},{3,13},{4,10},{5,11},{6,8},{7,9},{8,6},{9,7},... | collective-permute-start | bytes 122888 | tf_op jit(solution)/shard_map/ppermute | solution.py:42
  46.5 1.4 %collective-permute-start.12 = (bf16[80,256]{1,0:T(8,128)(2,1)S(1)}, bf16[80,256]{1,0:T(8,128)(2,1)S(1)}, u32[]{:S(2)}, u32[]{:S(2)}) collective-permute-start(bf16[80,256]{1,0:T(8,128)(2,1)S(1)} %get-tuple-element.49), channel_id=1, source_target_pairs={{0,2},{1,3},{2,0},{3,1},{4,6},{5,7},{6,4},{7,5},{8,10},{9,11},{10,... | collective-permute-start | bytes 122888 | tf_op jit(solution)/shard_map/ppermute | solution.py:42
  47.8 1.9 %collective-permute-start.13 = (bf16[80,256]{1,0:T(8,128)(2,1)S(1)}, bf16[80,256]{1,0:T(8,128)(2,1)S(1)}, u32[]{:S(2)}, u32[]{:S(2)}) collective-permute-start(bf16[80,256]{1,0:T(8,128)(2,1)S(1)} %get-tuple-element.48), channel_id=1, source_target_pairs={{0,6},{1,7},{2,4},{3,5},{4,2},{5,3},{6,0},{7,1},{8,14},{9,15},{10,... | collective-permute-start | bytes 122888 | tf_op jit(solution)/shard_map/ppermute | solution.py:42
  50.1 1.0 %collective-permute-done.11 = bf16[80,256]{1,0:T(8,128)(2,1)S(1)} collective-permute-done((bf16[80,256]{1,0:T(8,128)(2,1)S(1)}, bf16[80,256]{1,0:T(8,128)(2,1)S(1)}, u32[]{:S(2)}, u32[]{:S(2)}) %collective-permute-start.11) | collective-permute-done | bytes 40992 | tf_op jit(solution)/shard_map/ppermute | solution.py:42
  51.4 1.4 %collective-permute-done.13 = bf16[80,256]{1,0:T(8,128)(2,1)S(1)} collective-permute-done((bf16[80,256]{1,0:T(8,128)(2,1)S(1)}, bf16[80,256]{1,0:T(8,128)(2,1)S(1)}, u32[]{:S(2)}, u32[]{:S(2)}) %collective-permute-start.13) | collective-permute-done | bytes 40992 | tf_op jit(solution)/shard_map/ppermute | solution.py:42
  52.8 2.2 %collective-permute-start.14 = (bf16[80,256]{1,0:T(8,128)(2,1)S(1)}, bf16[80,256]{1,0:T(8,128)(2,1)S(1)}, u32[]{:S(2)}, u32[]{:S(2)}) collective-permute-start(bf16[80,256]{1,0:T(8,128)(2,1)S(1)} %get-tuple-element.44), channel_id=1, source_target_pairs={{0,10},{1,11},{2,8},{3,9},{4,14},{5,15},{6,12},{7,13},{8,2},{9,3},... | collective-permute-start | bytes 122888 | tf_op jit(solution)/shard_map/ppermute | solution.py:42
  55.0 1.6 %collective-permute-start.15 = (bf16[80,256]{1,0:T(8,128)(2,1)S(1)}, bf16[80,256]{1,0:T(8,128)(2,1)S(1)}, u32[]{:S(2)}, u32[]{:S(2)}) collective-permute-start(bf16[80,256]{1,0:T(8,128)(2,1)S(1)} %get-tuple-element.44), channel_id=1, source_target_pairs={{0,14},{1,15},{2,12},{3,13},{4,10},{5,11},{6,8},{7,9},{8,6},{9,7},... | collective-permute-start | bytes 122888 | tf_op jit(solution)/shard_map/ppermute | solution.py:42
  56.6 1.2 %collective-permute-start.16 = (bf16[80,256]{1,0:T(8,128)(2,1)S(1)}, bf16[80,256]{1,0:T(8,128)(2,1)S(1)}, u32[]{:S(2)}, u32[]{:S(2)}) collective-permute-start(bf16[80,256]{1,0:T(8,128)(2,1)S(1)} %get-tuple-element.44), channel_id=1, source_target_pairs={{0,8},{1,9},{2,10},{3,11},{4,12},{5,13},{6,14},{7,15},{8,0},{9,1},... | collective-permute-start | bytes 122888 | tf_op jit(solution)/shard_map/ppermute | solution.py:42
  57.7 1.9 %collective-permute-start.17 = (bf16[80,256]{1,0:T(8,128)(2,1)S(1)}, bf16[80,256]{1,0:T(8,128)(2,1)S(1)}, u32[]{:S(2)}, u32[]{:S(2)}) collective-permute-start(bf16[80,256]{1,0:T(8,128)(2,1)S(1)} %get-tuple-element.44), channel_id=1, source_target_pairs={{0,12},{1,13},{2,14},{3,15},{4,8},{5,9},{6,10},{7,11},{8,4},{9,5},... | collective-permute-start | bytes 122888 | tf_op jit(solution)/shard_map/ppermute | solution.py:42
  60.3 1.3 %collective-permute-start.19 = (bf16[80,256]{1,0:T(8,128)(2,1)S(1)}, bf16[80,256]{1,0:T(8,128)(2,1)S(1)}, u32[]{:S(2)}, u32[]{:S(2)}) collective-permute-start(bf16[80,256]{1,0:T(8,128)(2,1)S(1)} %get-tuple-element.44), channel_id=1, source_target_pairs={{0,6},{1,7},{2,4},{3,5},{4,2},{5,3},{6,0},{7,1},{8,14},{9,15},{10,... | collective-permute-start | bytes 122888 | tf_op jit(solution)/shard_map/ppermute | solution.py:42
  61.8 1.4 %collective-permute-start.20 = (bf16[80,256]{1,0:T(8,128)(2,1)S(1)}, bf16[80,256]{1,0:T(8,128)(2,1)S(1)}, u32[]{:S(2)}, u32[]{:S(2)}) collective-permute-start(bf16[80,256]{1,0:T(8,128)(2,1)S(1)} %get-tuple-element.44), channel_id=1, source_target_pairs={{0,4},{1,5},{2,6},{3,7},{4,0},{5,1},{6,2},{7,3},{8,12},{9,13},{10,... | collective-permute-start | bytes 122888 | tf_op jit(solution)/shard_map/ppermute | solution.py:42
  63.6 1.6 %collective-permute-done.19 = bf16[80,256]{1,0:T(8,128)(2,1)S(1)} collective-permute-done((bf16[80,256]{1,0:T(8,128)(2,1)S(1)}, bf16[80,256]{1,0:T(8,128)(2,1)S(1)}, u32[]{:S(2)}, u32[]{:S(2)}) %collective-permute-start.19) | collective-permute-done | bytes 40992 | tf_op jit(solution)/shard_map/ppermute | solution.py:42
  66.5 1.0 %collective-permute-done.21.other_ref = bf16[640,256]{1,0:T(8,128)(2,1)S(1)} collective-permute-done((bf16[640,256]{1,0:T(8,128)(2,1)S(1)}, bf16[640,256]{1,0:T(8,128)(2,1)S(1)}, u32[]{:S(2)}, u32[]{:S(2)}) %collective-permute-start.21) | collective-permute-done | bytes 327712 | tf_op jit(solution)/shard_map/ppermute | solution.py:25
  67.5 1.7 %shard_map.188 = f32[5,256,256]{2,1,0:T(8,128)} custom-call(s32[3]{0:T(128)S(1)} %pad_add_fusion.place_ref.refs_0_, bf16[640,256]{1,0:T(8,128)(2,1)S(1)} %constant_dynamic-update-slice_fusion.own_ref, bf16[640,256]{1,0:T(8,128)(2,1)S(1)} %collective-permute-done.21.other_ref), custom_call_target="tpu_custom_call" | custom-call | bytes 1966092 | tf_op jit(solution)/shard_map/pallas_call | solution.py:483
  (71 shorter events, 8.9 us)
Async XLA Ops:
  0.6 27.3 %copy-start.9 = (bf16[128,256]{1,0:T(8,128)(2,1)S(1)}, bf16[128,256]{1,0:T(8,128)(2,1)}, u32[]{:S(2)}) copy-start(bf16[128,256]{1,0:T(8,128)(2,1)} %constant.55.clone.refs_14_) | copy-start | bytes 196612
  2.1 1.0 %copy-start = (bf16[16,32,256]{2,1,0:T(8,128)(2,1)S(1)}, bf16[16,32,256]{2,1,0:T(8,128)(2,1)}, u32[]{:S(2)}) copy-start(bf16[16,32,256]{2,1,0:T(8,128)(2,1)} %param.17) | copy-start | bytes 786436
  5.8 22.1 %copy-start.2 = (bf16[2,128,384]{2,1,0:T(8,128)(2,1)S(1)}, bf16[2,128,384]{2,1,0:T(8,128)(2,1)}, u32[]{:S(2)}) copy-start(bf16[2,128,384]{2,1,0:T(8,128)(2,1)} %constant.53.clone.refs_12_) | copy-start | bytes 589828
  5.8 22.1 %copy-start.10 = (f32[2,16,384]{2,1,0:T(8,128)S(1)}, f32[2,16,384]{2,1,0:T(8,128)}, u32[]{:S(2)}) copy-start(f32[2,16,384]{2,1,0:T(8,128)} %constant.61.refs_13_) | copy-start | bytes 147460
  6.5 15.1 %collective-permute-start = (bf16[368,256]{1,0:T(8,128)(2,1)S(1)}, bf16[368,256]{1,0:T(8,128)(2,1)S(1)}, u32[]{:S(2)}, u32[]{:S(2)}) collective-permute-start(bf16[368,256]{1,0:T(8,128)(2,1)S(1)} %get-tuple-element.25), channel_id=1, source_target_pairs={{0,4},{4,0},{8,12},{12,8},{1,5},{5,1},{9,13},{13,9},{2,6},{6,2},{1... | collective-permute-start | bytes 565256 | tf_op jit(solution)/shard_map/ppermute | solution.py:25
  9.5 12.1 %collective-permute-start.1 = (bf16[368,256]{1,0:T(8,128)(2,1)S(1)}, bf16[368,256]{1,0:T(8,128)(2,1)S(1)}, u32[]{:S(2)}, u32[]{:S(2)}) collective-permute-start(bf16[368,256]{1,0:T(8,128)(2,1)S(1)} %get-tuple-element.26), channel_id=1, source_target_pairs={{4,8},{8,4},{5,9},{9,5},{6,10},{10,6},{7,11},{11,7},{20,24},{24,20... | collective-permute-start | bytes 565256 | tf_op jit(solution)/shard_map/ppermute | solution.py:31
  10.2 9.3 %collective-permute-start.2 = (bf16[48,256]{1,0:T(8,128)(2,1)S(1)}, bf16[48,256]{1,0:T(8,128)(2,1)S(1)}, u32[]{:S(2)}, u32[]{:S(2)}) collective-permute-start(bf16[48,256]{1,0:T(8,128)(2,1)S(1)} %get-tuple-element.27), channel_id=1, source_target_pairs={{0,8},{4,12},{8,0},{12,4},{1,9},{5,13},{9,1},{13,5},{2,10},{6,14},... | collective-permute-start | bytes 73736 | tf_op jit(solution)/shard_map/ppermute | solution.py:25
  14.1 7.5 %collective-permute-start.3 = (bf16[48,256]{1,0:T(8,128)(2,1)S(1)}, bf16[48,256]{1,0:T(8,128)(2,1)S(1)}, u32[]{:S(2)}, u32[]{:S(2)}) collective-permute-start(bf16[48,256]{1,0:T(8,128)(2,1)S(1)} %get-tuple-element.28), channel_id=1, source_target_pairs={{0,12},{12,0},{1,13},{13,1},{2,14},{14,2},{3,15},{15,3},{16,28},{2... | collective-permute-start | bytes 73736 | tf_op jit(solution)/shard_map/ppermute | solution.py:589
  21.6 0.9 %copy-start.1 = (bf16[256,256]{1,0:T(8,128)(2,1)S(1)}, bf16[256,256]{1,0:T(8,128)(2,1)}, u32[]{:S(2)}) copy-start(bf16[256,256]{1,0:T(8,128)(2,1)} %refs_15_.1) | copy-start | bytes 393220
  23.2 4.7 %copy-start.4 = (bf16[256,256]{1,0:T(8,128)(2,1)S(1)}, bf16[256,256]{1,0:T(8,128)(2,1)}, u32[]{:S(2)}) copy-start(bf16[256,256]{1,0:T(8,128)(2,1)} %refs_16_.1) | copy-start | bytes 393220
  23.2 4.7 %copy-start.6 = (bf16[256,256]{1,0:T(8,128)(2,1)S(1)}, bf16[256,256]{1,0:T(8,128)(2,1)}, u32[]{:S(2)}) copy-start(bf16[256,256]{1,0:T(8,128)(2,1)} %refs_18_.1) | copy-start | bytes 393220
  23.3 4.8 %copy-start.7 = (bf16[256,256]{1,0:T(8,128)(2,1)S(1)}, bf16[256,256]{1,0:T(8,128)(2,1)}, u32[]{:S(2)}) copy-start(bf16[256,256]{1,0:T(8,128)(2,1)} %refs_19_.1) | copy-start | bytes 393220
  23.3 4.8 %copy-start.8 = (bf16[2,128,192]{2,1,0:T(8,128)(2,1)S(1)}, bf16[2,128,192]{2,1,0:T(8,128)(2,1)}, u32[]{:S(2)}) copy-start(bf16[2,128,192]{2,1,0:T(8,128)(2,1)} %constant.52.clone.refs_11_) | copy-start | bytes 294916
  24.4 3.5 %collective-permute-start.4 = (bf16[576,256]{1,0:T(8,128)(2,1)S(1)}, bf16[576,256]{1,0:T(8,128)(2,1)S(1)}, u32[]{:S(2)}, u32[]{:S(2)}) collective-permute-start(bf16[576,256]{1,0:T(8,128)(2,1)S(1)} %get-tuple-element.29), channel_id=1, source_target_pairs={{0,1},{1,0},{2,3},{3,2},{4,5},{5,4},{6,7},{7,6},{8,9},{9,8},{10,11... | collective-permute-start | bytes 884744 | tf_op jit(solution)/shard_map/ppermute | solution.py:25
  24.5 3.4 %collective-permute-start.5 = (bf16[576,256]{1,0:T(8,128)(2,1)S(1)}, bf16[576,256]{1,0:T(8,128)(2,1)S(1)}, u32[]{:S(2)}, u32[]{:S(2)}) collective-permute-start(bf16[576,256]{1,0:T(8,128)(2,1)S(1)} %get-tuple-element.30), channel_id=1, source_target_pairs={{1,2},{2,1},{5,6},{6,5},{9,10},{10,9},{13,14},{14,13},{17,18},{18,... | collective-permute-start | bytes 884744 | tf_op jit(solution)/shard_map/ppermute | solution.py:31
  25.2 0.9 %copy-start.3 = (bf16[256,256]{1,0:T(8,128)(2,1)S(1)}, bf16[256,256]{1,0:T(8,128)(2,1)}, u32[]{:S(2)}) copy-start(bf16[256,256]{1,0:T(8,128)(2,1)} %refs_16_.1) | copy-start | bytes 393220
  31.6 6.3 %collective-permute-start.6 = (bf16[640,256]{1,0:T(8,128)(2,1)S(1)}, bf16[640,256]{1,0:T(8,128)(2,1)S(1)}, u32[]{:S(2)}, u32[]{:S(2)}) collective-permute-start(bf16[640,256]{1,0:T(8,128)(2,1)S(1)} %get-tuple-element.42), channel_id=1, source_target_pairs={{0,1},{1,0},{2,3},{3,2},{4,5},{5,4},{6,7},{7,6},{8,9},{9,8},{10,11... | collective-permute-start | bytes 983048 | tf_op jit(solution)/shard_map/ppermute | solution.py:25
  38.1 8.4 %collective-permute-start.7 = (bf16[112,256]{1,0:T(8,128)(2,1)S(1)}, bf16[112,256]{1,0:T(8,128)(2,1)S(1)}, u32[]{:S(2)}, u32[]{:S(2)}) collective-permute-start(bf16[112,256]{1,0:T(8,128)(2,1)S(1)} %pad_maximum_fusion), channel_id=1, source_target_pairs={{0,8},{1,9},{2,10},{3,11},{4,12},{5,13},{6,14},{7,15},{8,0},{9,1},... | collective-permute-start | bytes 172040 | tf_op jit(solution)/shard_map/ppermute | solution.py:42
  38.2 9.7 %collective-permute-start.8 = (bf16[112,256]{1,0:T(8,128)(2,1)S(1)}, bf16[112,256]{1,0:T(8,128)(2,1)S(1)}, u32[]{:S(2)}, u32[]{:S(2)}) collective-permute-start(bf16[112,256]{1,0:T(8,128)(2,1)S(1)} %pad_maximum_fusion.1), channel_id=1, source_target_pairs={{0,12},{1,13},{2,14},{3,15},{4,8},{5,9},{6,10},{7,11},{8,4},{9,5},... | collective-permute-start | bytes 172040 | tf_op jit(solution)/shard_map/ppermute | solution.py:42
  41.2 8.6 %collective-permute-start.9 = (bf16[112,256]{1,0:T(8,128)(2,1)S(1)}, bf16[112,256]{1,0:T(8,128)(2,1)S(1)}, u32[]{:S(2)}, u32[]{:S(2)}) collective-permute-start(bf16[112,256]{1,0:T(8,128)(2,1)S(1)} %pad_maximum_fusion.2), channel_id=1, source_target_pairs={{0,4},{1,5},{2,6},{3,7},{4,0},{5,1},{6,2},{7,3},{8,12},{9,13},{10,... | collective-permute-start | bytes 172040 | tf_op jit(solution)/shard_map/ppermute | solution.py:42
  41.7 8.4 %collective-permute-start.10 = (bf16[80,256]{1,0:T(8,128)(2,1)S(1)}, bf16[80,256]{1,0:T(8,128)(2,1)S(1)}, u32[]{:S(2)}, u32[]{:S(2)}) collective-permute-start(bf16[80,256]{1,0:T(8,128)(2,1)S(1)} %get-tuple-element.47), channel_id=1, source_target_pairs={{0,10},{1,11},{2,8},{3,9},{4,14},{5,15},{6,12},{7,13},{8,2},{9,3},... | collective-permute-start | bytes 122888 | tf_op jit(solution)/shard_map/ppermute | solution.py:42
  44.0 7.1 %collective-permute-start.11 = (bf16[80,256]{1,0:T(8,128)(2,1)S(1)}, bf16[80,256]{1,0:T(8,128)(2,1)S(1)}, u32[]{:S(2)}, u32[]{:S(2)}) collective-permute-start(bf16[80,256]{1,0:T(8,128)(2,1)S(1)} %get-tuple-element.50), channel_id=1, source_target_pairs={{0,14},{1,15},{2,12},{3,13},{4,10},{5,11},{6,8},{7,9},{8,6},{9,7},... | collective-permute-start | bytes 122888 | tf_op jit(solution)/shard_map/ppermute | solution.py:42
  46.5 4.9 %collective-permute-start.12 = (bf16[80,256]{1,0:T(8,128)(2,1)S(1)}, bf16[80,256]{1,0:T(8,128)(2,1)S(1)}, u32[]{:S(2)}, u32[]{:S(2)}) collective-permute-start(bf16[80,256]{1,0:T(8,128)(2,1)S(1)} %get-tuple-element.49), channel_id=1, source_target_pairs={{0,2},{1,3},{2,0},{3,1},{4,6},{5,7},{6,4},{7,5},{8,10},{9,11},{10,... | collective-permute-start | bytes 122888 | tf_op jit(solution)/shard_map/ppermute | solution.py:42
  47.8 4.9 %collective-permute-start.13 = (bf16[80,256]{1,0:T(8,128)(2,1)S(1)}, bf16[80,256]{1,0:T(8,128)(2,1)S(1)}, u32[]{:S(2)}, u32[]{:S(2)}) collective-permute-start(bf16[80,256]{1,0:T(8,128)(2,1)S(1)} %get-tuple-element.48), channel_id=1, source_target_pairs={{0,6},{1,7},{2,4},{3,5},{4,2},{5,3},{6,0},{7,1},{8,14},{9,15},{10,... | collective-permute-start | bytes 122888 | tf_op jit(solution)/shard_map/ppermute | solution.py:42
  52.8 7.5 %collective-permute-start.14 = (bf16[80,256]{1,0:T(8,128)(2,1)S(1)}, bf16[80,256]{1,0:T(8,128)(2,1)S(1)}, u32[]{:S(2)}, u32[]{:S(2)}) collective-permute-start(bf16[80,256]{1,0:T(8,128)(2,1)S(1)} %get-tuple-element.44), channel_id=1, source_target_pairs={{0,10},{1,11},{2,8},{3,9},{4,14},{5,15},{6,12},{7,13},{8,2},{9,3},... | collective-permute-start | bytes 122888 | tf_op jit(solution)/shard_map/ppermute | solution.py:42
  55.0 6.8 %collective-permute-start.15 = (bf16[80,256]{1,0:T(8,128)(2,1)S(1)}, bf16[80,256]{1,0:T(8,128)(2,1)S(1)}, u32[]{:S(2)}, u32[]{:S(2)}) collective-permute-start(bf16[80,256]{1,0:T(8,128)(2,1)S(1)} %get-tuple-element.44), channel_id=1, source_target_pairs={{0,14},{1,15},{2,12},{3,13},{4,10},{5,11},{6,8},{7,9},{8,6},{9,7},... | collective-permute-start | bytes 122888 | tf_op jit(solution)/shard_map/ppermute | solution.py:42
  56.6 6.6 %collective-permute-start.16 = (bf16[80,256]{1,0:T(8,128)(2,1)S(1)}, bf16[80,256]{1,0:T(8,128)(2,1)S(1)}, u32[]{:S(2)}, u32[]{:S(2)}) collective-permute-start(bf16[80,256]{1,0:T(8,128)(2,1)S(1)} %get-tuple-element.44), channel_id=1, source_target_pairs={{0,8},{1,9},{2,10},{3,11},{4,12},{5,13},{6,14},{7,15},{8,0},{9,1},... | collective-permute-start | bytes 122888 | tf_op jit(solution)/shard_map/ppermute | solution.py:42
  57.7 5.8 %collective-permute-start.17 = (bf16[80,256]{1,0:T(8,128)(2,1)S(1)}, bf16[80,256]{1,0:T(8,128)(2,1)S(1)}, u32[]{:S(2)}, u32[]{:S(2)}) collective-permute-start(bf16[80,256]{1,0:T(8,128)(2,1)S(1)} %get-tuple-element.44), channel_id=1, source_target_pairs={{0,12},{1,13},{2,14},{3,15},{4,8},{5,9},{6,10},{7,11},{8,4},{9,5},... | collective-permute-start | bytes 122888 | tf_op jit(solution)/shard_map/ppermute | solution.py:42
  59.6 4.0 %collective-permute-start.18 = (bf16[80,256]{1,0:T(8,128)(2,1)S(1)}, bf16[80,256]{1,0:T(8,128)(2,1)S(1)}, u32[]{:S(2)}, u32[]{:S(2)}) collective-permute-start(bf16[80,256]{1,0:T(8,128)(2,1)S(1)} %get-tuple-element.44), channel_id=1, source_target_pairs={{0,2},{1,3},{2,0},{3,1},{4,6},{5,7},{6,4},{7,5},{8,10},{9,11},{10,... | collective-permute-start | bytes 122888 | tf_op jit(solution)/shard_map/ppermute | solution.py:42
  60.3 4.9 %collective-permute-start.19 = (bf16[80,256]{1,0:T(8,128)(2,1)S(1)}, bf16[80,256]{1,0:T(8,128)(2,1)S(1)}, u32[]{:S(2)}, u32[]{:S(2)}) collective-permute-start(bf16[80,256]{1,0:T(8,128)(2,1)S(1)} %get-tuple-element.44), channel_id=1, source_target_pairs={{0,6},{1,7},{2,4},{3,5},{4,2},{5,3},{6,0},{7,1},{8,14},{9,15},{10,... | collective-permute-start | bytes 122888 | tf_op jit(solution)/shard_map/ppermute | solution.py:42
  61.8 4.0 %collective-permute-start.20 = (bf16[80,256]{1,0:T(8,128)(2,1)S(1)}, bf16[80,256]{1,0:T(8,128)(2,1)S(1)}, u32[]{:S(2)}, u32[]{:S(2)}) collective-permute-start(bf16[80,256]{1,0:T(8,128)(2,1)S(1)} %get-tuple-element.44), channel_id=1, source_target_pairs={{0,4},{1,5},{2,6},{3,7},{4,0},{5,1},{6,2},{7,3},{8,12},{9,13},{10,... | collective-permute-start | bytes 122888 | tf_op jit(solution)/shard_map/ppermute | solution.py:42
  65.8 1.6 %collective-permute-start.21 = (bf16[640,256]{1,0:T(8,128)(2,1)S(1)}, bf16[640,256]{1,0:T(8,128)(2,1)S(1)}, u32[]{:S(2)}, u32[]{:S(2)}) collective-permute-start(bf16[640,256]{1,0:T(8,128)(2,1)S(1)} %constant_dynamic-update-slice_fusion.own_ref), channel_id=1, source_target_pairs={{0,1},{1,0},{2,3},{3,2},{4,5},{5,4},{6,7},{7,6},{8,9},{9,8},{10,11... | collective-permute-start | bytes 983048 | tf_op jit(solution)/shard_map/ppermute | solution.py:25
  (6 other events, 4.4 us)

commit v4 on v3

--- a/solution.py
+++ b/solution.py
@@ -29,17 +29,6 @@
     count = lax.axis_size(axis)
     pairs = [(i, i + 1) for i in range(1, count - 1, 2)]
     return lax.ppermute(block, axis, pairs + [(j, i) for i, j in pairs])
-
-
-def swapped_both(block, wide_bits, narrow_bits):
-    wide_count = lax.axis_size("wide")
-    narrow_count = lax.axis_size("narrow")
-    pairs = [
-        (w * narrow_count + n, (w ^ wide_bits) * narrow_count + (n ^ narrow_bits))
-        for w in range(wide_count)
-        for n in range(narrow_count)
-    ]
-    return lax.ppermute(block, ("wide", "narrow"), pairs)
 
 
 def dot(left, right):
@@ -162,29 +151,76 @@
         }
 
 
+def fetch(sources, targets, sems):
+    copies = [
+        pltpu.make_async_copy(source, target, sems.at[k])
+        for k, (source, target) in enumerate(zip(sources, targets))
+    ]
+    for copy in copies:
+        copy.start()
+    return copies
+
+
 def pack_kernel(
     shape,
     units,
     place_ref,
-    own_ref,
-    cotangent_ref,
-    mask_ref,
-    rows_ref,
-    target_x_ref,
-    target_y_ref,
+    own_hbm,
+    cotangent_hbm,
+    mask_hbm,
+    rows_hbm,
+    target_x_hbm,
+    target_y_hbm,
+    count_hbm,
     first_ref,
     second_ref,
     third_ref,
     fourth_ref,
     mesh_ref,
     own_rows_ref,
+    mask_ref,
+    rows_ref,
+    target_x_ref,
+    target_y_ref,
+    count_ref,
+    sems,
 ):
     edge, own_nodes, halo = shape.edge, shape.own_nodes, shape.halo
     held = rows_ref.shape[0]
     even = place_ref[0] % 2 == 0
-    row_count = place_ref[1]
+    odd = jnp.logical_not(even)
+    starts = [
+        pl.multiple_of(jnp.where(upward, shape.cells - halo, 0), shape.tile_y)
+        for upward in (even, odd)
+    ]
+    copies = fetch(
+        [
+            count_hbm,
+            target_x_hbm,
+            target_y_hbm,
+            rows_hbm,
+            cotangent_hbm,
+            mask_hbm,
+            own_hbm.at[pl.ds(starts[0], halo)],
+            own_hbm.at[pl.ds(starts[1], halo)],
+        ],
+        [
+            count_ref,
+            target_x_ref,
+            target_y_ref,
+            rows_ref,
+            mesh_ref.at[:own_nodes],
+            mask_ref,
+            first_ref.at[:halo],
+            second_ref.at[:halo],
+        ],
+        sems,
+    )
+    for copy in copies[:4]:
+        copy.wait()
+    row_count = count_ref[0]
     target_x = target_x_ref[...]
-    column = target_y_ref[...] - place_ref[2] * shape.tile_y
+    column = target_y_ref[...] - place_ref[1] * shape.tile_y
     slot = lax.broadcasted_iota(jnp.int32, (1, held), 1)
     column = jnp.where(slot < row_count, column, LANES - 1)
     line = lax.broadcasted_iota(jnp.int32, (16, held), 0)
@@ -195,21 +231,28 @@
     repeat = lane % held == lax.broadcasted_iota(jnp.int32, (held, LANES), 0)
     spread = dot(fields.astype(F32).astype(BF16), jnp.where(repeat, 1.0, 0.0).astype(BF16))
     lane = lax.broadcasted_iota(jnp.int32, (16, LANES), 1)
-
-    mesh_ref[:own_nodes] = cotangent_ref[...]
-    mesh_ref[own_nodes:] = mask_ref[...]
-    targets = (own_rows_ref, first_ref, third_ref, second_ref, fourth_ref)
-    for ref, number in zip(targets, (0, 1, 2, 3, 3)):
+    for number, ref in enumerate((own_rows_ref, first_ref, third_ref, fourth_ref)):
         at = ref.shape[0] - held - 16
         ref[at : at + held] = rows_ref[...]
         ref[at + held :] = jnp.where(lane // held == number, spread, 0.0).astype(BF16)
-    for ref, upward in ((first_ref, even), (second_ref, jnp.logical_not(even))):
-        start = pl.multiple_of(jnp.where(upward, shape.cells - halo, 0), shape.tile_y)
-        ref[:halo] = own_ref[pl.ds(start, halo)]
+
+    for copy in copies[4:6]:
+        copy.wait()
+    mesh_ref[own_nodes:] = jnp.zeros((own_nodes, mesh_ref.shape[1]), BF16)
+    mesh_ref[own_nodes:, : mask_ref.shape[1]] = mask_ref[...].astype(F32).astype(BF16)
+    for ref, upward in ((first_ref, even), (second_ref, odd)):
         start = pl.multiple_of(jnp.where(upward, own_nodes - edge, 0), 16)
         ref[halo : halo + edge] = mesh_ref[pl.ds(start, edge)]
         start = pl.multiple_of(jnp.where(upward, 2 * own_nodes - edge, own_nodes), 16)
         ref[halo + edge : halo + 2 * edge] = mesh_ref[pl.ds(start, edge)]
+    for copy in copies[6:]:
+        copy.wait()
+
+
+def load_kernel(count, *refs):
+    sources, targets, sems = refs[1 : 1 + count], refs[1 + count : 1 + 2 * count], refs[-1]
+    for copy in fetch(sources, targets, sems):
+        copy.wait()
 
 
 def blend_kernel(shape, units, unit_rows, *refs):
@@ -227,14 +270,9 @@
     def held(k, at, n):
         if k == 0:
             return own_rows_ref[at : at + n]
-        if k == 1:
-            return near[first_row + at : first_row + at + n]
-        if k < units - 1:
-            return arrived[k][at : at + n]
-        value = between[first_row + at : first_row + at + n]
-        if units > 3:
-            value = value + arrived[-1][at : at + n]
-        return value
+        if k == 1 or units == 3:
+            return arrived[k - 1][first_row + at : first_row + at + n]
+        return arrived[k][at : at + n]
 
     total = unit_rows * units
     for k in range(units):
@@ -267,7 +305,7 @@
         [facing(shape.halo, mesh, False), mesh_ref[...], facing(shape.halo, mesh, True)], axis=0
     )
     stack_ref[...] = stack
-    narrow_even = place_ref[2] % 2 == 0
+    narrow_even = place_ref[1] % 2 == 0
     column = pl.multiple_of(jnp.where(narrow_even, shape.tile_y - SIDE, 0), SIDE)
     other = pl.multiple_of(jnp.where(narrow_even, 0, shape.tile_y - SIDE), SIDE)
     to_left = dot(side_ref[0], stack).astype(BF16)
@@ -461,31 +499,37 @@
     kept_ref[...] = grads_ref[pl.ds(kept_at, half)]
 
 
-def finish_kernel(scales, place_ref, own_ref, other_ref, out_ref):
-    even = place_ref[2] % 2 == 0
-    half = own_ref.shape[0]
-    channels = own_ref.shape[1]
-    for k, scale in enumerate(scales):
-        for start, stop, lower in ((0, half, True), (half, 2 * half, False)):
-            at = max(k * channels, start)
-            end = min((k + 1) * channels, stop)
-            if at >= end:
-                continue
-            own, other = own_ref[at - start : end - start], other_ref[at - start : end - start]
-            value = jnp.where(even, own, other) if lower else jnp.where(even, other, own)
-            out_ref[k, at - k * channels : end - k * channels] = value.astype(F32) * scale
-
-
-def call(kernel, out_shapes, operands, scratch=(), scalars=1, flops=0):
-    specs = [pl.BlockSpec(memory_space=pltpu.SMEM)] * scalars
-    specs += [pl.BlockSpec(memory_space=pltpu.VMEM)] * (len(operands) - scalars)
+def finish_kernel(scales, kept, *refs):
+    place_ref, part_ref, out_ref, wide_ref, sems = refs[0], refs[1], refs[-3], refs[-2], refs[-1]
+    half, channels = part_ref.shape
+    upper = place_ref[1] % 2 if kept else 1 - place_ref[1] % 2
+    step = channels // 2
+    count = half // step
+    copies = []
+    for k in range(count):
+        scale = jnp.where(upper == 0, scales[k // 2], scales[(count + k) // 2])
+        rows = slice(k * step, (k + 1) * step)
+        wide_ref[rows] = part_ref[rows].astype(F32) * scale
+        target = pl.ds(pl.multiple_of(upper * half + k * step, step), step)
+        copies.append(pltpu.make_async_copy(wide_ref.at[rows], out_ref.at[target], sems.at[k]))
+        copies[-1].start()
+    for copy in copies:
+        copy.wait()
+
+
+def call(
+    kernel, out_shapes, operands, scratch=(), spaces="", out_space=pltpu.VMEM, flops=0, aliases=None
+):
+    kinds = {"s": pltpu.SMEM, "v": pltpu.VMEM, "h": pltpu.HBM}
+    spaces = spaces + "v" * (len(operands) - len(spaces))
     moved = sum(math.prod(o.shape) * o.dtype.itemsize for o in list(operands) + list(out_shapes))
     return pl.pallas_call(
         kernel,
         out_shape=tuple(out_shapes),
-        in_specs=specs,
-        out_specs=tuple(pl.BlockSpec(memory_space=pltpu.VMEM) for _ in out_shapes),
+        in_specs=[pl.BlockSpec(memory_space=kinds[space]) for space in spaces],
+        out_specs=tuple(pl.BlockSpec(memory_space=out_space) for _ in out_shapes),
         scratch_shapes=list(scratch),
+        input_output_aliases=aliases or {},
         compiler_params=pltpu.CompilerParams(vmem_limit_bytes=VMEM_LIMIT),
         cost_estimate=pl.CostEstimate(flops=flops, bytes_accessed=moved, transcendentals=0),
     )(*operands)
@@ -526,8 +570,9 @@
     narrow_at = lax.axis_index("narrow")
     held_rows = boundary_rows.shape[0]
     shape = Shape(tile_x, tile_y)
-    table = {name: jnp.asarray(value, BF16) for name, value in shape.tables().items()}
-    table["match"] = table["match"].astype(F32)
+    table = shape.tables()
+    names = list(table)
+    fixed = [jnp.asarray(table[name], F32 if name == "match" else BF16) for name in names]
 
     live = jnp.arange(held_rows) < row_count[0]
     column = target_y - narrow_at * tile_y
@@ -562,16 +607,17 @@
 
     cells = grid_state.reshape(-1, channels)
     cotangent = mesh_cotangent.reshape(-1, channels)
-    mask = g2m_mask.astype(BF16).transpose(1, 2, 0).reshape(-1, 36)
-    mask = jnp.pad(mask, ((0, 0), (0, channels - 36)))
-    place = jnp.stack([wide_at, row_count[0], narrow_at])
+    mask = g2m_mask.transpose(1, 2, 0).reshape(-1, 36)
+    place = jnp.stack([wide_at, narrow_at])
     struct = jax.ShapeDtypeStruct
     long = struct((shape.halo + 2 * shape.edge + unit_rows + 16, channels), BF16)
+    plain = struct((shape.halo + 2 * shape.edge, channels), BF16)
     short = struct((unit_rows + 16, channels), BF16)
+    dma = pltpu.SemaphoreType.DMA
     if whole_column:
         first, second, third, fourth, mesh, own_rows = call(
             functools.partial(pack_kernel, shape, units),
-            [long, long, short, short, struct((2 * shape.own_nodes, channels), BF16), short],
+            [long, plain, short, short, struct((2 * shape.own_nodes, channels), BF16), short],
             [
                 place,
                 cells,
@@ -580,19 +626,28 @@
                 rows,
                 target_x.reshape(1, -1),
                 target_y.reshape(1, -1),
+                row_count,
             ],
+            scratch=[
+                pltpu.VMEM(mask.shape, jnp.int32),
+                pltpu.VMEM(rows.shape, BF16),
+                pltpu.VMEM((1, held_rows), jnp.int32),
+                pltpu.VMEM((1, held_rows), jnp.int32),
+                pltpu.SMEM((1,), jnp.int32),
+                dma((8,)),
+            ],
+            spaces="shhhhhhh",
         )
-        arrived = [
-            swapped(first, "wide", 1),
-            swapped_between(second, "wide"),
-            swapped(third, "wide", 2),
-            lax.ppermute(fourth, "wide", [(0, 3), (3, 0)]),
-        ]
+        third = swapped(third, "wide", 2)
+        fourth = swapped(fourth, "wide", 3)
+        first_in = swapped(first, "wide", 1)
+        arrived = [first_in, swapped_between(second, "wide"), third, fourth]
     else:
 
         def with_meta(slot):
             return [rows, meta_rows(row_live, row_x, row_y, tile_x, unit_rows, slot, units)]
 
+        mask = jnp.pad(mask.astype(BF16), ((0, 0), (0, channels - 36)))
         mesh = jnp.concatenate([cotangent, mask])
         own_rows = jnp.concatenate(with_meta(0))
         edge = shape.edge
@@ -604,6 +659,16 @@
         second = jnp.concatenate([jnp.where(upward, to_prev, to_next)] + with_meta(2))
         arrived = [swapped(first, "wide", 1), swapped_between(second, "wide")]
 
+    source = [cells, w_force, w_embed, w_message, w_level_one, w_level_two] + fixed
+    loaded = call(
+        functools.partial(load_kernel, len(source)),
+        [struct(x.shape, x.dtype) for x in source],
+        [own_rows] + source,
+        scratch=[dma((len(source),))],
+        spaces="v" + "h" * len(source),
+    )
+    cells, w_force, w_embed, w_message, w_level_one, w_level_two = loaded[:6]
+    table = dict(zip(names, loaded[6:]))
     total_rows = unit_rows * units
     stack_rows = 4 * shape.edge + 2 * shape.own_nodes
     payload = struct((shape.side + 2 * shape.side_nodes, channels), BF16)
@@ -619,6 +684,7 @@
         ],
         [place, cells, mesh, w_force, table["to_side"], own_rows] + arrived,
         scratch=[pltpu.VMEM((total_rows, channels), BF16)],
+        spaces="s",
         flops=2 * shape.center * total_rows * channels,
     )
     second = swapped_between(second, "narrow")
@@ -632,7 +698,6 @@
             struct((shape.cells, channels), F32),
         ],
         [blended, w_embed, w_message],
-        scalars=0,
         flops=4 * shape.center * channels * channels,
     )
     grad_rows_total = 5 * channels
@@ -674,35 +739,38 @@
             pltpu.VMEM((shape.cells, channels), BF16),
             pltpu.VMEM((grad_rows_total, channels), F32),
         ],
+        spaces="s",
         flops=12 * shape.cells * channels * channels,
     )
 
     piece = kept + swapped(sent, "narrow", 1).astype(F32)
     back_blocks = back.reshape(units, unit_rows, channels)
     row_back = back_blocks[0].astype(F32)
-    others = narrow_count // 2
-    if wide_count * others <= 8:
-        group = wide_count * others
-        part = piece.shape[0] // group
-        at = wide_at * others + narrow_at // 2
-        rounded = piece.astype(BF16)
-        own = lax.dynamic_slice_in_dim(piece, at * part, part)
-        order = sorted(range(1, group), key=lambda k: (k // others < 2, k % others == 0))
-        for k in order:
-            wide_bits, narrow_bits = k // others, k % others
-            sent = lax.dynamic_slice_in_dim(rounded, (at ^ k) * part, part)
-            if narrow_bits == 0 and whole_column:
-                sent = jnp.concatenate([sent, back_blocks[wide_bits]])
-            got = swapped_both(sent, wide_bits, 2 * narrow_bits).astype(F32)
-            own = own + got[:part]
-            if narrow_bits == 0 and whole_column:
-                row_back = row_back + got[part:]
-        own = own.astype(BF16)
-        gathered = jnp.zeros((group * part, channels), BF16)
-        gathered = lax.dynamic_update_slice_in_dim(gathered, own, at * part, 0)
-        for k in order:
-            got = swapped_both(own, k // others, 2 * (k % others))
-            gathered = lax.dynamic_update_slice_in_dim(gathered, got, (at ^ k) * part, 0)
+    if wide_count == 4 and narrow_count == 4:
+
+        def split(block, upper):
+            half = block.shape[0] // 2
+            sent = lax.dynamic_slice_in_dim(block, (1 - upper) * half, half)
+            return sent, lax.dynamic_slice_in_dim(block, upper * half, half)
+
+        def joined(block, other, upper):
+            low, high = jnp.where(upper == 0, block, other), jnp.where(upper == 0, other, block)
+            return jnp.concatenate([low, high])
+
+        sent, kept = split(piece, narrow_at // 2)
+        piece = kept + swapped(sent.astype(BF16), "narrow", 2).astype(F32)
+        sent, kept = split(piece, wide_at % 2)
+        part = kept.shape[0]
+        sent = jnp.concatenate([sent.astype(BF16), back_blocks[1], back_blocks[3]])
+        got = swapped(sent, "wide", 1).astype(F32)
+        row_back = row_back + got[part : part + unit_rows]
+        far = (back_blocks[2].astype(F32) + got[part + unit_rows :]).astype(BF16)
+        rounded = (kept + got[:part]).astype(BF16)
+        got = swapped(jnp.concatenate([rounded, far]), "wide", 2).astype(F32)
+        row_back = row_back + got[part:]
+        gathered = (rounded.astype(F32) + got[:part]).astype(BF16)
+        gathered = joined(gathered, swapped(gathered, "wide", 1), wide_at % 2)
+        gathered = joined(gathered, swapped(gathered, "narrow", 2), narrow_at // 2)
     else:
         bits = [1 << k for k in range(1, narrow_count.bit_length() - 1)]
         for bit in bits:
@@ -748,11 +816,27 @@
     cell_total = shape.cells * wide_count * narrow_count
     row_total = held_rows * wide_count * narrow_count
     sizes = [row_total, cell_total, cell_total, cell_total // 16, cell_total // 64]
+    scales = [1.0 / math.sqrt(size) for size in sizes]
+    result = struct((5 * channels, channels), F32)
+    scratch = [pltpu.VMEM((5 * channels // 2, channels), F32), dma((5,))]
     (weight_grads,) = call(
-        functools.partial(finish_kernel, [1.0 / math.sqrt(size) for size in sizes]),
-        [struct((5, channels, channels), F32)],
-        [place, gathered, other],
-    )
+        functools.partial(finish_kernel, scales, True),
+        [result],
+        [place, gathered],
+        scratch=scratch,
+        spaces="sv",
+        out_space=pltpu.HBM,
+    )
+    (weight_grads,) = call(
+        functools.partial(finish_kernel, scales, False),
+        [result],
+        [place, other, weight_grads],
+        scratch=scratch,
+        spaces="svh",
+        out_space=pltpu.HBM,
+        aliases={2: 0},
+    )
+    weight_grads = weight_grads.reshape(5, channels, channels)
     return (grad_state.reshape(tile_x, tile_y, channels), row_back, weight_grads)
 
 

time: 69.8 us -> 76 us (1.089)
  starting transfers between devices: 40 us -> 21 us
  waiting for transfers between devices: 10.7 us -> 25.9 us
  local copies, waits for them, and re-layouts: 7.27 us -> 14.1 us
  Pallas kernels: 8.06 us -> 11.6 us
    ppermute x15 -> x0, starting transfers between devices: 26.6 us -> none  [the longest x14 21.8 us: swapped_both(): return lax.ppermute(block, ('wide', 'narrow'), pairs)]
    ppermute x5 -> x11, waiting for transfers between devices: 2.85 us -> 25.9 us  [swapped(): return lax.ppermute(block, axis, [(i, i ^ bits) for i in range(count)])]
    ppermute x15 -> x0, waiting for transfers between devices: 7.83 us -> none  [the longest x14 5.73 us: swapped_both(): return lax.ppermute(block, ('wide', 'narrow'), pairs)]
    ppermute x5 -> x11, starting transfers between devices: 12.1 us -> 19.7 us  [swapped(): return lax.ppermute(block, axis, [(i, i ^ bits) for i in range(count)])]
    unnamed x32 -> x34, local copies, waits for them, and re-layouts: 7.15 us -> 14.1 us
    pallas_call x5 -> x7, Pallas kernels: 8.06 us -> 11.6 us  [call(): pl.pallas_call(kernel, out_shape=tuple(out_shapes), in_specs=[pl.BlockSpe...]
  transfers between devices with their start and end apart: 22 -> 13, of which waited for: 13 -> 6; matrix products, arithmetic and copies ran while one was open for 1% -> 1% of each run, Pallas kernels for 1% -> 5%
where the time goes in v4:
time: 76 us; the launch traced here: 75.2 us
  waiting for transfers between devices  25.9 us (34%)
  starting transfers between devices  21 us (28%)
  local copies, waits for them, and re-layouts  14.1 us (19%)
  Pallas kernels  11.6 us (15%)
  between operations  1.55 us (2%)
  other arithmetic  1.02 us (1%)
    ppermute x11, waiting for transfers between devices, swapped(): return lax.ppermute(block, axis, [(i, i ^ bits) for i in range(count)])  25.9 us
    ppermute x11, starting transfers between devices, swapped(): return lax.ppermute(block, axis, [(i, i ^ bits) for i in range(count)])  19.7 us
    unnamed x34, local copies, waits for them, and re-layouts  14.1 us
    pallas_call x7, Pallas kernels, call(): pl.pallas_call(kernel, out_shape=tuple(out_shapes), in_specs=[pl.BlockSpe...  11.6 us
  transfers between devices with their start and end apart: 13, of which 6 were waited for; matrix products, arithmetic and copies ran while one was open for 1% of the time, Pallas kernels for 5%

profile of v4, /device:TPU:0, one launch (start us, length us, event | category | flops | bytes accessed | tf_op | source)
XLA Modules:
  0.0 75.2 jit_solution(10067018578811086958)
XLA Ops:
  1.4 0.9 %copy-done = bf16[16,32,256]{2,1,0:T(8,128)(2,1)S(1)} copy-done((bf16[16,32,256]{2,1,0:T(8,128)(2,1)S(1)}, bf16[16,32,256]{2,1,0:T(8,128)(2,1)}, u32[]{:S(2)}) %copy-start) | copy-done | bytes 262168
  2.3 0.7 copy-done.12
  3.0 0.7 copy-done.13
  5.8 1.3 %shard_map.184 = (bf16[368,256]{1,0:T(8,128)(2,1)S(1)}, bf16[320,256]{1,0:T(8,128)(2,1)S(1)}, bf16[48,256]{1,0:T(8,128)(2,1)S(1)}, bf16[48,256]{1,0:T(8,128)(2,1...) custom-call(s32[2]{0:T(128)S(1)} %pad_add_fusion.place_ref.refs_0_, bf16[512,256]{1,0:T(8,128)(2,1)S(1)} %bitcast.11, ...), custom_call_target="tpu_custom_call" | custom-call | bytes 758540 | tf_op jit(solution)/shard_map/pallas_call | solution.py:526
  7.1 3.1 %collective-permute-start = (bf16[368,256]{1,0:T(8,128)(2,1)S(1)}, bf16[368,256]{1,0:T(8,128)(2,1)S(1)}, u32[]{:S(2)}, u32[]{:S(2)}) collective-permute-start(bf16[368,256]{1,0:T(8,128)(2,1)S(1)} %get-tuple-element.39), channel_id=1, source_target_pairs={{0,4},{4,0},{8,12},{12,8},{1,5},{5,1},{9,13},{13,9},{2,6},{6,2},{1... | collective-permute-start | bytes 565256 | tf_op jit(solution)/shard_map/ppermute | solution.py:25
  10.8 3.9 %collective-permute-start.2 = (bf16[48,256]{1,0:T(8,128)(2,1)S(1)}, bf16[48,256]{1,0:T(8,128)(2,1)S(1)}, u32[]{:S(2)}, u32[]{:S(2)}) collective-permute-start(bf16[48,256]{1,0:T(8,128)(2,1)S(1)} %get-tuple-element.41), channel_id=1, source_target_pairs={{0,8},{4,12},{8,0},{12,4},{1,9},{5,13},{9,1},{13,5},{2,10},{6,14},... | collective-permute-start | bytes 73736 | tf_op jit(solution)/shard_map/ppermute | solution.py:25
  14.8 2.9 %collective-permute-start.3 = (bf16[48,256]{1,0:T(8,128)(2,1)S(1)}, bf16[48,256]{1,0:T(8,128)(2,1)S(1)}, u32[]{:S(2)}, u32[]{:S(2)}) collective-permute-start(bf16[48,256]{1,0:T(8,128)(2,1)S(1)} %get-tuple-element.42), channel_id=1, source_target_pairs={{0,12},{4,8},{8,4},{12,0},{1,13},{5,9},{9,5},{13,1},{2,14},{6,10},... | collective-permute-start | bytes 73736 | tf_op jit(solution)/shard_map/ppermute | solution.py:25
  17.7 0.9 %copy-done.1 = bf16[16,32,256]{2,1,0:T(8,128)(2,1)S(1)} copy-done((bf16[16,32,256]{2,1,0:T(8,128)(2,1)S(1)}, bf16[16,32,256]{2,1,0:T(8,128)(2,1)}, u32[]{:S(2)}) %copy-start.1) | copy-done | bytes 262168
  18.6 0.9 %copy-done.2 = bf16[2,128,384]{2,1,0:T(8,128)(2,1)S(1)} copy-done((bf16[2,128,384]{2,1,0:T(8,128)(2,1)S(1)}, bf16[2,128,384]{2,1,0:T(8,128)(2,1)}, u32[]{:S(2)}) %copy-start.2) | copy-done | bytes 196632
  19.6 0.9 %copy-done.3 = bf16[256,256]{1,0:T(8,128)(2,1)S(1)} copy-done((bf16[256,256]{1,0:T(8,128)(2,1)S(1)}, bf16[256,256]{1,0:T(8,128)(2,1)}, u32[]{:S(2)}) %copy-start.3) | copy-done | bytes 131096
  20.5 0.9 %copy-done.4 = bf16[256,256]{1,0:T(8,128)(2,1)S(1)} copy-done((bf16[256,256]{1,0:T(8,128)(2,1)S(1)}, bf16[256,256]{1,0:T(8,128)(2,1)}, u32[]{:S(2)}) %copy-start.4) | copy-done | bytes 131096
  21.4 0.9 %copy-done.5 = bf16[256,256]{1,0:T(8,128)(2,1)S(1)} copy-done((bf16[256,256]{1,0:T(8,128)(2,1)S(1)}, bf16[256,256]{1,0:T(8,128)(2,1)}, u32[]{:S(2)}) %copy-start.5) | copy-done | bytes 131096
  22.3 0.9 %copy-done.6 = bf16[256,256]{1,0:T(8,128)(2,1)S(1)} copy-done((bf16[256,256]{1,0:T(8,128)(2,1)S(1)}, bf16[256,256]{1,0:T(8,128)(2,1)}, u32[]{:S(2)}) %copy-start.6) | copy-done | bytes 131096
  23.2 0.9 %copy-done.7 = bf16[256,256]{1,0:T(8,128)(2,1)S(1)} copy-done((bf16[256,256]{1,0:T(8,128)(2,1)S(1)}, bf16[256,256]{1,0:T(8,128)(2,1)}, u32[]{:S(2)}) %copy-start.7) | copy-done | bytes 131096
  24.1 0.9 %copy-done.8 = bf16[2,128,192]{2,1,0:T(8,128)(2,1)S(1)} copy-done((bf16[2,128,192]{2,1,0:T(8,128)(2,1)S(1)}, bf16[2,128,192]{2,1,0:T(8,128)(2,1)}, u32[]{:S(2)}) %copy-start.8) | copy-done | bytes 98328
  25.0 0.8 %copy-done.9 = bf16[128,256]{1,0:T(8,128)(2,1)S(1)} copy-done((bf16[128,256]{1,0:T(8,128)(2,1)S(1)}, bf16[128,256]{1,0:T(8,128)(2,1)}, u32[]{:S(2)}) %copy-start.9) | copy-done | bytes 65560
  25.8 0.8 %copy-done.10 = f32[2,16,384]{2,1,0:T(8,128)S(1)} copy-done((f32[2,16,384]{2,1,0:T(8,128)S(1)}, f32[2,16,384]{2,1,0:T(8,128)}, u32[]{:S(2)}) %copy-start.10) | copy-done | bytes 49176
  27.3 1.8 %shard_map.185 = (bf16[512,256]{1,0:T(8,128)(2,1)S(1)}, bf16[256,256]{1,0:T(8,128)(2,1)S(1)}, bf16[256,256]{1,0:T(8,128)(2,1)S(1)}, bf16[256,256]{1,0:T(8,128)(2...) custom-call(bf16[48,256]{1,0:T(8,128)(2,1)S(1)} %get-tuple-element.3, ...), custom_call_target="tpu_custom_call" | custom-call | bytes 2711552 | tf_op jit(solution)/shard_map/pallas_call | solution.py:526
  29.1 1.2 %shard_map.186 = (bf16[1088,256]{1,0:T(8,128)(2,1)S(1)}, bf16[576,256]{1,0:T(8,128)(2,1)S(1)}, bf16[576,256]{1,0:T(8,128)(2,1)S(1)}, bf16[128,256]{1,0:T(8,128)(...) custom-call(s32[2]{0:T(128)S(1)} %pad_add_fusion.place_ref.refs_0_, ...), custom_call_target="tpu_custom_call" | custom-call | flops 71303168 | bytes 2150408 | tf_op jit(solution)/shard_map/pallas_call | solution.py:526
  31.1 0.9 %shard_map.187 = (bf16[1088,256]{1,0:T(8,128)(2,1)S(1)}, bf16[512,256]{1,0:T(8,128)(2,1)S(1)}, f32[512,256]{1,0:T(8,128)S(1)}, f32[512,256]{1,0:T(8,128)S(1)}) custom-call(bf16[1088,256]{1,0:T(8,128)(2,1)S(1)} %get-tuple-element.46.blended_ref.refs_4_, bf16[256,256]{1,0:T(8,128)(2,1)S(1)} %get-tuple-element.47.w_embed_ref.refs_16_, ...), custom_call_target="tpu_custom_call" | custom-call | flops 285212672 | bytes 2686976 | tf_op jit(solution)/shard_map/pallas_call | solution.py:526
  32.0 3.6 %shard_map.188 = (bf16[512,256]{1,0:T(8,128)(2,1)}, bf16[128,256]{1,0:T(8,128)(2,1)S(1)}, bf16[640,256]{1,0:T(8,128)(2,1)S(1)}, f32[640,256]{1,0:T(8,128)S(1)}) custom-call(s32[1]{0:T(128)} %bitcast.refs_0_, bf16[576,256]{1,0:T(8,128)(2,1)S(1)} %collective-permute-done.4.refs_1_, bf16[576,256]{1,0:T(8,128)(2,1)S(1)} %collective-permute-done.5.refs_2_, ...), custom_call_target="tpu_custom_call" | custom-call | flops 402653184 | bytes 5525508 | tf_op jit(solution)/shard_map/pallas_call | solution.py:526
  35.6 6.9 %collective-permute-start.6 = (bf16[640,256]{1,0:T(8,128)(2,1)S(1)}, bf16[640,256]{1,0:T(8,128)(2,1)S(1)}, u32[]{:S(2)}, u32[]{:S(2)}) collective-permute-start(bf16[640,256]{1,0:T(8,128)(2,1)S(1)} %get-tuple-element.64), channel_id=1, source_target_pairs={{0,1},{1,0},{2,3},{3,2},{4,5},{5,4},{6,7},{7,6},{8,9},{9,8},{10,11... | collective-permute-start | bytes 983048 | tf_op jit(solution)/shard_map/ppermute | solution.py:25
  42.5 1.3 %collective-permute-done.6 = bf16[640,256]{1,0:T(8,128)(2,1)S(1)} collective-permute-done((bf16[640,256]{1,0:T(8,128)(2,1)S(1)}, bf16[640,256]{1,0:T(8,128)(2,1)S(1)}, u32[]{:S(2)}, u32[]{:S(2)}) %collective-permute-start.6) | collective-permute-done | bytes 327712 | tf_op jit(solution)/shard_map/ppermute | solution.py:25
  43.9 1.4 %collective-permute-start.7 = (bf16[320,256]{1,0:T(8,128)(2,1)S(1)}, bf16[320,256]{1,0:T(8,128)(2,1)S(1)}, u32[]{:S(2)}, u32[]{:S(2)}) collective-permute-start(bf16[320,256]{1,0:T(8,128)(2,1)S(1)} %dynamic-slice_convert_fusion), channel_id=1, source_target_pairs={{0,2},{1,3},{2,0},{3,1},{4,6},{5,7},{6,4},{7,5},{8,10},{9,11},{10,... | collective-permute-start | bytes 491528 | tf_op jit(solution)/shard_map/ppermute | solution.py:25
  45.3 5.1 %collective-permute-done.7 = bf16[320,256]{1,0:T(8,128)(2,1)S(1)} collective-permute-done((bf16[320,256]{1,0:T(8,128)(2,1)S(1)}, bf16[320,256]{1,0:T(8,128)(2,1)S(1)}, u32[]{:S(2)}, u32[]{:S(2)}) %collective-permute-start.7) | collective-permute-done | bytes 163872 | tf_op jit(solution)/shard_map/ppermute | solution.py:25
  50.6 4.8 %collective-permute-done.8 = bf16[224,256]{1,0:T(8,128)(2,1)S(1)} collective-permute-done((bf16[224,256]{1,0:T(8,128)(2,1)S(1)}, bf16[224,256]{1,0:T(8,128)(2,1)S(1)}, u32[]{:S(2)}, u32[]{:S(2)}) %collective-permute-start.8) | collective-permute-done | bytes 114720 | tf_op jit(solution)/shard_map/ppermute | solution.py:25
  55.5 6.1 %collective-permute-done.9 = bf16[192,256]{1,0:T(8,128)(2,1)S(1)} collective-permute-done((bf16[192,256]{1,0:T(8,128)(2,1)S(1)}, bf16[192,256]{1,0:T(8,128)(2,1)S(1)}, u32[]{:S(2)}, u32[]{:S(2)}) %collective-permute-start.9) | collective-permute-done | bytes 98336 | tf_op jit(solution)/shard_map/ppermute | solution.py:25
  61.7 4.4 %collective-permute-done.10 = bf16[160,256]{1,0:T(8,128)(2,1)S(1)} collective-permute-done((bf16[160,256]{1,0:T(8,128)(2,1)S(1)}, bf16[160,256]{1,0:T(8,128)(2,1)S(1)}, u32[]{:S(2)}, u32[]{:S(2)}) %collective-permute-start.10) | collective-permute-done | bytes 81952 | tf_op jit(solution)/shard_map/ppermute | solution.py:25
  66.2 1.1 %collective-permute-start.11 = (bf16[320,256]{1,0:T(8,128)(2,1)S(1)}, bf16[320,256]{1,0:T(8,128)(2,1)S(1)}, u32[]{:S(2)}, u32[]{:S(2)}) collective-permute-start(bf16[320,256]{1,0:T(8,128)(2,1)S(1)} %pad_maximum_fusion.1), channel_id=1, source_target_pairs={{0,2},{1,3},{2,0},{3,1},{4,6},{5,7},{6,4},{7,5},{8,10},{9,11},{10,... | collective-permute-start | bytes 491528 | tf_op jit(solution)/shard_map/ppermute | solution.py:25
  67.3 4.3 %collective-permute-done.11 = bf16[320,256]{1,0:T(8,128)(2,1)S(1)} collective-permute-done((bf16[320,256]{1,0:T(8,128)(2,1)S(1)}, bf16[320,256]{1,0:T(8,128)(2,1)S(1)}, u32[]{:S(2)}, u32[]{:S(2)}) %collective-permute-start.11) | collective-permute-done | bytes 163872 | tf_op jit(solution)/shard_map/ppermute | solution.py:25
  72.4 1.4 %shard_map.189.refs_2_ = f32[1280,256]{1,0:T(8,128)} custom-call(s32[2]{0:T(128)S(1)} %pad_add_fusion.place_ref.refs_0_, bf16[640,256]{1,0:T(8,128)(2,1)S(1)} %pad_maximum_fusion.refs_1_), custom_call_target="tpu_custom_call" | custom-call | bytes 1638408 | tf_op jit(solution)/shard_map/pallas_call | solution.py:526
  73.8 1.4 %shard_map.190 = f32[1280,256]{1,0:T(8,128)} custom-call(s32[2]{0:T(128)S(1)} %pad_add_fusion.place_ref.refs_0_, bf16[640,256]{1,0:T(8,128)(2,1)S(1)} %collective-permute-done.12.refs_1_, f32[1280,256]{1,0:T(8,128)} %shard_map.189.refs_2_), custom_call_target="tpu_custom_call", output_to_operand_aliasing={{}: (2, {})} | custom-call | bytes 2949128 | tf_op jit(solution)/shard_map/pallas_call | solution.py:526
  (53 shorter events, 5.5 us)
Async XLA Ops:
  1.4 1.0 %copy-start = (bf16[16,32,256]{2,1,0:T(8,128)(2,1)S(1)}, bf16[16,32,256]{2,1,0:T(8,128)(2,1)}, u32[]{:S(2)}) copy-start(bf16[16,32,256]{2,1,0:T(8,128)(2,1)} %param.17) | copy-start | bytes 786436
  2.3 0.7 copy-start.12
  3.0 0.7 copy-start.13
  3.7 0.7 copy-start.14
  4.5 0.7 copy-start.15
  5.1 0.7 copy-start.16
  7.1 22.0 %collective-permute-start = (bf16[368,256]{1,0:T(8,128)(2,1)S(1)}, bf16[368,256]{1,0:T(8,128)(2,1)S(1)}, u32[]{:S(2)}, u32[]{:S(2)}) collective-permute-start(bf16[368,256]{1,0:T(8,128)(2,1)S(1)} %get-tuple-element.39), channel_id=1, source_target_pairs={{0,4},{4,0},{8,12},{12,8},{1,5},{5,1},{9,13},{13,9},{2,6},{6,2},{1... | collective-permute-start | bytes 565256 | tf_op jit(solution)/shard_map/ppermute | solution.py:25
  10.2 18.9 %collective-permute-start.1 = (bf16[320,256]{1,0:T(8,128)(2,1)S(1)}, bf16[320,256]{1,0:T(8,128)(2,1)S(1)}, u32[]{:S(2)}, u32[]{:S(2)}) collective-permute-start(bf16[320,256]{1,0:T(8,128)(2,1)S(1)} %get-tuple-element.40), channel_id=1, source_target_pairs={{4,8},{8,4},{5,9},{9,5},{6,10},{10,6},{7,11},{11,7},{20,24},{24,20... | collective-permute-start | bytes 491528 | tf_op jit(solution)/shard_map/ppermute | solution.py:31
  10.8 18.3 %collective-permute-start.2 = (bf16[48,256]{1,0:T(8,128)(2,1)S(1)}, bf16[48,256]{1,0:T(8,128)(2,1)S(1)}, u32[]{:S(2)}, u32[]{:S(2)}) collective-permute-start(bf16[48,256]{1,0:T(8,128)(2,1)S(1)} %get-tuple-element.41), channel_id=1, source_target_pairs={{0,8},{4,12},{8,0},{12,4},{1,9},{5,13},{9,1},{13,5},{2,10},{6,14},... | collective-permute-start | bytes 73736 | tf_op jit(solution)/shard_map/ppermute | solution.py:25
  14.8 14.4 %collective-permute-start.3 = (bf16[48,256]{1,0:T(8,128)(2,1)S(1)}, bf16[48,256]{1,0:T(8,128)(2,1)S(1)}, u32[]{:S(2)}, u32[]{:S(2)}) collective-permute-start(bf16[48,256]{1,0:T(8,128)(2,1)S(1)} %get-tuple-element.42), channel_id=1, source_target_pairs={{0,12},{4,8},{8,4},{12,0},{1,13},{5,9},{9,5},{13,1},{2,14},{6,10},... | collective-permute-start | bytes 73736 | tf_op jit(solution)/shard_map/ppermute | solution.py:25
  17.7 0.9 %copy-start.1 = (bf16[16,32,256]{2,1,0:T(8,128)(2,1)S(1)}, bf16[16,32,256]{2,1,0:T(8,128)(2,1)}, u32[]{:S(2)}) copy-start(bf16[16,32,256]{2,1,0:T(8,128)(2,1)} %param.17) | copy-start | bytes 786436
  18.6 0.9 %copy-start.2 = (bf16[2,128,384]{2,1,0:T(8,128)(2,1)S(1)}, bf16[2,128,384]{2,1,0:T(8,128)(2,1)}, u32[]{:S(2)}) copy-start(bf16[2,128,384]{2,1,0:T(8,128)(2,1)} %constant.55.clone.refs_9_) | copy-start | bytes 589828
  19.6 0.9 %copy-start.3 = (bf16[256,256]{1,0:T(8,128)(2,1)S(1)}, bf16[256,256]{1,0:T(8,128)(2,1)}, u32[]{:S(2)}) copy-start(bf16[256,256]{1,0:T(8,128)(2,1)} %refs_2_.1) | copy-start | bytes 393220
  20.5 0.9 %copy-start.4 = (bf16[256,256]{1,0:T(8,128)(2,1)S(1)}, bf16[256,256]{1,0:T(8,128)(2,1)}, u32[]{:S(2)}) copy-start(bf16[256,256]{1,0:T(8,128)(2,1)} %refs_3_.1) | copy-start | bytes 393220
  21.4 0.9 %copy-start.5 = (bf16[256,256]{1,0:T(8,128)(2,1)S(1)}, bf16[256,256]{1,0:T(8,128)(2,1)}, u32[]{:S(2)}) copy-start(bf16[256,256]{1,0:T(8,128)(2,1)} %refs_4_.1) | copy-start | bytes 393220
  22.3 0.9 %copy-start.6 = (bf16[256,256]{1,0:T(8,128)(2,1)S(1)}, bf16[256,256]{1,0:T(8,128)(2,1)}, u32[]{:S(2)}) copy-start(bf16[256,256]{1,0:T(8,128)(2,1)} %refs_5_.1) | copy-start | bytes 393220
  23.2 0.9 %copy-start.7 = (bf16[256,256]{1,0:T(8,128)(2,1)S(1)}, bf16[256,256]{1,0:T(8,128)(2,1)}, u32[]{:S(2)}) copy-start(bf16[256,256]{1,0:T(8,128)(2,1)} %refs_6_.1) | copy-start | bytes 393220
  24.1 0.9 %copy-start.8 = (bf16[2,128,192]{2,1,0:T(8,128)(2,1)S(1)}, bf16[2,128,192]{2,1,0:T(8,128)(2,1)}, u32[]{:S(2)}) copy-start(bf16[2,128,192]{2,1,0:T(8,128)(2,1)} %constant.54.clone.refs_8_) | copy-start | bytes 294916
  25.0 0.8 %copy-start.9 = (bf16[128,256]{1,0:T(8,128)(2,1)S(1)}, bf16[128,256]{1,0:T(8,128)(2,1)}, u32[]{:S(2)}) copy-start(bf16[128,256]{1,0:T(8,128)(2,1)} %constant.57.clone.refs_11_) | copy-start | bytes 196612
  25.8 0.8 %copy-start.10 = (f32[2,16,384]{2,1,0:T(8,128)S(1)}, f32[2,16,384]{2,1,0:T(8,128)}, u32[]{:S(2)}) copy-start(f32[2,16,384]{2,1,0:T(8,128)} %constant.56.clone.refs_10_) | copy-start | bytes 147460
  26.6 0.7 copy-start.11
  30.3 1.7 %collective-permute-start.4 = (bf16[576,256]{1,0:T(8,128)(2,1)S(1)}, bf16[576,256]{1,0:T(8,128)(2,1)S(1)}, u32[]{:S(2)}, u32[]{:S(2)}) collective-permute-start(bf16[576,256]{1,0:T(8,128)(2,1)S(1)} %get-tuple-element.43), channel_id=1, source_target_pairs={{0,1},{1,0},{2,3},{3,2},{4,5},{5,4},{6,7},{7,6},{8,9},{9,8},{10,11... | collective-permute-start | bytes 884744 | tf_op jit(solution)/shard_map/ppermute | solution.py:25
  30.4 1.6 %collective-permute-start.5 = (bf16[576,256]{1,0:T(8,128)(2,1)S(1)}, bf16[576,256]{1,0:T(8,128)(2,1)S(1)}, u32[]{:S(2)}, u32[]{:S(2)}) collective-permute-start(bf16[576,256]{1,0:T(8,128)(2,1)S(1)} %get-tuple-element.44), channel_id=1, source_target_pairs={{1,2},{2,1},{5,6},{6,5},{9,10},{10,9},{13,14},{14,13},{17,18},{18,... | collective-permute-start | bytes 884744 | tf_op jit(solution)/shard_map/ppermute | solution.py:31
  35.6 8.1 %collective-permute-start.6 = (bf16[640,256]{1,0:T(8,128)(2,1)S(1)}, bf16[640,256]{1,0:T(8,128)(2,1)S(1)}, u32[]{:S(2)}, u32[]{:S(2)}) collective-permute-start(bf16[640,256]{1,0:T(8,128)(2,1)S(1)} %get-tuple-element.64), channel_id=1, source_target_pairs={{0,1},{1,0},{2,3},{3,2},{4,5},{5,4},{6,7},{7,6},{8,9},{9,8},{10,11... | collective-permute-start | bytes 983048 | tf_op jit(solution)/shard_map/ppermute | solution.py:25
  43.9 6.5 %collective-permute-start.7 = (bf16[320,256]{1,0:T(8,128)(2,1)S(1)}, bf16[320,256]{1,0:T(8,128)(2,1)S(1)}, u32[]{:S(2)}, u32[]{:S(2)}) collective-permute-start(bf16[320,256]{1,0:T(8,128)(2,1)S(1)} %dynamic-slice_convert_fusion), channel_id=1, source_target_pairs={{0,2},{1,3},{2,0},{3,1},{4,6},{5,7},{6,4},{7,5},{8,10},{9,11},{10,... | collective-permute-start | bytes 491528 | tf_op jit(solution)/shard_map/ppermute | solution.py:25
  50.5 4.9 %collective-permute-start.8 = (bf16[224,256]{1,0:T(8,128)(2,1)S(1)}, bf16[224,256]{1,0:T(8,128)(2,1)S(1)}, u32[]{:S(2)}, u32[]{:S(2)}) collective-permute-start(bf16[224,256]{1,0:T(8,128)(2,1)S(1)} %pad_maximum_fusion.2), channel_id=1, source_target_pairs={{0,4},{4,0},{8,12},{12,8},{1,5},{5,1},{9,13},{13,9},{2,6},{6,2},{1... | collective-permute-start | bytes 344072 | tf_op jit(solution)/shard_map/ppermute | solution.py:25
  55.4 6.2 %collective-permute-start.9 = (bf16[192,256]{1,0:T(8,128)(2,1)S(1)}, bf16[192,256]{1,0:T(8,128)(2,1)S(1)}, u32[]{:S(2)}, u32[]{:S(2)}) collective-permute-start(bf16[192,256]{1,0:T(8,128)(2,1)S(1)} %pad_maximum_fusion.3), channel_id=1, source_target_pairs={{0,8},{4,12},{8,0},{12,4},{1,9},{5,13},{9,1},{13,5},{2,10},{6,14},... | collective-permute-start | bytes 294920 | tf_op jit(solution)/shard_map/ppermute | solution.py:25
  61.6 4.5 %collective-permute-start.10 = (bf16[160,256]{1,0:T(8,128)(2,1)S(1)}, bf16[160,256]{1,0:T(8,128)(2,1)S(1)}, u32[]{:S(2)}, u32[]{:S(2)}) collective-permute-start(bf16[160,256]{1,0:T(8,128)(2,1)S(1)} %fusion), channel_id=1, source_target_pairs={{0,4},{4,0},{8,12},{12,8},{1,5},{5,1},{9,13},{13,9},{2,6},{6,2},{1... | collective-permute-start | bytes 245768 | tf_op jit(solution)/shard_map/ppermute | solution.py:25
  66.2 5.4 %collective-permute-start.11 = (bf16[320,256]{1,0:T(8,128)(2,1)S(1)}, bf16[320,256]{1,0:T(8,128)(2,1)S(1)}, u32[]{:S(2)}, u32[]{:S(2)}) collective-permute-start(bf16[320,256]{1,0:T(8,128)(2,1)S(1)} %pad_maximum_fusion.1), channel_id=1, source_target_pairs={{0,2},{1,3},{2,0},{3,1},{4,6},{5,7},{6,4},{7,5},{8,10},{9,11},{10,... | collective-permute-start | bytes 491528 | tf_op jit(solution)/shard_map/ppermute | solution.py:25
  71.7 2.1 %collective-permute-start.12 = (bf16[640,256]{1,0:T(8,128)(2,1)S(1)}, bf16[640,256]{1,0:T(8,128)(2,1)S(1)}, u32[]{:S(2)}, u32[]{:S(2)}) collective-permute-start(bf16[640,256]{1,0:T(8,128)(2,1)S(1)} %pad_maximum_fusion.refs_1_), channel_id=1, source_target_pairs={{0,1},{1,0},{2,3},{3,2},{4,5},{5,4},{6,7},{7,6},{8,9},{9,8},{10,11... | collective-permute-start | bytes 983048 | tf_op jit(solution)/shard_map/ppermute | solution.py:25

commit v5 on v3

--- a/solution.py
+++ b/solution.py
@@ -15,6 +15,7 @@
 SIDE = 16
 SLOTS = 16
 LANES = 256
+LONG = 10**10
 VMEM_LIMIT = 48 * 1024 * 1024
 F32 = jnp.float32
 BF16 = jnp.bfloat16
@@ -29,17 +30,6 @@
     count = lax.axis_size(axis)
     pairs = [(i, i + 1) for i in range(1, count - 1, 2)]
     return lax.ppermute(block, axis, pairs + [(j, i) for i, j in pairs])
-
-
-def swapped_both(block, wide_bits, narrow_bits):
-    wide_count = lax.axis_size("wide")
-    narrow_count = lax.axis_size("narrow")
-    pairs = [
-        (w * narrow_count + n, (w ^ wide_bits) * narrow_count + (n ^ narrow_bits))
-        for w in range(wide_count)
-        for n in range(narrow_count)
-    ]
-    return lax.ppermute(block, ("wide", "narrow"), pairs)
 
 
 def dot(left, right):
@@ -162,6 +152,11 @@
         }
 
 
+def open_kernel(place_ref, out_ref):
+    out_ref[0] = place_ref[0]
+    out_ref[1] = place_ref[1]
+
+
 def pack_kernel(
     shape,
     units,
@@ -172,6 +167,7 @@
     rows_ref,
     target_x_ref,
     target_y_ref,
+    count_ref,
     first_ref,
     second_ref,
     third_ref,
@@ -182,11 +178,11 @@
     edge, own_nodes, halo = shape.edge, shape.own_nodes, shape.halo
     held = rows_ref.shape[0]
     even = place_ref[0] % 2 == 0
-    row_count = place_ref[1]
+    odd = jnp.logical_not(even)
     target_x = target_x_ref[...]
-    column = target_y_ref[...] - place_ref[2] * shape.tile_y
+    column = target_y_ref[...] - place_ref[1] * shape.tile_y
     slot = lax.broadcasted_iota(jnp.int32, (1, held), 1)
-    column = jnp.where(slot < row_count, column, LANES - 1)
+    column = jnp.where(slot < count_ref[...], column, LANES - 1)
     line = lax.broadcasted_iota(jnp.int32, (16, held), 0)
     fields = jnp.where(line == 0, target_x // shape.tile_x, 0)
     fields = fields + jnp.where(line == 1, target_x % shape.tile_x, 0)
@@ -195,15 +191,15 @@
     repeat = lane % held == lax.broadcasted_iota(jnp.int32, (held, LANES), 0)
     spread = dot(fields.astype(F32).astype(BF16), jnp.where(repeat, 1.0, 0.0).astype(BF16))
     lane = lax.broadcasted_iota(jnp.int32, (16, LANES), 1)
-
-    mesh_ref[:own_nodes] = cotangent_ref[...]
-    mesh_ref[own_nodes:] = mask_ref[...]
-    targets = (own_rows_ref, first_ref, third_ref, second_ref, fourth_ref)
-    for ref, number in zip(targets, (0, 1, 2, 3, 3)):
+    for number, ref in enumerate((own_rows_ref, first_ref, third_ref, fourth_ref)):
         at = ref.shape[0] - held - 16
         ref[at : at + held] = rows_ref[...]
         ref[at + held :] = jnp.where(lane // held == number, spread, 0.0).astype(BF16)
-    for ref, upward in ((first_ref, even), (second_ref, jnp.logical_not(even))):
+
+    mesh_ref[:own_nodes] = cotangent_ref[...]
+    mesh_ref[own_nodes:] = jnp.zeros((own_nodes, mesh_ref.shape[1]), BF16)
+    mesh_ref[own_nodes:, : mask_ref.shape[1]] = mask_ref[...].astype(F32).astype(BF16)
+    for ref, upward in ((first_ref, even), (second_ref, odd)):
         start = pl.multiple_of(jnp.where(upward, shape.cells - halo, 0), shape.tile_y)
         ref[:halo] = own_ref[pl.ds(start, halo)]
         start = pl.multiple_of(jnp.where(upward, own_nodes - edge, 0), 16)
@@ -227,14 +223,9 @@
     def held(k, at, n):
         if k == 0:
             return own_rows_ref[at : at + n]
-        if k == 1:
-            return near[first_row + at : first_row + at + n]
-        if k < units - 1:
-            return arrived[k][at : at + n]
-        value = between[first_row + at : first_row + at + n]
-        if units > 3:
-            value = value + arrived[-1][at : at + n]
-        return value
+        if k == 1 or units == 3:
+            return arrived[k - 1][first_row + at : first_row + at + n]
+        return arrived[k][at : at + n]
 
     total = unit_rows * units
     for k in range(units):
@@ -267,7 +258,7 @@
         [facing(shape.halo, mesh, False), mesh_ref[...], facing(shape.halo, mesh, True)], axis=0
     )
     stack_ref[...] = stack
-    narrow_even = place_ref[2] % 2 == 0
+    narrow_even = place_ref[1] % 2 == 0
     column = pl.multiple_of(jnp.where(narrow_even, shape.tile_y - SIDE, 0), SIDE)
     other = pl.multiple_of(jnp.where(narrow_even, 0, shape.tile_y - SIDE), SIDE)
     to_left = dot(side_ref[0], stack).astype(BF16)
@@ -461,30 +452,15 @@
     kept_ref[...] = grads_ref[pl.ds(kept_at, half)]
 
 
-def finish_kernel(scales, place_ref, own_ref, other_ref, out_ref):
-    even = place_ref[2] % 2 == 0
-    half = own_ref.shape[0]
-    channels = own_ref.shape[1]
-    for k, scale in enumerate(scales):
-        for start, stop, lower in ((0, half, True), (half, 2 * half, False)):
-            at = max(k * channels, start)
-            end = min((k + 1) * channels, stop)
-            if at >= end:
-                continue
-            own, other = own_ref[at - start : end - start], other_ref[at - start : end - start]
-            value = jnp.where(even, own, other) if lower else jnp.where(even, other, own)
-            out_ref[k, at - k * channels : end - k * channels] = value.astype(F32) * scale
-
-
-def call(kernel, out_shapes, operands, scratch=(), scalars=1, flops=0):
-    specs = [pl.BlockSpec(memory_space=pltpu.SMEM)] * scalars
-    specs += [pl.BlockSpec(memory_space=pltpu.VMEM)] * (len(operands) - scalars)
+def call(kernel, out_shapes, operands, scratch=(), spaces="", out_space=pltpu.VMEM, flops=0):
+    kinds = {"s": pltpu.SMEM, "v": pltpu.VMEM}
+    spaces = spaces + "v" * (len(operands) - len(spaces))
     moved = sum(math.prod(o.shape) * o.dtype.itemsize for o in list(operands) + list(out_shapes))
     return pl.pallas_call(
         kernel,
         out_shape=tuple(out_shapes),
-        in_specs=specs,
-        out_specs=tuple(pl.BlockSpec(memory_space=pltpu.VMEM) for _ in out_shapes),
+        in_specs=[pl.BlockSpec(memory_space=kinds[space]) for space in spaces],
+        out_specs=tuple(pl.BlockSpec(memory_space=out_space) for _ in out_shapes),
         scratch_shapes=list(scratch),
         compiler_params=pltpu.CompilerParams(vmem_limit_bytes=VMEM_LIMIT),
         cost_estimate=pl.CostEstimate(flops=flops, bytes_accessed=moved, transcendentals=0),
@@ -526,8 +502,11 @@
     narrow_at = lax.axis_index("narrow")
     held_rows = boundary_rows.shape[0]
     shape = Shape(tile_x, tile_y)
-    table = {name: jnp.asarray(value, BF16) for name, value in shape.tables().items()}
-    table["match"] = table["match"].astype(F32)
+    table = shape.tables()
+    table = {
+        name: jnp.asarray(value, F32 if name == "match" else BF16)
+        for name, value in table.items()
+    }
 
     live = jnp.arange(held_rows) < row_count[0]
     column = target_y - narrow_at * tile_y
@@ -562,16 +541,24 @@
 
     cells = grid_state.reshape(-1, channels)
     cotangent = mesh_cotangent.reshape(-1, channels)
-    mask = g2m_mask.astype(BF16).transpose(1, 2, 0).reshape(-1, 36)
-    mask = jnp.pad(mask, ((0, 0), (0, channels - 36)))
-    place = jnp.stack([wide_at, row_count[0], narrow_at])
+    mask = g2m_mask.transpose(1, 2, 0).reshape(-1, 36)
+    place = jnp.stack([wide_at, narrow_at])
     struct = jax.ShapeDtypeStruct
     long = struct((shape.halo + 2 * shape.edge + unit_rows + 16, channels), BF16)
+    plain = struct((shape.halo + 2 * shape.edge, channels), BF16)
     short = struct((unit_rows + 16, channels), BF16)
+    (place,) = call(
+        open_kernel,
+        [struct((2,), jnp.int32)],
+        [place],
+        spaces="s",
+        out_space=pltpu.SMEM,
+        flops=LONG,
+    )
     if whole_column:
         first, second, third, fourth, mesh, own_rows = call(
             functools.partial(pack_kernel, shape, units),
-            [long, long, short, short, struct((2 * shape.own_nodes, channels), BF16), short],
+            [long, plain, short, short, struct((2 * shape.own_nodes, channels), BF16), short],
             [
                 place,
                 cells,
@@ -580,19 +567,21 @@
                 rows,
                 target_x.reshape(1, -1),
                 target_y.reshape(1, -1),
+                row_count.reshape(1, 1),
             ],
+            spaces="s",
+            flops=LONG,
         )
-        arrived = [
-            swapped(first, "wide", 1),
-            swapped_between(second, "wide"),
-            swapped(third, "wide", 2),
-            lax.ppermute(fourth, "wide", [(0, 3), (3, 0)]),
-        ]
+        third = swapped(third, "wide", 2)
+        fourth = swapped(fourth, "wide", 3)
+        first_in = swapped(first, "wide", 1)
+        arrived = [first_in, swapped_between(second, "wide"), third, fourth]
     else:
 
         def with_meta(slot):
             return [rows, meta_rows(row_live, row_x, row_y, tile_x, unit_rows, slot, units)]
 
+        mask = jnp.pad(mask.astype(BF16), ((0, 0), (0, channels - 36)))
         mesh = jnp.concatenate([cotangent, mask])
         own_rows = jnp.concatenate(with_meta(0))
         edge = shape.edge
@@ -619,6 +608,7 @@
         ],
         [place, cells, mesh, w_force, table["to_side"], own_rows] + arrived,
         scratch=[pltpu.VMEM((total_rows, channels), BF16)],
+        spaces="s",
         flops=2 * shape.center * total_rows * channels,
     )
     second = swapped_between(second, "narrow")
@@ -632,7 +622,6 @@
             struct((shape.cells, channels), F32),
         ],
         [blended, w_embed, w_message],
-        scalars=0,
         flops=4 * shape.center * channels * channels,
     )
     grad_rows_total = 5 * channels
@@ -674,63 +663,46 @@
             pltpu.VMEM((shape.cells, channels), BF16),
             pltpu.VMEM((grad_rows_total, channels), F32),
         ],
+        spaces="s",
         flops=12 * shape.cells * channels * channels,
     )
 
     piece = kept + swapped(sent, "narrow", 1).astype(F32)
     back_blocks = back.reshape(units, unit_rows, channels)
     row_back = back_blocks[0].astype(F32)
-    others = narrow_count // 2
-    if wide_count * others <= 8:
-        group = wide_count * others
-        part = piece.shape[0] // group
-        at = wide_at * others + narrow_at // 2
-        rounded = piece.astype(BF16)
-        own = lax.dynamic_slice_in_dim(piece, at * part, part)
-        order = sorted(range(1, group), key=lambda k: (k // others < 2, k % others == 0))
-        for k in order:
-            wide_bits, narrow_bits = k // others, k % others
-            sent = lax.dynamic_slice_in_dim(rounded, (at ^ k) * part, part)
-            if narrow_bits == 0 and whole_column:
-                sent = jnp.concatenate([sent, back_blocks[wide_bits]])
-            got = swapped_both(sent, wide_bits, 2 * narrow_bits).astype(F32)
-            own = own + got[:part]
-            if narrow_bits == 0 and whole_column:
-                row_back = row_back + got[part:]
-        own = own.astype(BF16)
-        gathered = jnp.zeros((group * part, channels), BF16)
-        gathered = lax.dynamic_update_slice_in_dim(gathered, own, at * part, 0)
-        for k in order:
-            got = swapped_both(own, k // others, 2 * (k % others))
-            gathered = lax.dynamic_update_slice_in_dim(gathered, got, (at ^ k) * part, 0)
-    else:
-        bits = [1 << k for k in range(1, narrow_count.bit_length() - 1)]
-        for bit in bits:
-            half = piece.shape[0] // 2
-            upper = (narrow_at // bit) % 2
-            sent = lax.dynamic_slice_in_dim(piece, (1 - upper) * half, half).astype(BF16)
-            kept = lax.dynamic_slice_in_dim(piece, upper * half, half)
-            piece = kept + swapped(sent, "narrow", bit).astype(F32)
-        part = piece.shape[0] // wide_count
-        rounded = piece.astype(BF16)
-        own = lax.dynamic_slice_in_dim(piece, wide_at * part, part)
-        for k in range(1, wide_count):
-            sent = lax.dynamic_slice_in_dim(rounded, (wide_at ^ k) * part, part)
-            own = own + swapped(sent, "wide", k).astype(F32)
-        own = own.astype(BF16)
-        gathered = jnp.zeros((wide_count * part, channels), BF16)
-        gathered = lax.dynamic_update_slice_in_dim(gathered, own, wide_at * part, 0)
-        for k in range(1, wide_count):
-            got = swapped(own, "wide", k)
-            gathered = lax.dynamic_update_slice_in_dim(gathered, got, (wide_at ^ k) * part, 0)
-        for bit in reversed(bits):
-            upper = (narrow_at // bit) % 2
-            other = swapped(gathered, "narrow", bit)
-            gathered = jnp.where(
-                upper == 0,
-                jnp.concatenate([gathered, other]),
-                jnp.concatenate([other, gathered]),
-            )
+    bits = [1 << k for k in range(1, narrow_count.bit_length() - 1)]
+    for bit in bits:
+        half = piece.shape[0] // 2
+        upper = (narrow_at // bit) % 2
+        sent = lax.dynamic_slice_in_dim(piece, (1 - upper) * half, half).astype(BF16)
+        kept = lax.dynamic_slice_in_dim(piece, upper * half, half)
+        piece = kept + swapped(sent, "narrow", bit).astype(F32)
+    part = piece.shape[0] // wide_count
+    rounded = piece.astype(BF16)
+    own = lax.dynamic_slice_in_dim(piece, wide_at * part, part)
+    order = sorted(range(1, wide_count), reverse=True)
+    for k in order:
+        sent = lax.dynamic_slice_in_dim(rounded, (wide_at ^ k) * part, part)
+        if whole_column:
+            sent = jnp.concatenate([sent, back_blocks[k]])
+        got = swapped(sent, "wide", k).astype(F32)
+        own = own + got[:part]
+        if whole_column:
+            row_back = row_back + got[part:]
+    own = own.astype(BF16)
+    gathered = jnp.zeros((wide_count * part, channels), BF16)
+    gathered = lax.dynamic_update_slice_in_dim(gathered, own, wide_at * part, 0)
+    for k in order:
+        got = swapped(own, "wide", k)
+        gathered = lax.dynamic_update_slice_in_dim(gathered, got, (wide_at ^ k) * part, 0)
+    for bit in reversed(bits):
+        upper = (narrow_at // bit) % 2
+        other = swapped(gathered, "narrow", bit)
+        gathered = jnp.where(
+            upper == 0,
+            jnp.concatenate([gathered, other]),
+            jnp.concatenate([other, gathered]),
+        )
     other = swapped(gathered, "narrow", 1)
     if whole_column:
         row_back = row_back.astype(BF16)
@@ -748,11 +720,13 @@
     cell_total = shape.cells * wide_count * narrow_count
     row_total = held_rows * wide_count * narrow_count
     sizes = [row_total, cell_total, cell_total, cell_total // 16, cell_total // 64]
-    (weight_grads,) = call(
-        functools.partial(finish_kernel, [1.0 / math.sqrt(size) for size in sizes]),
-        [struct((5, channels, channels), F32)],
-        [place, gathered, other],
-    )
+    scales = np.array([1.0 / math.sqrt(size) for size in sizes], np.float32)
+    totals = jnp.where(
+        narrow_at % 2 == 0,
+        jnp.concatenate([gathered, other]),
+        jnp.concatenate([other, gathered]),
+    )
+    weight_grads = totals.reshape(5, channels, channels).astype(F32) * scales[:, None, None]
     return (grad_state.reshape(tile_x, tile_y, channels), row_back, weight_grads)
 
 

time: 69.8 us -> 62.8 us (0.90)
  starting transfers between devices: 40 us -> 29.9 us
  waiting for transfers between devices: 10.7 us -> 20.8 us
  local copies, waits for them, and re-layouts: 7.27 us -> 0.18 us
  other arithmetic: 1.62 us -> 2.48 us
    ppermute x15 -> x0, starting transfers between devices: 26.6 us -> none  [the longest x14 21.8 us: swapped_both(): return lax.ppermute(block, ('wide', 'narrow'), pairs)]
    ppermute x5 -> x14, waiting for transfers between devices: 2.85 us -> 20.8 us  [swapped(): return lax.ppermute(block, axis, [(i, i ^ bits) for i in range(count)])]
    ppermute x5 -> x14, starting transfers between devices: 12.1 us -> 28.5 us  [swapped(): return lax.ppermute(block, axis, [(i, i ^ bits) for i in range(count)])]
    ppermute x15 -> x0, waiting for transfers between devices: 7.83 us -> none  [the longest x14 5.73 us: swapped_both(): return lax.ppermute(block, ('wide', 'narrow'), pairs)]
    unnamed x32 -> x34, local copies, waits for them, and re-layouts: 7.15 us -> 0.09 us
    mul x0 -> x1, other arithmetic: none -> 1.24 us  [local(): totals.reshape(5, channels, channels).astype(F32) * scales[:, None, None]]
    reshape x1 -> x0, other arithmetic: 0.72 us -> none  [local(): mask = g2m_mask.astype(BF16).transpose(1, 2, 0).reshape(-1, 36)]
  transfers between devices with their start and end apart: 22 -> 16, of which waited for: 13 -> 11; matrix products, arithmetic and copies ran while one was open for 1% -> 1% of each run, Pallas kernels for 1% -> 1%
where the time goes in v5:
time: 62.8 us; the launch traced here: 62.6 us
  starting transfers between devices  29.9 us (48%)
  waiting for transfers between devices  20.8 us (33%)
  Pallas kernels  7.54 us (12%)
  other arithmetic  2.48 us (4%)
  between operations  1.68 us (3%)
    ppermute x14, starting transfers between devices, swapped(): return lax.ppermute(block, axis, [(i, i ^ bits) for i in range(count)])  28.5 us
    ppermute x14, waiting for transfers between devices, swapped(): return lax.ppermute(block, axis, [(i, i ^ bits) for i in range(count)])  20.8 us
    pallas_call x5, Pallas kernels, call(): pl.pallas_call(kernel, out_shape=tuple(out_shapes), in_specs=[pl.BlockSpe...  7.54 us
    ppermute x2, starting transfers between devices, swapped_between(): return lax.ppermute(block, axis, pairs + [(j, i) for i, j in pairs])  1.34 us
  transfers between devices with their start and end apart: 16, of which 11 were waited for; matrix products, arithmetic and copies ran while one was open for 1% of the time, Pallas kernels for 1%

profile of v5, /device:TPU:0, one launch (start us, length us, event | category | flops | bytes accessed | tf_op | source)
XLA Modules:
  0.0 62.6 jit_solution(4703716653963078518)
XLA Ops:
  0.7 1.1 %shard_map.193.place_ref.refs_0_ = s32[2]{0:T(128)S(1)} custom-call(s32[2]{0:T(128)S(1)} %pad_add_fusion.place_ref), custom_call_target="tpu_custom_call" | custom-call | flops 10000000000 | bytes 16 | tf_op jit(solution)/shard_map/pallas_call | solution.py:459
  2.6 0.7 %shard_map.194 = (bf16[368,256]{1,0:T(8,128)(2,1)S(1)}, bf16[320,256]{1,0:T(8,128)(2,1)S(1)}, bf16[48,256]{1,0:T(8,128)(2,1)S(1)}, bf16[48,256]{1,0:T(8,128)(2,1...) custom-call(s32[2]{0:T(128)S(1)} %shard_map.193.place_ref.refs_0_, bf16[512,256]{1,0:T(8,128)(2,1)S(1)} %bitcast.14, ...), custom_call_target="tpu_custom_call" | custom-call | flops 10000000000 | bytes 758540 | tf_op jit(solution)/shard_map/pallas_call | solution.py:459
  3.4 3.1 %collective-permute-start = (bf16[368,256]{1,0:T(8,128)(2,1)S(1)}, bf16[368,256]{1,0:T(8,128)(2,1)S(1)}, u32[]{:S(2)}, u32[]{:S(2)}) collective-permute-start(bf16[368,256]{1,0:T(8,128)(2,1)S(1)} %get-tuple-element.25), channel_id=1, source_target_pairs={{0,4},{4,0},{8,12},{12,8},{1,5},{5,1},{9,13},{13,9},{2,6},{6,2},{1... | collective-permute-start | bytes 565256 | tf_op jit(solution)/shard_map/ppermute | solution.py:26
  6.5 0.7 %collective-permute-start.1 = (bf16[320,256]{1,0:T(8,128)(2,1)S(1)}, bf16[320,256]{1,0:T(8,128)(2,1)S(1)}, u32[]{:S(2)}, u32[]{:S(2)}) collective-permute-start(bf16[320,256]{1,0:T(8,128)(2,1)S(1)} %get-tuple-element.26), channel_id=1, source_target_pairs={{4,8},{8,4},{5,9},{9,5},{6,10},{10,6},{7,11},{11,7},{20,24},{24,20... | collective-permute-start | bytes 491528 | tf_op jit(solution)/shard_map/ppermute | solution.py:32
  7.2 3.9 %collective-permute-start.2 = (bf16[48,256]{1,0:T(8,128)(2,1)S(1)}, bf16[48,256]{1,0:T(8,128)(2,1)S(1)}, u32[]{:S(2)}, u32[]{:S(2)}) collective-permute-start(bf16[48,256]{1,0:T(8,128)(2,1)S(1)} %get-tuple-element.27), channel_id=1, source_target_pairs={{0,8},{4,12},{8,0},{12,4},{1,9},{5,13},{9,1},{13,5},{2,10},{6,14},... | collective-permute-start | bytes 73736 | tf_op jit(solution)/shard_map/ppermute | solution.py:26
  11.1 2.9 %collective-permute-start.3 = (bf16[48,256]{1,0:T(8,128)(2,1)S(1)}, bf16[48,256]{1,0:T(8,128)(2,1)S(1)}, u32[]{:S(2)}, u32[]{:S(2)}) collective-permute-start(bf16[48,256]{1,0:T(8,128)(2,1)S(1)} %get-tuple-element.28), channel_id=1, source_target_pairs={{0,12},{4,8},{8,4},{12,0},{1,13},{5,9},{9,5},{13,1},{2,14},{6,10},... | collective-permute-start | bytes 73736 | tf_op jit(solution)/shard_map/ppermute | solution.py:26
  14.0 2.5 %collective-permute-done.2.refs_8_ = bf16[48,256]{1,0:T(8,128)(2,1)S(1)} collective-permute-done((bf16[48,256]{1,0:T(8,128)(2,1)S(1)}, bf16[48,256]{1,0:T(8,128)(2,1)S(1)}, u32[]{:S(2)}, u32[]{:S(2)}) %collective-permute-start.2) | collective-permute-done | bytes 24608 | tf_op jit(solution)/shard_map/ppermute | solution.py:26
  16.5 0.3 collective-permute-done.3.refs_9_
  16.9 1.2 %shard_map.195 = (bf16[1088,256]{1,0:T(8,128)(2,1)S(1)}, bf16[576,256]{1,0:T(8,128)(2,1)S(1)}, bf16[576,256]{1,0:T(8,128)(2,1)S(1)}, bf16[128,256]{1,0:T(8,128)(...) custom-call(s32[2]{0:T(128)S(1)} %shard_map.193.place_ref.refs_0_, bf16[512,256]{1,0:T(8,128)(2,1)S(1)} %bitcast.15, ...), custom_call_target="tpu_custom_call" | custom-call | flops 71303168 | bytes 2150408 | tf_op jit(solution)/shard_map/pallas_call | solution.py:459
  18.1 0.7 %collective-permute-start.5 = (bf16[576,256]{1,0:T(8,128)(2,1)S(1)}, bf16[576,256]{1,0:T(8,128)(2,1)S(1)}, u32[]{:S(2)}, u32[]{:S(2)}) collective-permute-start(bf16[576,256]{1,0:T(8,128)(2,1)S(1)} %get-tuple-element.30), channel_id=1, source_target_pairs={{1,2},{2,1},{5,6},{6,5},{9,10},{10,9},{13,14},{14,13},{17,18},{18,... | collective-permute-start | bytes 884744 | tf_op jit(solution)/shard_map/ppermute | solution.py:32
  18.8 0.9 %shard_map.196 = (bf16[1088,256]{1,0:T(8,128)(2,1)S(1)}, bf16[512,256]{1,0:T(8,128)(2,1)S(1)}, f32[512,256]{1,0:T(8,128)S(1)}, f32[512,256]{1,0:T(8,128)S(1)}) custom-call(bf16[1088,256]{1,0:T(8,128)(2,1)S(1)} %get-tuple-element.32.blended_ref.refs_4_, bf16[256,256]{1,0:T(8,128)(2,1)S(1)} %copy-done.3, bf16[256,256]{1,0:T(8,128)(2,1)S(1)} %copy-done.4), custom_call_target="tpu_custom_call" | custom-call | flops 285212672 | bytes 2686976 | tf_op jit(solution)/shard_map/pallas_call | solution.py:459
  19.8 3.6 %shard_map.197 = (bf16[512,256]{1,0:T(8,128)(2,1)}, bf16[128,256]{1,0:T(8,128)(2,1)S(1)}, bf16[640,256]{1,0:T(8,128)(2,1)S(1)}, f32[640,256]{1,0:T(8,128)S(1)}) custom-call(s32[1]{0:T(128)} %bitcast.refs_0_, bf16[576,256]{1,0:T(8,128)(2,1)S(1)} %collective-permute-done.4.refs_1_, bf16[576,256]{1,0:T(8,128)(2,1)S(1)} %collective-permute-done.5.refs_2_, ...), custom_call_target="tpu_custom_call" | custom-call | flops 402653184 | bytes 5525508 | tf_op jit(solution)/shard_map/pallas_call | solution.py:459
  23.4 6.9 %collective-permute-start.6 = (bf16[640,256]{1,0:T(8,128)(2,1)S(1)}, bf16[640,256]{1,0:T(8,128)(2,1)S(1)}, u32[]{:S(2)}, u32[]{:S(2)}) collective-permute-start(bf16[640,256]{1,0:T(8,128)(2,1)S(1)} %get-tuple-element.42), channel_id=1, source_target_pairs={{0,1},{1,0},{2,3},{3,2},{4,5},{5,4},{6,7},{7,6},{8,9},{9,8},{10,11... | collective-permute-start | bytes 983048 | tf_op jit(solution)/shard_map/ppermute | solution.py:26
  30.2 1.3 %collective-permute-done.6 = bf16[640,256]{1,0:T(8,128)(2,1)S(1)} collective-permute-done((bf16[640,256]{1,0:T(8,128)(2,1)S(1)}, bf16[640,256]{1,0:T(8,128)(2,1)S(1)}, u32[]{:S(2)}, u32[]{:S(2)}) %collective-permute-start.6) | collective-permute-done | bytes 327712 | tf_op jit(solution)/shard_map/ppermute | solution.py:26
  31.6 1.4 %collective-permute-start.7 = (bf16[320,256]{1,0:T(8,128)(2,1)S(1)}, bf16[320,256]{1,0:T(8,128)(2,1)S(1)}, u32[]{:S(2)}, u32[]{:S(2)}) collective-permute-start(bf16[320,256]{1,0:T(8,128)(2,1)S(1)} %dynamic-slice_convert_fusion), channel_id=1, source_target_pairs={{0,2},{1,3},{2,0},{3,1},{4,6},{5,7},{6,4},{7,5},{8,10},{9,11},{10,... | collective-permute-start | bytes 491528 | tf_op jit(solution)/shard_map/ppermute | solution.py:26
  33.1 5.1 %collective-permute-done.7 = bf16[320,256]{1,0:T(8,128)(2,1)S(1)} collective-permute-done((bf16[320,256]{1,0:T(8,128)(2,1)S(1)}, bf16[320,256]{1,0:T(8,128)(2,1)S(1)}, u32[]{:S(2)}, u32[]{:S(2)}) %collective-permute-start.7) | collective-permute-done | bytes 163872 | tf_op jit(solution)/shard_map/ppermute | solution.py:26
  38.2 2.9 %collective-permute-start.8 = (bf16[112,256]{1,0:T(8,128)(2,1)S(1)}, bf16[112,256]{1,0:T(8,128)(2,1)S(1)}, u32[]{:S(2)}, u32[]{:S(2)}) collective-permute-start(bf16[112,256]{1,0:T(8,128)(2,1)S(1)} %pad_maximum_fusion), channel_id=1, source_target_pairs={{0,12},{4,8},{8,4},{12,0},{1,13},{5,9},{9,5},{13,1},{2,14},{6,10},... | collective-permute-start | bytes 172040 | tf_op jit(solution)/shard_map/ppermute | solution.py:26
  41.2 1.5 %collective-permute-start.10 = (bf16[112,256]{1,0:T(8,128)(2,1)S(1)}, bf16[112,256]{1,0:T(8,128)(2,1)S(1)}, u32[]{:S(2)}, u32[]{:S(2)}) collective-permute-start(bf16[112,256]{1,0:T(8,128)(2,1)S(1)} %pad_maximum_fusion.2), channel_id=1, source_target_pairs={{0,4},{4,0},{8,12},{12,8},{1,5},{5,1},{9,13},{13,9},{2,6},{6,2},{1... | collective-permute-start | bytes 172040 | tf_op jit(solution)/shard_map/ppermute | solution.py:26
  42.7 1.6 %collective-permute-done.8 = bf16[112,256]{1,0:T(8,128)(2,1)S(1)} collective-permute-done((bf16[112,256]{1,0:T(8,128)(2,1)S(1)}, bf16[112,256]{1,0:T(8,128)(2,1)S(1)}, u32[]{:S(2)}, u32[]{:S(2)}) %collective-permute-start.8) | collective-permute-done | bytes 57376 | tf_op jit(solution)/shard_map/ppermute | solution.py:26
  44.3 2.1 %collective-permute-done.9 = bf16[112,256]{1,0:T(8,128)(2,1)S(1)} collective-permute-done((bf16[112,256]{1,0:T(8,128)(2,1)S(1)}, bf16[112,256]{1,0:T(8,128)(2,1)S(1)}, u32[]{:S(2)}, u32[]{:S(2)}) %collective-permute-start.9) | collective-permute-done | bytes 57376 | tf_op jit(solution)/shard_map/ppermute | solution.py:26
  46.5 0.1 collective-permute-done.10
  46.7 2.3 %collective-permute-start.11 = (bf16[80,256]{1,0:T(8,128)(2,1)S(1)}, bf16[80,256]{1,0:T(8,128)(2,1)S(1)}, u32[]{:S(2)}, u32[]{:S(2)}) collective-permute-start(bf16[80,256]{1,0:T(8,128)(2,1)S(1)} %get-tuple-element.44), channel_id=1, source_target_pairs={{0,12},{4,8},{8,4},{12,0},{1,13},{5,9},{9,5},{13,1},{2,14},{6,10},... | collective-permute-start | bytes 122888 | tf_op jit(solution)/shard_map/ppermute | solution.py:26
  48.9 2.2 %collective-permute-start.13 = (bf16[80,256]{1,0:T(8,128)(2,1)S(1)}, bf16[80,256]{1,0:T(8,128)(2,1)S(1)}, u32[]{:S(2)}, u32[]{:S(2)}) collective-permute-start(bf16[80,256]{1,0:T(8,128)(2,1)S(1)} %get-tuple-element.44), channel_id=1, source_target_pairs={{0,4},{4,0},{8,12},{12,8},{1,5},{5,1},{9,13},{13,9},{2,6},{6,2},{1... | collective-permute-start | bytes 122888 | tf_op jit(solution)/shard_map/ppermute | solution.py:26
  51.1 1.5 %collective-permute-done.11 = bf16[80,256]{1,0:T(8,128)(2,1)S(1)} collective-permute-done((bf16[80,256]{1,0:T(8,128)(2,1)S(1)}, bf16[80,256]{1,0:T(8,128)(2,1)S(1)}, u32[]{:S(2)}, u32[]{:S(2)}) %collective-permute-start.11) | collective-permute-done | bytes 40992 | tf_op jit(solution)/shard_map/ppermute | solution.py:26
  52.6 1.2 %collective-permute-done.12 = bf16[80,256]{1,0:T(8,128)(2,1)S(1)} collective-permute-done((bf16[80,256]{1,0:T(8,128)(2,1)S(1)}, bf16[80,256]{1,0:T(8,128)(2,1)S(1)}, u32[]{:S(2)}, u32[]{:S(2)}) %collective-permute-start.12) | collective-permute-done | bytes 40992 | tf_op jit(solution)/shard_map/ppermute | solution.py:26
  53.9 1.3 %collective-permute-start.14 = (bf16[320,256]{1,0:T(8,128)(2,1)S(1)}, bf16[320,256]{1,0:T(8,128)(2,1)S(1)}, u32[]{:S(2)}, u32[]{:S(2)}) collective-permute-start(bf16[320,256]{1,0:T(8,128)(2,1)S(1)} %constant_dynamic-update-slice_fusion), channel_id=1, source_target_pairs={{0,2},{1,3},{2,0},{3,1},{4,6},{5,7},{6,4},{7,5},{8,10},{9,11},{10,... | collective-permute-start | bytes 491528 | tf_op jit(solution)/shard_map/ppermute | solution.py:26
  55.2 4.1 %collective-permute-done.14 = bf16[320,256]{1,0:T(8,128)(2,1)S(1)} collective-permute-done((bf16[320,256]{1,0:T(8,128)(2,1)S(1)}, bf16[320,256]{1,0:T(8,128)(2,1)S(1)}, u32[]{:S(2)}, u32[]{:S(2)}) %collective-permute-start.14) | collective-permute-done | bytes 163872 | tf_op jit(solution)/shard_map/ppermute | solution.py:26
  59.3 0.1 maximum_select_fusion.1
  59.5 0.6 fusion.1
  60.1 1.0 %collective-permute-done.15 = bf16[640,256]{1,0:T(8,128)(2,1)S(1)} collective-permute-done((bf16[640,256]{1,0:T(8,128)(2,1)S(1)}, bf16[640,256]{1,0:T(8,128)(2,1)S(1)}, u32[]{:S(2)}, u32[]{:S(2)}) %collective-permute-start.15) | collective-permute-done | bytes 327712 | tf_op jit(solution)/shard_map/ppermute | solution.py:26
  61.1 0.2 maximum_select_fusion
  61.4 1.2 %convert_multiply_fusion = f32[5,256,256]{2,1,0:T(8,128)} fusion(bf16[5,256,256]{2,1,0:T(8,128)(2,1)S(1)} %bitcast.20, f32[5]{0:T(128)S(1)} %copy-done.16), kind=kLoop, calls=%fused_computation | loop fusion | flops 655360 | bytes 1966100 | tf_op jit(solution)/shard_map/mul | solution.py:729
  (60 shorter events, 0.6 us)
Async XLA Ops:
  0.7 1.8 %copy-start.11 = (bf16[4,8,256]{2,1,0:T(8,128)(2,1)S(1)}, bf16[4,8,256]{2,1,0:T(8,128)(2,1)}, u32[]{:S(2)}) copy-start(bf16[4,8,256]{2,1,0:T(8,128)(2,1)} %param.24) | copy-start | bytes 49156
  0.7 1.8 %copy-start.12 = (s32[36,4,8]{0,2,1:T(8,128)S(1)}, s32[36,4,8]{0,2,1:T(8,128)}, u32[]{:S(2)}) copy-start(s32[36,4,8]{0,2,1:T(8,128)} %param.23) | copy-start | bytes 13828
  0.7 1.9 %copy-start.13 = (bf16[32,256]{1,0:T(8,128)(2,1)S(1)}, bf16[32,256]{1,0:T(8,128)(2,1)}, u32[]{:S(2)}) copy-start(bf16[32,256]{1,0:T(8,128)(2,1)} %rows_ref.1) | copy-start | bytes 49156
  0.7 1.9 %copy-start.14 = (s32[32]{0:T(128)S(1)}, s32[32]{0:T(128)}, u32[]{:S(2)}) copy-start(s32[32]{0:T(128)} %param.21) | copy-start | bytes 388
  0.7 1.9 %copy-start.15 = (s32[32]{0:T(128)S(1)}, s32[32]{0:T(128)}, u32[]{:S(2)}) copy-start(s32[32]{0:T(128)} %param.22) | copy-start | bytes 388
  2.6 14.2 %copy-start = (bf16[256,256]{1,0:T(8,128)(2,1)S(1)}, bf16[256,256]{1,0:T(8,128)(2,1)}, u32[]{:S(2)}) copy-start(bf16[256,256]{1,0:T(8,128)(2,1)} %refs_15_.1) | copy-start | bytes 393220
  2.6 14.2 %copy-start.10 = (bf16[2,32,128]{2,1,0:T(8,128)(2,1)S(1)}, bf16[2,32,128]{2,1,0:T(8,128)(2,1)}, u32[]{:S(2)}) copy-start(bf16[2,32,128]{2,1,0:T(8,128)(2,1)} %constant.63.clone.refs_4_) | copy-start | bytes 49156
  2.6 16.2 %copy-start.3 = (bf16[256,256]{1,0:T(8,128)(2,1)S(1)}, bf16[256,256]{1,0:T(8,128)(2,1)}, u32[]{:S(2)}) copy-start(bf16[256,256]{1,0:T(8,128)(2,1)} %refs_16_.1) | copy-start | bytes 393220
  2.6 16.2 %copy-start.4 = (bf16[256,256]{1,0:T(8,128)(2,1)S(1)}, bf16[256,256]{1,0:T(8,128)(2,1)}, u32[]{:S(2)}) copy-start(bf16[256,256]{1,0:T(8,128)(2,1)} %refs_17_.1) | copy-start | bytes 393220
  3.4 16.4 %copy-start.2 = (bf16[2,128,384]{2,1,0:T(8,128)(2,1)S(1)}, bf16[2,128,384]{2,1,0:T(8,128)(2,1)}, u32[]{:S(2)}) copy-start(bf16[2,128,384]{2,1,0:T(8,128)(2,1)} %constant.65.clone.refs_12_) | copy-start | bytes 589828
  3.4 16.4 %copy-start.5 = (bf16[256,256]{1,0:T(8,128)(2,1)S(1)}, bf16[256,256]{1,0:T(8,128)(2,1)}, u32[]{:S(2)}) copy-start(bf16[256,256]{1,0:T(8,128)(2,1)} %refs_18_.1) | copy-start | bytes 393220
  3.4 16.4 %copy-start.6 = (bf16[256,256]{1,0:T(8,128)(2,1)S(1)}, bf16[256,256]{1,0:T(8,128)(2,1)}, u32[]{:S(2)}) copy-start(bf16[256,256]{1,0:T(8,128)(2,1)} %refs_19_.1) | copy-start | bytes 393220
  3.4 16.4 %copy-start.7 = (bf16[2,128,192]{2,1,0:T(8,128)(2,1)S(1)}, bf16[2,128,192]{2,1,0:T(8,128)(2,1)}, u32[]{:S(2)}) copy-start(bf16[2,128,192]{2,1,0:T(8,128)(2,1)} %constant.64.clone.refs_11_) | copy-start | bytes 294916
  3.4 16.4 %copy-start.8 = (bf16[128,256]{1,0:T(8,128)(2,1)S(1)}, bf16[128,256]{1,0:T(8,128)(2,1)}, u32[]{:S(2)}) copy-start(bf16[128,256]{1,0:T(8,128)(2,1)} %constant.67.clone.refs_14_) | copy-start | bytes 196612
  3.4 16.4 %copy-start.9 = (f32[2,16,384]{2,1,0:T(8,128)S(1)}, f32[2,16,384]{2,1,0:T(8,128)}, u32[]{:S(2)}) copy-start(f32[2,16,384]{2,1,0:T(8,128)} %constant.66.clone.refs_13_) | copy-start | bytes 147460
  3.4 13.4 %collective-permute-start = (bf16[368,256]{1,0:T(8,128)(2,1)S(1)}, bf16[368,256]{1,0:T(8,128)(2,1)S(1)}, u32[]{:S(2)}, u32[]{:S(2)}) collective-permute-start(bf16[368,256]{1,0:T(8,128)(2,1)S(1)} %get-tuple-element.25), channel_id=1, source_target_pairs={{0,4},{4,0},{8,12},{12,8},{1,5},{5,1},{9,13},{13,9},{2,6},{6,2},{1... | collective-permute-start | bytes 565256 | tf_op jit(solution)/shard_map/ppermute | solution.py:26
  6.5 10.3 %collective-permute-start.1 = (bf16[320,256]{1,0:T(8,128)(2,1)S(1)}, bf16[320,256]{1,0:T(8,128)(2,1)S(1)}, u32[]{:S(2)}, u32[]{:S(2)}) collective-permute-start(bf16[320,256]{1,0:T(8,128)(2,1)S(1)} %get-tuple-element.26), channel_id=1, source_target_pairs={{4,8},{8,4},{5,9},{9,5},{6,10},{10,6},{7,11},{11,7},{20,24},{24,20... | collective-permute-start | bytes 491528 | tf_op jit(solution)/shard_map/ppermute | solution.py:32
  7.2 9.3 %collective-permute-start.2 = (bf16[48,256]{1,0:T(8,128)(2,1)S(1)}, bf16[48,256]{1,0:T(8,128)(2,1)S(1)}, u32[]{:S(2)}, u32[]{:S(2)}) collective-permute-start(bf16[48,256]{1,0:T(8,128)(2,1)S(1)} %get-tuple-element.27), channel_id=1, source_target_pairs={{0,8},{4,12},{8,0},{12,4},{1,9},{5,13},{9,1},{13,5},{2,10},{6,14},... | collective-permute-start | bytes 73736 | tf_op jit(solution)/shard_map/ppermute | solution.py:26
  11.1 5.7 %collective-permute-start.3 = (bf16[48,256]{1,0:T(8,128)(2,1)S(1)}, bf16[48,256]{1,0:T(8,128)(2,1)S(1)}, u32[]{:S(2)}, u32[]{:S(2)}) collective-permute-start(bf16[48,256]{1,0:T(8,128)(2,1)S(1)} %get-tuple-element.28), channel_id=1, source_target_pairs={{0,12},{4,8},{8,4},{12,0},{1,13},{5,9},{9,5},{13,1},{2,14},{6,10},... | collective-permute-start | bytes 73736 | tf_op jit(solution)/shard_map/ppermute | solution.py:26
  18.0 1.7 %collective-permute-start.4 = (bf16[576,256]{1,0:T(8,128)(2,1)S(1)}, bf16[576,256]{1,0:T(8,128)(2,1)S(1)}, u32[]{:S(2)}, u32[]{:S(2)}) collective-permute-start(bf16[576,256]{1,0:T(8,128)(2,1)S(1)} %get-tuple-element.29), channel_id=1, source_target_pairs={{0,1},{1,0},{2,3},{3,2},{4,5},{5,4},{6,7},{7,6},{8,9},{9,8},{10,11... | collective-permute-start | bytes 884744 | tf_op jit(solution)/shard_map/ppermute | solution.py:26
  18.1 1.7 %collective-permute-start.5 = (bf16[576,256]{1,0:T(8,128)(2,1)S(1)}, bf16[576,256]{1,0:T(8,128)(2,1)S(1)}, u32[]{:S(2)}, u32[]{:S(2)}) collective-permute-start(bf16[576,256]{1,0:T(8,128)(2,1)S(1)} %get-tuple-element.30), channel_id=1, source_target_pairs={{1,2},{2,1},{5,6},{6,5},{9,10},{10,9},{13,14},{14,13},{17,18},{18,... | collective-permute-start | bytes 884744 | tf_op jit(solution)/shard_map/ppermute | solution.py:32
  23.4 8.1 %collective-permute-start.6 = (bf16[640,256]{1,0:T(8,128)(2,1)S(1)}, bf16[640,256]{1,0:T(8,128)(2,1)S(1)}, u32[]{:S(2)}, u32[]{:S(2)}) collective-permute-start(bf16[640,256]{1,0:T(8,128)(2,1)S(1)} %get-tuple-element.42), channel_id=1, source_target_pairs={{0,1},{1,0},{2,3},{3,2},{4,5},{5,4},{6,7},{7,6},{8,9},{9,8},{10,11... | collective-permute-start | bytes 983048 | tf_op jit(solution)/shard_map/ppermute | solution.py:26
  31.6 6.5 %collective-permute-start.7 = (bf16[320,256]{1,0:T(8,128)(2,1)S(1)}, bf16[320,256]{1,0:T(8,128)(2,1)S(1)}, u32[]{:S(2)}, u32[]{:S(2)}) collective-permute-start(bf16[320,256]{1,0:T(8,128)(2,1)S(1)} %dynamic-slice_convert_fusion), channel_id=1, source_target_pairs={{0,2},{1,3},{2,0},{3,1},{4,6},{5,7},{6,4},{7,5},{8,10},{9,11},{10,... | collective-permute-start | bytes 491528 | tf_op jit(solution)/shard_map/ppermute | solution.py:26
  38.2 6.1 %collective-permute-start.8 = (bf16[112,256]{1,0:T(8,128)(2,1)S(1)}, bf16[112,256]{1,0:T(8,128)(2,1)S(1)}, u32[]{:S(2)}, u32[]{:S(2)}) collective-permute-start(bf16[112,256]{1,0:T(8,128)(2,1)S(1)} %pad_maximum_fusion), channel_id=1, source_target_pairs={{0,12},{4,8},{8,4},{12,0},{1,13},{5,9},{9,5},{13,1},{2,14},{6,10},... | collective-permute-start | bytes 172040 | tf_op jit(solution)/shard_map/ppermute | solution.py:26
  41.1 5.3 %collective-permute-start.9 = (bf16[112,256]{1,0:T(8,128)(2,1)S(1)}, bf16[112,256]{1,0:T(8,128)(2,1)S(1)}, u32[]{:S(2)}, u32[]{:S(2)}) collective-permute-start(bf16[112,256]{1,0:T(8,128)(2,1)S(1)} %pad_maximum_fusion.1), channel_id=1, source_target_pairs={{0,8},{4,12},{8,0},{12,4},{1,9},{5,13},{9,1},{13,5},{2,10},{6,14},... | collective-permute-start | bytes 172040 | tf_op jit(solution)/shard_map/ppermute | solution.py:26
  41.2 5.4 %collective-permute-start.10 = (bf16[112,256]{1,0:T(8,128)(2,1)S(1)}, bf16[112,256]{1,0:T(8,128)(2,1)S(1)}, u32[]{:S(2)}, u32[]{:S(2)}) collective-permute-start(bf16[112,256]{1,0:T(8,128)(2,1)S(1)} %pad_maximum_fusion.2), channel_id=1, source_target_pairs={{0,4},{4,0},{8,12},{12,8},{1,5},{5,1},{9,13},{13,9},{2,6},{6,2},{1... | collective-permute-start | bytes 172040 | tf_op jit(solution)/shard_map/ppermute | solution.py:26
  46.6 14.7 %copy-start.16 = (f32[5]{0:T(128)S(1)}, f32[5]{0:T(128)}, u32[]{:S(2)}) copy-start(f32[5]{0:T(128)} %constant.72) | copy-start | bytes 64
  46.7 6.0 %collective-permute-start.11 = (bf16[80,256]{1,0:T(8,128)(2,1)S(1)}, bf16[80,256]{1,0:T(8,128)(2,1)S(1)}, u32[]{:S(2)}, u32[]{:S(2)}) collective-permute-start(bf16[80,256]{1,0:T(8,128)(2,1)S(1)} %get-tuple-element.44), channel_id=1, source_target_pairs={{0,12},{4,8},{8,4},{12,0},{1,13},{5,9},{9,5},{13,1},{2,14},{6,10},... | collective-permute-start | bytes 122888 | tf_op jit(solution)/shard_map/ppermute | solution.py:26
  48.9 4.9 %collective-permute-start.12 = (bf16[80,256]{1,0:T(8,128)(2,1)S(1)}, bf16[80,256]{1,0:T(8,128)(2,1)S(1)}, u32[]{:S(2)}, u32[]{:S(2)}) collective-permute-start(bf16[80,256]{1,0:T(8,128)(2,1)S(1)} %get-tuple-element.44), channel_id=1, source_target_pairs={{0,8},{4,12},{8,0},{12,4},{1,9},{5,13},{9,1},{13,5},{2,10},{6,14},... | collective-permute-start | bytes 122888 | tf_op jit(solution)/shard_map/ppermute | solution.py:26
  48.9 4.9 %collective-permute-start.13 = (bf16[80,256]{1,0:T(8,128)(2,1)S(1)}, bf16[80,256]{1,0:T(8,128)(2,1)S(1)}, u32[]{:S(2)}, u32[]{:S(2)}) collective-permute-start(bf16[80,256]{1,0:T(8,128)(2,1)S(1)} %get-tuple-element.44), channel_id=1, source_target_pairs={{0,4},{4,0},{8,12},{12,8},{1,5},{5,1},{9,13},{13,9},{2,6},{6,2},{1... | collective-permute-start | bytes 122888 | tf_op jit(solution)/shard_map/ppermute | solution.py:26
  53.9 5.4 %collective-permute-start.14 = (bf16[320,256]{1,0:T(8,128)(2,1)S(1)}, bf16[320,256]{1,0:T(8,128)(2,1)S(1)}, u32[]{:S(2)}, u32[]{:S(2)}) collective-permute-start(bf16[320,256]{1,0:T(8,128)(2,1)S(1)} %constant_dynamic-update-slice_fusion), channel_id=1, source_target_pairs={{0,2},{1,3},{2,0},{3,1},{4,6},{5,7},{6,4},{7,5},{8,10},{9,11},{10,... | collective-permute-start | bytes 491528 | tf_op jit(solution)/shard_map/ppermute | solution.py:26
  59.4 1.7 %collective-permute-start.15 = (bf16[640,256]{1,0:T(8,128)(2,1)S(1)}, bf16[640,256]{1,0:T(8,128)(2,1)S(1)}, u32[]{:S(2)}, u32[]{:S(2)}) collective-permute-start(bf16[640,256]{1,0:T(8,128)(2,1)S(1)} %maximum_select_fusion.1), channel_id=1, source_target_pairs={{0,1},{1,0},{2,3},{3,2},{4,5},{5,4},{6,7},{7,6},{8,9},{9,8},{10,11... | collective-permute-start | bytes 983048 | tf_op jit(solution)/shard_map/ppermute | solution.py:26
  (1 other events, 1.8 us)

commit v6 on v5

--- a/solution.py
+++ b/solution.py
@@ -10,10 +10,9 @@
 from jax.sharding import PartitionSpec as P
 
 CAP = 16
-REACH = 9
-NODES_OUT = 2
-SIDE = 16
-SLOTS = 16
+REACH = 1
+BLOCK = 16
+COLUMN = 32
 LANES = 256
 LONG = 10**10
 VMEM_LIMIT = 48 * 1024 * 1024
@@ -59,12 +58,6 @@
 
 def pieces(start, stop, size):
     return [(at, min(size, stop - at)) for at in range(start, stop, size)]
-
-
-def two_halves(value):
-    high = value.astype(BF16)
-    low = (value - high.astype(F32)).astype(BF16)
-    return jnp.concatenate([high, low], axis=0)
 
 
 class Shape:
@@ -75,81 +68,40 @@
         self.rows_x = tile_x + 2 * REACH
         self.halo = REACH * tile_y
         self.center = self.rows_x * tile_y
-        self.side = self.rows_x * SIDE
-        self.pitch = tile_y + 2 * SIDE
         self.node_x = tile_x // 4
         self.node_y = tile_y // 4
-        self.out_x = self.node_x + 2 * NODES_OUT
-        self.nodes = self.out_x * SLOTS
-        self.edge = NODES_OUT * self.node_y
-        self.own_nodes = self.node_x * self.node_y
-        self.window = 6 * self.pitch
-        self.side_nodes = NODES_OUT * self.out_x
-
-    def center_row(self, at_x, at_y, kind):
-        edge, own = self.edge, self.own_nodes
-        if at_x < NODES_OUT:
-            return kind * edge + at_x * self.node_y + at_y
-        at_x -= NODES_OUT
-        if at_x < self.node_x:
-            return 2 * edge + kind * own + at_x * self.node_y + at_y
-        at_x -= self.node_x
-        return 2 * edge + 2 * own + kind * edge + at_x * self.node_y + at_y
-
-    def tables(self):
-        stack = 4 * self.edge + 2 * self.own_nodes
-        side = self.side_nodes
-        to_left = np.zeros((2 * side, stack), np.float32)
-        to_right = np.zeros((2 * side, stack), np.float32)
-        for kind in range(2):
-            for at_x in range(self.out_x):
-                for k in range(NODES_OUT):
-                    row = kind * side + at_x * NODES_OUT + k
-                    to_left[row, self.center_row(at_x, k, kind)] = 1
-                    last = self.node_y - NODES_OUT + k
-                    to_right[row, self.center_row(at_x, last, kind)] = 1
-        place = np.zeros((2, self.nodes, stack + 4 * side), np.float32)
-        for kind in range(2):
-            for at_x in range(self.out_x):
-                for slot in range(self.node_y + 2 * NODES_OUT):
-                    at_y = slot - NODES_OUT
-                    if at_y < 0:
-                        column = stack + kind * side + at_x * NODES_OUT + slot
-                    elif at_y < self.node_y:
-                        column = self.center_row(at_x, at_y, kind)
-                    else:
-                        k = at_y - self.node_y
-                        column = stack + 2 * side + kind * side + at_x * NODES_OUT + k
-                    place[kind, at_x * SLOTS + slot, column] = 1
-        spread = np.zeros((2, 128, self.window), np.float32)
-        match = np.zeros((2, SLOTS, self.window), np.float32)
-        for dx in range(6):
-            for at in range(self.pitch):
-                if at < self.tile_y:
-                    y = at
-                elif at < self.tile_y + SIDE:
-                    y = at - self.tile_y - SIDE
-                else:
-                    y = at - SIDE
-                quotient, rest = (y + REACH) // 4, (y + REACH) % 4
-                lane = dx * self.pitch + at
-                spread[0, dx * 6 + rest, lane] = 1
-                if 0 <= quotient < SLOTS:
-                    match[0, quotient, lane] = 1
-                if rest < 2:
-                    spread[1, dx * 6 + rest + 4, lane] = 1
-                    if 0 <= quotient - 1 < SLOTS:
-                        match[1, quotient - 1, lane] = 1
-        node = np.arange(self.nodes)
-        quad = node // SLOTS // 2 * SLOTS + node % SLOTS // 2
-        same = (quad[:, None] == quad[None, :]).astype(np.float32)
-        return {
-            "to_side": np.stack([to_left, to_right]),
-            "place": place,
-            "spread": spread,
-            "match": match,
-            "quad": np.concatenate([same, same], axis=1),
-        }
+        self.nodes = self.node_x * self.node_y
+        self.near_nodes = self.nodes + 2 * self.node_y
+        self.all_nodes = self.near_nodes + 2 * 8
+
+    def node_places(self, count):
+        node = lax.broadcasted_iota(jnp.int32, (count, 1), 0)
+        at_x, at_y = node // self.node_y, node % self.node_y
+        lower = node >= self.nodes + self.node_y
+        at_x = jnp.where(node < self.nodes, at_x, jnp.where(lower, self.node_x, -1))
+        side = node - self.near_nodes
+        at_x = jnp.where(side < 0, at_x, side % 8 - 1)
+        at_y = jnp.where(side < 0, at_y, jnp.where(side < 8, -1, self.node_y))
+        return at_x, at_y
+
+
+def edge_matrix(mask, node_x, node_y, row, column):
+    edges = None
+    for down in range(2):
+        for right in range(2):
+            shift_x, shift_y = row % 4 + 4 * down, column % 4 + 4 * right
+            code = jnp.where((shift_x < 6) & (shift_y < 6), shift_x * 6 + shift_y, -1)
+            entry = lax.broadcasted_iota(jnp.int32, (128, row.shape[1]), 0)
+            table = jnp.where(entry == code, 1.0, 0.0).astype(BF16)
+            match = (node_x == row // 4 - down) & (node_y == column // 4 - right)
+            term = jnp.where(match, dot(mask, table), 0.0)
+            edges = term if edges is None else edges + term
+    return edges
+
+
+def both_parts(value):
+    high = value.astype(BF16)
+    return high, (value - high.astype(F32)).astype(BF16)
 
 
 def open_kernel(place_ref, out_ref):
@@ -162,8 +114,7 @@
     units,
     place_ref,
     own_ref,
-    cotangent_ref,
-    mask_ref,
+    mask_in_ref,
     rows_ref,
     target_x_ref,
     target_y_ref,
@@ -172,10 +123,10 @@
     second_ref,
     third_ref,
     fourth_ref,
-    mesh_ref,
+    mask_ref,
     own_rows_ref,
 ):
-    edge, own_nodes, halo = shape.edge, shape.own_nodes, shape.halo
+    halo, node_y = shape.halo, shape.node_y
     held = rows_ref.shape[0]
     even = place_ref[0] % 2 == 0
     odd = jnp.logical_not(even)
@@ -196,29 +147,28 @@
         ref[at : at + held] = rows_ref[...]
         ref[at + held :] = jnp.where(lane // held == number, spread, 0.0).astype(BF16)
 
-    mesh_ref[:own_nodes] = cotangent_ref[...]
-    mesh_ref[own_nodes:] = jnp.zeros((own_nodes, mesh_ref.shape[1]), BF16)
-    mesh_ref[own_nodes:, : mask_ref.shape[1]] = mask_ref[...].astype(F32).astype(BF16)
+    mask = mask_in_ref[...].astype(F32)
+    mask_ref[...] = jnp.zeros(mask_ref.shape, F32)
+    mask_ref[:, : mask.shape[1]] = mask
     for ref, upward in ((first_ref, even), (second_ref, odd)):
-        start = pl.multiple_of(jnp.where(upward, shape.cells - halo, 0), shape.tile_y)
+        start = pl.multiple_of(jnp.where(upward, shape.cells - halo, 0), halo)
         ref[:halo] = own_ref[pl.ds(start, halo)]
-        start = pl.multiple_of(jnp.where(upward, own_nodes - edge, 0), 16)
-        ref[halo : halo + edge] = mesh_ref[pl.ds(start, edge)]
-        start = pl.multiple_of(jnp.where(upward, 2 * own_nodes - edge, own_nodes), 16)
-        ref[halo + edge : halo + 2 * edge] = mesh_ref[pl.ds(start, edge)]
+        start = pl.multiple_of(jnp.where(upward, shape.nodes - node_y, 0), 8)
+        chosen = mask_ref[pl.ds(start, node_y)]
+        block = jnp.concatenate([chosen, jnp.zeros((BLOCK - node_y, LANES), F32)], axis=0)
+        ref[halo : halo + BLOCK] = block.astype(BF16)
 
 
 def blend_kernel(shape, units, unit_rows, *refs):
-    (place_ref, own_ref, mesh_ref, w_force_ref, side_ref, own_rows_ref) = refs[:6]
+    (place_ref, own_ref, mask_ref, w_force_ref, own_rows_ref) = refs[:5]
     count = units if units > 3 else 2
-    arrived = refs[6 : 6 + count]
-    (blended_ref, first_ref, second_ref, stack_ref, rows_ref, key_ref) = refs[6 + count : 12 + count]
-    (projected_ref,) = refs[12 + count :]
+    arrived = refs[5 : 5 + count]
+    (blended_ref, first_ref, second_ref, masks_ref, rows_ref, key_ref) = refs[5 + count : 11 + count]
+    (projected_ref,) = refs[11 + count :]
     wide_at = place_ref[0]
     even = wide_at % 2 == 0
     near, between = arrived[0], arrived[1]
-    mesh = 2 * shape.edge
-    first_row = shape.halo + mesh
+    first_row = shape.halo + BLOCK
 
     def held(k, at, n):
         if k == 0:
@@ -254,17 +204,10 @@
         one, other = near[at : at + n], between[at : at + n]
         return jnp.where(even, one, other) if forward else jnp.where(even, other, one)
 
-    stack = jnp.concatenate(
-        [facing(shape.halo, mesh, False), mesh_ref[...], facing(shape.halo, mesh, True)], axis=0
-    )
-    stack_ref[...] = stack
-    narrow_even = place_ref[1] % 2 == 0
-    column = pl.multiple_of(jnp.where(narrow_even, shape.tile_y - SIDE, 0), SIDE)
-    other = pl.multiple_of(jnp.where(narrow_even, 0, shape.tile_y - SIDE), SIDE)
-    to_left = dot(side_ref[0], stack).astype(BF16)
-    to_right = dot(side_ref[1], stack).astype(BF16)
-    first_ref[shape.side :] = jnp.where(narrow_even, to_right, to_left)
-    second_ref[shape.side :] = jnp.where(narrow_even, to_left, to_right)
+    up = facing(shape.halo, BLOCK, False).astype(F32)[: shape.node_y]
+    down = facing(shape.halo, BLOCK, True).astype(F32)[: shape.node_y]
+    masks = jnp.concatenate([mask_ref[...], up, down], axis=0).astype(BF16)
+    masks_ref[...] = masks
 
     tile_y = shape.tile_y
     inner = shape.halo + shape.cells
@@ -282,15 +225,44 @@
             hit = jnp.where(cell == key, 1.0, 0.0).astype(BF16)
             value = value + dot(hit, projected_ref[k * width : (k + 1) * width])
         blended_ref[first : first + n] = value.astype(BF16)
-    for row in range(shape.rows_x):
-        target = slice(row * SIDE, (row + 1) * SIDE)
-        first_ref[target] = blended_ref[pl.ds(row * tile_y + column, SIDE)]
-        second_ref[target] = blended_ref[pl.ds(row * tile_y + other, SIDE)]
+    node = lax.broadcasted_iota(jnp.int32, (BLOCK, masks.shape[0]), 1)
+    line = lax.broadcasted_iota(jnp.int32, (BLOCK, masks.shape[0]), 0)
+    lower = node >= shape.nodes + shape.node_y
+    node_x = jnp.where(
+        node < shape.nodes, node // shape.node_y, jnp.where(lower, shape.node_x, -1)
+    )
+    cell = lax.broadcasted_iota(jnp.int32, (COLUMN, shape.center), 1)
+    row = lax.broadcasted_iota(jnp.int32, (COLUMN, shape.center), 0)
+    narrow_even = place_ref[1] % 2 == 0
+    for ref, last in ((first_ref, narrow_even), (second_ref, jnp.logical_not(narrow_even))):
+        column = jnp.where(last, tile_y - 1, 0)
+        hit = jnp.where(cell == row * tile_y + column, 1.0, 0.0).astype(BF16)
+        ref[:COLUMN] = dot(hit, blended_ref[...]).astype(BF16)
+        node_y = jnp.where(last, shape.node_y - 1, 0)
+        hit = (node_x == line - 1) & (node % shape.node_y == node_y)
+        ref[COLUMN:] = dot(jnp.where(hit, 1.0, 0.0).astype(BF16), masks).astype(BF16)
 
 
 def forward_kernel(
-    shape, blended_ref, w_embed_ref, w_message_ref, message_ref, latent_ref, embed_ref, slope_ref
+    shape,
+    blended_ref,
+    masks_ref,
+    w_embed_ref,
+    w_message_ref,
+    message_ref,
+    latent_ref,
+    embed_ref,
+    slope_ref,
+    edges_ref,
 ):
+    lane = lax.broadcasted_iota(jnp.int32, (1, shape.center + 2 * COLUMN), 1)
+    side = lane - shape.center
+    row = jnp.where(side < 0, lane // shape.tile_y, side % COLUMN)
+    right = jnp.where(side < COLUMN, 0, shape.tile_y + 1)
+    column = jnp.where(side < 0, lane % shape.tile_y + 1, right)
+    node_x, node_y = shape.node_places(shape.nodes)
+    mask = masks_ref[: shape.nodes, :128]
+    edges_ref[...] = edge_matrix(mask, node_x, node_y, row, column).astype(BF16)
     inner = shape.halo + shape.cells
     jobs = pieces(0, shape.halo, 96) + pieces(shape.halo, inner, 128)
     jobs += pieces(inner, shape.center, 96)
@@ -309,116 +281,155 @@
             slope_ref[own : own + n] = message_slope
 
 
-def backward_kernel(shape, total_rows, *refs):
-    (
-        narrow_ref,
-        first_ref,
-        second_ref,
-        stack_ref,
-        blended_ref,
-        message_ref,
-        latent_ref,
-        embed_ref,
-        slope_ref,
-        rows_ref,
-        key_ref,
-        place_ref,
-        spread_ref,
-        match_ref,
-        quad_ref,
-        w_force_ref,
-        w_embed_ref,
-        w_message_ref,
-        w_one_ref,
-        w_two_ref,
-        state_ref,
-        back_ref,
-        sent_ref,
-        kept_ref,
-        padded_ref,
-        level_ref,
-        cover_ref,
-        pmb_ref,
-        peb_ref,
-        grads_ref,
-    ) = refs
-    tile_y, pitch = shape.tile_y, shape.pitch
-    channels = blended_ref.shape[1]
-
-    even = narrow_ref[0] % 2 == 0
-    first_at = pl.multiple_of(tile_y + jnp.where(even, SIDE, 0), SIDE)
-    second_at = pl.multiple_of(tile_y + jnp.where(even, 0, SIDE), SIDE)
-    for ref, offset in ((first_ref, first_at), (second_ref, second_at)):
-        for at, n in pieces(0, shape.side, 8 * SIDE):
-            blended = ref[at : at + n]
-            latent = (blended.astype(F32) + silu(dot(blended, w_embed_ref[...]))).astype(BF16)
-            message = silu(dot(latent, w_message_ref[...])).astype(BF16)
-            for t in range(n // SIDE):
-                row = (at // SIDE + t) * pitch + offset
-                padded_ref[pl.ds(row, SIDE)] = message[t * SIDE : (t + 1) * SIDE]
-    for row in range(shape.rows_x):
-        padded_ref[row * pitch : row * pitch + tile_y] = message_ref[
-            row * tile_y : (row + 1) * tile_y
-        ]
-
-    first, second = first_ref[shape.side :], second_ref[shape.side :]
-    stack = jnp.concatenate(
-        [stack_ref[...], jnp.where(even, second, first), jnp.where(even, first, second)], axis=0
-    )
-    cotangent = dot(place_ref[0], stack)
-    mask = dot(place_ref[1], stack[:, :128]).astype(BF16)
-    near = dot(mask, spread_ref[0])
-    far = dot(mask, spread_ref[1])
-    windows = []
-    for at_x in range(shape.out_x):
-        rows = slice(at_x * SLOTS, (at_x + 1) * SLOTS)
-        windows.append(near[rows] * match_ref[0] + far[rows] * match_ref[1])
-        level_ref[rows] = (
-            dot(
-                windows[-1].astype(BF16),
-                padded_ref[4 * at_x * pitch : 4 * at_x * pitch + shape.window],
-            )
-            / 6.0
-        ).astype(BF16)
-    turned = jnp.concatenate(windows, axis=0).T
-    node_x = lax.broadcasted_iota(jnp.int32, (tile_y, shape.nodes), 1) // SLOTS
-    for at_x in range(shape.tile_x):
-        quotient, rest = (at_x + REACH) // 4, (at_x + REACH) % 4
-        cover = jnp.where(node_x == quotient, turned[rest * pitch : rest * pitch + tile_y], 0.0)
-        if rest < 2:
-            again = (rest + 4) * pitch
-            cover = cover + jnp.where(
-                node_x == quotient - 1, turned[again : again + tile_y], 0.0
-            )
-        cover = cover.astype(BF16)
-        cover_ref[at_x * tile_y : (at_x + 1) * tile_y] = jnp.concatenate([cover, cover], axis=1)
-
-    level_one = level_ref[...]
+def mesh_kernel(
+    shape,
+    place_ref,
+    first_ref,
+    second_ref,
+    message_ref,
+    edges_ref,
+    cotangent_ref,
+    w_embed_ref,
+    w_message_ref,
+    w_one_ref,
+    w_two_ref,
+    level_ref,
+    to_near_ref,
+    to_between_ref,
+    one_ref,
+    one_bar_ref,
+    two_ref,
+    two_bar_ref,
+    messages_ref,
+):
+    even = place_ref[1] % 2 == 0
+    center = shape.center
+    first, second = first_ref[:COLUMN], second_ref[:COLUMN]
+    left, right = jnp.where(even, second, first), jnp.where(even, first, second)
+    blended = jnp.concatenate([left, right], axis=0)
+    latent = (blended.astype(F32) + silu(dot(blended, w_embed_ref[...]))).astype(BF16)
+    messages_ref[:center] = message_ref[...]
+    messages_ref[center:] = silu(dot(latent, w_message_ref[...])).astype(BF16)
+    level_one = (dot(edges_ref[...], messages_ref[...]) / 6.0).astype(BF16)
+
+    nodes, node_y = shape.nodes, shape.node_y
+    node = lax.broadcasted_iota(jnp.int32, (nodes, nodes), 0)
+    other = lax.broadcasted_iota(jnp.int32, (nodes, nodes), 1)
+    same = (node // (2 * node_y) == other // (2 * node_y)) & (
+        node % node_y // 2 == other % node_y // 2
+    )
+    quad = jnp.where(same, 1.0, 0.0).astype(BF16)
     pre_one = dot(level_one, w_one_ref[...])
     value, slope_one = silu_and_slope(pre_one)
-    state_one = level_one.astype(F32) + value
-    level_two = (0.25 * dot(quad_ref[...], two_halves(state_one))).astype(BF16)
+    high, low = both_parts(level_one.astype(F32) + value)
+    level_two = (0.25 * (dot(quad, high) + dot(quad, low))).astype(BF16)
     pre_two = dot(level_two, w_two_ref[...])
-    two_bar = dot(quad_ref[:, : shape.nodes], cotangent.astype(BF16))
+    two_bar = dot(quad, cotangent_ref[...])
     pre_two_bar = (two_bar * silu_and_slope(pre_two)[1]).astype(BF16)
     pooled_bar = two_bar + dot_right_t(pre_two_bar, w_two_ref[...])
-    one_bar = cotangent + 0.25 * pooled_bar
+    one_bar = cotangent_ref[...].astype(F32) + 0.25 * pooled_bar
     pre_one_bar = (one_bar * slope_one).astype(BF16)
-    level_bar = one_bar + dot_right_t(pre_one_bar, w_one_ref[...])
-
-    node = lax.broadcasted_iota(jnp.int32, (shape.nodes, channels), 0)
-    at_x, at_y = node // SLOTS, node % SLOTS
-    owned = (at_x >= NODES_OUT) & (at_x < NODES_OUT + shape.node_x)
-    owned = owned & (at_y >= NODES_OUT) & (at_y < NODES_OUT + shape.node_y)
-    first = owned & (at_x % 2 == 0) & (at_y % 2 == 0)
-    grads_ref[3 * channels : 4 * channels] = dot_left_t(
-        level_one, jnp.where(owned, pre_one_bar.astype(F32), 0.0).astype(BF16)
-    )
-    grads_ref[4 * channels :] = dot_left_t(
-        level_two, jnp.where(first, pre_two_bar.astype(F32), 0.0).astype(BF16)
-    )
-
-    both = two_halves(level_bar)
+    level_ref[...] = one_bar + dot_right_t(pre_one_bar, w_one_ref[...])
+    upward = place_ref[0] % 2 == 0
+    for ref, last in ((to_near_ref, upward), (to_between_ref, jnp.logical_not(upward))):
+        start = pl.multiple_of(jnp.where(last, nodes - node_y, 0), 8)
+        value = level_ref[pl.ds(start, node_y)]
+        high = value.astype(BF16).astype(F32)
+        ref[...] = jnp.concatenate([high, value - high], axis=0).astype(BF16)
+    node = lax.broadcasted_iota(jnp.int32, pre_two_bar.shape, 0)
+    chosen = (node // node_y % 2 == 0) & (node % 2 == 0)
+    one_ref[...] = level_one
+    one_bar_ref[...] = pre_one_bar
+    two_ref[...] = level_two
+    two_bar_ref[...] = jnp.where(chosen, pre_two_bar.astype(F32), 0.0).astype(BF16)
+
+
+def cover_kernel(
+    shape,
+    place_ref,
+    first_ref,
+    second_ref,
+    masks_ref,
+    one_ref,
+    one_bar_ref,
+    two_ref,
+    two_bar_ref,
+    cover_ref,
+    grads_ref,
+):
+    even = place_ref[1] % 2 == 0
+    first = first_ref[COLUMN:, :128].astype(F32)[:8]
+    second = second_ref[COLUMN:, :128].astype(F32)[:8]
+    left, right = jnp.where(even, second, first), jnp.where(even, first, second)
+    masks = jnp.concatenate([masks_ref[:, :128].astype(F32), left, right], axis=0).astype(BF16)
+    lane = lax.broadcasted_iota(jnp.int32, (1, shape.cells), 1)
+    node_x, node_y = shape.node_places(shape.all_nodes)
+    row, column = lane // shape.tile_y + 1, lane % shape.tile_y + 1
+    edges = edge_matrix(masks, node_x, node_y, row, column)
+    cover_ref[...] = jnp.concatenate([edges, edges], axis=0).T.astype(BF16)
+    channels = grads_ref.shape[1]
+    grads_ref[:channels] = dot_left_t(one_ref[...], one_bar_ref[...])
+    grads_ref[channels:] = dot_left_t(two_ref[...], two_bar_ref[...])
+
+
+def turn_kernel(
+    shape, place_ref, level_ref, near_ref, between_ref, near_levels_ref, first_ref, second_ref
+):
+    even = place_ref[0] % 2 == 0
+    node_y = shape.node_y
+    near = near_ref[...].astype(F32)
+    between = between_ref[...].astype(F32)
+    near, between = near[:node_y] + near[node_y:], between[:node_y] + between[node_y:]
+    levels = jnp.concatenate(
+        [level_ref[...], jnp.where(even, between, near), jnp.where(even, near, between)], axis=0
+    )
+    near_levels_ref[...] = levels
+    high, low = both_parts(levels)
+    node = lax.broadcasted_iota(jnp.int32, (8, shape.near_nodes), 1)
+    line = lax.broadcasted_iota(jnp.int32, (8, shape.near_nodes), 0)
+    lower = node >= shape.nodes + node_y
+    node_x = jnp.where(node < shape.nodes, node // node_y, jnp.where(lower, shape.node_x, -1))
+    narrow_even = place_ref[1] % 2 == 0
+    for ref, last in ((first_ref, narrow_even), (second_ref, jnp.logical_not(narrow_even))):
+        column = jnp.where(last, node_y - 1, 0)
+        hit = (node_x == line - 1) & (node % node_y == column)
+        hit = jnp.where(hit, 1.0, 0.0).astype(BF16)
+        ref[...] = jnp.concatenate([dot(hit, high), dot(hit, low)], axis=0).astype(BF16)
+
+
+def backward_kernel(
+    shape,
+    total_rows,
+    place_ref,
+    levels_ref,
+    first_ref,
+    second_ref,
+    cover_ref,
+    mesh_grads_ref,
+    blended_ref,
+    latent_ref,
+    embed_ref,
+    slope_ref,
+    rows_ref,
+    key_ref,
+    w_force_ref,
+    w_embed_ref,
+    w_message_ref,
+    state_ref,
+    back_ref,
+    sent_ref,
+    kept_ref,
+    pmb_ref,
+    peb_ref,
+    grads_ref,
+):
+    channels = blended_ref.shape[1]
+    even = place_ref[1] % 2 == 0
+    first, second = first_ref[...].astype(F32), second_ref[...].astype(F32)
+    first, second = first[:8] + first[8:], second[:8] + second[8:]
+    left, right = jnp.where(even, second, first), jnp.where(even, first, second)
+    high, low = both_parts(jnp.concatenate([levels_ref[...], left, right], axis=0))
+    both = jnp.concatenate([high, low], axis=0)
     for at, n in pieces(0, shape.cells, 128):
         rows = slice(at, at + n)
         message_bar = dot(cover_ref[rows], both) / 6.0
@@ -431,6 +442,7 @@
     own = slice(shape.halo, shape.halo + shape.cells)
     grads_ref[channels : 2 * channels] = dot_left_t(blended_ref[own], peb_ref[...])
     grads_ref[2 * channels : 3 * channels] = dot_left_t(latent_ref[...], pmb_ref[...])
+    grads_ref[3 * channels :] = mesh_grads_ref[...]
 
     width = min(total_rows, LANES)
     cell = lax.broadcasted_iota(jnp.int32, (shape.cells, width), 0) + shape.halo
@@ -445,7 +457,7 @@
     grads_ref[:channels] = grad_force
 
     half = sent_ref.shape[0]
-    upper = narrow_ref[0] % 2
+    upper = place_ref[1] % 2
     kept_at = pl.multiple_of(upper * half, half)
     sent_at = pl.multiple_of((1 - upper) * half, half)
     sent_ref[...] = grads_ref[pl.ds(sent_at, half)].astype(BF16)
@@ -502,12 +514,6 @@
     narrow_at = lax.axis_index("narrow")
     held_rows = boundary_rows.shape[0]
     shape = Shape(tile_x, tile_y)
-    table = shape.tables()
-    table = {
-        name: jnp.asarray(value, F32 if name == "match" else BF16)
-        for name, value in table.items()
-    }
-
     live = jnp.arange(held_rows) < row_count[0]
     column = target_y - narrow_at * tile_y
     whole_column = wide_count == 4 and held_rows * wide_count <= LANES
@@ -544,8 +550,8 @@
     mask = g2m_mask.transpose(1, 2, 0).reshape(-1, 36)
     place = jnp.stack([wide_at, narrow_at])
     struct = jax.ShapeDtypeStruct
-    long = struct((shape.halo + 2 * shape.edge + unit_rows + 16, channels), BF16)
-    plain = struct((shape.halo + 2 * shape.edge, channels), BF16)
+    long = struct((shape.halo + BLOCK + unit_rows + 16, channels), BF16)
+    plain = struct((shape.halo + BLOCK, channels), BF16)
     short = struct((unit_rows + 16, channels), BF16)
     (place,) = call(
         open_kernel,
@@ -556,13 +562,12 @@
         flops=LONG,
     )
     if whole_column:
-        first, second, third, fourth, mesh, own_rows = call(
+        first, second, third, fourth, mask, own_rows = call(
             functools.partial(pack_kernel, shape, units),
-            [long, plain, short, short, struct((2 * shape.own_nodes, channels), BF16), short],
+            [long, plain, short, short, struct((shape.nodes, channels), F32), short],
             [
                 place,
                 cells,
-                cotangent,
                 mask,
                 rows,
                 target_x.reshape(1, -1),
@@ -581,49 +586,90 @@
         def with_meta(slot):
             return [rows, meta_rows(row_live, row_x, row_y, tile_x, unit_rows, slot, units)]
 
-        mask = jnp.pad(mask.astype(BF16), ((0, 0), (0, channels - 36)))
-        mesh = jnp.concatenate([cotangent, mask])
+        mask = jnp.pad(mask.astype(F32), ((0, 0), (0, channels - 36)))
         own_rows = jnp.concatenate(with_meta(0))
-        edge = shape.edge
-        to_prev = [cells[: shape.halo], cotangent[:edge], mask[:edge]]
-        to_next = [cells[-shape.halo :], cotangent[-edge:], mask[-edge:]]
-        to_prev, to_next = jnp.concatenate(to_prev), jnp.concatenate(to_next)
+        line = shape.node_y
+        blank = jnp.zeros((BLOCK - line, channels), BF16)
+        to_prev = jnp.concatenate([cells[: shape.halo], mask[:line].astype(BF16), blank])
+        to_next = jnp.concatenate([cells[-shape.halo :], mask[-line:].astype(BF16), blank])
         upward = wide_at % 2 == 0
         first = jnp.concatenate([jnp.where(upward, to_next, to_prev)] + with_meta(1))
         second = jnp.concatenate([jnp.where(upward, to_prev, to_next)] + with_meta(2))
         arrived = [swapped(first, "wide", 1), swapped_between(second, "wide")]
 
     total_rows = unit_rows * units
-    stack_rows = 4 * shape.edge + 2 * shape.own_nodes
-    payload = struct((shape.side + 2 * shape.side_nodes, channels), BF16)
-    blended, first, second, stack, all_rows, keys = call(
+    payload = struct((COLUMN + BLOCK, channels), BF16)
+    blended, first, second, masks, all_rows, keys = call(
         functools.partial(blend_kernel, shape, units, unit_rows),
         [
             struct((shape.center, channels), BF16),
             payload,
             payload,
-            struct((stack_rows, channels), BF16),
+            struct((shape.near_nodes, channels), BF16),
             struct((total_rows, channels), BF16),
             struct((8, total_rows), jnp.int32),
         ],
-        [place, cells, mesh, w_force, table["to_side"], own_rows] + arrived,
+        [place, cells, mask, w_force, own_rows] + arrived,
         scratch=[pltpu.VMEM((total_rows, channels), BF16)],
         spaces="s",
         flops=2 * shape.center * total_rows * channels,
     )
     second = swapped_between(second, "narrow")
     first = swapped(first, "narrow", 1)
-    message, latent, embed_slope, message_slope = call(
+    message, latent, embed_slope, message_slope, edges = call(
         functools.partial(forward_kernel, shape),
         [
             struct((shape.center, channels), BF16),
             struct((shape.cells, channels), BF16),
             struct((shape.cells, channels), F32),
             struct((shape.cells, channels), F32),
+            struct((shape.nodes, shape.center + 2 * COLUMN), BF16),
         ],
-        [blended, w_embed, w_message],
+        [blended, masks, w_embed, w_message],
         flops=4 * shape.center * channels * channels,
     )
+    nodes = struct((shape.nodes, channels), BF16)
+    line = struct((2 * shape.node_y, channels), BF16)
+    level, to_near, to_between, *mesh_terms = call(
+        functools.partial(mesh_kernel, shape),
+        [struct((shape.nodes, channels), F32), line, line, nodes, nodes, nodes, nodes],
+        [
+            place,
+            first,
+            second,
+            message,
+            edges,
+            cotangent,
+            w_embed,
+            w_message,
+            w_level_one,
+            w_level_two,
+        ],
+        scratch=[pltpu.VMEM((shape.center + 2 * COLUMN, channels), BF16)],
+        spaces="s",
+        flops=2 * shape.center * channels * channels,
+    )
+    from_between = swapped_between(to_between, "wide")
+    from_near = swapped(to_near, "wide", 1)
+    cover, mesh_grads = call(
+        functools.partial(cover_kernel, shape),
+        [
+            struct((shape.cells, 2 * shape.all_nodes), BF16),
+            struct((2 * channels, channels), F32),
+        ],
+        [place, first, second, masks] + mesh_terms,
+        spaces="s",
+        flops=2 * shape.center * channels * channels,
+    )
+    side = struct((16, channels), BF16)
+    levels, first, second = call(
+        functools.partial(turn_kernel, shape),
+        [struct((shape.near_nodes, channels), F32), side, side],
+        [place, level, from_near, from_between],
+        spaces="s",
+    )
+    second = swapped_between(second, "narrow")
+    first = swapped(first, "narrow", 1)
     grad_rows_total = 5 * channels
     grad_state, back, sent, kept = call(
         functools.partial(backward_kernel, shape, total_rows),
@@ -634,31 +680,23 @@
             struct((grad_rows_total // 2, channels), F32),
         ],
         [
-            narrow_at.reshape(1),
+            place,
+            levels,
             first,
             second,
-            stack,
+            cover,
+            mesh_grads,
             blended,
-            message,
             latent,
             embed_slope,
             message_slope,
             all_rows,
             keys,
-            table["place"],
-            table["spread"],
-            table["match"],
-            table["quad"],
             w_force,
             w_embed,
             w_message,
-            w_level_one,
-            w_level_two,
         ],
         scratch=[
-            pltpu.VMEM((shape.rows_x * shape.pitch, channels), BF16),
-            pltpu.VMEM((shape.nodes, channels), BF16),
-            pltpu.VMEM((shape.cells, 2 * shape.nodes), BF16),
             pltpu.VMEM((shape.cells, channels), BF16),
             pltpu.VMEM((shape.cells, channels), BF16),
             pltpu.VMEM((grad_rows_total, channels), F32),

time: 62.8 us -> 71.6 us (1.14)
  starting transfers between devices: 29.9 us -> 34 us
  waiting for transfers between devices: 20.8 us -> 23.6 us
  Pallas kernels: 7.54 us -> 9.47 us
    ppermute x14 -> x16, starting transfers between devices: 28.5 us -> 31.4 us  [swapped(): return lax.ppermute(block, axis, [(i, i ^ bits) for i in range(count)])]
    ppermute x14 -> x16, waiting for transfers between devices: 20.8 us -> 23.6 us  [swapped(): return lax.ppermute(block, axis, [(i, i ^ bits) for i in range(count)])]
    pallas_call x5 -> x8, Pallas kernels: 7.54 us -> 9.47 us  [call(): pl.pallas_call(kernel, out_shape=tuple(out_shapes), in_specs=[pl.BlockSpe...]
    ppermute x2 -> x4, starting transfers between devices: 1.34 us -> 2.62 us  [swapped_between(): return lax.ppermute(block, axis, pairs + [(j, i) for i, j in pairs])]
  transfers between devices with their start and end apart: 16 -> 20, of which waited for: 11 -> 10; matrix products, arithmetic and copies ran while one was open for 1% -> 1% of each run, Pallas kernels for 1% -> 2%
where the time goes in v6:
time: 71.6 us; the launch traced here: 71.4 us
  starting transfers between devices  34 us (47%)
  waiting for transfers between devices  23.6 us (33%)
  Pallas kernels  9.47 us (13%)
  other arithmetic  2.48 us (3%)
  between operations  1.66 us (2%)
    ppermute x16, starting transfers between devices, swapped(): return lax.ppermute(block, axis, [(i, i ^ bits) for i in range(count)])  31.4 us
    ppermute x16, waiting for transfers between devices, swapped(): return lax.ppermute(block, axis, [(i, i ^ bits) for i in range(count)])  23.6 us
    pallas_call x8, Pallas kernels, call(): pl.pallas_call(kernel, out_shape=tuple(out_shapes), in_specs=[pl.BlockSpe...  9.47 us
    ppermute x4, starting transfers between devices, swapped_between(): return lax.ppermute(block, axis, pairs + [(j, i) for i, j in pairs])  2.62 us
  transfers between devices with their start and end apart: 20, of which 10 were waited for; matrix products, arithmetic and copies ran while one was open for 1% of the time, Pallas kernels for 2%

profile of v6, /device:TPU:0, one launch (start us, length us, event | category | flops | bytes accessed | tf_op | source)
XLA Modules:
  0.0 71.4 jit_solution(6614416666358994425)
XLA Ops:
  0.7 1.1 %shard_map.148.place_ref.refs_0_ = s32[2]{0:T(128)S(1)} custom-call(s32[2]{0:T(128)S(1)} %pad_add_fusion.place_ref), custom_call_target="tpu_custom_call" | custom-call | flops 10000000000 | bytes 16 | tf_op jit(solution)/shard_map/pallas_call | solution.py:471
  2.6 0.7 %shard_map.149 = (bf16[96,256]{1,0:T(8,128)(2,1)S(1)}, bf16[48,256]{1,0:T(8,128)(2,1)S(1)}, bf16[48,256]{1,0:T(8,128)(2,1)S(1)}, bf16[48,256]{1,0:T(8,128)(2,1)S...) custom-call(s32[2]{0:T(128)S(1)} %shard_map.148.place_ref.refs_0_, bf16[512,256]{1,0:T(8,128)(2,1)S(1)} %bitcast.14, ...), custom_call_target="tpu_custom_call" | custom-call | flops 10000000000 | bytes 463628 | tf_op jit(solution)/shard_map/pallas_call | solution.py:471
  3.4 3.0 %collective-permute-start = (bf16[96,256]{1,0:T(8,128)(2,1)S(1)}, bf16[96,256]{1,0:T(8,128)(2,1)S(1)}, u32[]{:S(2)}, u32[]{:S(2)}) collective-permute-start(bf16[96,256]{1,0:T(8,128)(2,1)S(1)} %get-tuple-element.38), channel_id=1, source_target_pairs={{0,4},{4,0},{8,12},{12,8},{1,5},{5,1},{9,13},{13,9},{2,6},{6,2},{1... | collective-permute-start | bytes 147464 | tf_op jit(solution)/shard_map/ppermute | solution.py:25
  6.4 0.7 collective-permute-start.1
  7.1 3.9 %collective-permute-start.2 = (bf16[48,256]{1,0:T(8,128)(2,1)S(1)}, bf16[48,256]{1,0:T(8,128)(2,1)S(1)}, u32[]{:S(2)}, u32[]{:S(2)}) collective-permute-start(bf16[48,256]{1,0:T(8,128)(2,1)S(1)} %get-tuple-element.40), channel_id=1, source_target_pairs={{0,8},{4,12},{8,0},{12,4},{1,9},{5,13},{9,1},{13,5},{2,10},{6,14},... | collective-permute-start | bytes 73736 | tf_op jit(solution)/shard_map/ppermute | solution.py:25
  11.0 2.9 %collective-permute-start.3 = (bf16[48,256]{1,0:T(8,128)(2,1)S(1)}, bf16[48,256]{1,0:T(8,128)(2,1)S(1)}, u32[]{:S(2)}, u32[]{:S(2)}) collective-permute-start(bf16[48,256]{1,0:T(8,128)(2,1)S(1)} %get-tuple-element.41), channel_id=1, source_target_pairs={{0,12},{4,8},{8,4},{12,0},{1,13},{5,9},{9,5},{13,1},{2,14},{6,10},... | collective-permute-start | bytes 73736 | tf_op jit(solution)/shard_map/ppermute | solution.py:25
  13.9 2.7 %collective-permute-done.3.refs_8_ = bf16[48,256]{1,0:T(8,128)(2,1)S(1)} collective-permute-done((bf16[48,256]{1,0:T(8,128)(2,1)S(1)}, bf16[48,256]{1,0:T(8,128)(2,1)S(1)}, u32[]{:S(2)}, u32[]{:S(2)}) %collective-permute-start.3) | collective-permute-done | bytes 24608 | tf_op jit(solution)/shard_map/ppermute | solution.py:25
  16.6 1.1 %shard_map.150 = (bf16[576,256]{1,0:T(8,128)(2,1)S(1)}, bf16[48,256]{1,0:T(8,128)(2,1)S(1)}, bf16[48,256]{1,0:T(8,128)(2,1)S(1)}, bf16[48,256]{1,0:T(8,128)(2,1)...) custom-call(s32[2]{0:T(128)S(1)} %shard_map.148.place_ref.refs_0_, bf16[512,256]{1,0:T(8,128)(2,1)S(1)} %bitcast.15, ...), custom_call_target="tpu_custom_call" | custom-call | flops 37748736 | bytes 1011720 | tf_op jit(solution)/shard_map/pallas_call | solution.py:471
  17.8 0.7 collective-permute-start.5
  18.5 0.7 %shard_map.151 = (bf16[576,256]{1,0:T(8,128)(2,1)S(1)}, bf16[512,256]{1,0:T(8,128)(2,1)S(1)}, f32[512,256]{1,0:T(8,128)S(1)}, f32[512,256]{1,0:T(8,128)S(1)}, bf16[32,640]{1,0:T(8,128)(2,1)S(1)}) custom-call(bf16[576,256]{1,0:T(8,128)(2,1)S(1)} %get-tuple-element.44.blended_ref, bf16[48,256]{1,0:T(8,128)(2,1)S(1)} %get-tuple-element.45.masks_ref, ...), custom_call_target="tpu_custom_call" | custom-call | flops 150994944 | bytes 2228224 | tf_op jit(solution)/shard_map/pallas_call | solution.py:471
  19.3 1.6 %shard_map.152 = (f32[32,256]{1,0:T(8,128)S(1)}, bf16[16,256]{1,0:T(8,128)(2,1)S(1)}, bf16[16,256]{1,0:T(8,128)(2,1)S(1)}, bf16[32,256]{1,0:T(8,128)(2,1)S(1)}, ...) custom-call(s32[2]{0:T(128)S(1)} %shard_map.148.place_ref.refs_0_, ...), custom_call_target="tpu_custom_call" | custom-call | flops 75497472 | bytes 1040392 | tf_op jit(solution)/shard_map/pallas_call | solution.py:471
  21.0 0.7 collective-permute-start.7
  21.7 3.0 %collective-permute-done.6.near_ref = bf16[16,256]{1,0:T(8,128)(2,1)S(1)} collective-permute-done((bf16[16,256]{1,0:T(8,128)(2,1)S(1)}, bf16[16,256]{1,0:T(8,128)(2,1)S(1)}, u32[]{:S(2)}, u32[]{:S(2)}) %collective-permute-start.6) | collective-permute-done | bytes 8224 | tf_op jit(solution)/shard_map/ppermute | solution.py:25
  24.6 0.7 shard_map.153
  25.3 3.0 %collective-permute-start.8 = (bf16[16,256]{1,0:T(8,128)(2,1)S(1)}, bf16[16,256]{1,0:T(8,128)(2,1)S(1)}, u32[]{:S(2)}, u32[]{:S(2)}) collective-permute-start(bf16[16,256]{1,0:T(8,128)(2,1)S(1)} %get-tuple-element.52), channel_id=1, source_target_pairs={{0,1},{1,0},{2,3},{3,2},{4,5},{5,4},{6,7},{7,6},{8,9},{9,8},{10,11... | collective-permute-start | bytes 24584 | tf_op jit(solution)/shard_map/ppermute | solution.py:25
  29.0 0.9 %shard_map.154 = (bf16[512,128]{1,0:T(8,128)(2,1)S(1)}, f32[512,256]{1,0:T(8,128)S(1)}) custom-call(s32[2]{0:T(128)S(1)} %shard_map.148.place_ref.refs_0_, bf16[48,256]{1,0:T(8,128)(2,1)S(1)} %collective-permute-done.4.first_ref, bf16[48,256]{1,0:T(8,128)(2,1)S(1)} %collective-permute-done.5.second_ref, bf16[48,256]{1,0:T(8,128)(2,1)S(1)} %get-tuple-element.45.masks_ref, ...), custom_call_target="tpu_custom_call" | custom-call | flops 75497472 | bytes 794632 | tf_op jit(solution)/shard_map/pallas_call | solution.py:471
  30.0 2.5 %shard_map.155 = (bf16[512,256]{1,0:T(8,128)(2,1)}, bf16[128,256]{1,0:T(8,128)(2,1)S(1)}, bf16[640,256]{1,0:T(8,128)(2,1)S(1)}, f32[640,256]{1,0:T(8,128)S(1)}) custom-call(s32[2]{0:T(128)S(1)} %shard_map.148.place_ref.refs_0_, f32[48,256]{1,0:T(8,128)S(1)} %get-tuple-element.51.levels_ref, bf16[16,256]{1,0:T(8,128)(2,1)S(1)} %collective-permute-done.8.first_ref, ...), custom_call_target="tpu_custom_call" | custom-call | flops 402653184 | bytes 4100104 | tf_op jit(solution)/shard_map/pallas_call | solution.py:471
  32.5 3.9 %collective-permute-start.10 = (bf16[640,256]{1,0:T(8,128)(2,1)S(1)}, bf16[640,256]{1,0:T(8,128)(2,1)S(1)}, u32[]{:S(2)}, u32[]{:S(2)}) collective-permute-start(bf16[640,256]{1,0:T(8,128)(2,1)S(1)} %get-tuple-element.68), channel_id=1, source_target_pairs={{0,1},{1,0},{2,3},{3,2},{4,5},{5,4},{6,7},{7,6},{8,9},{9,8},{10,11... | collective-permute-start | bytes 983048 | tf_op jit(solution)/shard_map/ppermute | solution.py:25
  36.4 1.3 %collective-permute-done.10 = bf16[640,256]{1,0:T(8,128)(2,1)S(1)} collective-permute-done((bf16[640,256]{1,0:T(8,128)(2,1)S(1)}, bf16[640,256]{1,0:T(8,128)(2,1)S(1)}, u32[]{:S(2)}, u32[]{:S(2)}) %collective-permute-start.10) | collective-permute-done | bytes 327712 | tf_op jit(solution)/shard_map/ppermute | solution.py:25
  37.8 2.0 %collective-permute-start.11 = (bf16[320,256]{1,0:T(8,128)(2,1)S(1)}, bf16[320,256]{1,0:T(8,128)(2,1)S(1)}, u32[]{:S(2)}, u32[]{:S(2)}) collective-permute-start(bf16[320,256]{1,0:T(8,128)(2,1)S(1)} %dynamic-slice_convert_fusion), channel_id=1, source_target_pairs={{0,2},{1,3},{2,0},{3,1},{4,6},{5,7},{6,4},{7,5},{8,10},{9,11},{10,... | collective-permute-start | bytes 491528 | tf_op jit(solution)/shard_map/ppermute | solution.py:25
  39.8 4.5 %collective-permute-done.11 = bf16[320,256]{1,0:T(8,128)(2,1)S(1)} collective-permute-done((bf16[320,256]{1,0:T(8,128)(2,1)S(1)}, bf16[320,256]{1,0:T(8,128)(2,1)S(1)}, u32[]{:S(2)}, u32[]{:S(2)}) %collective-permute-start.11) | collective-permute-done | bytes 163872 | tf_op jit(solution)/shard_map/ppermute | solution.py:25
  44.4 3.0 %collective-permute-start.12 = (bf16[112,256]{1,0:T(8,128)(2,1)S(1)}, bf16[112,256]{1,0:T(8,128)(2,1)S(1)}, u32[]{:S(2)}, u32[]{:S(2)}) collective-permute-start(bf16[112,256]{1,0:T(8,128)(2,1)S(1)} %pad_maximum_fusion), channel_id=1, source_target_pairs={{0,12},{4,8},{8,4},{12,0},{1,13},{5,9},{9,5},{13,1},{2,14},{6,10},... | collective-permute-start | bytes 172040 | tf_op jit(solution)/shard_map/ppermute | solution.py:25
  47.4 2.5 %collective-permute-start.13 = (bf16[112,256]{1,0:T(8,128)(2,1)S(1)}, bf16[112,256]{1,0:T(8,128)(2,1)S(1)}, u32[]{:S(2)}, u32[]{:S(2)}) collective-permute-start(bf16[112,256]{1,0:T(8,128)(2,1)S(1)} %pad_maximum_fusion.1), channel_id=1, source_target_pairs={{0,8},{4,12},{8,0},{12,4},{1,9},{5,13},{9,1},{13,5},{2,10},{6,14},... | collective-permute-start | bytes 172040 | tf_op jit(solution)/shard_map/ppermute | solution.py:25
  50.5 3.0 %collective-permute-done.13 = bf16[112,256]{1,0:T(8,128)(2,1)S(1)} collective-permute-done((bf16[112,256]{1,0:T(8,128)(2,1)S(1)}, bf16[112,256]{1,0:T(8,128)(2,1)S(1)}, u32[]{:S(2)}, u32[]{:S(2)}) %collective-permute-start.13) | collective-permute-done | bytes 57376 | tf_op jit(solution)/shard_map/ppermute | solution.py:25
  54.2 3.5 %collective-permute-start.15 = (bf16[80,256]{1,0:T(8,128)(2,1)S(1)}, bf16[80,256]{1,0:T(8,128)(2,1)S(1)}, u32[]{:S(2)}, u32[]{:S(2)}) collective-permute-start(bf16[80,256]{1,0:T(8,128)(2,1)S(1)} %get-tuple-element.70), channel_id=1, source_target_pairs={{0,12},{4,8},{8,4},{12,0},{1,13},{5,9},{9,5},{13,1},{2,14},{6,10},... | collective-permute-start | bytes 122888 | tf_op jit(solution)/shard_map/ppermute | solution.py:25
  57.7 0.9 %collective-permute-start.17 = (bf16[80,256]{1,0:T(8,128)(2,1)S(1)}, bf16[80,256]{1,0:T(8,128)(2,1)S(1)}, u32[]{:S(2)}, u32[]{:S(2)}) collective-permute-start(bf16[80,256]{1,0:T(8,128)(2,1)S(1)} %get-tuple-element.70), channel_id=1, source_target_pairs={{0,4},{4,0},{8,12},{12,8},{1,5},{5,1},{9,13},{13,9},{2,6},{6,2},{1... | collective-permute-start | bytes 122888 | tf_op jit(solution)/shard_map/ppermute | solution.py:25
  58.7 1.5 %collective-permute-done.15 = bf16[80,256]{1,0:T(8,128)(2,1)S(1)} collective-permute-done((bf16[80,256]{1,0:T(8,128)(2,1)S(1)}, bf16[80,256]{1,0:T(8,128)(2,1)S(1)}, u32[]{:S(2)}, u32[]{:S(2)}) %collective-permute-start.15) | collective-permute-done | bytes 40992 | tf_op jit(solution)/shard_map/ppermute | solution.py:25
  60.2 2.5 %collective-permute-done.16 = bf16[80,256]{1,0:T(8,128)(2,1)S(1)} collective-permute-done((bf16[80,256]{1,0:T(8,128)(2,1)S(1)}, bf16[80,256]{1,0:T(8,128)(2,1)S(1)}, u32[]{:S(2)}, u32[]{:S(2)}) %collective-permute-start.16) | collective-permute-done | bytes 40992 | tf_op jit(solution)/shard_map/ppermute | solution.py:25
  62.7 1.8 %collective-permute-start.18 = (bf16[320,256]{1,0:T(8,128)(2,1)S(1)}, bf16[320,256]{1,0:T(8,128)(2,1)S(1)}, u32[]{:S(2)}, u32[]{:S(2)}) collective-permute-start(bf16[320,256]{1,0:T(8,128)(2,1)S(1)} %constant_dynamic-update-slice_fusion), channel_id=1, source_target_pairs={{0,2},{1,3},{2,0},{3,1},{4,6},{5,7},{6,4},{7,5},{8,10},{9,11},{10,... | collective-permute-start | bytes 491528 | tf_op jit(solution)/shard_map/ppermute | solution.py:25
  64.4 3.6 %collective-permute-done.18 = bf16[320,256]{1,0:T(8,128)(2,1)S(1)} collective-permute-done((bf16[320,256]{1,0:T(8,128)(2,1)S(1)}, bf16[320,256]{1,0:T(8,128)(2,1)S(1)}, u32[]{:S(2)}, u32[]{:S(2)}) %collective-permute-start.18) | collective-permute-done | bytes 163872 | tf_op jit(solution)/shard_map/ppermute | solution.py:25
  68.9 1.0 %collective-permute-done.19 = bf16[640,256]{1,0:T(8,128)(2,1)S(1)} collective-permute-done((bf16[640,256]{1,0:T(8,128)(2,1)S(1)}, bf16[640,256]{1,0:T(8,128)(2,1)S(1)}, u32[]{:S(2)}, u32[]{:S(2)}) %collective-permute-start.19) | collective-permute-done | bytes 327712 | tf_op jit(solution)/shard_map/ppermute | solution.py:25
  70.1 1.2 %convert_multiply_fusion = f32[5,256,256]{2,1,0:T(8,128)} fusion(bf16[5,256,256]{2,1,0:T(8,128)(2,1)S(1)} %bitcast.20, f32[5]{0:T(128)S(1)} %copy-done.11), kind=kLoop, calls=%fused_computation | loop fusion | flops 655360 | bytes 1966100 | tf_op jit(solution)/shard_map/mul | solution.py:767
  (61 shorter events, 3.4 us)
Async XLA Ops:
  0.7 1.8 %copy-start.3 = (bf16[16,32,256]{2,1,0:T(8,128)(2,1)S(1)}, bf16[16,32,256]{2,1,0:T(8,128)(2,1)}, u32[]{:S(2)}) copy-start(bf16[16,32,256]{2,1,0:T(8,128)(2,1)} %param.13) | copy-start | bytes 786436
  0.7 1.8 %copy-start.7 = (s32[36,4,8]{0,2,1:T(8,128)S(1)}, s32[36,4,8]{0,2,1:T(8,128)}, u32[]{:S(2)}) copy-start(s32[36,4,8]{0,2,1:T(8,128)} %param.18) | copy-start | bytes 13828
  0.7 1.8 %copy-start.8 = (bf16[32,256]{1,0:T(8,128)(2,1)S(1)}, bf16[32,256]{1,0:T(8,128)(2,1)}, u32[]{:S(2)}) copy-start(bf16[32,256]{1,0:T(8,128)(2,1)} %rows_ref.1) | copy-start | bytes 49156
  0.7 1.8 %copy-start.9 = (s32[32]{0:T(128)S(1)}, s32[32]{0:T(128)}, u32[]{:S(2)}) copy-start(s32[32]{0:T(128)} %param.16) | copy-start | bytes 388
  0.7 1.8 %copy-start.10 = (s32[32]{0:T(128)S(1)}, s32[32]{0:T(128)}, u32[]{:S(2)}) copy-start(s32[32]{0:T(128)} %param.17) | copy-start | bytes 388
  2.6 14.0 %copy-start.2 = (bf16[256,256]{1,0:T(8,128)(2,1)S(1)}, bf16[256,256]{1,0:T(8,128)(2,1)}, u32[]{:S(2)}) copy-start(bf16[256,256]{1,0:T(8,128)(2,1)} %w_force_ref.1) | copy-start | bytes 393220
  2.6 15.9 %copy-start = (bf16[256,256]{1,0:T(8,128)(2,1)S(1)}, bf16[256,256]{1,0:T(8,128)(2,1)}, u32[]{:S(2)}) copy-start(bf16[256,256]{1,0:T(8,128)(2,1)} %w_embed_ref.5) | copy-start | bytes 393220
  2.6 15.9 %copy-start.1 = (bf16[256,256]{1,0:T(8,128)(2,1)S(1)}, bf16[256,256]{1,0:T(8,128)(2,1)}, u32[]{:S(2)}) copy-start(bf16[256,256]{1,0:T(8,128)(2,1)} %w_message_ref.5) | copy-start | bytes 393220
  2.6 16.7 %copy-start.4 = (bf16[256,256]{1,0:T(8,128)(2,1)S(1)}, bf16[256,256]{1,0:T(8,128)(2,1)}, u32[]{:S(2)}) copy-start(bf16[256,256]{1,0:T(8,128)(2,1)} %w_one_ref.1) | copy-start | bytes 393220
  2.6 16.7 %copy-start.5 = (bf16[256,256]{1,0:T(8,128)(2,1)S(1)}, bf16[256,256]{1,0:T(8,128)(2,1)}, u32[]{:S(2)}) copy-start(bf16[256,256]{1,0:T(8,128)(2,1)} %w_two_ref.1) | copy-start | bytes 393220
  2.6 16.7 %copy-start.6 = (bf16[4,8,256]{2,1,0:T(8,128)(2,1)S(1)}, bf16[4,8,256]{2,1,0:T(8,128)(2,1)}, u32[]{:S(2)}) copy-start(bf16[4,8,256]{2,1,0:T(8,128)(2,1)} %param.19) | copy-start | bytes 49156
  3.4 13.2 %collective-permute-start = (bf16[96,256]{1,0:T(8,128)(2,1)S(1)}, bf16[96,256]{1,0:T(8,128)(2,1)S(1)}, u32[]{:S(2)}, u32[]{:S(2)}) collective-permute-start(bf16[96,256]{1,0:T(8,128)(2,1)S(1)} %get-tuple-element.38), channel_id=1, source_target_pairs={{0,4},{4,0},{8,12},{12,8},{1,5},{5,1},{9,13},{13,9},{2,6},{6,2},{1... | collective-permute-start | bytes 147464 | tf_op jit(solution)/shard_map/ppermute | solution.py:25
  6.4 7.5 %collective-permute-start.1 = (bf16[48,256]{1,0:T(8,128)(2,1)S(1)}, bf16[48,256]{1,0:T(8,128)(2,1)S(1)}, u32[]{:S(2)}, u32[]{:S(2)}) collective-permute-start(bf16[48,256]{1,0:T(8,128)(2,1)S(1)} %get-tuple-element.39), channel_id=1, source_target_pairs={{4,8},{8,4},{5,9},{9,5},{6,10},{10,6},{7,11},{11,7},{20,24},{24,20... | collective-permute-start | bytes 73736 | tf_op jit(solution)/shard_map/ppermute | solution.py:31
  7.1 6.8 %collective-permute-start.2 = (bf16[48,256]{1,0:T(8,128)(2,1)S(1)}, bf16[48,256]{1,0:T(8,128)(2,1)S(1)}, u32[]{:S(2)}, u32[]{:S(2)}) collective-permute-start(bf16[48,256]{1,0:T(8,128)(2,1)S(1)} %get-tuple-element.40), channel_id=1, source_target_pairs={{0,8},{4,12},{8,0},{12,4},{1,9},{5,13},{9,1},{13,5},{2,10},{6,14},... | collective-permute-start | bytes 73736 | tf_op jit(solution)/shard_map/ppermute | solution.py:25
  11.0 5.6 %collective-permute-start.3 = (bf16[48,256]{1,0:T(8,128)(2,1)S(1)}, bf16[48,256]{1,0:T(8,128)(2,1)S(1)}, u32[]{:S(2)}, u32[]{:S(2)}) collective-permute-start(bf16[48,256]{1,0:T(8,128)(2,1)S(1)} %get-tuple-element.41), channel_id=1, source_target_pairs={{0,12},{4,8},{8,4},{12,0},{1,13},{5,9},{9,5},{13,1},{2,14},{6,10},... | collective-permute-start | bytes 73736 | tf_op jit(solution)/shard_map/ppermute | solution.py:25
  17.7 1.5 %collective-permute-start.4 = (bf16[48,256]{1,0:T(8,128)(2,1)S(1)}, bf16[48,256]{1,0:T(8,128)(2,1)S(1)}, u32[]{:S(2)}, u32[]{:S(2)}) collective-permute-start(bf16[48,256]{1,0:T(8,128)(2,1)S(1)} %get-tuple-element.42), channel_id=1, source_target_pairs={{0,1},{1,0},{2,3},{3,2},{4,5},{5,4},{6,7},{7,6},{8,9},{9,8},{10,11... | collective-permute-start | bytes 73736 | tf_op jit(solution)/shard_map/ppermute | solution.py:25
  17.8 1.5 %collective-permute-start.5 = (bf16[48,256]{1,0:T(8,128)(2,1)S(1)}, bf16[48,256]{1,0:T(8,128)(2,1)S(1)}, u32[]{:S(2)}, u32[]{:S(2)}) collective-permute-start(bf16[48,256]{1,0:T(8,128)(2,1)S(1)} %get-tuple-element.43), channel_id=1, source_target_pairs={{1,2},{2,1},{5,6},{6,5},{9,10},{10,9},{13,14},{14,13},{17,18},{18,... | collective-permute-start | bytes 73736 | tf_op jit(solution)/shard_map/ppermute | solution.py:31
  20.9 3.7 %collective-permute-start.6 = (bf16[16,256]{1,0:T(8,128)(2,1)S(1)}, bf16[16,256]{1,0:T(8,128)(2,1)S(1)}, u32[]{:S(2)}, u32[]{:S(2)}) collective-permute-start(bf16[16,256]{1,0:T(8,128)(2,1)S(1)} %get-tuple-element.49), channel_id=1, source_target_pairs={{0,4},{4,0},{8,12},{12,8},{1,5},{5,1},{9,13},{13,9},{2,6},{6,2},{1... | collective-permute-start | bytes 24584 | tf_op jit(solution)/shard_map/ppermute | solution.py:25
  21.0 3.6 %collective-permute-start.7 = (bf16[16,256]{1,0:T(8,128)(2,1)S(1)}, bf16[16,256]{1,0:T(8,128)(2,1)S(1)}, u32[]{:S(2)}, u32[]{:S(2)}) collective-permute-start(bf16[16,256]{1,0:T(8,128)(2,1)S(1)} %get-tuple-element.50), channel_id=1, source_target_pairs={{4,8},{8,4},{5,9},{9,5},{6,10},{10,6},{7,11},{11,7},{20,24},{24,20... | collective-permute-start | bytes 24584 | tf_op jit(solution)/shard_map/ppermute | solution.py:31
  25.3 4.6 %collective-permute-start.8 = (bf16[16,256]{1,0:T(8,128)(2,1)S(1)}, bf16[16,256]{1,0:T(8,128)(2,1)S(1)}, u32[]{:S(2)}, u32[]{:S(2)}) collective-permute-start(bf16[16,256]{1,0:T(8,128)(2,1)S(1)} %get-tuple-element.52), channel_id=1, source_target_pairs={{0,1},{1,0},{2,3},{3,2},{4,5},{5,4},{6,7},{7,6},{8,9},{9,8},{10,11... | collective-permute-start | bytes 24584 | tf_op jit(solution)/shard_map/ppermute | solution.py:25
  28.3 1.6 %collective-permute-start.9 = (bf16[16,256]{1,0:T(8,128)(2,1)S(1)}, bf16[16,256]{1,0:T(8,128)(2,1)S(1)}, u32[]{:S(2)}, u32[]{:S(2)}) collective-permute-start(bf16[16,256]{1,0:T(8,128)(2,1)S(1)} %get-tuple-element.53), channel_id=1, source_target_pairs={{1,2},{2,1},{5,6},{6,5},{9,10},{10,9},{13,14},{14,13},{17,18},{18,... | collective-permute-start | bytes 24584 | tf_op jit(solution)/shard_map/ppermute | solution.py:31
  32.5 5.2 %collective-permute-start.10 = (bf16[640,256]{1,0:T(8,128)(2,1)S(1)}, bf16[640,256]{1,0:T(8,128)(2,1)S(1)}, u32[]{:S(2)}, u32[]{:S(2)}) collective-permute-start(bf16[640,256]{1,0:T(8,128)(2,1)S(1)} %get-tuple-element.68), channel_id=1, source_target_pairs={{0,1},{1,0},{2,3},{3,2},{4,5},{5,4},{6,7},{7,6},{8,9},{9,8},{10,11... | collective-permute-start | bytes 983048 | tf_op jit(solution)/shard_map/ppermute | solution.py:25
  37.8 6.5 %collective-permute-start.11 = (bf16[320,256]{1,0:T(8,128)(2,1)S(1)}, bf16[320,256]{1,0:T(8,128)(2,1)S(1)}, u32[]{:S(2)}, u32[]{:S(2)}) collective-permute-start(bf16[320,256]{1,0:T(8,128)(2,1)S(1)} %dynamic-slice_convert_fusion), channel_id=1, source_target_pairs={{0,2},{1,3},{2,0},{3,1},{4,6},{5,7},{6,4},{7,5},{8,10},{9,11},{10,... | collective-permute-start | bytes 491528 | tf_op jit(solution)/shard_map/ppermute | solution.py:25
  44.4 6.1 %collective-permute-start.12 = (bf16[112,256]{1,0:T(8,128)(2,1)S(1)}, bf16[112,256]{1,0:T(8,128)(2,1)S(1)}, u32[]{:S(2)}, u32[]{:S(2)}) collective-permute-start(bf16[112,256]{1,0:T(8,128)(2,1)S(1)} %pad_maximum_fusion), channel_id=1, source_target_pairs={{0,12},{4,8},{8,4},{12,0},{1,13},{5,9},{9,5},{13,1},{2,14},{6,10},... | collective-permute-start | bytes 172040 | tf_op jit(solution)/shard_map/ppermute | solution.py:25
  47.4 6.1 %collective-permute-start.13 = (bf16[112,256]{1,0:T(8,128)(2,1)S(1)}, bf16[112,256]{1,0:T(8,128)(2,1)S(1)}, u32[]{:S(2)}, u32[]{:S(2)}) collective-permute-start(bf16[112,256]{1,0:T(8,128)(2,1)S(1)} %pad_maximum_fusion.1), channel_id=1, source_target_pairs={{0,8},{4,12},{8,0},{12,4},{1,9},{5,13},{9,1},{13,5},{2,10},{6,14},... | collective-permute-start | bytes 172040 | tf_op jit(solution)/shard_map/ppermute | solution.py:25
  49.9 4.2 %collective-permute-start.14 = (bf16[112,256]{1,0:T(8,128)(2,1)S(1)}, bf16[112,256]{1,0:T(8,128)(2,1)S(1)}, u32[]{:S(2)}, u32[]{:S(2)}) collective-permute-start(bf16[112,256]{1,0:T(8,128)(2,1)S(1)} %pad_maximum_fusion.2), channel_id=1, source_target_pairs={{0,4},{4,0},{8,12},{12,8},{1,5},{5,1},{9,13},{13,9},{2,6},{6,2},{1... | collective-permute-start | bytes 172040 | tf_op jit(solution)/shard_map/ppermute | solution.py:25
  54.2 16.0 %copy-start.11 = (f32[5]{0:T(128)S(1)}, f32[5]{0:T(128)}, u32[]{:S(2)}) copy-start(f32[5]{0:T(128)} %constant.57) | copy-start | bytes 64
  54.2 6.0 %collective-permute-start.15 = (bf16[80,256]{1,0:T(8,128)(2,1)S(1)}, bf16[80,256]{1,0:T(8,128)(2,1)S(1)}, u32[]{:S(2)}, u32[]{:S(2)}) collective-permute-start(bf16[80,256]{1,0:T(8,128)(2,1)S(1)} %get-tuple-element.70), channel_id=1, source_target_pairs={{0,12},{4,8},{8,4},{12,0},{1,13},{5,9},{9,5},{13,1},{2,14},{6,10},... | collective-permute-start | bytes 122888 | tf_op jit(solution)/shard_map/ppermute | solution.py:25
  57.7 4.9 %collective-permute-start.16 = (bf16[80,256]{1,0:T(8,128)(2,1)S(1)}, bf16[80,256]{1,0:T(8,128)(2,1)S(1)}, u32[]{:S(2)}, u32[]{:S(2)}) collective-permute-start(bf16[80,256]{1,0:T(8,128)(2,1)S(1)} %get-tuple-element.70), channel_id=1, source_target_pairs={{0,8},{4,12},{8,0},{12,4},{1,9},{5,13},{9,1},{13,5},{2,10},{6,14},... | collective-permute-start | bytes 122888 | tf_op jit(solution)/shard_map/ppermute | solution.py:25
  57.7 4.9 %collective-permute-start.17 = (bf16[80,256]{1,0:T(8,128)(2,1)S(1)}, bf16[80,256]{1,0:T(8,128)(2,1)S(1)}, u32[]{:S(2)}, u32[]{:S(2)}) collective-permute-start(bf16[80,256]{1,0:T(8,128)(2,1)S(1)} %get-tuple-element.70), channel_id=1, source_target_pairs={{0,4},{4,0},{8,12},{12,8},{1,5},{5,1},{9,13},{13,9},{2,6},{6,2},{1... | collective-permute-start | bytes 122888 | tf_op jit(solution)/shard_map/ppermute | solution.py:25
  62.7 5.4 %collective-permute-start.18 = (bf16[320,256]{1,0:T(8,128)(2,1)S(1)}, bf16[320,256]{1,0:T(8,128)(2,1)S(1)}, u32[]{:S(2)}, u32[]{:S(2)}) collective-permute-start(bf16[320,256]{1,0:T(8,128)(2,1)S(1)} %constant_dynamic-update-slice_fusion), channel_id=1, source_target_pairs={{0,2},{1,3},{2,0},{3,1},{4,6},{5,7},{6,4},{7,5},{8,10},{9,11},{10,... | collective-permute-start | bytes 491528 | tf_op jit(solution)/shard_map/ppermute | solution.py:25
  68.2 1.7 %collective-permute-start.19 = (bf16[640,256]{1,0:T(8,128)(2,1)S(1)}, bf16[640,256]{1,0:T(8,128)(2,1)S(1)}, u32[]{:S(2)}, u32[]{:S(2)}) collective-permute-start(bf16[640,256]{1,0:T(8,128)(2,1)S(1)} %maximum_select_fusion.1), channel_id=1, source_target_pairs={{0,1},{1,0},{2,3},{3,2},{4,5},{5,4},{6,7},{7,6},{8,9},{9,8},{10,11... | collective-permute-start | bytes 983048 | tf_op jit(solution)/shard_map/ppermute | solution.py:25

commit v7 on v5

--- a/solution.py
+++ b/solution.py
@@ -259,8 +259,6 @@
     )
     stack_ref[...] = stack
     narrow_even = place_ref[1] % 2 == 0
-    column = pl.multiple_of(jnp.where(narrow_even, shape.tile_y - SIDE, 0), SIDE)
-    other = pl.multiple_of(jnp.where(narrow_even, 0, shape.tile_y - SIDE), SIDE)
     to_left = dot(side_ref[0], stack).astype(BF16)
     to_right = dot(side_ref[1], stack).astype(BF16)
     first_ref[shape.side :] = jnp.where(narrow_even, to_right, to_left)
@@ -281,11 +279,15 @@
         for k, key in enumerate(keys):
             hit = jnp.where(cell == key, 1.0, 0.0).astype(BF16)
             value = value + dot(hit, projected_ref[k * width : (k + 1) * width])
-        blended_ref[first : first + n] = value.astype(BF16)
-    for row in range(shape.rows_x):
-        target = slice(row * SIDE, (row + 1) * SIDE)
-        first_ref[target] = blended_ref[pl.ds(row * tile_y + column, SIDE)]
-        second_ref[target] = blended_ref[pl.ds(row * tile_y + other, SIDE)]
+        value = value.astype(BF16)
+        blended_ref[first : first + n] = value
+        for t in range(n // tile_y):
+            row = first // tile_y + t
+            target = slice(row * SIDE, (row + 1) * SIDE)
+            low = value[t * tile_y : t * tile_y + SIDE]
+            high = value[(t + 1) * tile_y - SIDE : (t + 1) * tile_y]
+            first_ref[target] = jnp.where(narrow_even, high, low)
+            second_ref[target] = jnp.where(narrow_even, low, high)
 
 
 def forward_kernel(
@@ -312,8 +314,8 @@
 def backward_kernel(shape, total_rows, *refs):
     (
         narrow_ref,
+        second_ref,
         first_ref,
-        second_ref,
         stack_ref,
         blended_ref,
         message_ref,
@@ -635,8 +637,8 @@
         ],
         [
             narrow_at.reshape(1),
+            second,
             first,
-            second,
             stack,
             blended,
             message,

time: 62.8 us -> 62 us (0.987)
  waiting for transfers between devices: 20.8 us -> 19.9 us
    ppermute x14, waiting for transfers between devices: 20.8 us -> 19.9 us  [swapped(): return lax.ppermute(block, axis, [(i, i ^ bits) for i in range(count)])]
  transfers between devices with their start and end apart: 16 -> 16, of which waited for: 11 -> 12; matrix products, arithmetic and copies ran while one was open for 1% -> 1% of each run, Pallas kernels for 1% -> 1%
where the time goes in v7:
time: 62 us; the launch traced here: 61.8 us
  starting transfers between devices  30.2 us (49%)
  waiting for transfers between devices  19.9 us (32%)
  Pallas kernels  7.4 us (12%)
  other arithmetic  2.48 us (4%)
  between operations  1.63 us (3%)
    ppermute x14, starting transfers between devices, swapped(): return lax.ppermute(block, axis, [(i, i ^ bits) for i in range(count)])  28.8 us
    ppermute x14, waiting for transfers between devices, swapped(): return lax.ppermute(block, axis, [(i, i ^ bits) for i in range(count)])  19.9 us
    pallas_call x5, Pallas kernels, call(): pl.pallas_call(kernel, out_shape=tuple(out_shapes), in_specs=[pl.BlockSpe...  7.4 us
    ppermute x2, starting transfers between devices, swapped_between(): return lax.ppermute(block, axis, pairs + [(j, i) for i, j in pairs])  1.34 us
  transfers between devices with their start and end apart: 16, of which 12 were waited for; matrix products, arithmetic and copies ran while one was open for 1% of the time, Pallas kernels for 1%

profile of v7, /device:TPU:0, one launch (start us, length us, event | category | flops | bytes accessed | tf_op | source)
XLA Modules:
  0.0 61.8 jit_solution(16831852812573885016)
XLA Ops:
  0.7 1.1 %shard_map.193.place_ref.refs_0_ = s32[2]{0:T(128)S(1)} custom-call(s32[2]{0:T(128)S(1)} %pad_add_fusion.place_ref), custom_call_target="tpu_custom_call" | custom-call | flops 10000000000 | bytes 16 | tf_op jit(solution)/shard_map/pallas_call | solution.py:461
  2.6 0.7 %shard_map.194 = (bf16[368,256]{1,0:T(8,128)(2,1)S(1)}, bf16[320,256]{1,0:T(8,128)(2,1)S(1)}, bf16[48,256]{1,0:T(8,128)(2,1)S(1)}, bf16[48,256]{1,0:T(8,128)(2,1...) custom-call(s32[2]{0:T(128)S(1)} %shard_map.193.place_ref.refs_0_, bf16[512,256]{1,0:T(8,128)(2,1)S(1)} %bitcast.14, ...), custom_call_target="tpu_custom_call" | custom-call | flops 10000000000 | bytes 758540 | tf_op jit(solution)/shard_map/pallas_call | solution.py:461
  3.4 3.1 %collective-permute-start = (bf16[368,256]{1,0:T(8,128)(2,1)S(1)}, bf16[368,256]{1,0:T(8,128)(2,1)S(1)}, u32[]{:S(2)}, u32[]{:S(2)}) collective-permute-start(bf16[368,256]{1,0:T(8,128)(2,1)S(1)} %get-tuple-element.25), channel_id=1, source_target_pairs={{0,4},{4,0},{8,12},{12,8},{1,5},{5,1},{9,13},{13,9},{2,6},{6,2},{1... | collective-permute-start | bytes 565256 | tf_op jit(solution)/shard_map/ppermute | solution.py:26
  6.5 0.7 %collective-permute-start.1 = (bf16[320,256]{1,0:T(8,128)(2,1)S(1)}, bf16[320,256]{1,0:T(8,128)(2,1)S(1)}, u32[]{:S(2)}, u32[]{:S(2)}) collective-permute-start(bf16[320,256]{1,0:T(8,128)(2,1)S(1)} %get-tuple-element.26), channel_id=1, source_target_pairs={{4,8},{8,4},{5,9},{9,5},{6,10},{10,6},{7,11},{11,7},{20,24},{24,20... | collective-permute-start | bytes 491528 | tf_op jit(solution)/shard_map/ppermute | solution.py:32
  7.2 3.9 %collective-permute-start.2 = (bf16[48,256]{1,0:T(8,128)(2,1)S(1)}, bf16[48,256]{1,0:T(8,128)(2,1)S(1)}, u32[]{:S(2)}, u32[]{:S(2)}) collective-permute-start(bf16[48,256]{1,0:T(8,128)(2,1)S(1)} %get-tuple-element.27), channel_id=1, source_target_pairs={{0,8},{4,12},{8,0},{12,4},{1,9},{5,13},{9,1},{13,5},{2,10},{6,14},... | collective-permute-start | bytes 73736 | tf_op jit(solution)/shard_map/ppermute | solution.py:26
  11.1 2.9 %collective-permute-start.3 = (bf16[48,256]{1,0:T(8,128)(2,1)S(1)}, bf16[48,256]{1,0:T(8,128)(2,1)S(1)}, u32[]{:S(2)}, u32[]{:S(2)}) collective-permute-start(bf16[48,256]{1,0:T(8,128)(2,1)S(1)} %get-tuple-element.28), channel_id=1, source_target_pairs={{0,12},{4,8},{8,4},{12,0},{1,13},{5,9},{9,5},{13,1},{2,14},{6,10},... | collective-permute-start | bytes 73736 | tf_op jit(solution)/shard_map/ppermute | solution.py:26
  14.0 2.5 %collective-permute-done.2.refs_8_ = bf16[48,256]{1,0:T(8,128)(2,1)S(1)} collective-permute-done((bf16[48,256]{1,0:T(8,128)(2,1)S(1)}, bf16[48,256]{1,0:T(8,128)(2,1)S(1)}, u32[]{:S(2)}, u32[]{:S(2)}) %collective-permute-start.2) | collective-permute-done | bytes 24608 | tf_op jit(solution)/shard_map/ppermute | solution.py:26
  16.5 0.3 collective-permute-done.3.refs_9_
  16.9 1.0 %shard_map.195 = (bf16[1088,256]{1,0:T(8,128)(2,1)S(1)}, bf16[576,256]{1,0:T(8,128)(2,1)S(1)}, bf16[576,256]{1,0:T(8,128)(2,1)S(1)}, bf16[128,256]{1,0:T(8,128)(...) custom-call(s32[2]{0:T(128)S(1)} %shard_map.193.place_ref.refs_0_, bf16[512,256]{1,0:T(8,128)(2,1)S(1)} %bitcast.15, ...), custom_call_target="tpu_custom_call" | custom-call | flops 71303168 | bytes 2150408 | tf_op jit(solution)/shard_map/pallas_call | solution.py:461
  17.9 0.7 %collective-permute-start.4 = (bf16[576,256]{1,0:T(8,128)(2,1)S(1)}, bf16[576,256]{1,0:T(8,128)(2,1)S(1)}, u32[]{:S(2)}, u32[]{:S(2)}) collective-permute-start(bf16[576,256]{1,0:T(8,128)(2,1)S(1)} %get-tuple-element.29), channel_id=1, source_target_pairs={{1,2},{2,1},{5,6},{6,5},{9,10},{10,9},{13,14},{14,13},{17,18},{18,... | collective-permute-start | bytes 884744 | tf_op jit(solution)/shard_map/ppermute | solution.py:32
  18.6 2.9 %collective-permute-start.5 = (bf16[576,256]{1,0:T(8,128)(2,1)S(1)}, bf16[576,256]{1,0:T(8,128)(2,1)S(1)}, u32[]{:S(2)}, u32[]{:S(2)}) collective-permute-start(bf16[576,256]{1,0:T(8,128)(2,1)S(1)} %get-tuple-element.30), channel_id=1, source_target_pairs={{0,1},{1,0},{2,3},{3,2},{4,5},{5,4},{6,7},{7,6},{8,9},{9,8},{10,11... | collective-permute-start | bytes 884744 | tf_op jit(solution)/shard_map/ppermute | solution.py:26
  21.5 0.9 %shard_map.196 = (bf16[1088,256]{1,0:T(8,128)(2,1)S(1)}, bf16[512,256]{1,0:T(8,128)(2,1)S(1)}, f32[512,256]{1,0:T(8,128)S(1)}, f32[512,256]{1,0:T(8,128)S(1)}) custom-call(bf16[1088,256]{1,0:T(8,128)(2,1)S(1)} %get-tuple-element.32.blended_ref.refs_4_, bf16[256,256]{1,0:T(8,128)(2,1)S(1)} %copy-done.3, bf16[256,256]{1,0:T(8,128)(2,1)S(1)} %copy-done.4), custom_call_target="tpu_custom_call" | custom-call | flops 285212672 | bytes 2686976 | tf_op jit(solution)/shard_map/pallas_call | solution.py:461
  22.4 0.3 collective-permute-done.5.refs_2_
  22.7 3.6 %shard_map.197 = (bf16[512,256]{1,0:T(8,128)(2,1)}, bf16[128,256]{1,0:T(8,128)(2,1)S(1)}, bf16[640,256]{1,0:T(8,128)(2,1)S(1)}, f32[640,256]{1,0:T(8,128)S(1)}) custom-call(s32[1]{0:T(128)} %bitcast.refs_0_, bf16[576,256]{1,0:T(8,128)(2,1)S(1)} %collective-permute-done.4.refs_1_, bf16[576,256]{1,0:T(8,128)(2,1)S(1)} %collective-permute-done.5.refs_2_, ...), custom_call_target="tpu_custom_call" | custom-call | flops 402653184 | bytes 5525508 | tf_op jit(solution)/shard_map/pallas_call | solution.py:461
  26.3 3.1 %collective-permute-start.6 = (bf16[640,256]{1,0:T(8,128)(2,1)S(1)}, bf16[640,256]{1,0:T(8,128)(2,1)S(1)}, u32[]{:S(2)}, u32[]{:S(2)}) collective-permute-start(bf16[640,256]{1,0:T(8,128)(2,1)S(1)} %get-tuple-element.42), channel_id=1, source_target_pairs={{0,1},{1,0},{2,3},{3,2},{4,5},{5,4},{6,7},{7,6},{8,9},{9,8},{10,11... | collective-permute-start | bytes 983048 | tf_op jit(solution)/shard_map/ppermute | solution.py:26
  29.4 1.3 %collective-permute-done.6 = bf16[640,256]{1,0:T(8,128)(2,1)S(1)} collective-permute-done((bf16[640,256]{1,0:T(8,128)(2,1)S(1)}, bf16[640,256]{1,0:T(8,128)(2,1)S(1)}, u32[]{:S(2)}, u32[]{:S(2)}) %collective-permute-start.6) | collective-permute-done | bytes 327712 | tf_op jit(solution)/shard_map/ppermute | solution.py:26
  30.8 2.1 %collective-permute-start.7 = (bf16[320,256]{1,0:T(8,128)(2,1)S(1)}, bf16[320,256]{1,0:T(8,128)(2,1)S(1)}, u32[]{:S(2)}, u32[]{:S(2)}) collective-permute-start(bf16[320,256]{1,0:T(8,128)(2,1)S(1)} %dynamic-slice_convert_fusion), channel_id=1, source_target_pairs={{0,2},{1,3},{2,0},{3,1},{4,6},{5,7},{6,4},{7,5},{8,10},{9,11},{10,... | collective-permute-start | bytes 491528 | tf_op jit(solution)/shard_map/ppermute | solution.py:26
  32.9 4.5 %collective-permute-done.7 = bf16[320,256]{1,0:T(8,128)(2,1)S(1)} collective-permute-done((bf16[320,256]{1,0:T(8,128)(2,1)S(1)}, bf16[320,256]{1,0:T(8,128)(2,1)S(1)}, u32[]{:S(2)}, u32[]{:S(2)}) %collective-permute-start.7) | collective-permute-done | bytes 163872 | tf_op jit(solution)/shard_map/ppermute | solution.py:26
  37.4 2.9 %collective-permute-start.8 = (bf16[112,256]{1,0:T(8,128)(2,1)S(1)}, bf16[112,256]{1,0:T(8,128)(2,1)S(1)}, u32[]{:S(2)}, u32[]{:S(2)}) collective-permute-start(bf16[112,256]{1,0:T(8,128)(2,1)S(1)} %pad_maximum_fusion), channel_id=1, source_target_pairs={{0,12},{4,8},{8,4},{12,0},{1,13},{5,9},{9,5},{13,1},{2,14},{6,10},... | collective-permute-start | bytes 172040 | tf_op jit(solution)/shard_map/ppermute | solution.py:26
  40.4 1.5 %collective-permute-start.10 = (bf16[112,256]{1,0:T(8,128)(2,1)S(1)}, bf16[112,256]{1,0:T(8,128)(2,1)S(1)}, u32[]{:S(2)}, u32[]{:S(2)}) collective-permute-start(bf16[112,256]{1,0:T(8,128)(2,1)S(1)} %pad_maximum_fusion.2), channel_id=1, source_target_pairs={{0,4},{4,0},{8,12},{12,8},{1,5},{5,1},{9,13},{13,9},{2,6},{6,2},{1... | collective-permute-start | bytes 172040 | tf_op jit(solution)/shard_map/ppermute | solution.py:26
  41.9 1.6 %collective-permute-done.8 = bf16[112,256]{1,0:T(8,128)(2,1)S(1)} collective-permute-done((bf16[112,256]{1,0:T(8,128)(2,1)S(1)}, bf16[112,256]{1,0:T(8,128)(2,1)S(1)}, u32[]{:S(2)}, u32[]{:S(2)}) %collective-permute-start.8) | collective-permute-done | bytes 57376 | tf_op jit(solution)/shard_map/ppermute | solution.py:26
  43.6 2.1 %collective-permute-done.9 = bf16[112,256]{1,0:T(8,128)(2,1)S(1)} collective-permute-done((bf16[112,256]{1,0:T(8,128)(2,1)S(1)}, bf16[112,256]{1,0:T(8,128)(2,1)S(1)}, u32[]{:S(2)}, u32[]{:S(2)}) %collective-permute-start.9) | collective-permute-done | bytes 57376 | tf_op jit(solution)/shard_map/ppermute | solution.py:26
  45.9 2.2 %collective-permute-start.11 = (bf16[80,256]{1,0:T(8,128)(2,1)S(1)}, bf16[80,256]{1,0:T(8,128)(2,1)S(1)}, u32[]{:S(2)}, u32[]{:S(2)}) collective-permute-start(bf16[80,256]{1,0:T(8,128)(2,1)S(1)} %get-tuple-element.44), channel_id=1, source_target_pairs={{0,12},{4,8},{8,4},{12,0},{1,13},{5,9},{9,5},{13,1},{2,14},{6,10},... | collective-permute-start | bytes 122888 | tf_op jit(solution)/shard_map/ppermute | solution.py:26
  48.1 2.2 %collective-permute-start.13 = (bf16[80,256]{1,0:T(8,128)(2,1)S(1)}, bf16[80,256]{1,0:T(8,128)(2,1)S(1)}, u32[]{:S(2)}, u32[]{:S(2)}) collective-permute-start(bf16[80,256]{1,0:T(8,128)(2,1)S(1)} %get-tuple-element.44), channel_id=1, source_target_pairs={{0,4},{4,0},{8,12},{12,8},{1,5},{5,1},{9,13},{13,9},{2,6},{6,2},{1... | collective-permute-start | bytes 122888 | tf_op jit(solution)/shard_map/ppermute | solution.py:26
  50.3 1.5 %collective-permute-done.11 = bf16[80,256]{1,0:T(8,128)(2,1)S(1)} collective-permute-done((bf16[80,256]{1,0:T(8,128)(2,1)S(1)}, bf16[80,256]{1,0:T(8,128)(2,1)S(1)}, u32[]{:S(2)}, u32[]{:S(2)}) %collective-permute-start.11) | collective-permute-done | bytes 40992 | tf_op jit(solution)/shard_map/ppermute | solution.py:26
  51.9 1.2 %collective-permute-done.12 = bf16[80,256]{1,0:T(8,128)(2,1)S(1)} collective-permute-done((bf16[80,256]{1,0:T(8,128)(2,1)S(1)}, bf16[80,256]{1,0:T(8,128)(2,1)S(1)}, u32[]{:S(2)}, u32[]{:S(2)}) %collective-permute-start.12) | collective-permute-done | bytes 40992 | tf_op jit(solution)/shard_map/ppermute | solution.py:26
  53.1 1.9 %collective-permute-start.14 = (bf16[320,256]{1,0:T(8,128)(2,1)S(1)}, bf16[320,256]{1,0:T(8,128)(2,1)S(1)}, u32[]{:S(2)}, u32[]{:S(2)}) collective-permute-start(bf16[320,256]{1,0:T(8,128)(2,1)S(1)} %constant_dynamic-update-slice_fusion), channel_id=1, source_target_pairs={{0,2},{1,3},{2,0},{3,1},{4,6},{5,7},{6,4},{7,5},{8,10},{9,11},{10,... | collective-permute-start | bytes 491528 | tf_op jit(solution)/shard_map/ppermute | solution.py:26
  55.0 3.5 %collective-permute-done.14 = bf16[320,256]{1,0:T(8,128)(2,1)S(1)} collective-permute-done((bf16[320,256]{1,0:T(8,128)(2,1)S(1)}, bf16[320,256]{1,0:T(8,128)(2,1)S(1)}, u32[]{:S(2)}, u32[]{:S(2)}) %collective-permute-start.14) | collective-permute-done | bytes 163872 | tf_op jit(solution)/shard_map/ppermute | solution.py:26
  58.7 0.6 fusion.1
  59.3 1.0 %collective-permute-done.15 = bf16[640,256]{1,0:T(8,128)(2,1)S(1)} collective-permute-done((bf16[640,256]{1,0:T(8,128)(2,1)S(1)}, bf16[640,256]{1,0:T(8,128)(2,1)S(1)}, u32[]{:S(2)}, u32[]{:S(2)}) %collective-permute-start.15) | collective-permute-done | bytes 327712 | tf_op jit(solution)/shard_map/ppermute | solution.py:26
  60.3 0.2 maximum_select_fusion
  60.6 1.2 %convert_multiply_fusion = f32[5,256,256]{2,1,0:T(8,128)} fusion(bf16[5,256,256]{2,1,0:T(8,128)(2,1)S(1)} %bitcast.20, f32[5]{0:T(128)S(1)} %copy-done.16), kind=kLoop, calls=%fused_computation | loop fusion | flops 655360 | bytes 1966100 | tf_op jit(solution)/shard_map/mul | solution.py:731
  (60 shorter events, 0.8 us)
Async XLA Ops:
  0.7 1.8 %copy-start.11 = (bf16[4,8,256]{2,1,0:T(8,128)(2,1)S(1)}, bf16[4,8,256]{2,1,0:T(8,128)(2,1)}, u32[]{:S(2)}) copy-start(bf16[4,8,256]{2,1,0:T(8,128)(2,1)} %param.24) | copy-start | bytes 49156
  0.7 1.8 %copy-start.12 = (s32[36,4,8]{0,2,1:T(8,128)S(1)}, s32[36,4,8]{0,2,1:T(8,128)}, u32[]{:S(2)}) copy-start(s32[36,4,8]{0,2,1:T(8,128)} %param.23) | copy-start | bytes 13828
  0.7 1.9 %copy-start.13 = (bf16[32,256]{1,0:T(8,128)(2,1)S(1)}, bf16[32,256]{1,0:T(8,128)(2,1)}, u32[]{:S(2)}) copy-start(bf16[32,256]{1,0:T(8,128)(2,1)} %rows_ref.1) | copy-start | bytes 49156
  0.7 1.9 %copy-start.14 = (s32[32]{0:T(128)S(1)}, s32[32]{0:T(128)}, u32[]{:S(2)}) copy-start(s32[32]{0:T(128)} %param.21) | copy-start | bytes 388
  0.7 1.9 %copy-start.15 = (s32[32]{0:T(128)S(1)}, s32[32]{0:T(128)}, u32[]{:S(2)}) copy-start(s32[32]{0:T(128)} %param.22) | copy-start | bytes 388
  2.6 14.2 %copy-start = (bf16[256,256]{1,0:T(8,128)(2,1)S(1)}, bf16[256,256]{1,0:T(8,128)(2,1)}, u32[]{:S(2)}) copy-start(bf16[256,256]{1,0:T(8,128)(2,1)} %refs_15_.1) | copy-start | bytes 393220
  2.6 14.2 %copy-start.10 = (bf16[2,32,128]{2,1,0:T(8,128)(2,1)S(1)}, bf16[2,32,128]{2,1,0:T(8,128)(2,1)}, u32[]{:S(2)}) copy-start(bf16[2,32,128]{2,1,0:T(8,128)(2,1)} %constant.63.clone.refs_4_) | copy-start | bytes 49156
  2.6 18.9 %copy-start.3 = (bf16[256,256]{1,0:T(8,128)(2,1)S(1)}, bf16[256,256]{1,0:T(8,128)(2,1)}, u32[]{:S(2)}) copy-start(bf16[256,256]{1,0:T(8,128)(2,1)} %refs_16_.1) | copy-start | bytes 393220
  2.6 18.9 %copy-start.4 = (bf16[256,256]{1,0:T(8,128)(2,1)S(1)}, bf16[256,256]{1,0:T(8,128)(2,1)}, u32[]{:S(2)}) copy-start(bf16[256,256]{1,0:T(8,128)(2,1)} %refs_17_.1) | copy-start | bytes 393220
  3.4 19.3 %copy-start.2 = (bf16[2,128,384]{2,1,0:T(8,128)(2,1)S(1)}, bf16[2,128,384]{2,1,0:T(8,128)(2,1)}, u32[]{:S(2)}) copy-start(bf16[2,128,384]{2,1,0:T(8,128)(2,1)} %constant.65.clone.refs_12_) | copy-start | bytes 589828
  3.4 19.3 %copy-start.5 = (bf16[256,256]{1,0:T(8,128)(2,1)S(1)}, bf16[256,256]{1,0:T(8,128)(2,1)}, u32[]{:S(2)}) copy-start(bf16[256,256]{1,0:T(8,128)(2,1)} %refs_18_.1) | copy-start | bytes 393220
  3.4 19.3 %copy-start.6 = (bf16[256,256]{1,0:T(8,128)(2,1)S(1)}, bf16[256,256]{1,0:T(8,128)(2,1)}, u32[]{:S(2)}) copy-start(bf16[256,256]{1,0:T(8,128)(2,1)} %refs_19_.1) | copy-start | bytes 393220
  3.4 19.3 %copy-start.7 = (bf16[2,128,192]{2,1,0:T(8,128)(2,1)S(1)}, bf16[2,128,192]{2,1,0:T(8,128)(2,1)}, u32[]{:S(2)}) copy-start(bf16[2,128,192]{2,1,0:T(8,128)(2,1)} %constant.64.clone.refs_11_) | copy-start | bytes 294916
  3.4 19.3 %copy-start.8 = (bf16[128,256]{1,0:T(8,128)(2,1)S(1)}, bf16[128,256]{1,0:T(8,128)(2,1)}, u32[]{:S(2)}) copy-start(bf16[128,256]{1,0:T(8,128)(2,1)} %constant.67.clone.refs_14_) | copy-start | bytes 196612
  3.4 19.3 %copy-start.9 = (f32[2,16,384]{2,1,0:T(8,128)S(1)}, f32[2,16,384]{2,1,0:T(8,128)}, u32[]{:S(2)}) copy-start(f32[2,16,384]{2,1,0:T(8,128)} %constant.66.clone.refs_13_) | copy-start | bytes 147460
  3.4 13.4 %collective-permute-start = (bf16[368,256]{1,0:T(8,128)(2,1)S(1)}, bf16[368,256]{1,0:T(8,128)(2,1)S(1)}, u32[]{:S(2)}, u32[]{:S(2)}) collective-permute-start(bf16[368,256]{1,0:T(8,128)(2,1)S(1)} %get-tuple-element.25), channel_id=1, source_target_pairs={{0,4},{4,0},{8,12},{12,8},{1,5},{5,1},{9,13},{13,9},{2,6},{6,2},{1... | collective-permute-start | bytes 565256 | tf_op jit(solution)/shard_map/ppermute | solution.py:26
  6.5 10.3 %collective-permute-start.1 = (bf16[320,256]{1,0:T(8,128)(2,1)S(1)}, bf16[320,256]{1,0:T(8,128)(2,1)S(1)}, u32[]{:S(2)}, u32[]{:S(2)}) collective-permute-start(bf16[320,256]{1,0:T(8,128)(2,1)S(1)} %get-tuple-element.26), channel_id=1, source_target_pairs={{4,8},{8,4},{5,9},{9,5},{6,10},{10,6},{7,11},{11,7},{20,24},{24,20... | collective-permute-start | bytes 491528 | tf_op jit(solution)/shard_map/ppermute | solution.py:32
  7.2 9.3 %collective-permute-start.2 = (bf16[48,256]{1,0:T(8,128)(2,1)S(1)}, bf16[48,256]{1,0:T(8,128)(2,1)S(1)}, u32[]{:S(2)}, u32[]{:S(2)}) collective-permute-start(bf16[48,256]{1,0:T(8,128)(2,1)S(1)} %get-tuple-element.27), channel_id=1, source_target_pairs={{0,8},{4,12},{8,0},{12,4},{1,9},{5,13},{9,1},{13,5},{2,10},{6,14},... | collective-permute-start | bytes 73736 | tf_op jit(solution)/shard_map/ppermute | solution.py:26
  11.1 5.7 %collective-permute-start.3 = (bf16[48,256]{1,0:T(8,128)(2,1)S(1)}, bf16[48,256]{1,0:T(8,128)(2,1)S(1)}, u32[]{:S(2)}, u32[]{:S(2)}) collective-permute-start(bf16[48,256]{1,0:T(8,128)(2,1)S(1)} %get-tuple-element.28), channel_id=1, source_target_pairs={{0,12},{4,8},{8,4},{12,0},{1,13},{5,9},{9,5},{13,1},{2,14},{6,10},... | collective-permute-start | bytes 73736 | tf_op jit(solution)/shard_map/ppermute | solution.py:26
  17.9 4.5 %collective-permute-start.4 = (bf16[576,256]{1,0:T(8,128)(2,1)S(1)}, bf16[576,256]{1,0:T(8,128)(2,1)S(1)}, u32[]{:S(2)}, u32[]{:S(2)}) collective-permute-start(bf16[576,256]{1,0:T(8,128)(2,1)S(1)} %get-tuple-element.29), channel_id=1, source_target_pairs={{1,2},{2,1},{5,6},{6,5},{9,10},{10,9},{13,14},{14,13},{17,18},{18,... | collective-permute-start | bytes 884744 | tf_op jit(solution)/shard_map/ppermute | solution.py:32
  18.6 4.1 %collective-permute-start.5 = (bf16[576,256]{1,0:T(8,128)(2,1)S(1)}, bf16[576,256]{1,0:T(8,128)(2,1)S(1)}, u32[]{:S(2)}, u32[]{:S(2)}) collective-permute-start(bf16[576,256]{1,0:T(8,128)(2,1)S(1)} %get-tuple-element.30), channel_id=1, source_target_pairs={{0,1},{1,0},{2,3},{3,2},{4,5},{5,4},{6,7},{7,6},{8,9},{9,8},{10,11... | collective-permute-start | bytes 884744 | tf_op jit(solution)/shard_map/ppermute | solution.py:26
  26.3 4.4 %collective-permute-start.6 = (bf16[640,256]{1,0:T(8,128)(2,1)S(1)}, bf16[640,256]{1,0:T(8,128)(2,1)S(1)}, u32[]{:S(2)}, u32[]{:S(2)}) collective-permute-start(bf16[640,256]{1,0:T(8,128)(2,1)S(1)} %get-tuple-element.42), channel_id=1, source_target_pairs={{0,1},{1,0},{2,3},{3,2},{4,5},{5,4},{6,7},{7,6},{8,9},{9,8},{10,11... | collective-permute-start | bytes 983048 | tf_op jit(solution)/shard_map/ppermute | solution.py:26
  30.8 6.6 %collective-permute-start.7 = (bf16[320,256]{1,0:T(8,128)(2,1)S(1)}, bf16[320,256]{1,0:T(8,128)(2,1)S(1)}, u32[]{:S(2)}, u32[]{:S(2)}) collective-permute-start(bf16[320,256]{1,0:T(8,128)(2,1)S(1)} %dynamic-slice_convert_fusion), channel_id=1, source_target_pairs={{0,2},{1,3},{2,0},{3,1},{4,6},{5,7},{6,4},{7,5},{8,10},{9,11},{10,... | collective-permute-start | bytes 491528 | tf_op jit(solution)/shard_map/ppermute | solution.py:26
  37.4 6.1 %collective-permute-start.8 = (bf16[112,256]{1,0:T(8,128)(2,1)S(1)}, bf16[112,256]{1,0:T(8,128)(2,1)S(1)}, u32[]{:S(2)}, u32[]{:S(2)}) collective-permute-start(bf16[112,256]{1,0:T(8,128)(2,1)S(1)} %pad_maximum_fusion), channel_id=1, source_target_pairs={{0,12},{4,8},{8,4},{12,0},{1,13},{5,9},{9,5},{13,1},{2,14},{6,10},... | collective-permute-start | bytes 172040 | tf_op jit(solution)/shard_map/ppermute | solution.py:26
  40.4 5.3 %collective-permute-start.9 = (bf16[112,256]{1,0:T(8,128)(2,1)S(1)}, bf16[112,256]{1,0:T(8,128)(2,1)S(1)}, u32[]{:S(2)}, u32[]{:S(2)}) collective-permute-start(bf16[112,256]{1,0:T(8,128)(2,1)S(1)} %pad_maximum_fusion.1), channel_id=1, source_target_pairs={{0,8},{4,12},{8,0},{12,4},{1,9},{5,13},{9,1},{13,5},{2,10},{6,14},... | collective-permute-start | bytes 172040 | tf_op jit(solution)/shard_map/ppermute | solution.py:26
  40.4 5.4 %collective-permute-start.10 = (bf16[112,256]{1,0:T(8,128)(2,1)S(1)}, bf16[112,256]{1,0:T(8,128)(2,1)S(1)}, u32[]{:S(2)}, u32[]{:S(2)}) collective-permute-start(bf16[112,256]{1,0:T(8,128)(2,1)S(1)} %pad_maximum_fusion.2), channel_id=1, source_target_pairs={{0,4},{4,0},{8,12},{12,8},{1,5},{5,1},{9,13},{13,9},{2,6},{6,2},{1... | collective-permute-start | bytes 172040 | tf_op jit(solution)/shard_map/ppermute | solution.py:26
  45.8 14.7 %copy-start.16 = (f32[5]{0:T(128)S(1)}, f32[5]{0:T(128)}, u32[]{:S(2)}) copy-start(f32[5]{0:T(128)} %constant.72) | copy-start | bytes 64
  45.9 6.0 %collective-permute-start.11 = (bf16[80,256]{1,0:T(8,128)(2,1)S(1)}, bf16[80,256]{1,0:T(8,128)(2,1)S(1)}, u32[]{:S(2)}, u32[]{:S(2)}) collective-permute-start(bf16[80,256]{1,0:T(8,128)(2,1)S(1)} %get-tuple-element.44), channel_id=1, source_target_pairs={{0,12},{4,8},{8,4},{12,0},{1,13},{5,9},{9,5},{13,1},{2,14},{6,10},... | collective-permute-start | bytes 122888 | tf_op jit(solution)/shard_map/ppermute | solution.py:26
  48.1 4.9 %collective-permute-start.12 = (bf16[80,256]{1,0:T(8,128)(2,1)S(1)}, bf16[80,256]{1,0:T(8,128)(2,1)S(1)}, u32[]{:S(2)}, u32[]{:S(2)}) collective-permute-start(bf16[80,256]{1,0:T(8,128)(2,1)S(1)} %get-tuple-element.44), channel_id=1, source_target_pairs={{0,8},{4,12},{8,0},{12,4},{1,9},{5,13},{9,1},{13,5},{2,10},{6,14},... | collective-permute-start | bytes 122888 | tf_op jit(solution)/shard_map/ppermute | solution.py:26
  48.1 4.9 %collective-permute-start.13 = (bf16[80,256]{1,0:T(8,128)(2,1)S(1)}, bf16[80,256]{1,0:T(8,128)(2,1)S(1)}, u32[]{:S(2)}, u32[]{:S(2)}) collective-permute-start(bf16[80,256]{1,0:T(8,128)(2,1)S(1)} %get-tuple-element.44), channel_id=1, source_target_pairs={{0,4},{4,0},{8,12},{12,8},{1,5},{5,1},{9,13},{13,9},{2,6},{6,2},{1... | collective-permute-start | bytes 122888 | tf_op jit(solution)/shard_map/ppermute | solution.py:26
  53.1 5.4 %collective-permute-start.14 = (bf16[320,256]{1,0:T(8,128)(2,1)S(1)}, bf16[320,256]{1,0:T(8,128)(2,1)S(1)}, u32[]{:S(2)}, u32[]{:S(2)}) collective-permute-start(bf16[320,256]{1,0:T(8,128)(2,1)S(1)} %constant_dynamic-update-slice_fusion), channel_id=1, source_target_pairs={{0,2},{1,3},{2,0},{3,1},{4,6},{5,7},{6,4},{7,5},{8,10},{9,11},{10,... | collective-permute-start | bytes 491528 | tf_op jit(solution)/shard_map/ppermute | solution.py:26
  58.6 1.7 %collective-permute-start.15 = (bf16[640,256]{1,0:T(8,128)(2,1)S(1)}, bf16[640,256]{1,0:T(8,128)(2,1)S(1)}, u32[]{:S(2)}, u32[]{:S(2)}) collective-permute-start(bf16[640,256]{1,0:T(8,128)(2,1)S(1)} %maximum_select_fusion.1), channel_id=1, source_target_pairs={{0,1},{1,0},{2,3},{3,2},{4,5},{5,4},{6,7},{7,6},{8,9},{9,8},{10,11... | collective-permute-start | bytes 983048 | tf_op jit(solution)/shard_map/ppermute | solution.py:26
  (1 other events, 1.8 us)

commit v8 on v7

--- a/solution.py
+++ b/solution.py
@@ -171,7 +171,6 @@
     first_ref,
     second_ref,
     third_ref,
-    fourth_ref,
     mesh_ref,
     own_rows_ref,
 ):
@@ -191,7 +190,7 @@
     repeat = lane % held == lax.broadcasted_iota(jnp.int32, (held, LANES), 0)
     spread = dot(fields.astype(F32).astype(BF16), jnp.where(repeat, 1.0, 0.0).astype(BF16))
     lane = lax.broadcasted_iota(jnp.int32, (16, LANES), 1)
-    for number, ref in enumerate((own_rows_ref, first_ref, third_ref, fourth_ref)):
+    for number, ref in enumerate((own_rows_ref, first_ref, third_ref)):
         at = ref.shape[0] - held - 16
         ref[at : at + held] = rows_ref[...]
         ref[at + held :] = jnp.where(lane // held == number, spread, 0.0).astype(BF16)
@@ -210,7 +209,7 @@
 
 def blend_kernel(shape, units, unit_rows, *refs):
     (place_ref, own_ref, mesh_ref, w_force_ref, side_ref, own_rows_ref) = refs[:6]
-    count = units if units > 3 else 2
+    count = units - 1
     arrived = refs[6 : 6 + count]
     (blended_ref, first_ref, second_ref, stack_ref, rows_ref, key_ref) = refs[6 + count : 12 + count]
     (projected_ref,) = refs[12 + count :]
@@ -225,7 +224,8 @@
             return own_rows_ref[at : at + n]
         if k == 1 or units == 3:
             return arrived[k - 1][first_row + at : first_row + at + n]
-        return arrived[k][at : at + n]
+        start = (k - 2) * (unit_rows + 16) + at
+        return arrived[2][start : start + n]
 
     total = unit_rows * units
     for k in range(units):
@@ -233,6 +233,8 @@
     blocks = []
     if total <= LANES:
         metas = [held(k, unit_rows, 16).astype(F32) for k in range(units)]
+        if units > 3:
+            metas[3] = pltpu.roll(metas[3], 2 * unit_rows, axis=1)
         blocks.append(functools.reduce(lambda a, b: a + b, metas)[:, :total])
     else:
         for k in range(units):
@@ -558,9 +560,9 @@
         flops=LONG,
     )
     if whole_column:
-        first, second, third, fourth, mesh, own_rows = call(
+        first, second, third, mesh, own_rows = call(
             functools.partial(pack_kernel, shape, units),
-            [long, plain, short, short, struct((2 * shape.own_nodes, channels), BF16), short],
+            [long, plain, short, struct((2 * shape.own_nodes, channels), BF16), short],
             [
                 place,
                 cells,
@@ -574,10 +576,10 @@
             spaces="s",
             flops=LONG,
         )
-        third = swapped(third, "wide", 2)
-        fourth = swapped(fourth, "wide", 3)
         first_in = swapped(first, "wide", 1)
-        arrived = [first_in, swapped_between(second, "wide"), third, fourth]
+        second_in = swapped_between(second, "wide")
+        onward = jnp.concatenate([third, first_in[plain.shape[0] :]])
+        arrived = [first_in, second_in, swapped(onward, "wide", 2)]
     else:
 
         def with_meta(slot):

time: 62 us -> 62.7 us (1.011)
  waiting for transfers between devices: 19.9 us -> 24.4 us
  starting transfers between devices: 30.2 us -> 26.4 us
    ppermute x14 -> x13, waiting for transfers between devices: 19.9 us -> 24.4 us  [swapped(): return lax.ppermute(block, axis, [(i, i ^ bits) for i in range(count)])]
    ppermute x14 -> x13, starting transfers between devices: 28.8 us -> 25 us  [swapped(): return lax.ppermute(block, axis, [(i, i ^ bits) for i in range(count)])]
  transfers between devices with their start and end apart: 16 -> 15, of which waited for: 12 -> 12; matrix products, arithmetic and copies ran while one was open for 1% -> 1% of each run, Pallas kernels for 1% -> 1%
where the time goes in v8:
time: 62.7 us; the launch traced here: 62.5 us
  starting transfers between devices  26.4 us (42%)
  waiting for transfers between devices  24.4 us (39%)
  Pallas kernels  7.4 us (12%)
  other arithmetic  2.49 us (4%)
  between operations  1.62 us (3%)
    ppermute x13, starting transfers between devices, swapped(): return lax.ppermute(block, axis, [(i, i ^ bits) for i in range(count)])  25 us
    ppermute x13, waiting for transfers between devices, swapped(): return lax.ppermute(block, axis, [(i, i ^ bits) for i in range(count)])  24.4 us
    pallas_call x5, Pallas kernels, call(): pl.pallas_call(kernel, out_shape=tuple(out_shapes), in_specs=[pl.BlockSpe...  7.4 us
    ppermute x2, starting transfers between devices, swapped_between(): return lax.ppermute(block, axis, pairs + [(j, i) for i, j in pairs])  1.34 us
  transfers between devices with their start and end apart: 15, of which 12 were waited for; matrix products, arithmetic and copies ran while one was open for 1% of the time, Pallas kernels for 1%

profile of v8, /device:TPU:0, one launch (start us, length us, event | category | flops | bytes accessed | tf_op | source)
XLA Modules:
  0.0 62.5 jit_solution(12468157378888078741)
XLA Ops:
  0.7 1.1 %shard_map.193.place_ref.refs_0_ = s32[2]{0:T(128)S(1)} custom-call(s32[2]{0:T(128)S(1)} %pad_add_fusion.place_ref), custom_call_target="tpu_custom_call" | custom-call | flops 10000000000 | bytes 16 | tf_op jit(solution)/shard_map/pallas_call | solution.py:463
  2.6 0.7 %shard_map.194 = (bf16[368,256]{1,0:T(8,128)(2,1)S(1)}, bf16[320,256]{1,0:T(8,128)(2,1)S(1)}, bf16[48,256]{1,0:T(8,128)(2,1)S(1)}, bf16[64,256]{1,0:T(8,128)(2,1)S(1)}, bf16[48,256]{1,0:T(8,128)(2,1)S(1)}) custom-call(s32[2]{0:T(128)S(1)} %shard_map.193.place_ref.refs_0_, bf16[512,256]{1,0:T(8,128)(2,1)S(1)} %bitcast.14, bf16[32,256]{1,0:T(8,128)(2,1)S(1)} %bitcast.16, ...), custom_call_target="tpu_custom_call" | custom-call | flops 10000000000 | bytes 733964 | tf_op jit(solution)/shard_map/pallas_call | solution.py:463
  3.4 3.1 %collective-permute-start = (bf16[368,256]{1,0:T(8,128)(2,1)S(1)}, bf16[368,256]{1,0:T(8,128)(2,1)S(1)}, u32[]{:S(2)}, u32[]{:S(2)}) collective-permute-start(bf16[368,256]{1,0:T(8,128)(2,1)S(1)} %get-tuple-element.24), channel_id=1, source_target_pairs={{0,4},{4,0},{8,12},{12,8},{1,5},{5,1},{9,13},{13,9},{2,6},{6,2},{1... | collective-permute-start | bytes 565256 | tf_op jit(solution)/shard_map/ppermute | solution.py:26
  6.5 0.7 %collective-permute-start.1 = (bf16[320,256]{1,0:T(8,128)(2,1)S(1)}, bf16[320,256]{1,0:T(8,128)(2,1)S(1)}, u32[]{:S(2)}, u32[]{:S(2)}) collective-permute-start(bf16[320,256]{1,0:T(8,128)(2,1)S(1)} %get-tuple-element.25), channel_id=1, source_target_pairs={{4,8},{8,4},{5,9},{9,5},{6,10},{10,6},{7,11},{11,7},{20,24},{24,20... | collective-permute-start | bytes 491528 | tf_op jit(solution)/shard_map/ppermute | solution.py:32
  7.2 4.1 %collective-permute-done.refs_6_ = bf16[368,256]{1,0:T(8,128)(2,1)S(1)} collective-permute-done((bf16[368,256]{1,0:T(8,128)(2,1)S(1)}, bf16[368,256]{1,0:T(8,128)(2,1)S(1)}, u32[]{:S(2)}, u32[]{:S(2)}) %collective-permute-start) | collective-permute-done | bytes 188448 | tf_op jit(solution)/shard_map/ppermute | solution.py:26
  11.3 2.8 %collective-permute-start.2 = (bf16[96,256]{1,0:T(8,128)(2,1)S(1)}, bf16[96,256]{1,0:T(8,128)(2,1)S(1)}, u32[]{:S(2)}, u32[]{:S(2)}) collective-permute-start(bf16[96,256]{1,0:T(8,128)(2,1)S(1)} %pad_maximum_fusion.3), channel_id=1, source_target_pairs={{0,8},{4,12},{8,0},{12,4},{1,9},{5,13},{9,1},{13,5},{2,10},{6,14},... | collective-permute-start | bytes 147464 | tf_op jit(solution)/shard_map/ppermute | solution.py:26
  14.1 2.4 %collective-permute-done.2.refs_8_ = bf16[96,256]{1,0:T(8,128)(2,1)S(1)} collective-permute-done((bf16[96,256]{1,0:T(8,128)(2,1)S(1)}, bf16[96,256]{1,0:T(8,128)(2,1)S(1)}, u32[]{:S(2)}, u32[]{:S(2)}) %collective-permute-start.2) | collective-permute-done | bytes 49184 | tf_op jit(solution)/shard_map/ppermute | solution.py:26
  16.5 1.0 %shard_map.195 = (bf16[1088,256]{1,0:T(8,128)(2,1)S(1)}, bf16[576,256]{1,0:T(8,128)(2,1)S(1)}, bf16[576,256]{1,0:T(8,128)(2,1)S(1)}, bf16[128,256]{1,0:T(8,128)(...) custom-call(s32[2]{0:T(128)S(1)} %shard_map.193.place_ref.refs_0_, bf16[512,256]{1,0:T(8,128)(2,1)S(1)} %bitcast.15, ...), custom_call_target="tpu_custom_call" | custom-call | flops 71303168 | bytes 2150408 | tf_op jit(solution)/shard_map/pallas_call | solution.py:463
  17.6 0.7 %collective-permute-start.3 = (bf16[576,256]{1,0:T(8,128)(2,1)S(1)}, bf16[576,256]{1,0:T(8,128)(2,1)S(1)}, u32[]{:S(2)}, u32[]{:S(2)}) collective-permute-start(bf16[576,256]{1,0:T(8,128)(2,1)S(1)} %get-tuple-element.27), channel_id=1, source_target_pairs={{1,2},{2,1},{5,6},{6,5},{9,10},{10,9},{13,14},{14,13},{17,18},{18,... | collective-permute-start | bytes 884744 | tf_op jit(solution)/shard_map/ppermute | solution.py:32
  18.2 2.9 %collective-permute-start.4 = (bf16[576,256]{1,0:T(8,128)(2,1)S(1)}, bf16[576,256]{1,0:T(8,128)(2,1)S(1)}, u32[]{:S(2)}, u32[]{:S(2)}) collective-permute-start(bf16[576,256]{1,0:T(8,128)(2,1)S(1)} %get-tuple-element.28), channel_id=1, source_target_pairs={{0,1},{1,0},{2,3},{3,2},{4,5},{5,4},{6,7},{7,6},{8,9},{9,8},{10,11... | collective-permute-start | bytes 884744 | tf_op jit(solution)/shard_map/ppermute | solution.py:26
  21.1 0.9 %shard_map.196 = (bf16[1088,256]{1,0:T(8,128)(2,1)S(1)}, bf16[512,256]{1,0:T(8,128)(2,1)S(1)}, f32[512,256]{1,0:T(8,128)S(1)}, f32[512,256]{1,0:T(8,128)S(1)}) custom-call(bf16[1088,256]{1,0:T(8,128)(2,1)S(1)} %get-tuple-element.30.blended_ref.refs_4_, bf16[256,256]{1,0:T(8,128)(2,1)S(1)} %copy-done.3, bf16[256,256]{1,0:T(8,128)(2,1)S(1)} %copy-done.4), custom_call_target="tpu_custom_call" | custom-call | flops 285212672 | bytes 2686976 | tf_op jit(solution)/shard_map/pallas_call | solution.py:463
  22.1 0.3 collective-permute-done.4.refs_2_
  22.4 3.6 %shard_map.197 = (bf16[512,256]{1,0:T(8,128)(2,1)}, bf16[128,256]{1,0:T(8,128)(2,1)S(1)}, bf16[640,256]{1,0:T(8,128)(2,1)S(1)}, f32[640,256]{1,0:T(8,128)S(1)}) custom-call(s32[1]{0:T(128)} %bitcast.refs_0_, bf16[576,256]{1,0:T(8,128)(2,1)S(1)} %collective-permute-done.3.refs_1_, bf16[576,256]{1,0:T(8,128)(2,1)S(1)} %collective-permute-done.4.refs_2_, ...), custom_call_target="tpu_custom_call" | custom-call | flops 402653184 | bytes 5525508 | tf_op jit(solution)/shard_map/pallas_call | solution.py:463
  26.0 3.1 %collective-permute-start.5 = (bf16[640,256]{1,0:T(8,128)(2,1)S(1)}, bf16[640,256]{1,0:T(8,128)(2,1)S(1)}, u32[]{:S(2)}, u32[]{:S(2)}) collective-permute-start(bf16[640,256]{1,0:T(8,128)(2,1)S(1)} %get-tuple-element.40), channel_id=1, source_target_pairs={{0,1},{1,0},{2,3},{3,2},{4,5},{5,4},{6,7},{7,6},{8,9},{9,8},{10,11... | collective-permute-start | bytes 983048 | tf_op jit(solution)/shard_map/ppermute | solution.py:26
  29.1 1.3 %collective-permute-done.5 = bf16[640,256]{1,0:T(8,128)(2,1)S(1)} collective-permute-done((bf16[640,256]{1,0:T(8,128)(2,1)S(1)}, bf16[640,256]{1,0:T(8,128)(2,1)S(1)}, u32[]{:S(2)}, u32[]{:S(2)}) %collective-permute-start.5) | collective-permute-done | bytes 327712 | tf_op jit(solution)/shard_map/ppermute | solution.py:26
  30.4 2.1 %collective-permute-start.6 = (bf16[320,256]{1,0:T(8,128)(2,1)S(1)}, bf16[320,256]{1,0:T(8,128)(2,1)S(1)}, u32[]{:S(2)}, u32[]{:S(2)}) collective-permute-start(bf16[320,256]{1,0:T(8,128)(2,1)S(1)} %dynamic-slice_convert_fusion), channel_id=1, source_target_pairs={{0,2},{1,3},{2,0},{3,1},{4,6},{5,7},{6,4},{7,5},{8,10},{9,11},{10,... | collective-permute-start | bytes 491528 | tf_op jit(solution)/shard_map/ppermute | solution.py:26
  32.5 4.5 %collective-permute-done.6 = bf16[320,256]{1,0:T(8,128)(2,1)S(1)} collective-permute-done((bf16[320,256]{1,0:T(8,128)(2,1)S(1)}, bf16[320,256]{1,0:T(8,128)(2,1)S(1)}, u32[]{:S(2)}, u32[]{:S(2)}) %collective-permute-start.6) | collective-permute-done | bytes 163872 | tf_op jit(solution)/shard_map/ppermute | solution.py:26
  37.1 4.1 %collective-permute-start.7 = (bf16[112,256]{1,0:T(8,128)(2,1)S(1)}, bf16[112,256]{1,0:T(8,128)(2,1)S(1)}, u32[]{:S(2)}, u32[]{:S(2)}) collective-permute-start(bf16[112,256]{1,0:T(8,128)(2,1)S(1)} %pad_maximum_fusion), channel_id=1, source_target_pairs={{0,12},{4,8},{8,4},{12,0},{1,13},{5,9},{9,5},{13,1},{2,14},{6,10},... | collective-permute-start | bytes 172040 | tf_op jit(solution)/shard_map/ppermute | solution.py:26
  41.2 0.6 %collective-permute-start.9 = (bf16[112,256]{1,0:T(8,128)(2,1)S(1)}, bf16[112,256]{1,0:T(8,128)(2,1)S(1)}, u32[]{:S(2)}, u32[]{:S(2)}) collective-permute-start(bf16[112,256]{1,0:T(8,128)(2,1)S(1)} %pad_maximum_fusion.2), channel_id=1, source_target_pairs={{0,4},{4,0},{8,12},{12,8},{1,5},{5,1},{9,13},{13,9},{2,6},{6,2},{1... | collective-permute-start | bytes 172040 | tf_op jit(solution)/shard_map/ppermute | solution.py:26
  41.8 2.1 %collective-permute-done.7 = bf16[112,256]{1,0:T(8,128)(2,1)S(1)} collective-permute-done((bf16[112,256]{1,0:T(8,128)(2,1)S(1)}, bf16[112,256]{1,0:T(8,128)(2,1)S(1)}, u32[]{:S(2)}, u32[]{:S(2)}) %collective-permute-start.7) | collective-permute-done | bytes 57376 | tf_op jit(solution)/shard_map/ppermute | solution.py:26
  44.0 2.3 %collective-permute-done.8 = bf16[112,256]{1,0:T(8,128)(2,1)S(1)} collective-permute-done((bf16[112,256]{1,0:T(8,128)(2,1)S(1)}, bf16[112,256]{1,0:T(8,128)(2,1)S(1)}, u32[]{:S(2)}, u32[]{:S(2)}) %collective-permute-start.8) | collective-permute-done | bytes 57376 | tf_op jit(solution)/shard_map/ppermute | solution.py:26
  46.3 0.1 collective-permute-done.9
  46.5 2.2 %collective-permute-start.10 = (bf16[80,256]{1,0:T(8,128)(2,1)S(1)}, bf16[80,256]{1,0:T(8,128)(2,1)S(1)}, u32[]{:S(2)}, u32[]{:S(2)}) collective-permute-start(bf16[80,256]{1,0:T(8,128)(2,1)S(1)} %get-tuple-element.42), channel_id=1, source_target_pairs={{0,12},{4,8},{8,4},{12,0},{1,13},{5,9},{9,5},{13,1},{2,14},{6,10},... | collective-permute-start | bytes 122888 | tf_op jit(solution)/shard_map/ppermute | solution.py:26
  48.7 2.3 %collective-permute-start.12 = (bf16[80,256]{1,0:T(8,128)(2,1)S(1)}, bf16[80,256]{1,0:T(8,128)(2,1)S(1)}, u32[]{:S(2)}, u32[]{:S(2)}) collective-permute-start(bf16[80,256]{1,0:T(8,128)(2,1)S(1)} %get-tuple-element.42), channel_id=1, source_target_pairs={{0,4},{4,0},{8,12},{12,8},{1,5},{5,1},{9,13},{13,9},{2,6},{6,2},{1... | collective-permute-start | bytes 122888 | tf_op jit(solution)/shard_map/ppermute | solution.py:26
  51.0 1.6 %collective-permute-done.10 = bf16[80,256]{1,0:T(8,128)(2,1)S(1)} collective-permute-done((bf16[80,256]{1,0:T(8,128)(2,1)S(1)}, bf16[80,256]{1,0:T(8,128)(2,1)S(1)}, u32[]{:S(2)}, u32[]{:S(2)}) %collective-permute-start.10) | collective-permute-done | bytes 40992 | tf_op jit(solution)/shard_map/ppermute | solution.py:26
  52.5 1.2 %collective-permute-done.11 = bf16[80,256]{1,0:T(8,128)(2,1)S(1)} collective-permute-done((bf16[80,256]{1,0:T(8,128)(2,1)S(1)}, bf16[80,256]{1,0:T(8,128)(2,1)S(1)}, u32[]{:S(2)}, u32[]{:S(2)}) %collective-permute-start.11) | collective-permute-done | bytes 40992 | tf_op jit(solution)/shard_map/ppermute | solution.py:26
  53.8 1.8 %collective-permute-start.13 = (bf16[320,256]{1,0:T(8,128)(2,1)S(1)}, bf16[320,256]{1,0:T(8,128)(2,1)S(1)}, u32[]{:S(2)}, u32[]{:S(2)}) collective-permute-start(bf16[320,256]{1,0:T(8,128)(2,1)S(1)} %constant_dynamic-update-slice_fusion), channel_id=1, source_target_pairs={{0,2},{1,3},{2,0},{3,1},{4,6},{5,7},{6,4},{7,5},{8,10},{9,11},{10,... | collective-permute-start | bytes 491528 | tf_op jit(solution)/shard_map/ppermute | solution.py:26
  55.6 3.6 %collective-permute-done.13 = bf16[320,256]{1,0:T(8,128)(2,1)S(1)} collective-permute-done((bf16[320,256]{1,0:T(8,128)(2,1)S(1)}, bf16[320,256]{1,0:T(8,128)(2,1)S(1)}, u32[]{:S(2)}, u32[]{:S(2)}) %collective-permute-start.13) | collective-permute-done | bytes 163872 | tf_op jit(solution)/shard_map/ppermute | solution.py:26
  59.4 0.6 fusion.1
  60.0 1.0 %collective-permute-done.14 = bf16[640,256]{1,0:T(8,128)(2,1)S(1)} collective-permute-done((bf16[640,256]{1,0:T(8,128)(2,1)S(1)}, bf16[640,256]{1,0:T(8,128)(2,1)S(1)}, u32[]{:S(2)}, u32[]{:S(2)}) %collective-permute-start.14) | collective-permute-done | bytes 327712 | tf_op jit(solution)/shard_map/ppermute | solution.py:26
  61.0 0.2 maximum_select_fusion
  61.3 1.2 %convert_multiply_fusion = f32[5,256,256]{2,1,0:T(8,128)} fusion(bf16[5,256,256]{2,1,0:T(8,128)(2,1)S(1)} %bitcast.20, f32[5]{0:T(128)S(1)} %copy-done.16), kind=kLoop, calls=%fused_computation | loop fusion | flops 655360 | bytes 1966100 | tf_op jit(solution)/shard_map/mul | solution.py:733
  (60 shorter events, 0.7 us)
Async XLA Ops:
  0.7 1.8 %copy-start.1 = (bf16[16,32,256]{2,1,0:T(8,128)(2,1)S(1)}, bf16[16,32,256]{2,1,0:T(8,128)(2,1)}, u32[]{:S(2)}) copy-start(bf16[16,32,256]{2,1,0:T(8,128)(2,1)} %param.18) | copy-start | bytes 786436
  0.7 1.8 %copy-start.11 = (bf16[4,8,256]{2,1,0:T(8,128)(2,1)S(1)}, bf16[4,8,256]{2,1,0:T(8,128)(2,1)}, u32[]{:S(2)}) copy-start(bf16[4,8,256]{2,1,0:T(8,128)(2,1)} %param.24) | copy-start | bytes 49156
  0.7 1.8 %copy-start.12 = (s32[36,4,8]{0,2,1:T(8,128)S(1)}, s32[36,4,8]{0,2,1:T(8,128)}, u32[]{:S(2)}) copy-start(s32[36,4,8]{0,2,1:T(8,128)} %param.23) | copy-start | bytes 13828
  0.7 1.9 %copy-start.13 = (bf16[32,256]{1,0:T(8,128)(2,1)S(1)}, bf16[32,256]{1,0:T(8,128)(2,1)}, u32[]{:S(2)}) copy-start(bf16[32,256]{1,0:T(8,128)(2,1)} %rows_ref.1) | copy-start | bytes 49156
  0.7 1.9 %copy-start.14 = (s32[32]{0:T(128)S(1)}, s32[32]{0:T(128)}, u32[]{:S(2)}) copy-start(s32[32]{0:T(128)} %param.21) | copy-start | bytes 388
  0.7 1.9 %copy-start.15 = (s32[32]{0:T(128)S(1)}, s32[32]{0:T(128)}, u32[]{:S(2)}) copy-start(s32[32]{0:T(128)} %param.22) | copy-start | bytes 388
  2.6 13.9 %copy-start = (bf16[256,256]{1,0:T(8,128)(2,1)S(1)}, bf16[256,256]{1,0:T(8,128)(2,1)}, u32[]{:S(2)}) copy-start(bf16[256,256]{1,0:T(8,128)(2,1)} %refs_15_.1) | copy-start | bytes 393220
  2.6 13.9 %copy-start.10 = (bf16[2,32,128]{2,1,0:T(8,128)(2,1)S(1)}, bf16[2,32,128]{2,1,0:T(8,128)(2,1)}, u32[]{:S(2)}) copy-start(bf16[2,32,128]{2,1,0:T(8,128)(2,1)} %constant.63.clone.refs_4_) | copy-start | bytes 49156
  2.6 18.5 %copy-start.3 = (bf16[256,256]{1,0:T(8,128)(2,1)S(1)}, bf16[256,256]{1,0:T(8,128)(2,1)}, u32[]{:S(2)}) copy-start(bf16[256,256]{1,0:T(8,128)(2,1)} %refs_16_.1) | copy-start | bytes 393220
  2.6 18.5 %copy-start.4 = (bf16[256,256]{1,0:T(8,128)(2,1)S(1)}, bf16[256,256]{1,0:T(8,128)(2,1)}, u32[]{:S(2)}) copy-start(bf16[256,256]{1,0:T(8,128)(2,1)} %refs_17_.1) | copy-start | bytes 393220
  3.4 19.0 %copy-start.2 = (bf16[2,128,384]{2,1,0:T(8,128)(2,1)S(1)}, bf16[2,128,384]{2,1,0:T(8,128)(2,1)}, u32[]{:S(2)}) copy-start(bf16[2,128,384]{2,1,0:T(8,128)(2,1)} %constant.65.clone.refs_12_) | copy-start | bytes 589828
  3.4 19.0 %copy-start.5 = (bf16[256,256]{1,0:T(8,128)(2,1)S(1)}, bf16[256,256]{1,0:T(8,128)(2,1)}, u32[]{:S(2)}) copy-start(bf16[256,256]{1,0:T(8,128)(2,1)} %refs_18_.1) | copy-start | bytes 393220
  3.4 19.0 %copy-start.6 = (bf16[256,256]{1,0:T(8,128)(2,1)S(1)}, bf16[256,256]{1,0:T(8,128)(2,1)}, u32[]{:S(2)}) copy-start(bf16[256,256]{1,0:T(8,128)(2,1)} %refs_19_.1) | copy-start | bytes 393220
  3.4 19.0 %copy-start.7 = (bf16[2,128,192]{2,1,0:T(8,128)(2,1)S(1)}, bf16[2,128,192]{2,1,0:T(8,128)(2,1)}, u32[]{:S(2)}) copy-start(bf16[2,128,192]{2,1,0:T(8,128)(2,1)} %constant.64.clone.refs_11_) | copy-start | bytes 294916
  3.4 18.9 %copy-start.8 = (bf16[128,256]{1,0:T(8,128)(2,1)S(1)}, bf16[128,256]{1,0:T(8,128)(2,1)}, u32[]{:S(2)}) copy-start(bf16[128,256]{1,0:T(8,128)(2,1)} %constant.67.clone.refs_14_) | copy-start | bytes 196612
  3.4 18.9 %copy-start.9 = (f32[2,16,384]{2,1,0:T(8,128)S(1)}, f32[2,16,384]{2,1,0:T(8,128)}, u32[]{:S(2)}) copy-start(f32[2,16,384]{2,1,0:T(8,128)} %constant.66.clone.refs_13_) | copy-start | bytes 147460
  3.4 7.8 %collective-permute-start = (bf16[368,256]{1,0:T(8,128)(2,1)S(1)}, bf16[368,256]{1,0:T(8,128)(2,1)S(1)}, u32[]{:S(2)}, u32[]{:S(2)}) collective-permute-start(bf16[368,256]{1,0:T(8,128)(2,1)S(1)} %get-tuple-element.24), channel_id=1, source_target_pairs={{0,4},{4,0},{8,12},{12,8},{1,5},{5,1},{9,13},{13,9},{2,6},{6,2},{1... | collective-permute-start | bytes 565256 | tf_op jit(solution)/shard_map/ppermute | solution.py:26
  6.5 7.6 %collective-permute-start.1 = (bf16[320,256]{1,0:T(8,128)(2,1)S(1)}, bf16[320,256]{1,0:T(8,128)(2,1)S(1)}, u32[]{:S(2)}, u32[]{:S(2)}) collective-permute-start(bf16[320,256]{1,0:T(8,128)(2,1)S(1)} %get-tuple-element.25), channel_id=1, source_target_pairs={{4,8},{8,4},{5,9},{9,5},{6,10},{10,6},{7,11},{11,7},{20,24},{24,20... | collective-permute-start | bytes 491528 | tf_op jit(solution)/shard_map/ppermute | solution.py:32
  11.3 5.2 %collective-permute-start.2 = (bf16[96,256]{1,0:T(8,128)(2,1)S(1)}, bf16[96,256]{1,0:T(8,128)(2,1)S(1)}, u32[]{:S(2)}, u32[]{:S(2)}) collective-permute-start(bf16[96,256]{1,0:T(8,128)(2,1)S(1)} %pad_maximum_fusion.3), channel_id=1, source_target_pairs={{0,8},{4,12},{8,0},{12,4},{1,9},{5,13},{9,1},{13,5},{2,10},{6,14},... | collective-permute-start | bytes 147464 | tf_op jit(solution)/shard_map/ppermute | solution.py:26
  17.6 4.5 %collective-permute-start.3 = (bf16[576,256]{1,0:T(8,128)(2,1)S(1)}, bf16[576,256]{1,0:T(8,128)(2,1)S(1)}, u32[]{:S(2)}, u32[]{:S(2)}) collective-permute-start(bf16[576,256]{1,0:T(8,128)(2,1)S(1)} %get-tuple-element.27), channel_id=1, source_target_pairs={{1,2},{2,1},{5,6},{6,5},{9,10},{10,9},{13,14},{14,13},{17,18},{18,... | collective-permute-start | bytes 884744 | tf_op jit(solution)/shard_map/ppermute | solution.py:32
  18.2 4.1 %collective-permute-start.4 = (bf16[576,256]{1,0:T(8,128)(2,1)S(1)}, bf16[576,256]{1,0:T(8,128)(2,1)S(1)}, u32[]{:S(2)}, u32[]{:S(2)}) collective-permute-start(bf16[576,256]{1,0:T(8,128)(2,1)S(1)} %get-tuple-element.28), channel_id=1, source_target_pairs={{0,1},{1,0},{2,3},{3,2},{4,5},{5,4},{6,7},{7,6},{8,9},{9,8},{10,11... | collective-permute-start | bytes 884744 | tf_op jit(solution)/shard_map/ppermute | solution.py:26
  26.0 4.4 %collective-permute-start.5 = (bf16[640,256]{1,0:T(8,128)(2,1)S(1)}, bf16[640,256]{1,0:T(8,128)(2,1)S(1)}, u32[]{:S(2)}, u32[]{:S(2)}) collective-permute-start(bf16[640,256]{1,0:T(8,128)(2,1)S(1)} %get-tuple-element.40), channel_id=1, source_target_pairs={{0,1},{1,0},{2,3},{3,2},{4,5},{5,4},{6,7},{7,6},{8,9},{9,8},{10,11... | collective-permute-start | bytes 983048 | tf_op jit(solution)/shard_map/ppermute | solution.py:26
  30.4 6.6 %collective-permute-start.6 = (bf16[320,256]{1,0:T(8,128)(2,1)S(1)}, bf16[320,256]{1,0:T(8,128)(2,1)S(1)}, u32[]{:S(2)}, u32[]{:S(2)}) collective-permute-start(bf16[320,256]{1,0:T(8,128)(2,1)S(1)} %dynamic-slice_convert_fusion), channel_id=1, source_target_pairs={{0,2},{1,3},{2,0},{3,1},{4,6},{5,7},{6,4},{7,5},{8,10},{9,11},{10,... | collective-permute-start | bytes 491528 | tf_op jit(solution)/shard_map/ppermute | solution.py:26
  37.1 6.9 %collective-permute-start.7 = (bf16[112,256]{1,0:T(8,128)(2,1)S(1)}, bf16[112,256]{1,0:T(8,128)(2,1)S(1)}, u32[]{:S(2)}, u32[]{:S(2)}) collective-permute-start(bf16[112,256]{1,0:T(8,128)(2,1)S(1)} %pad_maximum_fusion), channel_id=1, source_target_pairs={{0,12},{4,8},{8,4},{12,0},{1,13},{5,9},{9,5},{13,1},{2,14},{6,10},... | collective-permute-start | bytes 172040 | tf_op jit(solution)/shard_map/ppermute | solution.py:26
  41.2 5.1 %collective-permute-start.8 = (bf16[112,256]{1,0:T(8,128)(2,1)S(1)}, bf16[112,256]{1,0:T(8,128)(2,1)S(1)}, u32[]{:S(2)}, u32[]{:S(2)}) collective-permute-start(bf16[112,256]{1,0:T(8,128)(2,1)S(1)} %pad_maximum_fusion.1), channel_id=1, source_target_pairs={{0,8},{4,12},{8,0},{12,4},{1,9},{5,13},{9,1},{13,5},{2,10},{6,14},... | collective-permute-start | bytes 172040 | tf_op jit(solution)/shard_map/ppermute | solution.py:26
  41.2 5.3 %collective-permute-start.9 = (bf16[112,256]{1,0:T(8,128)(2,1)S(1)}, bf16[112,256]{1,0:T(8,128)(2,1)S(1)}, u32[]{:S(2)}, u32[]{:S(2)}) collective-permute-start(bf16[112,256]{1,0:T(8,128)(2,1)S(1)} %pad_maximum_fusion.2), channel_id=1, source_target_pairs={{0,4},{4,0},{8,12},{12,8},{1,5},{5,1},{9,13},{13,9},{2,6},{6,2},{1... | collective-permute-start | bytes 172040 | tf_op jit(solution)/shard_map/ppermute | solution.py:26
  46.5 14.8 %copy-start.16 = (f32[5]{0:T(128)S(1)}, f32[5]{0:T(128)}, u32[]{:S(2)}) copy-start(f32[5]{0:T(128)} %constant.72) | copy-start | bytes 64
  46.5 6.0 %collective-permute-start.10 = (bf16[80,256]{1,0:T(8,128)(2,1)S(1)}, bf16[80,256]{1,0:T(8,128)(2,1)S(1)}, u32[]{:S(2)}, u32[]{:S(2)}) collective-permute-start(bf16[80,256]{1,0:T(8,128)(2,1)S(1)} %get-tuple-element.42), channel_id=1, source_target_pairs={{0,12},{4,8},{8,4},{12,0},{1,13},{5,9},{9,5},{13,1},{2,14},{6,10},... | collective-permute-start | bytes 122888 | tf_op jit(solution)/shard_map/ppermute | solution.py:26
  48.7 5.0 %collective-permute-start.11 = (bf16[80,256]{1,0:T(8,128)(2,1)S(1)}, bf16[80,256]{1,0:T(8,128)(2,1)S(1)}, u32[]{:S(2)}, u32[]{:S(2)}) collective-permute-start(bf16[80,256]{1,0:T(8,128)(2,1)S(1)} %get-tuple-element.42), channel_id=1, source_target_pairs={{0,8},{4,12},{8,0},{12,4},{1,9},{5,13},{9,1},{13,5},{2,10},{6,14},... | collective-permute-start | bytes 122888 | tf_op jit(solution)/shard_map/ppermute | solution.py:26
  48.7 5.0 %collective-permute-start.12 = (bf16[80,256]{1,0:T(8,128)(2,1)S(1)}, bf16[80,256]{1,0:T(8,128)(2,1)S(1)}, u32[]{:S(2)}, u32[]{:S(2)}) collective-permute-start(bf16[80,256]{1,0:T(8,128)(2,1)S(1)} %get-tuple-element.42), channel_id=1, source_target_pairs={{0,4},{4,0},{8,12},{12,8},{1,5},{5,1},{9,13},{13,9},{2,6},{6,2},{1... | collective-permute-start | bytes 122888 | tf_op jit(solution)/shard_map/ppermute | solution.py:26
  53.8 5.4 %collective-permute-start.13 = (bf16[320,256]{1,0:T(8,128)(2,1)S(1)}, bf16[320,256]{1,0:T(8,128)(2,1)S(1)}, u32[]{:S(2)}, u32[]{:S(2)}) collective-permute-start(bf16[320,256]{1,0:T(8,128)(2,1)S(1)} %constant_dynamic-update-slice_fusion), channel_id=1, source_target_pairs={{0,2},{1,3},{2,0},{3,1},{4,6},{5,7},{6,4},{7,5},{8,10},{9,11},{10,... | collective-permute-start | bytes 491528 | tf_op jit(solution)/shard_map/ppermute | solution.py:26
  59.3 1.7 %collective-permute-start.14 = (bf16[640,256]{1,0:T(8,128)(2,1)S(1)}, bf16[640,256]{1,0:T(8,128)(2,1)S(1)}, u32[]{:S(2)}, u32[]{:S(2)}) collective-permute-start(bf16[640,256]{1,0:T(8,128)(2,1)S(1)} %maximum_select_fusion.1), channel_id=1, source_target_pairs={{0,1},{1,0},{2,3},{3,2},{4,5},{5,4},{6,7},{7,6},{8,9},{9,8},{10,11... | collective-permute-start | bytes 983048 | tf_op jit(solution)/shard_map/ppermute | solution.py:26

commit v9 on v7

--- a/solution.py
+++ b/solution.py
@@ -680,23 +680,20 @@
         kept = lax.dynamic_slice_in_dim(piece, upper * half, half)
         piece = kept + swapped(sent, "narrow", bit).astype(F32)
     part = piece.shape[0] // wide_count
-    rounded = piece.astype(BF16)
-    own = lax.dynamic_slice_in_dim(piece, wide_at * part, part)
-    order = sorted(range(1, wide_count), reverse=True)
-    for k in order:
-        sent = lax.dynamic_slice_in_dim(rounded, (wide_at ^ k) * part, part)
-        if whole_column:
-            sent = jnp.concatenate([sent, back_blocks[k]])
-        got = swapped(sent, "wide", k).astype(F32)
-        own = own + got[:part]
-        if whole_column:
-            row_back = row_back + got[part:]
-    own = own.astype(BF16)
-    gathered = jnp.zeros((wide_count * part, channels), BF16)
-    gathered = lax.dynamic_update_slice_in_dim(gathered, own, wide_at * part, 0)
-    for k in order:
-        got = swapped(own, "wide", k)
-        gathered = lax.dynamic_update_slice_in_dim(gathered, got, (wide_at ^ k) * part, 0)
+    rounded = piece.astype(BF16).reshape(wide_count, part, channels)
+    if whole_column:
+        ordered = [
+            lax.dynamic_slice_in_dim(back_blocks, wide_at ^ k, 1) for k in range(wide_count)
+        ]
+        rounded = jnp.concatenate([rounded, jnp.concatenate(ordered)], axis=1)
+    got = lax.all_to_all(rounded, "wide", split_axis=0, concat_axis=0, tiled=True)
+    got = got.astype(F32).sum(axis=0)
+    if whole_column:
+        row_back = got[part:]
+    own = got[:part].astype(BF16)
+    copies = jnp.broadcast_to(own, (wide_count, part, channels))
+    gathered = lax.all_to_all(copies, "wide", split_axis=0, concat_axis=0, tiled=True)
+    gathered = gathered.reshape(wide_count * part, channels)
     for bit in reversed(bits):
         upper = (narrow_at // bit) % 2
         other = swapped(gathered, "narrow", bit)

time: 62 us -> 67.4 us (1.087)
  blocking collectives: 0 us -> 21.1 us
  starting transfers between devices: 30.2 us -> 20.9 us
  waiting for transfers between devices: 19.9 us -> 13.7 us
    all_to_all x0 -> x2, blocking collectives: none -> 21.1 us  [the longest x1 11.8 us: local(): lax.all_to_all(rounded, 'wide', split_axis=0, concat_axis=0, tiled=True)]
    ppermute x14 -> x8, starting transfers between devices: 28.8 us -> 19.6 us  [swapped(): return lax.ppermute(block, axis, [(i, i ^ bits) for i in range(count)])]
    ppermute x14 -> x8, waiting for transfers between devices: 19.9 us -> 13.7 us  [swapped(): return lax.ppermute(block, axis, [(i, i ^ bits) for i in range(count)])]
  transfers between devices with their start and end apart: 16 -> 10, of which waited for: 12 -> 7; matrix products, arithmetic and copies ran while one was open for 1% -> 1% of each run, Pallas kernels for 1% -> 1%
where the time goes in v9:
time: 67.4 us; the launch traced here: 67.2 us
  blocking collectives  21.1 us (31%)
  starting transfers between devices  20.9 us (31%)
  waiting for transfers between devices  13.7 us (20%)
  Pallas kernels  7.4 us (11%)
  other arithmetic  1.84 us (3%)
  between operations  1.59 us (2%)
  local copies, waits for them, and re-layouts  0.75 us (1%)
    ppermute x8, starting transfers between devices, swapped(): return lax.ppermute(block, axis, [(i, i ^ bits) for i in range(count)])  19.6 us
    ppermute x8, waiting for transfers between devices, swapped(): return lax.ppermute(block, axis, [(i, i ^ bits) for i in range(count)])  13.7 us
    all_to_all x1, blocking collectives, local(): lax.all_to_all(rounded, 'wide', split_axis=0, concat_axis=0, tiled=True)  11.8 us
    all_to_all x1, blocking collectives, local(): lax.all_to_all(copies, 'wide', split_axis=0, concat_axis=0, tiled=True)  9.22 us
    pallas_call x5, Pallas kernels, call(): pl.pallas_call(kernel, out_shape=tuple(out_shapes), in_specs=[pl.BlockSpe...  7.4 us
  transfers between devices with their start and end apart: 10, of which 7 were waited for; matrix products, arithmetic and copies ran while one was open for 1% of the time, Pallas kernels for 1%

profile of v9, /device:TPU:0, one launch (start us, length us, event | category | flops | bytes accessed | tf_op | source)
XLA Modules:
  0.0 67.2 jit_solution(16043548331959538009)
XLA Ops:
  0.6 0.1 pad_add_fusion.place_ref
  0.7 1.1 %shard_map.193.place_ref.refs_0_ = s32[2]{0:T(128)S(1)} custom-call(s32[2]{0:T(128)S(1)} %pad_add_fusion.place_ref), custom_call_target="tpu_custom_call" | custom-call | flops 10000000000 | bytes 16 | tf_op jit(solution)/shard_map/pallas_call | solution.py:461
  2.6 0.0 copy-start.10
  2.6 0.7 %shard_map.194 = (bf16[368,256]{1,0:T(8,128)(2,1)S(1)}, bf16[320,256]{1,0:T(8,128)(2,1)S(1)}, bf16[48,256]{1,0:T(8,128)(2,1)S(1)}, bf16[48,256]{1,0:T(8,128)(2,1...) custom-call(s32[2]{0:T(128)S(1)} %shard_map.193.place_ref.refs_0_, bf16[512,256]{1,0:T(8,128)(2,1)S(1)} %bitcast.17, ...), custom_call_target="tpu_custom_call" | custom-call | flops 10000000000 | bytes 758540 | tf_op jit(solution)/shard_map/pallas_call | solution.py:461
  3.4 0.0 copy-start.8
  3.4 3.1 %collective-permute-start = (bf16[368,256]{1,0:T(8,128)(2,1)S(1)}, bf16[368,256]{1,0:T(8,128)(2,1)S(1)}, u32[]{:S(2)}, u32[]{:S(2)}) collective-permute-start(bf16[368,256]{1,0:T(8,128)(2,1)S(1)} %get-tuple-element.25), channel_id=1, source_target_pairs={{0,4},{4,0},{8,12},{12,8},{1,5},{5,1},{9,13},{13,9},{2,6},{6,2},{1... | collective-permute-start | bytes 565256 | tf_op jit(solution)/shard_map/ppermute | solution.py:26
  6.5 0.7 collective-permute-start.1
  7.2 3.9 %collective-permute-start.2 = (bf16[48,256]{1,0:T(8,128)(2,1)S(1)}, bf16[48,256]{1,0:T(8,128)(2,1)S(1)}, u32[]{:S(2)}, u32[]{:S(2)}) collective-permute-start(bf16[48,256]{1,0:T(8,128)(2,1)S(1)} %get-tuple-element.27), channel_id=1, source_target_pairs={{0,8},{4,12},{8,0},{12,4},{1,9},{5,13},{9,1},{13,5},{2,10},{6,14},... | collective-permute-start | bytes 73736 | tf_op jit(solution)/shard_map/ppermute | solution.py:26
  11.1 2.9 %collective-permute-start.3 = (bf16[48,256]{1,0:T(8,128)(2,1)S(1)}, bf16[48,256]{1,0:T(8,128)(2,1)S(1)}, u32[]{:S(2)}, u32[]{:S(2)}) collective-permute-start(bf16[48,256]{1,0:T(8,128)(2,1)S(1)} %get-tuple-element.28), channel_id=1, source_target_pairs={{0,12},{4,8},{8,4},{12,0},{1,13},{5,9},{9,5},{13,1},{2,14},{6,10},... | collective-permute-start | bytes 73736 | tf_op jit(solution)/shard_map/ppermute | solution.py:26
  14.0 2.5 %collective-permute-done.2.refs_8_ = bf16[48,256]{1,0:T(8,128)(2,1)S(1)} collective-permute-done((bf16[48,256]{1,0:T(8,128)(2,1)S(1)}, bf16[48,256]{1,0:T(8,128)(2,1)S(1)}, u32[]{:S(2)}, u32[]{:S(2)}) %collective-permute-start.2) | collective-permute-done | bytes 24608 | tf_op jit(solution)/shard_map/ppermute | solution.py:26
  16.5 0.3 collective-permute-done.3.refs_9_
  16.9 1.0 %shard_map.195 = (bf16[1088,256]{1,0:T(8,128)(2,1)S(1)}, bf16[576,256]{1,0:T(8,128)(2,1)S(1)}, bf16[576,256]{1,0:T(8,128)(2,1)S(1)}, bf16[128,256]{1,0:T(8,128)(...) custom-call(s32[2]{0:T(128)S(1)} %shard_map.193.place_ref.refs_0_, bf16[512,256]{1,0:T(8,128)(2,1)S(1)} %bitcast.18, ...), custom_call_target="tpu_custom_call" | custom-call | flops 71303168 | bytes 2150408 | tf_op jit(solution)/shard_map/pallas_call | solution.py:461
  17.9 0.7 %collective-permute-start.4 = (bf16[576,256]{1,0:T(8,128)(2,1)S(1)}, bf16[576,256]{1,0:T(8,128)(2,1)S(1)}, u32[]{:S(2)}, u32[]{:S(2)}) collective-permute-start(bf16[576,256]{1,0:T(8,128)(2,1)S(1)} %get-tuple-element.29), channel_id=1, source_target_pairs={{1,2},{2,1},{5,6},{6,5},{9,10},{10,9},{13,14},{14,13},{17,18},{18,... | collective-permute-start | bytes 884744 | tf_op jit(solution)/shard_map/ppermute | solution.py:32
  18.6 2.9 %collective-permute-start.5 = (bf16[576,256]{1,0:T(8,128)(2,1)S(1)}, bf16[576,256]{1,0:T(8,128)(2,1)S(1)}, u32[]{:S(2)}, u32[]{:S(2)}) collective-permute-start(bf16[576,256]{1,0:T(8,128)(2,1)S(1)} %get-tuple-element.30), channel_id=1, source_target_pairs={{0,1},{1,0},{2,3},{3,2},{4,5},{5,4},{6,7},{7,6},{8,9},{9,8},{10,11... | collective-permute-start | bytes 884744 | tf_op jit(solution)/shard_map/ppermute | solution.py:26
  21.5 0.9 %shard_map.196 = (bf16[1088,256]{1,0:T(8,128)(2,1)S(1)}, bf16[512,256]{1,0:T(8,128)(2,1)S(1)}, f32[512,256]{1,0:T(8,128)S(1)}, f32[512,256]{1,0:T(8,128)S(1)}) custom-call(bf16[1088,256]{1,0:T(8,128)(2,1)S(1)} %get-tuple-element.32.blended_ref.refs_4_, bf16[256,256]{1,0:T(8,128)(2,1)S(1)} %copy-done.3, bf16[256,256]{1,0:T(8,128)(2,1)S(1)} %copy-done.4), custom_call_target="tpu_custom_call" | custom-call | flops 285212672 | bytes 2686976 | tf_op jit(solution)/shard_map/pallas_call | solution.py:461
  22.4 0.3 collective-permute-done.5.refs_2_
  22.7 3.6 %shard_map.197 = (bf16[512,256]{1,0:T(8,128)(2,1)}, bf16[128,256]{1,0:T(8,128)(2,1)S(1)}, bf16[640,256]{1,0:T(8,128)(2,1)S(1)}, f32[640,256]{1,0:T(8,128)S(1)}) custom-call(s32[1]{0:T(128)} %bitcast.refs_0_, bf16[576,256]{1,0:T(8,128)(2,1)S(1)} %collective-permute-done.4.refs_1_, bf16[576,256]{1,0:T(8,128)(2,1)S(1)} %collective-permute-done.5.refs_2_, ...), custom_call_target="tpu_custom_call" | custom-call | flops 402653184 | bytes 5525508 | tf_op jit(solution)/shard_map/pallas_call | solution.py:461
  26.3 3.1 %collective-permute-start.6 = (bf16[640,256]{1,0:T(8,128)(2,1)S(1)}, bf16[640,256]{1,0:T(8,128)(2,1)S(1)}, u32[]{:S(2)}, u32[]{:S(2)}) collective-permute-start(bf16[640,256]{1,0:T(8,128)(2,1)S(1)} %get-tuple-element.41), channel_id=1, source_target_pairs={{0,1},{1,0},{2,3},{3,2},{4,5},{5,4},{6,7},{7,6},{8,9},{9,8},{10,11... | collective-permute-start | bytes 983048 | tf_op jit(solution)/shard_map/ppermute | solution.py:26
  29.4 1.3 %collective-permute-done.6 = bf16[640,256]{1,0:T(8,128)(2,1)S(1)} collective-permute-done((bf16[640,256]{1,0:T(8,128)(2,1)S(1)}, bf16[640,256]{1,0:T(8,128)(2,1)S(1)}, u32[]{:S(2)}, u32[]{:S(2)}) %collective-permute-start.6) | collective-permute-done | bytes 327712 | tf_op jit(solution)/shard_map/ppermute | solution.py:26
  30.7 0.1 convert_add_fusion
  30.8 2.1 %collective-permute-start.7 = (bf16[320,256]{1,0:T(8,128)(2,1)S(1)}, bf16[320,256]{1,0:T(8,128)(2,1)S(1)}, u32[]{:S(2)}, u32[]{:S(2)}) collective-permute-start(bf16[320,256]{1,0:T(8,128)(2,1)S(1)} %dynamic-slice_convert_fusion), channel_id=1, source_target_pairs={{0,2},{1,3},{2,0},{3,1},{4,6},{5,7},{6,4},{7,5},{8,10},{9,11},{10,... | collective-permute-start | bytes 491528 | tf_op jit(solution)/shard_map/ppermute | solution.py:26
  32.9 4.5 %collective-permute-done.7 = bf16[320,256]{1,0:T(8,128)(2,1)S(1)} collective-permute-done((bf16[320,256]{1,0:T(8,128)(2,1)S(1)}, bf16[320,256]{1,0:T(8,128)(2,1)S(1)}, u32[]{:S(2)}, u32[]{:S(2)}) %collective-permute-start.7) | collective-permute-done | bytes 163872 | tf_op jit(solution)/shard_map/ppermute | solution.py:26
  37.4 11.8 %all_to_all.10 = bf16[4,112,256]{2,1,0:T(8,128)(2,1)S(1)} all-to-all(bf16[4,112,256]{2,1,0:T(8,128)(2,1)S(1)} %maximum_maximum_fusion), channel_id=1, replica_groups=mesh['groups'=2,'wide'=4,'narrow'=4] {'wide'}, dimensions={0} | all-to-all | bytes 458752 | tf_op jit(solution)/shard_map/all_to_all | solution.py:689
  49.4 9.2 %all_to_all.11 = bf16[4,80,256]{2,1,0:T(8,128)(2,1)S(1)} all-to-all(bf16[4,80,256]{2,1,0:T(8,128)(2,1)S(1)} %broadcast_in_dim.3), channel_id=1, replica_groups=mesh['groups'=2,'wide'=4,'narrow'=4] {'wide'}, dimensions={0} | all-to-all | bytes 327680 | tf_op jit(solution)/shard_map/all_to_all | solution.py:695
  58.6 1.5 %collective-permute-start.8 = (bf16[320,256]{1,0:T(8,128)(2,1)S(1)}, bf16[320,256]{1,0:T(8,128)(2,1)S(1)}, u32[]{:S(2)}, u32[]{:S(2)}) collective-permute-start(bf16[320,256]{1,0:T(8,128)(2,1)S(1)} %bitcast.26), channel_id=1, source_target_pairs={{0,2},{1,3},{2,0},{3,1},{4,6},{5,7},{6,4},{7,5},{8,10},{9,11},{10,... | collective-permute-start | bytes 491528 | tf_op jit(solution)/shard_map/ppermute | solution.py:26
  60.0 3.8 %collective-permute-done.8 = bf16[320,256]{1,0:T(8,128)(2,1)S(1)} collective-permute-done((bf16[320,256]{1,0:T(8,128)(2,1)S(1)}, bf16[320,256]{1,0:T(8,128)(2,1)S(1)}, u32[]{:S(2)}, u32[]{:S(2)}) %collective-permute-start.8) | collective-permute-done | bytes 163872 | tf_op jit(solution)/shard_map/ppermute | solution.py:26
  63.9 0.1 maximum_select_fusion.1
  64.0 0.1 collective-permute-start.9
  64.1 0.6 slice.10
  64.7 1.0 %collective-permute-done.9 = bf16[640,256]{1,0:T(8,128)(2,1)S(1)} collective-permute-done((bf16[640,256]{1,0:T(8,128)(2,1)S(1)}, bf16[640,256]{1,0:T(8,128)(2,1)S(1)}, u32[]{:S(2)}, u32[]{:S(2)}) %collective-permute-start.9) | collective-permute-done | bytes 327712 | tf_op jit(solution)/shard_map/ppermute | solution.py:26
  65.7 0.2 maximum_select_fusion
  66.0 1.2 %convert_multiply_fusion = f32[5,256,256]{2,1,0:T(8,128)} fusion(bf16[5,256,256]{2,1,0:T(8,128)(2,1)S(1)} %bitcast.24, f32[5]{0:T(128)S(1)} %copy-done.16), kind=kLoop, calls=%fused_computation | loop fusion | flops 655360 | bytes 1966100 | tf_op jit(solution)/shard_map/mul | solution.py:728
  (42 shorter events, 0.2 us)
Async XLA Ops:
  0.7 1.8 %copy-start.1 = (bf16[16,32,256]{2,1,0:T(8,128)(2,1)S(1)}, bf16[16,32,256]{2,1,0:T(8,128)(2,1)}, u32[]{:S(2)}) copy-start(bf16[16,32,256]{2,1,0:T(8,128)(2,1)} %param.18) | copy-start | bytes 786436
  0.7 1.8 %copy-start.11 = (bf16[4,8,256]{2,1,0:T(8,128)(2,1)S(1)}, bf16[4,8,256]{2,1,0:T(8,128)(2,1)}, u32[]{:S(2)}) copy-start(bf16[4,8,256]{2,1,0:T(8,128)(2,1)} %param.24) | copy-start | bytes 49156
  0.7 1.8 %copy-start.12 = (s32[36,4,8]{0,2,1:T(8,128)S(1)}, s32[36,4,8]{0,2,1:T(8,128)}, u32[]{:S(2)}) copy-start(s32[36,4,8]{0,2,1:T(8,128)} %param.23) | copy-start | bytes 13828
  0.7 1.9 %copy-start.13 = (bf16[32,256]{1,0:T(8,128)(2,1)S(1)}, bf16[32,256]{1,0:T(8,128)(2,1)}, u32[]{:S(2)}) copy-start(bf16[32,256]{1,0:T(8,128)(2,1)} %rows_ref.1) | copy-start | bytes 49156
  0.7 1.9 %copy-start.14 = (s32[32]{0:T(128)S(1)}, s32[32]{0:T(128)}, u32[]{:S(2)}) copy-start(s32[32]{0:T(128)} %param.21) | copy-start | bytes 388
  0.7 1.9 %copy-start.15 = (s32[32]{0:T(128)S(1)}, s32[32]{0:T(128)}, u32[]{:S(2)}) copy-start(s32[32]{0:T(128)} %param.22) | copy-start | bytes 388
  2.6 14.2 %copy-start = (bf16[256,256]{1,0:T(8,128)(2,1)S(1)}, bf16[256,256]{1,0:T(8,128)(2,1)}, u32[]{:S(2)}) copy-start(bf16[256,256]{1,0:T(8,128)(2,1)} %refs_15_.1) | copy-start | bytes 393220
  2.6 14.2 %copy-start.10 = (bf16[2,32,128]{2,1,0:T(8,128)(2,1)S(1)}, bf16[2,32,128]{2,1,0:T(8,128)(2,1)}, u32[]{:S(2)}) copy-start(bf16[2,32,128]{2,1,0:T(8,128)(2,1)} %constant.63.clone.refs_4_) | copy-start | bytes 49156
  2.6 18.9 %copy-start.3 = (bf16[256,256]{1,0:T(8,128)(2,1)S(1)}, bf16[256,256]{1,0:T(8,128)(2,1)}, u32[]{:S(2)}) copy-start(bf16[256,256]{1,0:T(8,128)(2,1)} %refs_16_.1) | copy-start | bytes 393220
  2.6 18.9 %copy-start.4 = (bf16[256,256]{1,0:T(8,128)(2,1)S(1)}, bf16[256,256]{1,0:T(8,128)(2,1)}, u32[]{:S(2)}) copy-start(bf16[256,256]{1,0:T(8,128)(2,1)} %refs_17_.1) | copy-start | bytes 393220
  3.4 19.3 %copy-start.2 = (bf16[2,128,384]{2,1,0:T(8,128)(2,1)S(1)}, bf16[2,128,384]{2,1,0:T(8,128)(2,1)}, u32[]{:S(2)}) copy-start(bf16[2,128,384]{2,1,0:T(8,128)(2,1)} %constant.65.clone.refs_12_) | copy-start | bytes 589828
  3.4 19.3 %copy-start.5 = (bf16[256,256]{1,0:T(8,128)(2,1)S(1)}, bf16[256,256]{1,0:T(8,128)(2,1)}, u32[]{:S(2)}) copy-start(bf16[256,256]{1,0:T(8,128)(2,1)} %refs_18_.1) | copy-start | bytes 393220
  3.4 19.3 %copy-start.6 = (bf16[256,256]{1,0:T(8,128)(2,1)S(1)}, bf16[256,256]{1,0:T(8,128)(2,1)}, u32[]{:S(2)}) copy-start(bf16[256,256]{1,0:T(8,128)(2,1)} %refs_19_.1) | copy-start | bytes 393220
  3.4 19.3 %copy-start.7 = (bf16[2,128,192]{2,1,0:T(8,128)(2,1)S(1)}, bf16[2,128,192]{2,1,0:T(8,128)(2,1)}, u32[]{:S(2)}) copy-start(bf16[2,128,192]{2,1,0:T(8,128)(2,1)} %constant.64.clone.refs_11_) | copy-start | bytes 294916
  3.4 19.3 %copy-start.8 = (bf16[128,256]{1,0:T(8,128)(2,1)S(1)}, bf16[128,256]{1,0:T(8,128)(2,1)}, u32[]{:S(2)}) copy-start(bf16[128,256]{1,0:T(8,128)(2,1)} %constant.67.clone.refs_14_) | copy-start | bytes 196612
  3.4 19.3 %copy-start.9 = (f32[2,16,384]{2,1,0:T(8,128)S(1)}, f32[2,16,384]{2,1,0:T(8,128)}, u32[]{:S(2)}) copy-start(f32[2,16,384]{2,1,0:T(8,128)} %constant.66.clone.refs_13_) | copy-start | bytes 147460
  3.4 13.4 %collective-permute-start = (bf16[368,256]{1,0:T(8,128)(2,1)S(1)}, bf16[368,256]{1,0:T(8,128)(2,1)S(1)}, u32[]{:S(2)}, u32[]{:S(2)}) collective-permute-start(bf16[368,256]{1,0:T(8,128)(2,1)S(1)} %get-tuple-element.25), channel_id=1, source_target_pairs={{0,4},{4,0},{8,12},{12,8},{1,5},{5,1},{9,13},{13,9},{2,6},{6,2},{1... | collective-permute-start | bytes 565256 | tf_op jit(solution)/shard_map/ppermute | solution.py:26
  6.5 10.3 %collective-permute-start.1 = (bf16[320,256]{1,0:T(8,128)(2,1)S(1)}, bf16[320,256]{1,0:T(8,128)(2,1)S(1)}, u32[]{:S(2)}, u32[]{:S(2)}) collective-permute-start(bf16[320,256]{1,0:T(8,128)(2,1)S(1)} %get-tuple-element.26), channel_id=1, source_target_pairs={{4,8},{8,4},{5,9},{9,5},{6,10},{10,6},{7,11},{11,7},{20,24},{24,20... | collective-permute-start | bytes 491528 | tf_op jit(solution)/shard_map/ppermute | solution.py:32
  7.2 9.3 %collective-permute-start.2 = (bf16[48,256]{1,0:T(8,128)(2,1)S(1)}, bf16[48,256]{1,0:T(8,128)(2,1)S(1)}, u32[]{:S(2)}, u32[]{:S(2)}) collective-permute-start(bf16[48,256]{1,0:T(8,128)(2,1)S(1)} %get-tuple-element.27), channel_id=1, source_target_pairs={{0,8},{4,12},{8,0},{12,4},{1,9},{5,13},{9,1},{13,5},{2,10},{6,14},... | collective-permute-start | bytes 73736 | tf_op jit(solution)/shard_map/ppermute | solution.py:26
  11.1 5.7 %collective-permute-start.3 = (bf16[48,256]{1,0:T(8,128)(2,1)S(1)}, bf16[48,256]{1,0:T(8,128)(2,1)S(1)}, u32[]{:S(2)}, u32[]{:S(2)}) collective-permute-start(bf16[48,256]{1,0:T(8,128)(2,1)S(1)} %get-tuple-element.28), channel_id=1, source_target_pairs={{0,12},{4,8},{8,4},{12,0},{1,13},{5,9},{9,5},{13,1},{2,14},{6,10},... | collective-permute-start | bytes 73736 | tf_op jit(solution)/shard_map/ppermute | solution.py:26
  17.9 4.5 %collective-permute-start.4 = (bf16[576,256]{1,0:T(8,128)(2,1)S(1)}, bf16[576,256]{1,0:T(8,128)(2,1)S(1)}, u32[]{:S(2)}, u32[]{:S(2)}) collective-permute-start(bf16[576,256]{1,0:T(8,128)(2,1)S(1)} %get-tuple-element.29), channel_id=1, source_target_pairs={{1,2},{2,1},{5,6},{6,5},{9,10},{10,9},{13,14},{14,13},{17,18},{18,... | collective-permute-start | bytes 884744 | tf_op jit(solution)/shard_map/ppermute | solution.py:32
  18.6 4.1 %collective-permute-start.5 = (bf16[576,256]{1,0:T(8,128)(2,1)S(1)}, bf16[576,256]{1,0:T(8,128)(2,1)S(1)}, u32[]{:S(2)}, u32[]{:S(2)}) collective-permute-start(bf16[576,256]{1,0:T(8,128)(2,1)S(1)} %get-tuple-element.30), channel_id=1, source_target_pairs={{0,1},{1,0},{2,3},{3,2},{4,5},{5,4},{6,7},{7,6},{8,9},{9,8},{10,11... | collective-permute-start | bytes 884744 | tf_op jit(solution)/shard_map/ppermute | solution.py:26
  26.3 4.4 %collective-permute-start.6 = (bf16[640,256]{1,0:T(8,128)(2,1)S(1)}, bf16[640,256]{1,0:T(8,128)(2,1)S(1)}, u32[]{:S(2)}, u32[]{:S(2)}) collective-permute-start(bf16[640,256]{1,0:T(8,128)(2,1)S(1)} %get-tuple-element.41), channel_id=1, source_target_pairs={{0,1},{1,0},{2,3},{3,2},{4,5},{5,4},{6,7},{7,6},{8,9},{9,8},{10,11... | collective-permute-start | bytes 983048 | tf_op jit(solution)/shard_map/ppermute | solution.py:26
  30.8 6.6 %collective-permute-start.7 = (bf16[320,256]{1,0:T(8,128)(2,1)S(1)}, bf16[320,256]{1,0:T(8,128)(2,1)S(1)}, u32[]{:S(2)}, u32[]{:S(2)}) collective-permute-start(bf16[320,256]{1,0:T(8,128)(2,1)S(1)} %dynamic-slice_convert_fusion), channel_id=1, source_target_pairs={{0,2},{1,3},{2,0},{3,1},{4,6},{5,7},{6,4},{7,5},{8,10},{9,11},{10,... | collective-permute-start | bytes 491528 | tf_op jit(solution)/shard_map/ppermute | solution.py:26
  49.3 16.7 %copy-start.16 = (f32[5]{0:T(128)S(1)}, f32[5]{0:T(128)}, u32[]{:S(2)}) copy-start(f32[5]{0:T(128)} %constant.72) | copy-start | bytes 64
  58.6 5.3 %collective-permute-start.8 = (bf16[320,256]{1,0:T(8,128)(2,1)S(1)}, bf16[320,256]{1,0:T(8,128)(2,1)S(1)}, u32[]{:S(2)}, u32[]{:S(2)}) collective-permute-start(bf16[320,256]{1,0:T(8,128)(2,1)S(1)} %bitcast.26), channel_id=1, source_target_pairs={{0,2},{1,3},{2,0},{3,1},{4,6},{5,7},{6,4},{7,5},{8,10},{9,11},{10,... | collective-permute-start | bytes 491528 | tf_op jit(solution)/shard_map/ppermute | solution.py:26
  64.0 1.7 %collective-permute-start.9 = (bf16[640,256]{1,0:T(8,128)(2,1)S(1)}, bf16[640,256]{1,0:T(8,128)(2,1)S(1)}, u32[]{:S(2)}, u32[]{:S(2)}) collective-permute-start(bf16[640,256]{1,0:T(8,128)(2,1)S(1)} %maximum_select_fusion.1), channel_id=1, source_target_pairs={{0,1},{1,0},{2,3},{3,2},{4,5},{5,4},{6,7},{7,6},{8,9},{9,8},{10,11... | collective-permute-start | bytes 983048 | tf_op jit(solution)/shard_map/ppermute | solution.py:26

commit v10 on v7

--- a/solution.py
+++ b/solution.py
@@ -24,6 +24,11 @@
 def swapped(block, axis, bits):
     count = lax.axis_size(axis)
     return lax.ppermute(block, axis, [(i, i ^ bits) for i in range(count)])
+
+
+def shifted(block, axis, step):
+    count = lax.axis_size(axis)
+    return lax.ppermute(block, axis, [(i, (i + step) % count) for i in range(count)])
 
 
 def swapped_between(block, axis):
@@ -682,21 +687,23 @@
     part = piece.shape[0] // wide_count
     rounded = piece.astype(BF16)
     own = lax.dynamic_slice_in_dim(piece, wide_at * part, part)
-    order = sorted(range(1, wide_count), reverse=True)
-    for k in order:
-        sent = lax.dynamic_slice_in_dim(rounded, (wide_at ^ k) * part, part)
+    for k in range(1, wide_count):
+        target = (wide_at + k) % wide_count
+        sent = lax.dynamic_slice_in_dim(rounded, target * part, part)
         if whole_column:
-            sent = jnp.concatenate([sent, back_blocks[k]])
-        got = swapped(sent, "wide", k).astype(F32)
+            block = lax.dynamic_slice_in_dim(back_blocks, target ^ wide_at, 1)
+            sent = jnp.concatenate([sent, block[0]])
+        got = shifted(sent, "wide", k).astype(F32)
         own = own + got[:part]
         if whole_column:
             row_back = row_back + got[part:]
     own = own.astype(BF16)
     gathered = jnp.zeros((wide_count * part, channels), BF16)
     gathered = lax.dynamic_update_slice_in_dim(gathered, own, wide_at * part, 0)
-    for k in order:
-        got = swapped(own, "wide", k)
-        gathered = lax.dynamic_update_slice_in_dim(gathered, got, (wide_at ^ k) * part, 0)
+    for k in range(1, wide_count):
+        source = (wide_at - k) % wide_count
+        got = shifted(own, "wide", k)
+        gathered = lax.dynamic_update_slice_in_dim(gathered, got, source * part, 0)
     for bit in reversed(bits):
         upper = (narrow_at // bit) % 2
         other = swapped(gathered, "narrow", bit)

time: 62 us -> 61.6 us (level)
    ppermute x14 -> x8, starting transfers between devices: 28.8 us -> 19.8 us  [swapped(): return lax.ppermute(block, axis, [(i, i ^ bits) for i in range(count)])]
    ppermute x0 -> x6, starting transfers between devices: none -> 8.53 us  [shifted(): lax.ppermute(block, axis, [(i, (i + step) % count) for i in range(count)])]
    ppermute x0 -> x6, waiting for transfers between devices: none -> 6.67 us  [shifted(): lax.ppermute(block, axis, [(i, (i + step) % count) for i in range(count)])]
    ppermute x14 -> x8, waiting for transfers between devices: 19.9 us -> 13.4 us  [swapped(): return lax.ppermute(block, axis, [(i, i ^ bits) for i in range(count)])]
  transfers between devices with their start and end apart: 16 -> 16, of which waited for: 12 -> 13; matrix products, arithmetic and copies ran while one was open for 1% -> 1% of each run, Pallas kernels for 1% -> 1%
where the time goes in v10:
time: 61.6 us; the launch traced here: 61.4 us
  starting transfers between devices  29.7 us (48%)
  waiting for transfers between devices  20.1 us (33%)
  Pallas kernels  7.4 us (12%)
  other arithmetic  2.48 us (4%)
  between operations  1.61 us (3%)
    ppermute x8, starting transfers between devices, swapped(): return lax.ppermute(block, axis, [(i, i ^ bits) for i in range(count)])  19.8 us
    ppermute x8, waiting for transfers between devices, swapped(): return lax.ppermute(block, axis, [(i, i ^ bits) for i in range(count)])  13.4 us
    ppermute x6, starting transfers between devices, shifted(): lax.ppermute(block, axis, [(i, (i + step) % count) for i in range(count)])  8.53 us
    pallas_call x5, Pallas kernels, call(): pl.pallas_call(kernel, out_shape=tuple(out_shapes), in_specs=[pl.BlockSpe...  7.4 us
    ppermute x6, waiting for transfers between devices, shifted(): lax.ppermute(block, axis, [(i, (i + step) % count) for i in range(count)])  6.67 us
    ppermute x2, starting transfers between devices, swapped_between(): return lax.ppermute(block, axis, pairs + [(j, i) for i, j in pairs])  1.34 us
    mul x1, other arithmetic, local(): totals.reshape(5, channels, channels).astype(F32) * scales[:, None, None]  1.24 us
  transfers between devices with their start and end apart: 16, of which 13 were waited for; matrix products, arithmetic and copies ran while one was open for 1% of the time, Pallas kernels for 1%

profile of v10, /device:TPU:0, one launch (start us, length us, event | category | flops | bytes accessed | tf_op | source)
XLA Modules:
  0.0 61.4 jit_solution(6639661526538802462)
XLA Ops:
  0.7 1.1 %shard_map.193.place_ref.refs_0_ = s32[2]{0:T(128)S(1)} custom-call(s32[2]{0:T(128)S(1)} %pad_add_fusion.place_ref), custom_call_target="tpu_custom_call" | custom-call | flops 10000000000 | bytes 16 | tf_op jit(solution)/shard_map/pallas_call | solution.py:466
  2.6 0.7 %shard_map.194 = (bf16[368,256]{1,0:T(8,128)(2,1)S(1)}, bf16[320,256]{1,0:T(8,128)(2,1)S(1)}, bf16[48,256]{1,0:T(8,128)(2,1)S(1)}, bf16[48,256]{1,0:T(8,128)(2,1...) custom-call(s32[2]{0:T(128)S(1)} %shard_map.193.place_ref.refs_0_, bf16[512,256]{1,0:T(8,128)(2,1)S(1)} %bitcast.21, ...), custom_call_target="tpu_custom_call" | custom-call | flops 10000000000 | bytes 758540 | tf_op jit(solution)/shard_map/pallas_call | solution.py:466
  3.4 3.1 %collective-permute-start = (bf16[368,256]{1,0:T(8,128)(2,1)S(1)}, bf16[368,256]{1,0:T(8,128)(2,1)S(1)}, u32[]{:S(2)}, u32[]{:S(2)}) collective-permute-start(bf16[368,256]{1,0:T(8,128)(2,1)S(1)} %get-tuple-element.25), channel_id=1, source_target_pairs={{0,4},{4,0},{8,12},{12,8},{1,5},{5,1},{9,13},{13,9},{2,6},{6,2},{1... | collective-permute-start | bytes 565256 | tf_op jit(solution)/shard_map/ppermute | solution.py:26
  6.5 0.7 %collective-permute-start.1 = (bf16[320,256]{1,0:T(8,128)(2,1)S(1)}, bf16[320,256]{1,0:T(8,128)(2,1)S(1)}, u32[]{:S(2)}, u32[]{:S(2)}) collective-permute-start(bf16[320,256]{1,0:T(8,128)(2,1)S(1)} %get-tuple-element.26), channel_id=1, source_target_pairs={{4,8},{8,4},{5,9},{9,5},{6,10},{10,6},{7,11},{11,7},{20,24},{24,20... | collective-permute-start | bytes 491528 | tf_op jit(solution)/shard_map/ppermute | solution.py:37
  7.2 3.9 %collective-permute-start.2 = (bf16[48,256]{1,0:T(8,128)(2,1)S(1)}, bf16[48,256]{1,0:T(8,128)(2,1)S(1)}, u32[]{:S(2)}, u32[]{:S(2)}) collective-permute-start(bf16[48,256]{1,0:T(8,128)(2,1)S(1)} %get-tuple-element.27), channel_id=1, source_target_pairs={{0,8},{4,12},{8,0},{12,4},{1,9},{5,13},{9,1},{13,5},{2,10},{6,14},... | collective-permute-start | bytes 73736 | tf_op jit(solution)/shard_map/ppermute | solution.py:26
  11.1 2.9 %collective-permute-start.3 = (bf16[48,256]{1,0:T(8,128)(2,1)S(1)}, bf16[48,256]{1,0:T(8,128)(2,1)S(1)}, u32[]{:S(2)}, u32[]{:S(2)}) collective-permute-start(bf16[48,256]{1,0:T(8,128)(2,1)S(1)} %get-tuple-element.28), channel_id=1, source_target_pairs={{0,12},{4,8},{8,4},{12,0},{1,13},{5,9},{9,5},{13,1},{2,14},{6,10},... | collective-permute-start | bytes 73736 | tf_op jit(solution)/shard_map/ppermute | solution.py:26
  14.0 2.5 %collective-permute-done.2.refs_8_ = bf16[48,256]{1,0:T(8,128)(2,1)S(1)} collective-permute-done((bf16[48,256]{1,0:T(8,128)(2,1)S(1)}, bf16[48,256]{1,0:T(8,128)(2,1)S(1)}, u32[]{:S(2)}, u32[]{:S(2)}) %collective-permute-start.2) | collective-permute-done | bytes 24608 | tf_op jit(solution)/shard_map/ppermute | solution.py:26
  16.9 1.0 %shard_map.195 = (bf16[1088,256]{1,0:T(8,128)(2,1)S(1)}, bf16[576,256]{1,0:T(8,128)(2,1)S(1)}, bf16[576,256]{1,0:T(8,128)(2,1)S(1)}, bf16[128,256]{1,0:T(8,128)(...) custom-call(s32[2]{0:T(128)S(1)} %shard_map.193.place_ref.refs_0_, bf16[512,256]{1,0:T(8,128)(2,1)S(1)} %bitcast.22, ...), custom_call_target="tpu_custom_call" | custom-call | flops 71303168 | bytes 2150408 | tf_op jit(solution)/shard_map/pallas_call | solution.py:466
  17.9 0.7 %collective-permute-start.4 = (bf16[576,256]{1,0:T(8,128)(2,1)S(1)}, bf16[576,256]{1,0:T(8,128)(2,1)S(1)}, u32[]{:S(2)}, u32[]{:S(2)}) collective-permute-start(bf16[576,256]{1,0:T(8,128)(2,1)S(1)} %get-tuple-element.29), channel_id=1, source_target_pairs={{1,2},{2,1},{5,6},{6,5},{9,10},{10,9},{13,14},{14,13},{17,18},{18,... | collective-permute-start | bytes 884744 | tf_op jit(solution)/shard_map/ppermute | solution.py:37
  18.6 2.9 %collective-permute-start.5 = (bf16[576,256]{1,0:T(8,128)(2,1)S(1)}, bf16[576,256]{1,0:T(8,128)(2,1)S(1)}, u32[]{:S(2)}, u32[]{:S(2)}) collective-permute-start(bf16[576,256]{1,0:T(8,128)(2,1)S(1)} %get-tuple-element.30), channel_id=1, source_target_pairs={{0,1},{1,0},{2,3},{3,2},{4,5},{5,4},{6,7},{7,6},{8,9},{9,8},{10,11... | collective-permute-start | bytes 884744 | tf_op jit(solution)/shard_map/ppermute | solution.py:26
  21.5 0.9 %shard_map.196 = (bf16[1088,256]{1,0:T(8,128)(2,1)S(1)}, bf16[512,256]{1,0:T(8,128)(2,1)S(1)}, f32[512,256]{1,0:T(8,128)S(1)}, f32[512,256]{1,0:T(8,128)S(1)}) custom-call(bf16[1088,256]{1,0:T(8,128)(2,1)S(1)} %get-tuple-element.32.blended_ref.refs_4_, bf16[256,256]{1,0:T(8,128)(2,1)S(1)} %copy-done.3, bf16[256,256]{1,0:T(8,128)(2,1)S(1)} %copy-done.4), custom_call_target="tpu_custom_call" | custom-call | flops 285212672 | bytes 2686976 | tf_op jit(solution)/shard_map/pallas_call | solution.py:466
  22.7 3.6 %shard_map.197 = (bf16[512,256]{1,0:T(8,128)(2,1)}, bf16[128,256]{1,0:T(8,128)(2,1)S(1)}, bf16[640,256]{1,0:T(8,128)(2,1)S(1)}, f32[640,256]{1,0:T(8,128)S(1)}) custom-call(s32[1]{0:T(128)} %bitcast.refs_0_, bf16[576,256]{1,0:T(8,128)(2,1)S(1)} %collective-permute-done.4.refs_1_, bf16[576,256]{1,0:T(8,128)(2,1)S(1)} %collective-permute-done.5.refs_2_, ...), custom_call_target="tpu_custom_call" | custom-call | flops 402653184 | bytes 5525508 | tf_op jit(solution)/shard_map/pallas_call | solution.py:466
  26.3 3.1 %collective-permute-start.6 = (bf16[640,256]{1,0:T(8,128)(2,1)S(1)}, bf16[640,256]{1,0:T(8,128)(2,1)S(1)}, u32[]{:S(2)}, u32[]{:S(2)}) collective-permute-start(bf16[640,256]{1,0:T(8,128)(2,1)S(1)} %get-tuple-element.42), channel_id=1, source_target_pairs={{0,1},{1,0},{2,3},{3,2},{4,5},{5,4},{6,7},{7,6},{8,9},{9,8},{10,11... | collective-permute-start | bytes 983048 | tf_op jit(solution)/shard_map/ppermute | solution.py:26
  29.4 1.3 %collective-permute-done.6 = bf16[640,256]{1,0:T(8,128)(2,1)S(1)} collective-permute-done((bf16[640,256]{1,0:T(8,128)(2,1)S(1)}, bf16[640,256]{1,0:T(8,128)(2,1)S(1)}, u32[]{:S(2)}, u32[]{:S(2)}) %collective-permute-start.6) | collective-permute-done | bytes 327712 | tf_op jit(solution)/shard_map/ppermute | solution.py:26
  30.8 2.1 %collective-permute-start.7 = (bf16[320,256]{1,0:T(8,128)(2,1)S(1)}, bf16[320,256]{1,0:T(8,128)(2,1)S(1)}, u32[]{:S(2)}, u32[]{:S(2)}) collective-permute-start(bf16[320,256]{1,0:T(8,128)(2,1)S(1)} %dynamic-slice_convert_fusion), channel_id=1, source_target_pairs={{0,2},{1,3},{2,0},{3,1},{4,6},{5,7},{6,4},{7,5},{8,10},{9,11},{10,... | collective-permute-start | bytes 491528 | tf_op jit(solution)/shard_map/ppermute | solution.py:26
  32.9 4.5 %collective-permute-done.7 = bf16[320,256]{1,0:T(8,128)(2,1)S(1)} collective-permute-done((bf16[320,256]{1,0:T(8,128)(2,1)S(1)}, bf16[320,256]{1,0:T(8,128)(2,1)S(1)}, u32[]{:S(2)}, u32[]{:S(2)}) %collective-permute-start.7) | collective-permute-done | bytes 163872 | tf_op jit(solution)/shard_map/ppermute | solution.py:26
  37.4 0.8 %collective-permute-start.8 = (bf16[112,256]{1,0:T(8,128)(2,1)S(1)}, bf16[112,256]{1,0:T(8,128)(2,1)S(1)}, u32[]{:S(2)}, u32[]{:S(2)}) collective-permute-start(bf16[112,256]{1,0:T(8,128)(2,1)S(1)} %pad_maximum_fusion), channel_id=1, source_target_pairs={{0,4},{4,8},{8,12},{12,0},{1,5},{5,9},{9,13},{13,1},{2,6},{6,10},{... | collective-permute-start | bytes 172040 | tf_op jit(solution)/shard_map/ppermute | solution.py:31
  38.3 2.6 %collective-permute-start.9 = (bf16[112,256]{1,0:T(8,128)(2,1)S(1)}, bf16[112,256]{1,0:T(8,128)(2,1)S(1)}, u32[]{:S(2)}, u32[]{:S(2)}) collective-permute-start(bf16[112,256]{1,0:T(8,128)(2,1)S(1)} %pad_maximum_fusion.1), channel_id=1, source_target_pairs={{0,8},{4,12},{8,0},{12,4},{1,9},{5,13},{9,1},{13,5},{2,10},{6,14},... | collective-permute-start | bytes 172040 | tf_op jit(solution)/shard_map/ppermute | solution.py:31
  40.9 1.2 %collective-permute-start.10 = (bf16[112,256]{1,0:T(8,128)(2,1)S(1)}, bf16[112,256]{1,0:T(8,128)(2,1)S(1)}, u32[]{:S(2)}, u32[]{:S(2)}) collective-permute-start(bf16[112,256]{1,0:T(8,128)(2,1)S(1)} %pad_maximum_fusion.2), channel_id=1, source_target_pairs={{0,12},{4,0},{8,4},{12,8},{1,13},{5,1},{9,5},{13,9},{2,14},{6,2},{... | collective-permute-start | bytes 172040 | tf_op jit(solution)/shard_map/ppermute | solution.py:31
  42.1 1.9 %collective-permute-done.8 = bf16[112,256]{1,0:T(8,128)(2,1)S(1)} collective-permute-done((bf16[112,256]{1,0:T(8,128)(2,1)S(1)}, bf16[112,256]{1,0:T(8,128)(2,1)S(1)}, u32[]{:S(2)}, u32[]{:S(2)}) %collective-permute-start.8) | collective-permute-done | bytes 57376 | tf_op jit(solution)/shard_map/ppermute | solution.py:31
  44.0 1.3 %collective-permute-done.9 = bf16[112,256]{1,0:T(8,128)(2,1)S(1)} collective-permute-done((bf16[112,256]{1,0:T(8,128)(2,1)S(1)}, bf16[112,256]{1,0:T(8,128)(2,1)S(1)}, u32[]{:S(2)}, u32[]{:S(2)}) %collective-permute-start.9) | collective-permute-done | bytes 57376 | tf_op jit(solution)/shard_map/ppermute | solution.py:31
  45.5 1.1 %collective-permute-start.11 = (bf16[80,256]{1,0:T(8,128)(2,1)S(1)}, bf16[80,256]{1,0:T(8,128)(2,1)S(1)}, u32[]{:S(2)}, u32[]{:S(2)}) collective-permute-start(bf16[80,256]{1,0:T(8,128)(2,1)S(1)} %get-tuple-element.44), channel_id=1, source_target_pairs={{0,4},{4,8},{8,12},{12,0},{1,5},{5,9},{9,13},{13,1},{2,6},{6,10},{... | collective-permute-start | bytes 122888 | tf_op jit(solution)/shard_map/ppermute | solution.py:31
  46.7 2.1 %collective-permute-start.12 = (bf16[80,256]{1,0:T(8,128)(2,1)S(1)}, bf16[80,256]{1,0:T(8,128)(2,1)S(1)}, u32[]{:S(2)}, u32[]{:S(2)}) collective-permute-start(bf16[80,256]{1,0:T(8,128)(2,1)S(1)} %get-tuple-element.44), channel_id=1, source_target_pairs={{0,8},{4,12},{8,0},{12,4},{1,9},{5,13},{9,1},{13,5},{2,10},{6,14},... | collective-permute-start | bytes 122888 | tf_op jit(solution)/shard_map/ppermute | solution.py:31
  48.8 0.6 %collective-permute-start.13 = (bf16[80,256]{1,0:T(8,128)(2,1)S(1)}, bf16[80,256]{1,0:T(8,128)(2,1)S(1)}, u32[]{:S(2)}, u32[]{:S(2)}) collective-permute-start(bf16[80,256]{1,0:T(8,128)(2,1)S(1)} %get-tuple-element.44), channel_id=1, source_target_pairs={{0,12},{4,0},{8,4},{12,8},{1,13},{5,1},{9,5},{13,9},{2,14},{6,2},{... | collective-permute-start | bytes 122888 | tf_op jit(solution)/shard_map/ppermute | solution.py:31
  49.4 2.2 %collective-permute-done.11 = bf16[80,256]{1,0:T(8,128)(2,1)S(1)} collective-permute-done((bf16[80,256]{1,0:T(8,128)(2,1)S(1)}, bf16[80,256]{1,0:T(8,128)(2,1)S(1)}, u32[]{:S(2)}, u32[]{:S(2)}) %collective-permute-start.11) | collective-permute-done | bytes 40992 | tf_op jit(solution)/shard_map/ppermute | solution.py:31
  51.6 0.7 %collective-permute-done.12 = bf16[80,256]{1,0:T(8,128)(2,1)S(1)} collective-permute-done((bf16[80,256]{1,0:T(8,128)(2,1)S(1)}, bf16[80,256]{1,0:T(8,128)(2,1)S(1)}, u32[]{:S(2)}, u32[]{:S(2)}) %collective-permute-start.12) | collective-permute-done | bytes 40992 | tf_op jit(solution)/shard_map/ppermute | solution.py:31
  52.3 0.5 collective-permute-done.13
  52.8 1.7 %collective-permute-start.14 = (bf16[320,256]{1,0:T(8,128)(2,1)S(1)}, bf16[320,256]{1,0:T(8,128)(2,1)S(1)}, u32[]{:S(2)}, u32[]{:S(2)}) collective-permute-start(bf16[320,256]{1,0:T(8,128)(2,1)S(1)} %constant_dynamic-update-slice_fusion), channel_id=1, source_target_pairs={{0,2},{1,3},{2,0},{3,1},{4,6},{5,7},{6,4},{7,5},{8,10},{9,11},{10,... | collective-permute-start | bytes 491528 | tf_op jit(solution)/shard_map/ppermute | solution.py:26
  54.5 3.6 %collective-permute-done.14 = bf16[320,256]{1,0:T(8,128)(2,1)S(1)} collective-permute-done((bf16[320,256]{1,0:T(8,128)(2,1)S(1)}, bf16[320,256]{1,0:T(8,128)(2,1)S(1)}, u32[]{:S(2)}, u32[]{:S(2)}) %collective-permute-start.14) | collective-permute-done | bytes 163872 | tf_op jit(solution)/shard_map/ppermute | solution.py:26
  58.3 0.6 %fusion.1 = bf16[32,256]{1,0:T(8,128)(2,1)} fusion(f32[112,256]{1,0:T(8,128)S(1)} %convert_element_type.43, f32[112,256]{1,0:T(8,128)S(1)} %convert_element_type.42, f32[112,256]{1,0:T(8,128)S(1)} %convert_element_type.41, bf16[128,256]{1,0:T(8,128)(2,1)S(1)} %get-tuple-element.40), kind=kLoop, calls=%fused_computation.14 | loop fusion | flops 40960 | bytes 131072 | tf_op jit(solution)/shard_map/convert_element_type | solution.py:717
  59.0 1.0 %collective-permute-done.15 = bf16[640,256]{1,0:T(8,128)(2,1)S(1)} collective-permute-done((bf16[640,256]{1,0:T(8,128)(2,1)S(1)}, bf16[640,256]{1,0:T(8,128)(2,1)S(1)}, u32[]{:S(2)}, u32[]{:S(2)}) %collective-permute-start.15) | collective-permute-done | bytes 327712 | tf_op jit(solution)/shard_map/ppermute | solution.py:26
  60.2 1.2 %convert_multiply_fusion = f32[5,256,256]{2,1,0:T(8,128)} fusion(bf16[5,256,256]{2,1,0:T(8,128)(2,1)S(1)} %bitcast.28, f32[5]{0:T(128)S(1)} %copy-done.16), kind=kLoop, calls=%fused_computation | loop fusion | flops 655360 | bytes 1966100 | tf_op jit(solution)/shard_map/mul | solution.py:738
  (60 shorter events, 1.6 us)
Async XLA Ops:
  0.7 1.8 %copy-start.11 = (bf16[4,8,256]{2,1,0:T(8,128)(2,1)S(1)}, bf16[4,8,256]{2,1,0:T(8,128)(2,1)}, u32[]{:S(2)}) copy-start(bf16[4,8,256]{2,1,0:T(8,128)(2,1)} %param.24) | copy-start | bytes 49156
  0.7 1.8 %copy-start.12 = (s32[36,4,8]{0,2,1:T(8,128)S(1)}, s32[36,4,8]{0,2,1:T(8,128)}, u32[]{:S(2)}) copy-start(s32[36,4,8]{0,2,1:T(8,128)} %param.23) | copy-start | bytes 13828
  0.7 1.9 %copy-start.13 = (bf16[32,256]{1,0:T(8,128)(2,1)S(1)}, bf16[32,256]{1,0:T(8,128)(2,1)}, u32[]{:S(2)}) copy-start(bf16[32,256]{1,0:T(8,128)(2,1)} %rows_ref.1) | copy-start | bytes 49156
  0.7 1.9 %copy-start.14 = (s32[32]{0:T(128)S(1)}, s32[32]{0:T(128)}, u32[]{:S(2)}) copy-start(s32[32]{0:T(128)} %param.21) | copy-start | bytes 388
  0.7 1.9 %copy-start.15 = (s32[32]{0:T(128)S(1)}, s32[32]{0:T(128)}, u32[]{:S(2)}) copy-start(s32[32]{0:T(128)} %param.22) | copy-start | bytes 388
  2.6 14.2 %copy-start = (bf16[256,256]{1,0:T(8,128)(2,1)S(1)}, bf16[256,256]{1,0:T(8,128)(2,1)}, u32[]{:S(2)}) copy-start(bf16[256,256]{1,0:T(8,128)(2,1)} %refs_15_.1) | copy-start | bytes 393220
  2.6 14.2 %copy-start.10 = (bf16[2,32,128]{2,1,0:T(8,128)(2,1)S(1)}, bf16[2,32,128]{2,1,0:T(8,128)(2,1)}, u32[]{:S(2)}) copy-start(bf16[2,32,128]{2,1,0:T(8,128)(2,1)} %constant.97.clone.refs_4_) | copy-start | bytes 49156
  2.6 18.9 %copy-start.3 = (bf16[256,256]{1,0:T(8,128)(2,1)S(1)}, bf16[256,256]{1,0:T(8,128)(2,1)}, u32[]{:S(2)}) copy-start(bf16[256,256]{1,0:T(8,128)(2,1)} %refs_16_.1) | copy-start | bytes 393220
  2.6 18.9 %copy-start.4 = (bf16[256,256]{1,0:T(8,128)(2,1)S(1)}, bf16[256,256]{1,0:T(8,128)(2,1)}, u32[]{:S(2)}) copy-start(bf16[256,256]{1,0:T(8,128)(2,1)} %refs_17_.1) | copy-start | bytes 393220
  3.4 19.3 %copy-start.2 = (bf16[2,128,384]{2,1,0:T(8,128)(2,1)S(1)}, bf16[2,128,384]{2,1,0:T(8,128)(2,1)}, u32[]{:S(2)}) copy-start(bf16[2,128,384]{2,1,0:T(8,128)(2,1)} %constant.99.clone.refs_12_) | copy-start | bytes 589828
  3.4 19.3 %copy-start.5 = (bf16[256,256]{1,0:T(8,128)(2,1)S(1)}, bf16[256,256]{1,0:T(8,128)(2,1)}, u32[]{:S(2)}) copy-start(bf16[256,256]{1,0:T(8,128)(2,1)} %refs_18_.1) | copy-start | bytes 393220
  3.4 19.3 %copy-start.6 = (bf16[256,256]{1,0:T(8,128)(2,1)S(1)}, bf16[256,256]{1,0:T(8,128)(2,1)}, u32[]{:S(2)}) copy-start(bf16[256,256]{1,0:T(8,128)(2,1)} %refs_19_.1) | copy-start | bytes 393220
  3.4 19.3 %copy-start.7 = (bf16[2,128,192]{2,1,0:T(8,128)(2,1)S(1)}, bf16[2,128,192]{2,1,0:T(8,128)(2,1)}, u32[]{:S(2)}) copy-start(bf16[2,128,192]{2,1,0:T(8,128)(2,1)} %constant.98.clone.refs_11_) | copy-start | bytes 294916
  3.4 19.3 %copy-start.8 = (bf16[128,256]{1,0:T(8,128)(2,1)S(1)}, bf16[128,256]{1,0:T(8,128)(2,1)}, u32[]{:S(2)}) copy-start(bf16[128,256]{1,0:T(8,128)(2,1)} %constant.101.clone.refs_14_) | copy-start | bytes 196612
  3.4 19.3 %copy-start.9 = (f32[2,16,384]{2,1,0:T(8,128)S(1)}, f32[2,16,384]{2,1,0:T(8,128)}, u32[]{:S(2)}) copy-start(f32[2,16,384]{2,1,0:T(8,128)} %constant.100.clone.refs_13_) | copy-start | bytes 147460
  3.4 13.4 %collective-permute-start = (bf16[368,256]{1,0:T(8,128)(2,1)S(1)}, bf16[368,256]{1,0:T(8,128)(2,1)S(1)}, u32[]{:S(2)}, u32[]{:S(2)}) collective-permute-start(bf16[368,256]{1,0:T(8,128)(2,1)S(1)} %get-tuple-element.25), channel_id=1, source_target_pairs={{0,4},{4,0},{8,12},{12,8},{1,5},{5,1},{9,13},{13,9},{2,6},{6,2},{1... | collective-permute-start | bytes 565256 | tf_op jit(solution)/shard_map/ppermute | solution.py:26
  6.5 10.3 %collective-permute-start.1 = (bf16[320,256]{1,0:T(8,128)(2,1)S(1)}, bf16[320,256]{1,0:T(8,128)(2,1)S(1)}, u32[]{:S(2)}, u32[]{:S(2)}) collective-permute-start(bf16[320,256]{1,0:T(8,128)(2,1)S(1)} %get-tuple-element.26), channel_id=1, source_target_pairs={{4,8},{8,4},{5,9},{9,5},{6,10},{10,6},{7,11},{11,7},{20,24},{24,20... | collective-permute-start | bytes 491528 | tf_op jit(solution)/shard_map/ppermute | solution.py:37
  7.2 9.3 %collective-permute-start.2 = (bf16[48,256]{1,0:T(8,128)(2,1)S(1)}, bf16[48,256]{1,0:T(8,128)(2,1)S(1)}, u32[]{:S(2)}, u32[]{:S(2)}) collective-permute-start(bf16[48,256]{1,0:T(8,128)(2,1)S(1)} %get-tuple-element.27), channel_id=1, source_target_pairs={{0,8},{4,12},{8,0},{12,4},{1,9},{5,13},{9,1},{13,5},{2,10},{6,14},... | collective-permute-start | bytes 73736 | tf_op jit(solution)/shard_map/ppermute | solution.py:26
  11.1 5.7 %collective-permute-start.3 = (bf16[48,256]{1,0:T(8,128)(2,1)S(1)}, bf16[48,256]{1,0:T(8,128)(2,1)S(1)}, u32[]{:S(2)}, u32[]{:S(2)}) collective-permute-start(bf16[48,256]{1,0:T(8,128)(2,1)S(1)} %get-tuple-element.28), channel_id=1, source_target_pairs={{0,12},{4,8},{8,4},{12,0},{1,13},{5,9},{9,5},{13,1},{2,14},{6,10},... | collective-permute-start | bytes 73736 | tf_op jit(solution)/shard_map/ppermute | solution.py:26
  17.9 4.5 %collective-permute-start.4 = (bf16[576,256]{1,0:T(8,128)(2,1)S(1)}, bf16[576,256]{1,0:T(8,128)(2,1)S(1)}, u32[]{:S(2)}, u32[]{:S(2)}) collective-permute-start(bf16[576,256]{1,0:T(8,128)(2,1)S(1)} %get-tuple-element.29), channel_id=1, source_target_pairs={{1,2},{2,1},{5,6},{6,5},{9,10},{10,9},{13,14},{14,13},{17,18},{18,... | collective-permute-start | bytes 884744 | tf_op jit(solution)/shard_map/ppermute | solution.py:37
  18.6 4.1 %collective-permute-start.5 = (bf16[576,256]{1,0:T(8,128)(2,1)S(1)}, bf16[576,256]{1,0:T(8,128)(2,1)S(1)}, u32[]{:S(2)}, u32[]{:S(2)}) collective-permute-start(bf16[576,256]{1,0:T(8,128)(2,1)S(1)} %get-tuple-element.30), channel_id=1, source_target_pairs={{0,1},{1,0},{2,3},{3,2},{4,5},{5,4},{6,7},{7,6},{8,9},{9,8},{10,11... | collective-permute-start | bytes 884744 | tf_op jit(solution)/shard_map/ppermute | solution.py:26
  26.3 4.4 %collective-permute-start.6 = (bf16[640,256]{1,0:T(8,128)(2,1)S(1)}, bf16[640,256]{1,0:T(8,128)(2,1)S(1)}, u32[]{:S(2)}, u32[]{:S(2)}) collective-permute-start(bf16[640,256]{1,0:T(8,128)(2,1)S(1)} %get-tuple-element.42), channel_id=1, source_target_pairs={{0,1},{1,0},{2,3},{3,2},{4,5},{5,4},{6,7},{7,6},{8,9},{9,8},{10,11... | collective-permute-start | bytes 983048 | tf_op jit(solution)/shard_map/ppermute | solution.py:26
  30.8 6.6 %collective-permute-start.7 = (bf16[320,256]{1,0:T(8,128)(2,1)S(1)}, bf16[320,256]{1,0:T(8,128)(2,1)S(1)}, u32[]{:S(2)}, u32[]{:S(2)}) collective-permute-start(bf16[320,256]{1,0:T(8,128)(2,1)S(1)} %dynamic-slice_convert_fusion), channel_id=1, source_target_pairs={{0,2},{1,3},{2,0},{3,1},{4,6},{5,7},{6,4},{7,5},{8,10},{9,11},{10,... | collective-permute-start | bytes 491528 | tf_op jit(solution)/shard_map/ppermute | solution.py:26
  37.4 6.5 %collective-permute-start.8 = (bf16[112,256]{1,0:T(8,128)(2,1)S(1)}, bf16[112,256]{1,0:T(8,128)(2,1)S(1)}, u32[]{:S(2)}, u32[]{:S(2)}) collective-permute-start(bf16[112,256]{1,0:T(8,128)(2,1)S(1)} %pad_maximum_fusion), channel_id=1, source_target_pairs={{0,4},{4,8},{8,12},{12,0},{1,5},{5,9},{9,13},{13,1},{2,6},{6,10},{... | collective-permute-start | bytes 172040 | tf_op jit(solution)/shard_map/ppermute | solution.py:31
  38.3 7.1 %collective-permute-start.9 = (bf16[112,256]{1,0:T(8,128)(2,1)S(1)}, bf16[112,256]{1,0:T(8,128)(2,1)S(1)}, u32[]{:S(2)}, u32[]{:S(2)}) collective-permute-start(bf16[112,256]{1,0:T(8,128)(2,1)S(1)} %pad_maximum_fusion.1), channel_id=1, source_target_pairs={{0,8},{4,12},{8,0},{12,4},{1,9},{5,13},{9,1},{13,5},{2,10},{6,14},... | collective-permute-start | bytes 172040 | tf_op jit(solution)/shard_map/ppermute | solution.py:31
  40.9 4.5 %collective-permute-start.10 = (bf16[112,256]{1,0:T(8,128)(2,1)S(1)}, bf16[112,256]{1,0:T(8,128)(2,1)S(1)}, u32[]{:S(2)}, u32[]{:S(2)}) collective-permute-start(bf16[112,256]{1,0:T(8,128)(2,1)S(1)} %pad_maximum_fusion.2), channel_id=1, source_target_pairs={{0,12},{4,0},{8,4},{12,8},{1,13},{5,1},{9,5},{13,9},{2,14},{6,2},{... | collective-permute-start | bytes 172040 | tf_op jit(solution)/shard_map/ppermute | solution.py:31
  45.5 14.7 %copy-start.16 = (f32[5]{0:T(128)S(1)}, f32[5]{0:T(128)}, u32[]{:S(2)}) copy-start(f32[5]{0:T(128)} %constant.106) | copy-start | bytes 64
  45.5 6.0 %collective-permute-start.11 = (bf16[80,256]{1,0:T(8,128)(2,1)S(1)}, bf16[80,256]{1,0:T(8,128)(2,1)S(1)}, u32[]{:S(2)}, u32[]{:S(2)}) collective-permute-start(bf16[80,256]{1,0:T(8,128)(2,1)S(1)} %get-tuple-element.44), channel_id=1, source_target_pairs={{0,4},{4,8},{8,12},{12,0},{1,5},{5,9},{9,13},{13,1},{2,6},{6,10},{... | collective-permute-start | bytes 122888 | tf_op jit(solution)/shard_map/ppermute | solution.py:31
  46.7 5.6 %collective-permute-start.12 = (bf16[80,256]{1,0:T(8,128)(2,1)S(1)}, bf16[80,256]{1,0:T(8,128)(2,1)S(1)}, u32[]{:S(2)}, u32[]{:S(2)}) collective-permute-start(bf16[80,256]{1,0:T(8,128)(2,1)S(1)} %get-tuple-element.44), channel_id=1, source_target_pairs={{0,8},{4,12},{8,0},{12,4},{1,9},{5,13},{9,1},{13,5},{2,10},{6,14},... | collective-permute-start | bytes 122888 | tf_op jit(solution)/shard_map/ppermute | solution.py:31
  48.8 4.0 %collective-permute-start.13 = (bf16[80,256]{1,0:T(8,128)(2,1)S(1)}, bf16[80,256]{1,0:T(8,128)(2,1)S(1)}, u32[]{:S(2)}, u32[]{:S(2)}) collective-permute-start(bf16[80,256]{1,0:T(8,128)(2,1)S(1)} %get-tuple-element.44), channel_id=1, source_target_pairs={{0,12},{4,0},{8,4},{12,8},{1,13},{5,1},{9,5},{13,9},{2,14},{6,2},{... | collective-permute-start | bytes 122888 | tf_op jit(solution)/shard_map/ppermute | solution.py:31
  52.8 5.3 %collective-permute-start.14 = (bf16[320,256]{1,0:T(8,128)(2,1)S(1)}, bf16[320,256]{1,0:T(8,128)(2,1)S(1)}, u32[]{:S(2)}, u32[]{:S(2)}) collective-permute-start(bf16[320,256]{1,0:T(8,128)(2,1)S(1)} %constant_dynamic-update-slice_fusion), channel_id=1, source_target_pairs={{0,2},{1,3},{2,0},{3,1},{4,6},{5,7},{6,4},{7,5},{8,10},{9,11},{10,... | collective-permute-start | bytes 491528 | tf_op jit(solution)/shard_map/ppermute | solution.py:26
  58.2 1.7 %collective-permute-start.15 = (bf16[640,256]{1,0:T(8,128)(2,1)S(1)}, bf16[640,256]{1,0:T(8,128)(2,1)S(1)}, u32[]{:S(2)}, u32[]{:S(2)}) collective-permute-start(bf16[640,256]{1,0:T(8,128)(2,1)S(1)} %maximum_select_fusion.1), channel_id=1, source_target_pairs={{0,1},{1,0},{2,3},{3,2},{4,5},{5,4},{6,7},{7,6},{8,9},{9,8},{10,11... | collective-permute-start | bytes 983048 | tf_op jit(solution)/shard_map/ppermute | solution.py:26
  (1 other events, 1.8 us)

commit v11 on v10

--- a/solution.py
+++ b/solution.py
@@ -157,9 +157,8 @@
         }
 
 
-def open_kernel(place_ref, out_ref):
-    out_ref[0] = place_ref[0]
-    out_ref[1] = place_ref[1]
+def open_kernel(out_ref):
+    out_ref[...] = jnp.zeros(out_ref.shape, jnp.int32)
 
 
 def pack_kernel(
@@ -173,6 +172,7 @@
     target_x_ref,
     target_y_ref,
     count_ref,
+    zero_ref,
     first_ref,
     second_ref,
     third_ref,
@@ -187,7 +187,7 @@
     target_x = target_x_ref[...]
     column = target_y_ref[...] - place_ref[1] * shape.tile_y
     slot = lax.broadcasted_iota(jnp.int32, (1, held), 1)
-    column = jnp.where(slot < count_ref[...], column, LANES - 1)
+    column = jnp.where(slot < count_ref[...] + zero_ref[0:1, 0:1], column, LANES - 1)
     line = lax.broadcasted_iota(jnp.int32, (16, held), 0)
     fields = jnp.where(line == 0, target_x // shape.tile_x, 0)
     fields = fields + jnp.where(line == 1, target_x % shape.tile_x, 0)
@@ -554,14 +554,7 @@
     long = struct((shape.halo + 2 * shape.edge + unit_rows + 16, channels), BF16)
     plain = struct((shape.halo + 2 * shape.edge, channels), BF16)
     short = struct((unit_rows + 16, channels), BF16)
-    (place,) = call(
-        open_kernel,
-        [struct((2,), jnp.int32)],
-        [place],
-        spaces="s",
-        out_space=pltpu.SMEM,
-        flops=LONG,
-    )
+    (zero,) = call(open_kernel, [struct((8, 128), jnp.int32)], [], flops=LONG)
     if whole_column:
         first, second, third, fourth, mesh, own_rows = call(
             functools.partial(pack_kernel, shape, units),
@@ -575,6 +568,7 @@
                 target_x.reshape(1, -1),
                 target_y.reshape(1, -1),
                 row_count.reshape(1, 1),
+                zero,
             ],
             spaces="s",
             flops=LONG,

time: 61.6 us -> 60.6 us (0.984)
  Pallas kernels: 7.4 us -> 6.27 us
    pallas_call x5, Pallas kernels: 7.4 us -> 6.27 us  [call(): pl.pallas_call(kernel, out_shape=tuple(out_shapes), in_specs=[pl.BlockSpe...]
  transfers between devices with their start and end apart: 16 -> 16, of which waited for: 13 -> 13; matrix products, arithmetic and copies ran while one was open for 1% -> 1% of each run, Pallas kernels for 1% -> 2%
where the time goes in v11:
time: 60.6 us; the launch traced here: 60.4 us
  starting transfers between devices  29.7 us (49%)
  waiting for transfers between devices  20.1 us (33%)
  Pallas kernels  6.27 us (10%)
  other arithmetic  2.48 us (4%)
  between operations  1.7 us (3%)
    ppermute x8, starting transfers between devices, swapped(): return lax.ppermute(block, axis, [(i, i ^ bits) for i in range(count)])  19.8 us
    ppermute x8, waiting for transfers between devices, swapped(): return lax.ppermute(block, axis, [(i, i ^ bits) for i in range(count)])  13.4 us
    ppermute x6, starting transfers between devices, shifted(): lax.ppermute(block, axis, [(i, (i + step) % count) for i in range(count)])  8.53 us
    ppermute x6, waiting for transfers between devices, shifted(): lax.ppermute(block, axis, [(i, (i + step) % count) for i in range(count)])  6.67 us
    pallas_call x5, Pallas kernels, call(): pl.pallas_call(kernel, out_shape=tuple(out_shapes), in_specs=[pl.BlockSpe...  6.27 us
    ppermute x2, starting transfers between devices, swapped_between(): return lax.ppermute(block, axis, pairs + [(j, i) for i, j in pairs])  1.34 us
    mul x1, other arithmetic, local(): totals.reshape(5, channels, channels).astype(F32) * scales[:, None, None]  1.24 us
  transfers between devices with their start and end apart: 16, of which 13 were waited for; matrix products, arithmetic and copies ran while one was open for 1% of the time, Pallas kernels for 2%

profile of v11, /device:TPU:0, one launch (start us, length us, event | category | flops | bytes accessed | tf_op | source)
XLA Modules:
  0.0 60.4 jit_solution(132006937973217126)
XLA Ops:
  1.7 0.7 %shard_map.194 = (bf16[368,256]{1,0:T(8,128)(2,1)S(1)}, bf16[320,256]{1,0:T(8,128)(2,1)S(1)}, bf16[48,256]{1,0:T(8,128)(2,1)S(1)}, bf16[48,256]{1,0:T(8,128)(2,1...) custom-call(s32[2]{0:T(128)S(1)} %pad_add_fusion.place_ref.refs_0_, bf16[512,256]{1,0:T(8,128)(2,1)S(1)} %bitcast.21, ...), custom_call_target="tpu_custom_call" | custom-call | flops 10000000000 | bytes 762636 | tf_op jit(solution)/shard_map/pallas_call | solution.py:466
  2.5 3.1 %collective-permute-start = (bf16[368,256]{1,0:T(8,128)(2,1)S(1)}, bf16[368,256]{1,0:T(8,128)(2,1)S(1)}, u32[]{:S(2)}, u32[]{:S(2)}) collective-permute-start(bf16[368,256]{1,0:T(8,128)(2,1)S(1)} %get-tuple-element.25), channel_id=1, source_target_pairs={{0,4},{4,0},{8,12},{12,8},{1,5},{5,1},{9,13},{13,9},{2,6},{6,2},{1... | collective-permute-start | bytes 565256 | tf_op jit(solution)/shard_map/ppermute | solution.py:26
  5.5 0.7 %collective-permute-start.1 = (bf16[320,256]{1,0:T(8,128)(2,1)S(1)}, bf16[320,256]{1,0:T(8,128)(2,1)S(1)}, u32[]{:S(2)}, u32[]{:S(2)}) collective-permute-start(bf16[320,256]{1,0:T(8,128)(2,1)S(1)} %get-tuple-element.26), channel_id=1, source_target_pairs={{4,8},{8,4},{5,9},{9,5},{6,10},{10,6},{7,11},{11,7},{20,24},{24,20... | collective-permute-start | bytes 491528 | tf_op jit(solution)/shard_map/ppermute | solution.py:37
  6.2 3.9 %collective-permute-start.2 = (bf16[48,256]{1,0:T(8,128)(2,1)S(1)}, bf16[48,256]{1,0:T(8,128)(2,1)S(1)}, u32[]{:S(2)}, u32[]{:S(2)}) collective-permute-start(bf16[48,256]{1,0:T(8,128)(2,1)S(1)} %get-tuple-element.27), channel_id=1, source_target_pairs={{0,8},{4,12},{8,0},{12,4},{1,9},{5,13},{9,1},{13,5},{2,10},{6,14},... | collective-permute-start | bytes 73736 | tf_op jit(solution)/shard_map/ppermute | solution.py:26
  10.1 2.9 %collective-permute-start.3 = (bf16[48,256]{1,0:T(8,128)(2,1)S(1)}, bf16[48,256]{1,0:T(8,128)(2,1)S(1)}, u32[]{:S(2)}, u32[]{:S(2)}) collective-permute-start(bf16[48,256]{1,0:T(8,128)(2,1)S(1)} %get-tuple-element.28), channel_id=1, source_target_pairs={{0,12},{4,8},{8,4},{12,0},{1,13},{5,9},{9,5},{13,1},{2,14},{6,10},... | collective-permute-start | bytes 73736 | tf_op jit(solution)/shard_map/ppermute | solution.py:26
  13.0 2.5 %collective-permute-done.2.refs_8_ = bf16[48,256]{1,0:T(8,128)(2,1)S(1)} collective-permute-done((bf16[48,256]{1,0:T(8,128)(2,1)S(1)}, bf16[48,256]{1,0:T(8,128)(2,1)S(1)}, u32[]{:S(2)}, u32[]{:S(2)}) %collective-permute-start.2) | collective-permute-done | bytes 24608 | tf_op jit(solution)/shard_map/ppermute | solution.py:26
  15.5 0.3 collective-permute-done.3.refs_9_
  15.9 1.0 %shard_map.195 = (bf16[1088,256]{1,0:T(8,128)(2,1)S(1)}, bf16[576,256]{1,0:T(8,128)(2,1)S(1)}, bf16[576,256]{1,0:T(8,128)(2,1)S(1)}, bf16[128,256]{1,0:T(8,128)(...) custom-call(s32[2]{0:T(128)S(1)} %pad_add_fusion.place_ref.refs_0_, bf16[512,256]{1,0:T(8,128)(2,1)S(1)} %bitcast.22, ...), custom_call_target="tpu_custom_call" | custom-call | flops 71303168 | bytes 2150408 | tf_op jit(solution)/shard_map/pallas_call | solution.py:466
  16.9 0.7 %collective-permute-start.4 = (bf16[576,256]{1,0:T(8,128)(2,1)S(1)}, bf16[576,256]{1,0:T(8,128)(2,1)S(1)}, u32[]{:S(2)}, u32[]{:S(2)}) collective-permute-start(bf16[576,256]{1,0:T(8,128)(2,1)S(1)} %get-tuple-element.29), channel_id=1, source_target_pairs={{1,2},{2,1},{5,6},{6,5},{9,10},{10,9},{13,14},{14,13},{17,18},{18,... | collective-permute-start | bytes 884744 | tf_op jit(solution)/shard_map/ppermute | solution.py:37
  17.6 2.9 %collective-permute-start.5 = (bf16[576,256]{1,0:T(8,128)(2,1)S(1)}, bf16[576,256]{1,0:T(8,128)(2,1)S(1)}, u32[]{:S(2)}, u32[]{:S(2)}) collective-permute-start(bf16[576,256]{1,0:T(8,128)(2,1)S(1)} %get-tuple-element.30), channel_id=1, source_target_pairs={{0,1},{1,0},{2,3},{3,2},{4,5},{5,4},{6,7},{7,6},{8,9},{9,8},{10,11... | collective-permute-start | bytes 884744 | tf_op jit(solution)/shard_map/ppermute | solution.py:26
  20.5 0.9 %shard_map.196 = (bf16[1088,256]{1,0:T(8,128)(2,1)S(1)}, bf16[512,256]{1,0:T(8,128)(2,1)S(1)}, f32[512,256]{1,0:T(8,128)S(1)}, f32[512,256]{1,0:T(8,128)S(1)}) custom-call(bf16[1088,256]{1,0:T(8,128)(2,1)S(1)} %get-tuple-element.32.blended_ref.refs_4_, bf16[256,256]{1,0:T(8,128)(2,1)S(1)} %copy-done.3, bf16[256,256]{1,0:T(8,128)(2,1)S(1)} %copy-done.4), custom_call_target="tpu_custom_call" | custom-call | flops 285212672 | bytes 2686976 | tf_op jit(solution)/shard_map/pallas_call | solution.py:466
  21.7 3.6 %shard_map.197 = (bf16[512,256]{1,0:T(8,128)(2,1)}, bf16[128,256]{1,0:T(8,128)(2,1)S(1)}, bf16[640,256]{1,0:T(8,128)(2,1)S(1)}, f32[640,256]{1,0:T(8,128)S(1)}) custom-call(s32[1]{0:T(128)} %bitcast.refs_0_, bf16[576,256]{1,0:T(8,128)(2,1)S(1)} %collective-permute-done.4.refs_1_, bf16[576,256]{1,0:T(8,128)(2,1)S(1)} %collective-permute-done.5.refs_2_, ...), custom_call_target="tpu_custom_call" | custom-call | flops 402653184 | bytes 5525508 | tf_op jit(solution)/shard_map/pallas_call | solution.py:466
  25.3 3.1 %collective-permute-start.6 = (bf16[640,256]{1,0:T(8,128)(2,1)S(1)}, bf16[640,256]{1,0:T(8,128)(2,1)S(1)}, u32[]{:S(2)}, u32[]{:S(2)}) collective-permute-start(bf16[640,256]{1,0:T(8,128)(2,1)S(1)} %get-tuple-element.42), channel_id=1, source_target_pairs={{0,1},{1,0},{2,3},{3,2},{4,5},{5,4},{6,7},{7,6},{8,9},{9,8},{10,11... | collective-permute-start | bytes 983048 | tf_op jit(solution)/shard_map/ppermute | solution.py:26
  28.5 1.3 %collective-permute-done.6 = bf16[640,256]{1,0:T(8,128)(2,1)S(1)} collective-permute-done((bf16[640,256]{1,0:T(8,128)(2,1)S(1)}, bf16[640,256]{1,0:T(8,128)(2,1)S(1)}, u32[]{:S(2)}, u32[]{:S(2)}) %collective-permute-start.6) | collective-permute-done | bytes 327712 | tf_op jit(solution)/shard_map/ppermute | solution.py:26
  29.8 2.1 %collective-permute-start.7 = (bf16[320,256]{1,0:T(8,128)(2,1)S(1)}, bf16[320,256]{1,0:T(8,128)(2,1)S(1)}, u32[]{:S(2)}, u32[]{:S(2)}) collective-permute-start(bf16[320,256]{1,0:T(8,128)(2,1)S(1)} %dynamic-slice_convert_fusion), channel_id=1, source_target_pairs={{0,2},{1,3},{2,0},{3,1},{4,6},{5,7},{6,4},{7,5},{8,10},{9,11},{10,... | collective-permute-start | bytes 491528 | tf_op jit(solution)/shard_map/ppermute | solution.py:26
  31.9 4.5 %collective-permute-done.7 = bf16[320,256]{1,0:T(8,128)(2,1)S(1)} collective-permute-done((bf16[320,256]{1,0:T(8,128)(2,1)S(1)}, bf16[320,256]{1,0:T(8,128)(2,1)S(1)}, u32[]{:S(2)}, u32[]{:S(2)}) %collective-permute-start.7) | collective-permute-done | bytes 163872 | tf_op jit(solution)/shard_map/ppermute | solution.py:26
  36.5 0.8 %collective-permute-start.8 = (bf16[112,256]{1,0:T(8,128)(2,1)S(1)}, bf16[112,256]{1,0:T(8,128)(2,1)S(1)}, u32[]{:S(2)}, u32[]{:S(2)}) collective-permute-start(bf16[112,256]{1,0:T(8,128)(2,1)S(1)} %pad_maximum_fusion), channel_id=1, source_target_pairs={{0,4},{4,8},{8,12},{12,0},{1,5},{5,9},{9,13},{13,1},{2,6},{6,10},{... | collective-permute-start | bytes 172040 | tf_op jit(solution)/shard_map/ppermute | solution.py:31
  37.3 2.6 %collective-permute-start.9 = (bf16[112,256]{1,0:T(8,128)(2,1)S(1)}, bf16[112,256]{1,0:T(8,128)(2,1)S(1)}, u32[]{:S(2)}, u32[]{:S(2)}) collective-permute-start(bf16[112,256]{1,0:T(8,128)(2,1)S(1)} %pad_maximum_fusion.1), channel_id=1, source_target_pairs={{0,8},{4,12},{8,0},{12,4},{1,9},{5,13},{9,1},{13,5},{2,10},{6,14},... | collective-permute-start | bytes 172040 | tf_op jit(solution)/shard_map/ppermute | solution.py:31
  39.9 1.2 %collective-permute-start.10 = (bf16[112,256]{1,0:T(8,128)(2,1)S(1)}, bf16[112,256]{1,0:T(8,128)(2,1)S(1)}, u32[]{:S(2)}, u32[]{:S(2)}) collective-permute-start(bf16[112,256]{1,0:T(8,128)(2,1)S(1)} %pad_maximum_fusion.2), channel_id=1, source_target_pairs={{0,12},{4,0},{8,4},{12,8},{1,13},{5,1},{9,5},{13,9},{2,14},{6,2},{... | collective-permute-start | bytes 172040 | tf_op jit(solution)/shard_map/ppermute | solution.py:31
  41.1 1.9 %collective-permute-done.8 = bf16[112,256]{1,0:T(8,128)(2,1)S(1)} collective-permute-done((bf16[112,256]{1,0:T(8,128)(2,1)S(1)}, bf16[112,256]{1,0:T(8,128)(2,1)S(1)}, u32[]{:S(2)}, u32[]{:S(2)}) %collective-permute-start.8) | collective-permute-done | bytes 57376 | tf_op jit(solution)/shard_map/ppermute | solution.py:31
  43.0 1.3 %collective-permute-done.9 = bf16[112,256]{1,0:T(8,128)(2,1)S(1)} collective-permute-done((bf16[112,256]{1,0:T(8,128)(2,1)S(1)}, bf16[112,256]{1,0:T(8,128)(2,1)S(1)}, u32[]{:S(2)}, u32[]{:S(2)}) %collective-permute-start.9) | collective-permute-done | bytes 57376 | tf_op jit(solution)/shard_map/ppermute | solution.py:31
  44.5 1.1 %collective-permute-start.11 = (bf16[80,256]{1,0:T(8,128)(2,1)S(1)}, bf16[80,256]{1,0:T(8,128)(2,1)S(1)}, u32[]{:S(2)}, u32[]{:S(2)}) collective-permute-start(bf16[80,256]{1,0:T(8,128)(2,1)S(1)} %get-tuple-element.44), channel_id=1, source_target_pairs={{0,4},{4,8},{8,12},{12,0},{1,5},{5,9},{9,13},{13,1},{2,6},{6,10},{... | collective-permute-start | bytes 122888 | tf_op jit(solution)/shard_map/ppermute | solution.py:31
  45.7 2.1 %collective-permute-start.12 = (bf16[80,256]{1,0:T(8,128)(2,1)S(1)}, bf16[80,256]{1,0:T(8,128)(2,1)S(1)}, u32[]{:S(2)}, u32[]{:S(2)}) collective-permute-start(bf16[80,256]{1,0:T(8,128)(2,1)S(1)} %get-tuple-element.44), channel_id=1, source_target_pairs={{0,8},{4,12},{8,0},{12,4},{1,9},{5,13},{9,1},{13,5},{2,10},{6,14},... | collective-permute-start | bytes 122888 | tf_op jit(solution)/shard_map/ppermute | solution.py:31
  47.8 0.6 %collective-permute-start.13 = (bf16[80,256]{1,0:T(8,128)(2,1)S(1)}, bf16[80,256]{1,0:T(8,128)(2,1)S(1)}, u32[]{:S(2)}, u32[]{:S(2)}) collective-permute-start(bf16[80,256]{1,0:T(8,128)(2,1)S(1)} %get-tuple-element.44), channel_id=1, source_target_pairs={{0,12},{4,0},{8,4},{12,8},{1,13},{5,1},{9,5},{13,9},{2,14},{6,2},{... | collective-permute-start | bytes 122888 | tf_op jit(solution)/shard_map/ppermute | solution.py:31
  48.4 2.2 %collective-permute-done.11 = bf16[80,256]{1,0:T(8,128)(2,1)S(1)} collective-permute-done((bf16[80,256]{1,0:T(8,128)(2,1)S(1)}, bf16[80,256]{1,0:T(8,128)(2,1)S(1)}, u32[]{:S(2)}, u32[]{:S(2)}) %collective-permute-start.11) | collective-permute-done | bytes 40992 | tf_op jit(solution)/shard_map/ppermute | solution.py:31
  50.6 0.7 %collective-permute-done.12 = bf16[80,256]{1,0:T(8,128)(2,1)S(1)} collective-permute-done((bf16[80,256]{1,0:T(8,128)(2,1)S(1)}, bf16[80,256]{1,0:T(8,128)(2,1)S(1)}, u32[]{:S(2)}, u32[]{:S(2)}) %collective-permute-start.12) | collective-permute-done | bytes 40992 | tf_op jit(solution)/shard_map/ppermute | solution.py:31
  51.3 0.5 collective-permute-done.13
  51.8 1.7 %collective-permute-start.14 = (bf16[320,256]{1,0:T(8,128)(2,1)S(1)}, bf16[320,256]{1,0:T(8,128)(2,1)S(1)}, u32[]{:S(2)}, u32[]{:S(2)}) collective-permute-start(bf16[320,256]{1,0:T(8,128)(2,1)S(1)} %constant_dynamic-update-slice_fusion), channel_id=1, source_target_pairs={{0,2},{1,3},{2,0},{3,1},{4,6},{5,7},{6,4},{7,5},{8,10},{9,11},{10,... | collective-permute-start | bytes 491528 | tf_op jit(solution)/shard_map/ppermute | solution.py:26
  53.6 3.6 %collective-permute-done.14 = bf16[320,256]{1,0:T(8,128)(2,1)S(1)} collective-permute-done((bf16[320,256]{1,0:T(8,128)(2,1)S(1)}, bf16[320,256]{1,0:T(8,128)(2,1)S(1)}, u32[]{:S(2)}, u32[]{:S(2)}) %collective-permute-start.14) | collective-permute-done | bytes 163872 | tf_op jit(solution)/shard_map/ppermute | solution.py:26
  57.4 0.6 %fusion.1 = bf16[32,256]{1,0:T(8,128)(2,1)} fusion(f32[112,256]{1,0:T(8,128)S(1)} %convert_element_type.43, f32[112,256]{1,0:T(8,128)S(1)} %convert_element_type.42, f32[112,256]{1,0:T(8,128)S(1)} %convert_element_type.41, bf16[128,256]{1,0:T(8,128)(2,1)S(1)} %get-tuple-element.40), kind=kLoop, calls=%fused_computation.14 | loop fusion | flops 40960 | bytes 131072 | tf_op jit(solution)/shard_map/convert_element_type | solution.py:711
  58.0 1.0 %collective-permute-done.15 = bf16[640,256]{1,0:T(8,128)(2,1)S(1)} collective-permute-done((bf16[640,256]{1,0:T(8,128)(2,1)S(1)}, bf16[640,256]{1,0:T(8,128)(2,1)S(1)}, u32[]{:S(2)}, u32[]{:S(2)}) %collective-permute-start.15) | collective-permute-done | bytes 327712 | tf_op jit(solution)/shard_map/ppermute | solution.py:26
  59.2 1.2 %convert_multiply_fusion = f32[5,256,256]{2,1,0:T(8,128)} fusion(bf16[5,256,256]{2,1,0:T(8,128)(2,1)S(1)} %bitcast.28, f32[5]{0:T(128)S(1)} %copy-done.16), kind=kLoop, calls=%fused_computation | loop fusion | flops 655360 | bytes 1966100 | tf_op jit(solution)/shard_map/mul | solution.py:732
  (60 shorter events, 1.3 us)
Async XLA Ops:
  0.6 1.0 %copy-start.1 = (bf16[16,32,256]{2,1,0:T(8,128)(2,1)S(1)}, bf16[16,32,256]{2,1,0:T(8,128)(2,1)}, u32[]{:S(2)}) copy-start(bf16[16,32,256]{2,1,0:T(8,128)(2,1)} %param.18) | copy-start | bytes 786436
  0.6 0.9 %copy-start.11 = (bf16[4,8,256]{2,1,0:T(8,128)(2,1)S(1)}, bf16[4,8,256]{2,1,0:T(8,128)(2,1)}, u32[]{:S(2)}) copy-start(bf16[4,8,256]{2,1,0:T(8,128)(2,1)} %param.24) | copy-start | bytes 49156
  0.7 0.9 %copy-start.12 = (s32[36,4,8]{0,2,1:T(8,128)S(1)}, s32[36,4,8]{0,2,1:T(8,128)}, u32[]{:S(2)}) copy-start(s32[36,4,8]{0,2,1:T(8,128)} %param.23) | copy-start | bytes 13828
  0.7 0.9 %copy-start.13 = (bf16[32,256]{1,0:T(8,128)(2,1)S(1)}, bf16[32,256]{1,0:T(8,128)(2,1)}, u32[]{:S(2)}) copy-start(bf16[32,256]{1,0:T(8,128)(2,1)} %rows_ref.1) | copy-start | bytes 49156
  0.7 0.9 %copy-start.14 = (s32[32]{0:T(128)S(1)}, s32[32]{0:T(128)}, u32[]{:S(2)}) copy-start(s32[32]{0:T(128)} %param.21) | copy-start | bytes 388
  1.6 14.3 %copy-start = (bf16[256,256]{1,0:T(8,128)(2,1)S(1)}, bf16[256,256]{1,0:T(8,128)(2,1)}, u32[]{:S(2)}) copy-start(bf16[256,256]{1,0:T(8,128)(2,1)} %refs_15_.1) | copy-start | bytes 393220
  1.6 14.2 %copy-start.10 = (bf16[2,32,128]{2,1,0:T(8,128)(2,1)S(1)}, bf16[2,32,128]{2,1,0:T(8,128)(2,1)}, u32[]{:S(2)}) copy-start(bf16[2,32,128]{2,1,0:T(8,128)(2,1)} %constant.97.clone.refs_4_) | copy-start | bytes 49156
  1.6 18.9 %copy-start.3 = (bf16[256,256]{1,0:T(8,128)(2,1)S(1)}, bf16[256,256]{1,0:T(8,128)(2,1)}, u32[]{:S(2)}) copy-start(bf16[256,256]{1,0:T(8,128)(2,1)} %refs_16_.1) | copy-start | bytes 393220
  1.6 18.9 %copy-start.4 = (bf16[256,256]{1,0:T(8,128)(2,1)S(1)}, bf16[256,256]{1,0:T(8,128)(2,1)}, u32[]{:S(2)}) copy-start(bf16[256,256]{1,0:T(8,128)(2,1)} %refs_17_.1) | copy-start | bytes 393220
  2.4 19.3 %copy-start.2 = (bf16[2,128,384]{2,1,0:T(8,128)(2,1)S(1)}, bf16[2,128,384]{2,1,0:T(8,128)(2,1)}, u32[]{:S(2)}) copy-start(bf16[2,128,384]{2,1,0:T(8,128)(2,1)} %constant.99.clone.refs_12_) | copy-start | bytes 589828
  2.4 19.3 %copy-start.5 = (bf16[256,256]{1,0:T(8,128)(2,1)S(1)}, bf16[256,256]{1,0:T(8,128)(2,1)}, u32[]{:S(2)}) copy-start(bf16[256,256]{1,0:T(8,128)(2,1)} %refs_18_.1) | copy-start | bytes 393220
  2.4 19.3 %copy-start.6 = (bf16[256,256]{1,0:T(8,128)(2,1)S(1)}, bf16[256,256]{1,0:T(8,128)(2,1)}, u32[]{:S(2)}) copy-start(bf16[256,256]{1,0:T(8,128)(2,1)} %refs_19_.1) | copy-start | bytes 393220
  2.4 19.3 %copy-start.7 = (bf16[2,128,192]{2,1,0:T(8,128)(2,1)S(1)}, bf16[2,128,192]{2,1,0:T(8,128)(2,1)}, u32[]{:S(2)}) copy-start(bf16[2,128,192]{2,1,0:T(8,128)(2,1)} %constant.98.clone.refs_11_) | copy-start | bytes 294916
  2.4 19.3 %copy-start.8 = (bf16[128,256]{1,0:T(8,128)(2,1)S(1)}, bf16[128,256]{1,0:T(8,128)(2,1)}, u32[]{:S(2)}) copy-start(bf16[128,256]{1,0:T(8,128)(2,1)} %constant.101.clone.refs_14_) | copy-start | bytes 196612
  2.4 19.3 %copy-start.9 = (f32[2,16,384]{2,1,0:T(8,128)S(1)}, f32[2,16,384]{2,1,0:T(8,128)}, u32[]{:S(2)}) copy-start(f32[2,16,384]{2,1,0:T(8,128)} %constant.100.clone.refs_13_) | copy-start | bytes 147460
  2.5 13.4 %collective-permute-start = (bf16[368,256]{1,0:T(8,128)(2,1)S(1)}, bf16[368,256]{1,0:T(8,128)(2,1)S(1)}, u32[]{:S(2)}, u32[]{:S(2)}) collective-permute-start(bf16[368,256]{1,0:T(8,128)(2,1)S(1)} %get-tuple-element.25), channel_id=1, source_target_pairs={{0,4},{4,0},{8,12},{12,8},{1,5},{5,1},{9,13},{13,9},{2,6},{6,2},{1... | collective-permute-start | bytes 565256 | tf_op jit(solution)/shard_map/ppermute | solution.py:26
  5.5 10.3 %collective-permute-start.1 = (bf16[320,256]{1,0:T(8,128)(2,1)S(1)}, bf16[320,256]{1,0:T(8,128)(2,1)S(1)}, u32[]{:S(2)}, u32[]{:S(2)}) collective-permute-start(bf16[320,256]{1,0:T(8,128)(2,1)S(1)} %get-tuple-element.26), channel_id=1, source_target_pairs={{4,8},{8,4},{5,9},{9,5},{6,10},{10,6},{7,11},{11,7},{20,24},{24,20... | collective-permute-start | bytes 491528 | tf_op jit(solution)/shard_map/ppermute | solution.py:37
  6.2 9.3 %collective-permute-start.2 = (bf16[48,256]{1,0:T(8,128)(2,1)S(1)}, bf16[48,256]{1,0:T(8,128)(2,1)S(1)}, u32[]{:S(2)}, u32[]{:S(2)}) collective-permute-start(bf16[48,256]{1,0:T(8,128)(2,1)S(1)} %get-tuple-element.27), channel_id=1, source_target_pairs={{0,8},{4,12},{8,0},{12,4},{1,9},{5,13},{9,1},{13,5},{2,10},{6,14},... | collective-permute-start | bytes 73736 | tf_op jit(solution)/shard_map/ppermute | solution.py:26
  10.1 5.7 %collective-permute-start.3 = (bf16[48,256]{1,0:T(8,128)(2,1)S(1)}, bf16[48,256]{1,0:T(8,128)(2,1)S(1)}, u32[]{:S(2)}, u32[]{:S(2)}) collective-permute-start(bf16[48,256]{1,0:T(8,128)(2,1)S(1)} %get-tuple-element.28), channel_id=1, source_target_pairs={{0,12},{4,8},{8,4},{12,0},{1,13},{5,9},{9,5},{13,1},{2,14},{6,10},... | collective-permute-start | bytes 73736 | tf_op jit(solution)/shard_map/ppermute | solution.py:26
  16.9 4.5 %collective-permute-start.4 = (bf16[576,256]{1,0:T(8,128)(2,1)S(1)}, bf16[576,256]{1,0:T(8,128)(2,1)S(1)}, u32[]{:S(2)}, u32[]{:S(2)}) collective-permute-start(bf16[576,256]{1,0:T(8,128)(2,1)S(1)} %get-tuple-element.29), channel_id=1, source_target_pairs={{1,2},{2,1},{5,6},{6,5},{9,10},{10,9},{13,14},{14,13},{17,18},{18,... | collective-permute-start | bytes 884744 | tf_op jit(solution)/shard_map/ppermute | solution.py:37
  17.6 4.1 %collective-permute-start.5 = (bf16[576,256]{1,0:T(8,128)(2,1)S(1)}, bf16[576,256]{1,0:T(8,128)(2,1)S(1)}, u32[]{:S(2)}, u32[]{:S(2)}) collective-permute-start(bf16[576,256]{1,0:T(8,128)(2,1)S(1)} %get-tuple-element.30), channel_id=1, source_target_pairs={{0,1},{1,0},{2,3},{3,2},{4,5},{5,4},{6,7},{7,6},{8,9},{9,8},{10,11... | collective-permute-start | bytes 884744 | tf_op jit(solution)/shard_map/ppermute | solution.py:26
  25.3 4.4 %collective-permute-start.6 = (bf16[640,256]{1,0:T(8,128)(2,1)S(1)}, bf16[640,256]{1,0:T(8,128)(2,1)S(1)}, u32[]{:S(2)}, u32[]{:S(2)}) collective-permute-start(bf16[640,256]{1,0:T(8,128)(2,1)S(1)} %get-tuple-element.42), channel_id=1, source_target_pairs={{0,1},{1,0},{2,3},{3,2},{4,5},{5,4},{6,7},{7,6},{8,9},{9,8},{10,11... | collective-permute-start | bytes 983048 | tf_op jit(solution)/shard_map/ppermute | solution.py:26
  29.8 6.6 %collective-permute-start.7 = (bf16[320,256]{1,0:T(8,128)(2,1)S(1)}, bf16[320,256]{1,0:T(8,128)(2,1)S(1)}, u32[]{:S(2)}, u32[]{:S(2)}) collective-permute-start(bf16[320,256]{1,0:T(8,128)(2,1)S(1)} %dynamic-slice_convert_fusion), channel_id=1, source_target_pairs={{0,2},{1,3},{2,0},{3,1},{4,6},{5,7},{6,4},{7,5},{8,10},{9,11},{10,... | collective-permute-start | bytes 491528 | tf_op jit(solution)/shard_map/ppermute | solution.py:26
  36.5 6.5 %collective-permute-start.8 = (bf16[112,256]{1,0:T(8,128)(2,1)S(1)}, bf16[112,256]{1,0:T(8,128)(2,1)S(1)}, u32[]{:S(2)}, u32[]{:S(2)}) collective-permute-start(bf16[112,256]{1,0:T(8,128)(2,1)S(1)} %pad_maximum_fusion), channel_id=1, source_target_pairs={{0,4},{4,8},{8,12},{12,0},{1,5},{5,9},{9,13},{13,1},{2,6},{6,10},{... | collective-permute-start | bytes 172040 | tf_op jit(solution)/shard_map/ppermute | solution.py:31
  37.3 7.1 %collective-permute-start.9 = (bf16[112,256]{1,0:T(8,128)(2,1)S(1)}, bf16[112,256]{1,0:T(8,128)(2,1)S(1)}, u32[]{:S(2)}, u32[]{:S(2)}) collective-permute-start(bf16[112,256]{1,0:T(8,128)(2,1)S(1)} %pad_maximum_fusion.1), channel_id=1, source_target_pairs={{0,8},{4,12},{8,0},{12,4},{1,9},{5,13},{9,1},{13,5},{2,10},{6,14},... | collective-permute-start | bytes 172040 | tf_op jit(solution)/shard_map/ppermute | solution.py:31
  39.9 4.5 %collective-permute-start.10 = (bf16[112,256]{1,0:T(8,128)(2,1)S(1)}, bf16[112,256]{1,0:T(8,128)(2,1)S(1)}, u32[]{:S(2)}, u32[]{:S(2)}) collective-permute-start(bf16[112,256]{1,0:T(8,128)(2,1)S(1)} %pad_maximum_fusion.2), channel_id=1, source_target_pairs={{0,12},{4,0},{8,4},{12,8},{1,13},{5,1},{9,5},{13,9},{2,14},{6,2},{... | collective-permute-start | bytes 172040 | tf_op jit(solution)/shard_map/ppermute | solution.py:31
  44.5 14.7 %copy-start.16 = (f32[5]{0:T(128)S(1)}, f32[5]{0:T(128)}, u32[]{:S(2)}) copy-start(f32[5]{0:T(128)} %constant.106) | copy-start | bytes 64
  44.5 6.0 %collective-permute-start.11 = (bf16[80,256]{1,0:T(8,128)(2,1)S(1)}, bf16[80,256]{1,0:T(8,128)(2,1)S(1)}, u32[]{:S(2)}, u32[]{:S(2)}) collective-permute-start(bf16[80,256]{1,0:T(8,128)(2,1)S(1)} %get-tuple-element.44), channel_id=1, source_target_pairs={{0,4},{4,8},{8,12},{12,0},{1,5},{5,9},{9,13},{13,1},{2,6},{6,10},{... | collective-permute-start | bytes 122888 | tf_op jit(solution)/shard_map/ppermute | solution.py:31
  45.7 5.6 %collective-permute-start.12 = (bf16[80,256]{1,0:T(8,128)(2,1)S(1)}, bf16[80,256]{1,0:T(8,128)(2,1)S(1)}, u32[]{:S(2)}, u32[]{:S(2)}) collective-permute-start(bf16[80,256]{1,0:T(8,128)(2,1)S(1)} %get-tuple-element.44), channel_id=1, source_target_pairs={{0,8},{4,12},{8,0},{12,4},{1,9},{5,13},{9,1},{13,5},{2,10},{6,14},... | collective-permute-start | bytes 122888 | tf_op jit(solution)/shard_map/ppermute | solution.py:31
  47.8 4.0 %collective-permute-start.13 = (bf16[80,256]{1,0:T(8,128)(2,1)S(1)}, bf16[80,256]{1,0:T(8,128)(2,1)S(1)}, u32[]{:S(2)}, u32[]{:S(2)}) collective-permute-start(bf16[80,256]{1,0:T(8,128)(2,1)S(1)} %get-tuple-element.44), channel_id=1, source_target_pairs={{0,12},{4,0},{8,4},{12,8},{1,13},{5,1},{9,5},{13,9},{2,14},{6,2},{... | collective-permute-start | bytes 122888 | tf_op jit(solution)/shard_map/ppermute | solution.py:31
  51.8 5.3 %collective-permute-start.14 = (bf16[320,256]{1,0:T(8,128)(2,1)S(1)}, bf16[320,256]{1,0:T(8,128)(2,1)S(1)}, u32[]{:S(2)}, u32[]{:S(2)}) collective-permute-start(bf16[320,256]{1,0:T(8,128)(2,1)S(1)} %constant_dynamic-update-slice_fusion), channel_id=1, source_target_pairs={{0,2},{1,3},{2,0},{3,1},{4,6},{5,7},{6,4},{7,5},{8,10},{9,11},{10,... | collective-permute-start | bytes 491528 | tf_op jit(solution)/shard_map/ppermute | solution.py:26
  57.3 1.7 %collective-permute-start.15 = (bf16[640,256]{1,0:T(8,128)(2,1)S(1)}, bf16[640,256]{1,0:T(8,128)(2,1)S(1)}, u32[]{:S(2)}, u32[]{:S(2)}) collective-permute-start(bf16[640,256]{1,0:T(8,128)(2,1)S(1)} %maximum_select_fusion.1), channel_id=1, source_target_pairs={{0,1},{1,0},{2,3},{3,2},{4,5},{5,4},{6,7},{7,6},{8,9},{9,8},{10,11... | collective-permute-start | bytes 983048 | tf_op jit(solution)/shard_map/ppermute | solution.py:26
  (1 other events, 0.9 us)
